TPU v7x, 512 devices: a whole 4x4x16 slice. The times are simulated.
512 devices in a mesh: node: 16 (over z), ingroup: 32 (over y, x, core).
Axes of the slice: x: 4, y: 4, z: 16, core: 2. Of those that a mesh axis runs over, the one named last changes fastest.
Arguments:
- tokens: bfloat16 [2048, 7168], P(('node', 'ingroup')), may hold values from -6 to 6
- cotangent: bfloat16 [2048, 7168], P(('node', 'ingroup')), may hold values from -6 to 6
- groups: int32 [2048, 2], P(('node', 'ingroup')), may hold values from 0 to 15, as said below
- choices: int32 [2048, 2, 2], P(('node', 'ingroup')), may hold values from 0 to 3, as said below
- gates: bfloat16 [2048, 2, 2], P(('node', 'ingroup')), may hold values from 0.049804688 to 1
- up_weight: bfloat16 [7168, 65536], P(None, ('node', 'ingroup')), may hold values from -0.0625 to 0.0625
- down_weight: bfloat16 [65536, 7168], P(('node', 'ingroup')), may hold values from -0.1875 to 0.1875
Outputs:
- mixed: bfloat16 [2048, 7168], P(('node', 'ingroup'))
- grad_tokens: bfloat16 [2048, 7168], P(('node', 'ingroup'))
- grad_gates: bfloat16 [2048, 2, 2], P(('node', 'ingroup'))
Inputs may be any that keep to these rules, and one draw needn't show every extreme that they name: The two groups of a token differ. The tokens of one device name one group at most 1 times, and some device reaches that. Over all devices of one ingroup index, exactly 8 token-group pairs name each group; in some groups, at every ingroup index, all 8 of them name one common expert. `choices`: the two experts named within one group differ.
All inputs are finite; a program needn't handle non-finite values.
Results may differ from a plain program's by a relative error of at most 0.02.
Values may be sent and summed in bfloat16 or wider, within the bound.
No kernel may reach another device: no remote copies, remote signals or barrier semaphores. Data moves between devices by JAX's collectives and lax.ppermute only.
A program may use at most 64 MiB of HBM per device.

v0:
```python
import jax
import jax.numpy as jnp
from jax import lax
from jax.sharding import PartitionSpec as P

EXP_NODE = 4


def per_device(tokens, cotangent, groups, choices, gates, up_weight, down_weight):
    tok_count = tokens.shape[0]
    width = tokens.shape[1]
    nodes = lax.axis_size("node")
    members = lax.axis_size("ingroup")
    slices = members // EXP_NODE
    pairs = 2 * tok_count
    cap = (pairs + nodes - 1) // nodes
    rows = nodes * cap
    target = groups.reshape(pairs)
    picks = choices.reshape(pairs, 2)
    pair_gate = gates.reshape(pairs, 2).astype(jnp.float32)
    lane = jnp.arange(EXP_NODE, dtype=jnp.int32)
    onehot = (target[:, None] == jnp.arange(nodes, dtype=jnp.int32)[None, :]).astype(jnp.int32)
    rank = jnp.sum((jnp.cumsum(onehot, 0) - 1) * onehot, 1)
    cell = target * cap + rank
    place = (cell[None, :] == jnp.arange(rows, dtype=jnp.int32)[:, None]).astype(jnp.bfloat16)
    dense = jnp.sum(
        jnp.where(picks[:, :, None] == lane[None, None, :], pair_gate[:, :, None], 0.0), 1
    )
    copies_x = jnp.repeat(tokens, 2, 0)
    copies_dy = jnp.repeat(cotangent, 2, 0)
    send_x = (
        jnp.dot(place, copies_x, preferred_element_type=jnp.float32)
        .astype(jnp.bfloat16)
        .reshape(nodes, cap, width)
    )
    send_dy = (
        jnp.dot(place, copies_dy, preferred_element_type=jnp.float32)
        .astype(jnp.bfloat16)
        .reshape(nodes, cap, width)
    )
    send_table = (
        jnp.dot(place.astype(jnp.float32), dense, precision=lax.Precision.HIGHEST)
        .astype(jnp.bfloat16)
        .reshape(nodes, cap, EXP_NODE)
    )
    recv_x, recv_dy, recv_table = (
        lax.all_to_all(send_x, "node", split_axis=0, concat_axis=0, tiled=True),
        lax.all_to_all(send_dy, "node", split_axis=0, concat_axis=0, tiled=True),
        lax.all_to_all(send_table, "node", split_axis=0, concat_axis=0, tiled=True),
    )
    relay_x = recv_x.reshape(rows, width)
    relay_dy = recv_dy.reshape(rows, width)
    table = recv_table.reshape(rows, EXP_NODE).astype(jnp.float32)
    chosen = (table > 0.0).astype(jnp.int32)
    order = jnp.cumsum(chosen, 0) - 1
    slot_ids = jnp.arange(pairs, dtype=jnp.int32)
    pick_mask = (order.T[:, None, :] == slot_ids[None, :, None]) & (chosen.T[:, None, :] > 0)
    pick = pick_mask.astype(jnp.bfloat16)
    flat_pick = pick.reshape(EXP_NODE * pairs, rows)
    block_x = (
        jnp.dot(flat_pick, relay_x, preferred_element_type=jnp.float32)
        .astype(jnp.bfloat16)
        .reshape(EXP_NODE, pairs, width)
    )
    block_dy = (
        jnp.dot(flat_pick, relay_dy, preferred_element_type=jnp.float32)
        .astype(jnp.bfloat16)
        .reshape(EXP_NODE, pairs, width)
    )
    block_gate = jnp.sum(pick_mask.astype(jnp.float32) * table.T[:, None, :], -1).astype(
        jnp.bfloat16
    )
    out_x = jnp.repeat(block_x, slices, 0)
    out_dy = jnp.repeat(block_dy, slices, 0)
    out_gate = jnp.repeat(block_gate, slices, 0)[:, :, None]
    got_x, got_dy, got_gate = (
        lax.all_to_all(out_x, "ingroup", split_axis=0, concat_axis=0, tiled=True),
        lax.all_to_all(out_dy, "ingroup", split_axis=0, concat_axis=0, tiled=True),
        lax.all_to_all(out_gate, "ingroup", split_axis=0, concat_axis=0, tiled=True),
    )
    count = members * pairs
    expert_x = got_x.reshape(count, width)
    expert_dy = got_dy.reshape(count, width)
    gate_col = got_gate.reshape(count, 1).astype(jnp.float32)
    pre = jnp.dot(expert_x, up_weight, preferred_element_type=jnp.float32)
    active = jax.nn.silu(pre).astype(jnp.bfloat16)
    partial_out = jnp.dot(active, down_weight, preferred_element_type=jnp.float32).astype(
        jnp.bfloat16
    )
    back_hidden = lax.dot_general(
        expert_dy, down_weight, (((1,), (1,)), ((), ())), preferred_element_type=jnp.float32
    )
    sig = jax.nn.sigmoid(pre)
    grad_pre = (gate_col * back_hidden * sig * (1.0 + pre * (1.0 - sig))).astype(jnp.bfloat16)
    partial_dx = lax.dot_general(
        grad_pre, up_weight, (((1,), (1,)), ((), ())), preferred_element_type=jnp.float32
    ).astype(jnp.bfloat16)
    ret_out, ret_dx = (
        lax.all_to_all(
            partial_out.reshape(members, pairs, width),
            "ingroup",
            split_axis=0,
            concat_axis=0,
            tiled=True,
        ),
        lax.all_to_all(
            partial_dx.reshape(members, pairs, width),
            "ingroup",
            split_axis=0,
            concat_axis=0,
            tiled=True,
        ),
    )
    expert_out = jnp.sum(
        ret_out.reshape(EXP_NODE, slices, pairs, width), 1, dtype=jnp.float32
    ).astype(jnp.bfloat16)
    expert_dx = jnp.sum(ret_dx.reshape(EXP_NODE, slices, pairs, width), 1, dtype=jnp.float32)
    row_out = lax.dot_general(
        pick, expert_out, (((1,), (1,)), ((0,), (0,))), preferred_element_type=jnp.float32
    )
    row_dx = jnp.sum(
        lax.dot_general(
            pick_mask.astype(jnp.float32),
            expert_dx,
            (((1,), (1,)), ((0,), (0,))),
            precision=lax.Precision.HIGHEST,
        ),
        0,
    )
    group_dx = row_dx.astype(jnp.bfloat16)
    lower = chosen * (jnp.cumsum(chosen, 1) == 1).astype(jnp.int32)
    upper = chosen - lower
    lower_out = jnp.sum(lower.T.astype(jnp.float32)[:, :, None] * row_out, 0)
    upper_out = jnp.sum(upper.T.astype(jnp.float32)[:, :, None] * row_out, 0)
    both_out = jnp.stack([lower_out, upper_out], 1).astype(jnp.bfloat16)
    home_two, home_dx = (
        lax.all_to_all(
            both_out.reshape(nodes, cap, 2, width), "node", split_axis=0, concat_axis=0, tiled=True
        ),
        lax.all_to_all(
            group_dx.reshape(nodes, cap, width), "node", split_axis=0, concat_axis=0, tiled=True
        ),
    )
    pair_two = lax.dot_general(
        place,
        home_two.reshape(rows, 2 * width),
        (((0,), (0,)), ((), ())),
        preferred_element_type=jnp.float32,
    ).reshape(pairs, 2, width)
    pair_dx = lax.dot_general(
        place,
        home_dx.reshape(rows, width),
        (((0,), (0,)), ((), ())),
        preferred_element_type=jnp.float32,
    )
    low_id = jnp.minimum(picks[:, 0], picks[:, 1])
    high_id = jnp.maximum(picks[:, 0], picks[:, 1])
    low_gate = jnp.sum(jnp.where(lane[None, :] == low_id[:, None], dense, 0.0), 1)
    high_gate = jnp.sum(jnp.where(lane[None, :] == high_id[:, None], dense, 0.0), 1)
    pair_out = (
        (low_gate[:, None] * pair_two[:, 0] + high_gate[:, None] * pair_two[:, 1])
        .astype(jnp.bfloat16)
        .astype(jnp.float32)
    )
    dy_wide = copies_dy.astype(jnp.float32)
    low_dot = jnp.sum(dy_wide * pair_two[:, 0], -1)
    high_dot = jnp.sum(dy_wide * pair_two[:, 1], -1)
    grad_pick = jnp.where(picks == low_id[:, None], low_dot[:, None], high_dot[:, None])
    mixed = jnp.sum(pair_out.reshape(tok_count, 2, width), 1).astype(jnp.bfloat16)
    grad_tokens = jnp.sum(pair_dx.reshape(tok_count, 2, width), 1).astype(jnp.bfloat16)
    grad_gates = grad_pick.reshape(tok_count, 2, 2).astype(jnp.bfloat16)
    return (mixed, grad_tokens, grad_gates)


def solution(mesh):
    placed = (
        P(("node", "ingroup"), None),
        P(("node", "ingroup"), None),
        P(("node", "ingroup"), None),
        P(("node", "ingroup"), None, None),
        P(("node", "ingroup"), None, None),
        P(None, ("node", "ingroup")),
        P(("node", "ingroup"), None),
    )
    return jax.shard_map(
        per_device,
        mesh=mesh,
        in_specs=placed,
        out_specs=(
            P(("node", "ingroup"), None),
            P(("node", "ingroup"), None),
            P(("node", "ingroup"), None, None),
        ),
        check_vma=False,
    )
```

profile of v0, /device:TPU:18, one launch (start us, length us, event | category | flops | bytes accessed | tf_op | source)
XLA Modules:
  0.0 369.9 jit_solution(8232402578890761026)
XLA Ops:
  0.6 0.9 copy.130
  1.9 0.8 copy.129
  2.8 0.8 copy.128
  3.9 0.7 copy.131
  4.6 15.2 %all-to-all-start = ((bf16[16,1,4]{2,1,0:T(2,128)(2,1)}), bf16[16,1,4]{2,1,0:T(2,128)(2,1)S(1)}, u32[]{:S(2)}, u32[]{:S(2)}) async-start(bf16[16,1,4]{2,1,0:T(2,128)(2,1)} %copy.131), calls=%async_computation | async-start | bytes 16384 | tf_op jit(solution)/shard_map/all_to_all | solution.py:49
  19.8 0.9 broadcast_in_dim.75
  20.7 11.4 %all-to-all-done = bf16[16,1,4]{2,1,0:T(2,128)(2,1)S(1)} async-done(((bf16[16,1,4]{2,1,0:T(2,128)(2,1)}), bf16[16,1,4]{2,1,0:T(2,128)(2,1)S(1)}, u32[]{:S(2)}, u32[]{:S(2)}) %all-to-all-start) | async-done | bytes 160 | tf_op jit(solution)/shard_map/all_to_all | solution.py:49
  32.8 0.7 copy.141
  33.5 7.4 %all-to-all-start.5 = ((bf16[32,8,1]{1,2,0:T(2,128)(2,1)}), bf16[32,8,1]{1,2,0:T(2,128)(2,1)S(1)}, u32[]{:S(2)}, u32[]{:S(2)}) async-start(bf16[32,8,1]{1,2,0:T(2,128)(2,1)} %copy.141), calls=%async_computation.5 | async-start | bytes 32768 | tf_op jit(solution)/shard_map/all_to_all | solution.py:79
  40.9 0.3 fusion.6
  41.3 0.5 broadcast.124
  41.8 0.7 reduce.10
  42.5 0.8 reshape.306
  43.4 1.9 all-to-all-done.5
  45.3 3.5 all-to-all-start.1
  48.8 0.9 broadcast_in_dim.78
  50.1 0.7 reduce.11
  50.8 0.9 reshape.308
  51.7 14.2 %all-to-all-done.1 = bf16[16,2,3584]{2,1,0:T(2,128)(2,1)S(1)} async-done(((bf16[16,2,3584]{2,1,0:T(2,128)(2,1)}), bf16[16,2,3584]{2,1,0:T(2,128)(2,1)S(1)}, u32[]{:S(2)}, u32[]{:S(2)}) %all-to-all-start.1) | async-done | bytes 229408 | tf_op jit(solution)/shard_map/all_to_all | solution.py:47
  65.9 5.9 %all-to-all-start.6 = ((bf16[16,2,3584]{2,1,0:T(2,128)(2,1)}), bf16[16,2,3584]{2,1,0:T(2,128)(2,1)S(1)}, u32[]{:S(2)}, u32[]{:S(2)}) async-start(bf16[16,2,3584]{2,1,0:T(2,128)(2,1)} %reshape.308), calls=%async_computation.6 | async-start | bytes 458752 | tf_op jit(solution)/shard_map/all_to_all | solution.py:48
  72.2 16.9 %all-to-all-done.6 = bf16[16,2,3584]{2,1,0:T(2,128)(2,1)S(1)} async-done(((bf16[16,2,3584]{2,1,0:T(2,128)(2,1)}), bf16[16,2,3584]{2,1,0:T(2,128)(2,1)S(1)}, u32[]{:S(2)}, u32[]{:S(2)}) %all-to-all-start.6) | async-done | bytes 229408 | tf_op jit(solution)/shard_map/all_to_all | solution.py:48
  89.2 2.3 broadcast_in_dim.76
  91.4 7.7 %all-to-all-start.2 = ((bf16[32,8,7168]{2,1,0:T(8,128)(2,1)}), bf16[32,8,7168]{2,1,0:T(8,128)(2,1)}, u32[]{:S(2)}, u32[]{:S(2)}) async-start(bf16[32,8,7168]{2,1,0:T(8,128)(2,1)} %bitcast.125), calls=%async_computation.2 | async-start | bytes 7340032 | tf_op jit(solution)/shard_map/all_to_all | solution.py:77
  99.6 42.7 %all-to-all-done.2 = bf16[32,8,7168]{2,1,0:T(8,128)(2,1)} async-done(((bf16[32,8,7168]{2,1,0:T(8,128)(2,1)}), bf16[32,8,7168]{2,1,0:T(8,128)(2,1)}, u32[]{:S(2)}, u32[]{:S(2)}) %all-to-all-start.2) | async-done | bytes 3670048 | tf_op jit(solution)/shard_map/all_to_all | solution.py:77
  142.3 2.3 broadcast_in_dim.79
  144.6 9.3 %all-to-all-start.7 = ((bf16[32,8,7168]{2,1,0:T(8,128)(2,1)}), bf16[32,8,7168]{2,1,0:T(8,128)(2,1)}, u32[]{:S(2)}, u32[]{:S(2)}) async-start(bf16[32,8,7168]{2,1,0:T(8,128)(2,1)} %bitcast.124), calls=%async_computation.7 | async-start | bytes 7340032 | tf_op jit(solution)/shard_map/all_to_all | solution.py:78
  154.1 3.7 %fusion.10 = f32[256,128]{1,0:T(8,128)S(1)} fusion(bf16[7168,128]{1,0:T(8,128)(2,1)} %param.12, bf16[32,8,7168]{2,1,0:T(8,128)(2,1)} %all-to-all-done.2), kind=kOutput, calls=%fused_computation.19 | convolution fusion | flops 469762048 | bytes 5636096 | tf_op jit(solution)/shard_map/dot_general | solution.py:85
  157.8 39.3 %all-to-all-done.7 = bf16[32,8,7168]{2,1,0:T(8,128)(2,1)} async-done(((bf16[32,8,7168]{2,1,0:T(8,128)(2,1)}), bf16[32,8,7168]{2,1,0:T(8,128)(2,1)}, u32[]{:S(2)}, u32[]{:S(2)}) %all-to-all-start.7) | async-done | bytes 3670048 | tf_op jit(solution)/shard_map/all_to_all | solution.py:78
  197.1 8.5 %fusion.1 = bf16[32,8,7168]{2,1,0:T(8,128)(2,1)} fusion(bf16[7168,128]{1,0:T(8,128)(2,1)} %param.12, bf16[128,7168]{1,0:T(8,128)(2,1)S(1)} %copy-done, bf16[32,8,7168]{2,1,0:T(8,128)(2,1)} %all-to-all-done.7, f32[256,128]{1,0:T(8,128)S(1)} %fusion.10, f32[256]{0:T(256)S(1)} %reshape.286), kind=kOutput, calls=%fused_computation.3 | convolution fusion | flops 941686784 | bytes 11142144 | tf_op jit(solution)/shard_map/dot_general | solution.py:95
  205.7 9.3 %all-to-all-start.8 = ((bf16[32,8,7168]{2,1,0:T(8,128)(2,1)}), bf16[32,8,7168]{2,1,0:T(8,128)(2,1)}, u32[]{:S(2)}, u32[]{:S(2)}) async-start(bf16[32,8,7168]{2,1,0:T(8,128)(2,1)} %fusion.1), calls=%async_computation.8 | async-start | bytes 7340032 | tf_op jit(solution)/shard_map/all_to_all | solution.py:106
  215.0 2.9 fusion
  217.9 40.2 %all-to-all-done.8 = bf16[32,8,7168]{2,1,0:T(8,128)(2,1)} async-done(((bf16[32,8,7168]{2,1,0:T(8,128)(2,1)}), bf16[32,8,7168]{2,1,0:T(8,128)(2,1)}, u32[]{:S(2)}, u32[]{:S(2)}) %all-to-all-start.8) | async-done | bytes 3670048 | tf_op jit(solution)/shard_map/all_to_all | solution.py:106
  258.2 9.3 %all-to-all-start.3 = ((bf16[32,8,7168]{2,1,0:T(8,128)(2,1)}), bf16[32,8,7168]{2,1,0:T(8,128)(2,1)}, u32[]{:S(2)}, u32[]{:S(2)}) async-start(bf16[32,8,7168]{2,1,0:T(8,128)(2,1)} %fusion), calls=%async_computation.3 | async-start | bytes 7340032 | tf_op jit(solution)/shard_map/all_to_all | solution.py:99
  267.6 2.7 convert_reduce_fusion
  270.3 0.5 fusion.5
  270.7 0.7 reduce.12
  271.5 0.8 reshape.310
  272.3 38.3 %all-to-all-done.3 = bf16[32,8,7168]{2,1,0:T(8,128)(2,1)} async-done(((bf16[32,8,7168]{2,1,0:T(8,128)(2,1)}), bf16[32,8,7168]{2,1,0:T(8,128)(2,1)}, u32[]{:S(2)}, u32[]{:S(2)}) %all-to-all-start.3) | async-done | bytes 3670048 | tf_op jit(solution)/shard_map/all_to_all | solution.py:99
  310.6 5.4 %all-to-all-start.9 = ((bf16[16,2,3584]{2,1,0:T(2,128)(2,1)}), bf16[16,2,3584]{2,1,0:T(2,128)(2,1)S(1)}, u32[]{:S(2)}, u32[]{:S(2)}) async-start(bf16[16,2,3584]{2,1,0:T(2,128)(2,1)} %reshape.310), calls=%async_computation.9 | async-start | bytes 458752 | tf_op jit(solution)/shard_map/all_to_all | solution.py:140
  316.0 2.6 bitcast_reduce_fusion
  318.6 0.5 multiply_reduce_fusion.1
  319.2 1.2 copy.136
  320.4 11.9 %all-to-all-done.9 = bf16[16,2,3584]{2,1,0:T(2,128)(2,1)S(1)} async-done(((bf16[16,2,3584]{2,1,0:T(2,128)(2,1)}), bf16[16,2,3584]{2,1,0:T(2,128)(2,1)S(1)}, u32[]{:S(2)}, u32[]{:S(2)}) %all-to-all-start.9) | async-done | bytes 229408 | tf_op jit(solution)/shard_map/all_to_all | solution.py:140
  332.4 7.8 %all-to-all-start.4 = ((bf16[16,1,2,7168]{3,2,1,0:T(2,128)(2,1)}), bf16[16,1,2,7168]{3,2,1,0:T(2,128)(2,1)S(1)}, u32[]{:S(2)}, u32[]{:S(2)}) async-start(bf16[16,1,2,7168]{3,2,1,0:T(2,128)(2,1)} %copy.136), calls=%async_computation.4 | async-start | bytes 917504 | tf_op jit(solution)/shard_map/all_to_all | solution.py:137
  340.9 0.9 convolution_reduce_fusion
  341.8 25.3 %all-to-all-done.4 = bf16[16,1,2,7168]{3,2,1,0:T(2,128)(2,1)S(1)} async-done(((bf16[16,1,2,7168]{3,2,1,0:T(2,128)(2,1)}), bf16[16,1,2,7168]{3,2,1,0:T(2,128)(2,1)S(1)}, u32[]{:S(2)}, u32[]{:S(2)}) %all-to-all-start.4) | async-done | bytes 458784 | tf_op jit(solution)/shard_map/all_to_all | solution.py:137
  368.3 0.6 fusion.68
  368.9 1.0 fusion.41
  (57 shorter events, 4.9 us)
Async XLA Ops:
  0.6 196.5 %copy-start = (bf16[128,7168]{1,0:T(8,128)(2,1)S(1)}, bf16[128,7168]{1,0:T(8,128)(2,1)}, u32[]{:S(2)}) copy-start(bf16[128,7168]{1,0:T(8,128)(2,1)} %param.13) | copy-start | bytes 5505028
  4.6 27.6 %all-to-all-start = ((bf16[16,1,4]{2,1,0:T(2,128)(2,1)}), bf16[16,1,4]{2,1,0:T(2,128)(2,1)S(1)}, u32[]{:S(2)}, u32[]{:S(2)}) async-start(bf16[16,1,4]{2,1,0:T(2,128)(2,1)} %copy.131), calls=%async_computation | async-start | bytes 16384 | tf_op jit(solution)/shard_map/all_to_all | solution.py:49
  33.5 11.7 %all-to-all-start.5 = ((bf16[32,8,1]{1,2,0:T(2,128)(2,1)}), bf16[32,8,1]{1,2,0:T(2,128)(2,1)S(1)}, u32[]{:S(2)}, u32[]{:S(2)}) async-start(bf16[32,8,1]{1,2,0:T(2,128)(2,1)} %copy.141), calls=%async_computation.5 | async-start | bytes 32768 | tf_op jit(solution)/shard_map/all_to_all | solution.py:79
  45.3 20.6 %all-to-all-start.1 = ((bf16[16,2,3584]{2,1,0:T(2,128)(2,1)}), bf16[16,2,3584]{2,1,0:T(2,128)(2,1)S(1)}, u32[]{:S(2)}, u32[]{:S(2)}) async-start(bf16[16,2,3584]{2,1,0:T(2,128)(2,1)} %reshape.306), calls=%async_computation.1 | async-start | bytes 458752 | tf_op jit(solution)/shard_map/all_to_all | solution.py:47
  65.9 23.3 %all-to-all-start.6 = ((bf16[16,2,3584]{2,1,0:T(2,128)(2,1)}), bf16[16,2,3584]{2,1,0:T(2,128)(2,1)S(1)}, u32[]{:S(2)}, u32[]{:S(2)}) async-start(bf16[16,2,3584]{2,1,0:T(2,128)(2,1)} %reshape.308), calls=%async_computation.6 | async-start | bytes 458752 | tf_op jit(solution)/shard_map/all_to_all | solution.py:48
  91.4 50.9 %all-to-all-start.2 = ((bf16[32,8,7168]{2,1,0:T(8,128)(2,1)}), bf16[32,8,7168]{2,1,0:T(8,128)(2,1)}, u32[]{:S(2)}, u32[]{:S(2)}) async-start(bf16[32,8,7168]{2,1,0:T(8,128)(2,1)} %bitcast.125), calls=%async_computation.2 | async-start | bytes 7340032 | tf_op jit(solution)/shard_map/all_to_all | solution.py:77
  144.6 52.5 %all-to-all-start.7 = ((bf16[32,8,7168]{2,1,0:T(8,128)(2,1)}), bf16[32,8,7168]{2,1,0:T(8,128)(2,1)}, u32[]{:S(2)}, u32[]{:S(2)}) async-start(bf16[32,8,7168]{2,1,0:T(8,128)(2,1)} %bitcast.124), calls=%async_computation.7 | async-start | bytes 7340032 | tf_op jit(solution)/shard_map/all_to_all | solution.py:78
  205.7 52.5 %all-to-all-start.8 = ((bf16[32,8,7168]{2,1,0:T(8,128)(2,1)}), bf16[32,8,7168]{2,1,0:T(8,128)(2,1)}, u32[]{:S(2)}, u32[]{:S(2)}) async-start(bf16[32,8,7168]{2,1,0:T(8,128)(2,1)} %fusion.1), calls=%async_computation.8 | async-start | bytes 7340032 | tf_op jit(solution)/shard_map/all_to_all | solution.py:106
  258.2 52.4 %all-to-all-start.3 = ((bf16[32,8,7168]{2,1,0:T(8,128)(2,1)}), bf16[32,8,7168]{2,1,0:T(8,128)(2,1)}, u32[]{:S(2)}, u32[]{:S(2)}) async-start(bf16[32,8,7168]{2,1,0:T(8,128)(2,1)} %fusion), calls=%async_computation.3 | async-start | bytes 7340032 | tf_op jit(solution)/shard_map/all_to_all | solution.py:99
  310.6 21.7 %all-to-all-start.9 = ((bf16[16,2,3584]{2,1,0:T(2,128)(2,1)}), bf16[16,2,3584]{2,1,0:T(2,128)(2,1)S(1)}, u32[]{:S(2)}, u32[]{:S(2)}) async-start(bf16[16,2,3584]{2,1,0:T(2,128)(2,1)} %reshape.310), calls=%async_computation.9 | async-start | bytes 458752 | tf_op jit(solution)/shard_map/all_to_all | solution.py:140
  319.1 49.2 %copy-start.1 = (s32[4,2,2]{0,2,1:T(2,128)S(1)}, s32[4,2,2]{0,2,1:T(2,128)}, u32[]{:S(2)}) copy-start(s32[4,2,2]{0,2,1:T(2,128)} %param.10) | copy-start | bytes 196
  332.4 34.7 %all-to-all-start.4 = ((bf16[16,1,2,7168]{3,2,1,0:T(2,128)(2,1)}), bf16[16,1,2,7168]{3,2,1,0:T(2,128)(2,1)S(1)}, u32[]{:S(2)}, u32[]{:S(2)}) async-start(bf16[16,1,2,7168]{3,2,1,0:T(2,128)(2,1)} %copy.136), calls=%async_computation.4 | async-start | bytes 917504 | tf_op jit(solution)/shard_map/all_to_all | solution.py:137
where the time goes:
time: 371 us; the launch traced here: 370 us
  waiting for transfers between devices  242 us (65%)
  starting transfers between devices  80.9 us (22%)
  matrix products  18.7 us (5%)
  local copies, waits for them, and re-layouts  17.2 us (5%)
  other arithmetic  9.97 us (3%)
    all_to_all x1, waiting for transfers between devices, per_device(): lax.all_to_all(out_x, 'ingroup', split_axis=0, concat_axis=0, tiled=True)  42.7 us
    all_to_all x1, waiting for transfers between devices, per_device(): lax.all_to_all(partial_dx.reshape(members, pairs, width), 'ingroup', spli...  40.2 us
    all_to_all x1, waiting for transfers between devices, per_device(): lax.all_to_all(out_dy, 'ingroup', split_axis=0, concat_axis=0, tiled=True)  39.3 us
    all_to_all x1, waiting for transfers between devices, per_device(): lax.all_to_all(partial_out.reshape(members, pairs, width), 'ingroup', spl...  38.3 us
    all_to_all x1, waiting for transfers between devices, per_device(): lax.all_to_all(both_out.reshape(nodes, cap, 2, width), 'node', split_axis...  25.3 us
    all_to_all x1, waiting for transfers between devices, per_device(): lax.all_to_all(send_dy, 'node', split_axis=0, concat_axis=0, tiled=True)  16.9 us
    all_to_all x1, starting transfers between devices, per_device(): lax.all_to_all(send_table, 'node', split_axis=0, concat_axis=0, tiled=True)  15.2 us
    all_to_all x1, waiting for transfers between devices, per_device(): lax.all_to_all(send_x, 'node', split_axis=0, concat_axis=0, tiled=True)  14.2 us
  transfers between devices with their start and end apart: 10, of which 10 were waited for; matrix products, arithmetic and copies ran while one was open for 7% of the time, Pallas kernels for 0%

commit v1 on v0

v1 whole, which is shorter than its diff:
```python
import jax
import jax.numpy as jnp
from jax import lax
from jax.sharding import Mesh, PartitionSpec as P

EXP_NODE = 4
LANES = 128


def dot(a, b, dims):
    return lax.dot_general(a, b, (dims, ((), ())), preferred_element_type=jnp.float32)


def per_device(tokens, cotangent, groups, choices, gates, up_weight, down_weight):
    f32, bf16 = jnp.float32, jnp.bfloat16
    tok_count, width = tokens.shape
    nodes = lax.axis_size("node")
    experts = lax.axis_size("expert")
    slices = lax.axis_size("slice")
    hidden = up_weight.shape[1]
    pairs = 2 * tok_count
    part = width // slices
    expert = lax.axis_index("expert")
    me = lax.axis_index("slice")
    lane = jnp.arange(LANES, dtype=jnp.int32)
    node_ids = jnp.arange(nodes, dtype=jnp.int32)

    place = node_ids[:, None, None] == groups[None]
    token_at = jnp.any(place, 2).astype(bf16)
    dense = jnp.sum(
        jnp.where(choices[..., None] == lane, gates[..., None].astype(f32), 0.0), 2
    )
    table = jnp.sum(jnp.where(place[..., None], dense[None], 0.0), (1, 2)).astype(bf16)
    packed = jnp.concatenate([tokens, cotangent], 1)
    sent = jnp.concatenate(
        [
            dot(token_at, packed, ((1,), (0,))).astype(bf16).reshape(nodes, -1, LANES),
            jnp.pad(table[:, None, :], ((0, 0), (0, 7), (0, 0))),
        ],
        1,
    )

    both_weights = jnp.concatenate(
        [
            up_weight.reshape(slices, part, hidden),
            down_weight.T.reshape(slices, part, hidden),
        ],
        1,
    )
    sent, both_weights = lax.optimization_barrier((sent, both_weights))
    recv = lax.all_to_all(sent, "node", split_axis=0, concat_axis=0, tiled=True)

    shifts = [(0, 0), (2, 0), (2, 1), (1, 0), (3, 0), (1, 1), (3, 1), (0, 1)]
    chips = slices // 2

    def moved(index, shift, sign):
        return ((index // 2 + sign * shift[0]) % chips) * 2 + (index % 2 + shift[1]) % 2

    held = []
    for shift in shifts:
        block = lax.dynamic_index_in_dim(both_weights, moved(me, shift, 1), 0, False)
        if shift != (0, 0):
            block = lax.ppermute(
                block, "slice", [(i, moved(i, shift, 1)) for i in range(slices)]
            )
        held.append(block)

    used = jnp.any(recv[:, 2 * width // LANES, :] > 0, 1)
    rank = jnp.cumsum(used.astype(jnp.int32)) - 1
    slot = jnp.arange(pairs, dtype=jnp.int32)
    pick = ((rank[None, :] == slot[:, None]) & used[None, :]).astype(bf16)
    mine = dot(pick, recv.reshape(nodes, -1), ((1,), (0,))).astype(bf16)
    blocks = jnp.stack(
        [
            jnp.concatenate(
                [
                    mine[:, m * part : (m + 1) * part],
                    mine[:, width + m * part : width + (m + 1) * part],
                    mine[:, 2 * width : 2 * width + LANES],
                ],
                1,
            )
            for m in range(slices)
        ]
    )
    spread = jnp.broadcast_to(blocks[None], (experts,) + blocks.shape).reshape(
        experts * slices, pairs, -1
    )
    rows = lax.all_to_all(
        spread, ("expert", "slice"), split_axis=0, concat_axis=0, tiled=True
    ).reshape(experts * slices * pairs, -1)
    x = rows[:, :part]
    dy = rows[:, part : 2 * part]
    gate = jnp.sum(
        jnp.where(lane[None, :] == expert, rows[:, 2 * part :].astype(f32), 0.0), 1, keepdims=True
    )

    partial = jnp.stack(
        [
            jnp.concatenate(
                [dot(x, w[:part], ((1,), (0,))), dot(dy, w[part:], ((1,), (0,)))], 1
            ).astype(bf16)
            for w in held
        ]
    )
    order = jnp.stack([jnp.asarray(moved(me, s, -1)) for s in shifts])
    where_is = jnp.sum(
        jnp.where(
            order[None, :] == jnp.arange(slices)[:, None], jnp.arange(slices)[None, :], 0
        ),
        1,
    )
    outgoing = jnp.stack(
        [lax.dynamic_index_in_dim(partial, where_is[m], 0, False) for m in range(slices)]
    )
    incoming = lax.all_to_all(outgoing, "slice", split_axis=0, concat_axis=0, tiled=True)
    both = jnp.sum(incoming.astype(f32), 0)
    pre = both[:, :hidden]
    back = both[:, hidden:]
    sig = jax.nn.sigmoid(pre)
    active = (pre * sig).astype(bf16)
    grad_pre = (gate * back * sig * (1.0 + pre * (1.0 - sig))).astype(bf16)
    own = jnp.concatenate([active, grad_pre], 1)
    every = lax.all_to_all(
        jnp.broadcast_to(own[None], (slices,) + own.shape),
        "slice",
        split_axis=0,
        concat_axis=0,
        tiled=True,
    )

    out = jnp.zeros((x.shape[0], part), f32)
    dx = jnp.zeros((x.shape[0], part), f32)
    for i, w in enumerate(held):
        units = lax.dynamic_index_in_dim(every, order[i], 0, False)
        out = out + dot(units[:, :hidden], w[part:], ((1,), (1,)))
        dx = dx + dot(units[:, hidden:], w[:part], ((1,), (1,)))
    inner = jnp.where(gate > 0, jnp.sum(out * dy.astype(f32), 1, keepdims=True), 0.0)
    result = jnp.concatenate(
        [gate * out, dx, jnp.where(lane[None, :] == expert, inner, 0.0)], 1
    ).astype(bf16)

    parts_back = lax.all_to_all(
        result.reshape(experts * slices, pairs, -1),
        ("expert", "slice"),
        split_axis=0,
        concat_axis=0,
        tiled=True,
    ).reshape(experts, slices, pairs, -1)
    summed = jnp.sum(parts_back.astype(f32), 0)
    inner_all = jnp.sum(summed[:, :, 2 * part :], 0)
    full = jnp.concatenate(
        [summed[m, :, :part] for m in range(slices)]
        + [summed[m, :, part : 2 * part] for m in range(slices)]
        + [inner_all],
        1,
    ).astype(bf16)
    expanded = dot(pick, full, ((0,), (0,))).astype(bf16)
    expanded = jnp.pad(expanded, ((0, 0), (0, 7 * LANES))).reshape(nodes, -1, LANES)
    home = lax.all_to_all(expanded, "node", split_axis=0, concat_axis=0, tiled=True)

    home_rows = home[:, : 2 * width // LANES].reshape(nodes, -1)
    total = dot(token_at, home_rows, ((0,), (0,))).astype(bf16)
    inner_rows = home[:, 2 * width // LANES].astype(f32)
    pair_inner = jnp.sum(jnp.where(place[..., None], inner_rows[:, None, None, :], 0.0), 0)
    grad_gates = jnp.sum(
        jnp.where(choices[..., None] == lane, pair_inner[:, :, None, :], 0.0), -1
    ).astype(bf16)
    return (total[:, :width], total[:, width:], grad_gates)


def solution(mesh):
    nodes, members = mesh.devices.shape
    fine = Mesh(
        mesh.devices.reshape(nodes, EXP_NODE, members // EXP_NODE), ("node", "expert", "slice")
    )
    both = ("node", "expert", "slice")
    placed = (
        P(both, None),
        P(both, None),
        P(both, None),
        P(both, None, None),
        P(both, None, None),
        P(None, both),
        P(both, None),
    )
    return jax.shard_map(
        per_device,
        mesh=fine,
        in_specs=placed,
        out_specs=(P(both, None), P(both, None), P(both, None, None)),
        check_vma=False,
    )
```

time: 371 us -> 251 us (0.68)
  the two profiles are of different devices: /device:TPU:18 before, /device:TPU:2 now
where the time goes in v1:
time: 251 us; the launch traced here: 250 us
  blocking collectives  98.8 us (39%)
  waiting for transfers between devices  44.1 us (18%)
  starting transfers between devices  40.6 us (16%)
  matrix products  24.6 us (10%)
  between operations  17.1 us (7%)
  local copies, waits for them, and re-layouts  16.3 us (6%)
  other arithmetic  8.24 us (3%)
    all_to_all x1, blocking collectives, per_device(): recv = lax.all_to_all(sent, 'node', split_axis=0, concat_axis=0, tiled=True)  43.1 us
    all_to_all x1, blocking collectives, per_device(): lax.all_to_all(expanded, 'node', split_axis=0, concat_axis=0, tiled=True)  34 us
    dot_general x36, matrix products, dot(): lax.dot_general(a, b, (dims, ((), ())), preferred_element_type=jnp.float32)  24.6 us
    all_to_all x1, blocking collectives, per_device(): lax.all_to_all(result.reshape(experts * slices, pairs, -1), ('expert', 's...  21.7 us
    ppermute x7, starting transfers between devices, per_device(): lax.ppermute(block, 'slice', [(i, moved(i, shift, 1)) for i in range(slic...  21.4 us
    ppermute x7, waiting for transfers between devices, per_device(): lax.ppermute(block, 'slice', [(i, moved(i, shift, 1)) for i in range(slic...  15.1 us
    all_to_all x1, waiting for transfers between devices, per_device(): lax.all_to_all(jnp.broadcast_to(own[None], (slices,) + own.shape), 'slice...  14.5 us
    all_to_all x1, waiting for transfers between devices, per_device(): lax.all_to_all(outgoing, 'slice', split_axis=0, concat_axis=0, tiled=True)  14.4 us
  transfers between devices with their start and end apart: 10, of which 5 were waited for; matrix products, arithmetic and copies ran while one was open for 4% of the time, Pallas kernels for 0%

profile of v1, /device:TPU:2, one launch (start us, length us, event | category | flops | bytes accessed | tf_op | source)
XLA Modules:
  0.0 249.8 jit_solution(17032921693788020183)
XLA Ops:
  0.6 0.8 iota_compare_fusion.4
  1.4 0.7 convert_element_type.152
  2.1 0.8 select_reduce_fusion.4
  3.0 1.2 fusion.12
  4.3 3.3 %copy.31 = bf16[7168,128]{1,0:T(8,128)(2,1)S(1)} copy(bf16[7168,128]{0,1:T(8,128)(2,1)} %bitcast.239) | data formatting | bytes 3670016 | tf_op jit(solution)/shard_map/transpose | solution.py:46
  7.6 3.6 %pad_maximum_fusion = bf16[8,1792,128]{2,1,0:T(8,128)(2,1)} fusion(bf16[8,896,128]{2,1,0:T(8,128)(2,1)S(1)} %bitcast.216, bf16[8,896,128]{2,1,0:T(8,128)(2,1)} %bitcast.238), kind=kLoop, calls=%fused_computation.4 | loop fusion | flops 7340032 | bytes 7340032 | tf_op jit(solution)/shard_map/concatenate | solution.py:43
  11.2 43.1 %all_to_all.30 = bf16[16,120,128]{2,1,0:T(8,128)(2,1)S(1)} all-to-all(bf16[16,120,128]{2,1,0:T(8,128)(2,1)S(1)} %fusion.30), channel_id=1, replica_groups=mesh['node'=16,'expert'=4,'slice'=8] {'node'}, dimensions={0} | all-to-all | bytes 983040 | tf_op jit(solution)/shard_map/all_to_all | solution.py:51
  55.3 1.0 broadcast_in_dim.145
  56.3 7.6 %all-to-all-start.1 = ((bf16[32,8,1920]{2,1,0:T(8,128)(2,1)}), bf16[32,8,1920]{2,1,0:T(8,128)(2,1)S(1)}, u32[]{:S(2)}, u32[]{:S(2)}) async-start(bf16[32,8,1920]{2,1,0:T(8,128)(2,1)} %bitcast.13), calls=%async_computation.1 | async-start | bytes 1966080 | tf_op jit(solution)/shard_map/all_to_all | solution.py:89
  64.1 3.5 %dynamic-slice_bitcast_fusion.1 = (bf16[1792,128]{1,0:T(8,128)(2,1)}, bf16[1792,128]{1,0:T(8,128)(2,1)}, bf16[1792,128]{1,0:T(8,128)(2,1)}, bf16[1792,128]{1,0:T...) fusion(bf16[8,1792,128]{2,1,0:T(8,128)(2,1)} %pad_maximum_fusion, ...), kind=kLoop, calls=%fused_computation.69 | loop fusion | bytes 6422556 | tf_op jit(solution)/shard_map/jit(dynamic_index_in_dim)/squeeze | solution.py:61
  67.6 2.0 collective-permute-start.5
  69.7 2.1 collective-permute-start.6
  71.8 3.5 %collective-permute-start.4 = (bf16[1792,128]{1,0:T(8,128)(2,1)}, bf16[1792,128]{1,0:T(8,128)(2,1)S(1)}, u32[]{:S(2)}, u32[]{:S(2)}) collective-permute-start(bf16[1792,128]{1,0:T(8,128)(2,1)} %get-tuple-element.9), channel_id=1, source_target_pairs={{0,3},{1,2},{2,5},{3,4},{4,7},{5,6},{6,1},{7,0},{8,11},{9,10},{10,... | collective-permute-start | bytes 1376264 | tf_op jit(solution)/shard_map/ppermute | solution.py:63
  75.3 5.2 %collective-permute-start.1 = (bf16[1792,128]{1,0:T(8,128)(2,1)}, bf16[1792,128]{1,0:T(8,128)(2,1)S(1)}, u32[]{:S(2)}, u32[]{:S(2)}) collective-permute-start(bf16[1792,128]{1,0:T(8,128)(2,1)} %get-tuple-element.12), channel_id=1, source_target_pairs={{0,5},{1,4},{2,7},{3,6},{4,1},{5,0},{6,3},{7,2},{8,13},{9,12},{10,... | collective-permute-start | bytes 1376264 | tf_op jit(solution)/shard_map/ppermute | solution.py:63
  80.4 2.2 collective-permute-start
  82.9 0.7 fusion.136
  99.0 1.3 fusion.13
  100.3 1.2 fusion.14
  101.6 5.6 %collective-permute-done = bf16[1792,128]{1,0:T(8,128)(2,1)S(1)} collective-permute-done((bf16[1792,128]{1,0:T(8,128)(2,1)}, bf16[1792,128]{1,0:T(8,128)(2,1)S(1)}, u32[]{:S(2)}, u32[]{:S(2)}) %collective-permute-start) | collective-permute-done | bytes 458784 | tf_op jit(solution)/shard_map/ppermute | solution.py:63
  107.2 3.6 %collective-permute-start.2 = (bf16[1792,128]{1,0:T(8,128)(2,1)}, bf16[1792,128]{1,0:T(8,128)(2,1)S(1)}, u32[]{:S(2)}, u32[]{:S(2)}) collective-permute-start(bf16[1792,128]{1,0:T(8,128)(2,1)} %get-tuple-element.11), channel_id=1, source_target_pairs={{0,2},{1,3},{2,4},{3,5},{4,6},{5,7},{6,0},{7,1},{8,10},{9,11},{10,... | collective-permute-start | bytes 1376264 | tf_op jit(solution)/shard_map/ppermute | solution.py:63
  111.5 2.8 %collective-permute-start.3 = (bf16[1792,128]{1,0:T(8,128)(2,1)S(1)}, bf16[1792,128]{1,0:T(8,128)(2,1)S(1)}, u32[]{:S(2)}, u32[]{:S(2)}) collective-permute-start(bf16[1792,128]{1,0:T(8,128)(2,1)S(1)} %copy-done.12), channel_id=1, source_target_pairs={{0,6},{1,7},{2,0},{3,1},{4,2},{5,3},{6,4},{7,5},{8,14},{9,15},{10,... | collective-permute-start | bytes 1376264 | tf_op jit(solution)/shard_map/ppermute | solution.py:63
  114.9 7.4 %collective-permute-done.2 = bf16[1792,128]{1,0:T(8,128)(2,1)S(1)} collective-permute-done((bf16[1792,128]{1,0:T(8,128)(2,1)}, bf16[1792,128]{1,0:T(8,128)(2,1)S(1)}, u32[]{:S(2)}, u32[]{:S(2)}) %collective-permute-start.2) | collective-permute-done | bytes 458784 | tf_op jit(solution)/shard_map/ppermute | solution.py:63
  123.0 2.2 collective-permute-done.3
  128.4 0.7 dynamic-slice_dynamic-update-slice_fusion.6
  129.7 0.7 dynamic-slice_dynamic-update-slice_fusion.4
  131.7 0.7 dynamic-slice_dynamic-update-slice_fusion.1
  132.4 0.7 dynamic-slice_dynamic-update-slice_fusion
  133.0 6.7 %all-to-all-start.2 = ((bf16[8,256,256]{1,2,0:T(8,128)(2,1)}), bf16[8,256,256]{1,2,0:T(8,128)(2,1)S(1)}, u32[]{:S(2)}, u32[]{:S(2)}) async-start(bf16[8,256,256]{1,2,0:T(8,128)(2,1)} %dynamic-slice_dynamic-update-slice_fusion), calls=%async_computation.2 | async-start | bytes 2097152 | tf_op jit(solution)/shard_map/all_to_all | solution.py:116
  139.9 14.4 %all-to-all-done.2 = bf16[8,256,256]{1,2,0:T(8,128)(2,1)S(1)} async-done(((bf16[8,256,256]{1,2,0:T(8,128)(2,1)}), bf16[8,256,256]{1,2,0:T(8,128)(2,1)S(1)}, u32[]{:S(2)}, u32[]{:S(2)}) %all-to-all-start.2) | async-done | bytes 1048608 | tf_op jit(solution)/shard_map/all_to_all | solution.py:116
  154.6 1.0 broadcast_in_dim.149
  155.7 4.9 %all-to-all-start.3 = ((bf16[8,256,256]{2,1,0:T(8,128)(2,1)}), bf16[8,256,256]{2,1,0:T(8,128)(2,1)S(1)}, u32[]{:S(2)}, u32[]{:S(2)}) async-start(bf16[8,256,256]{2,1,0:T(8,128)(2,1)} %broadcast_in_dim.149), calls=%async_computation.3 | async-start | bytes 2097152 | tf_op jit(solution)/shard_map/all_to_all | solution.py:124
  160.6 14.5 %all-to-all-done.3 = bf16[8,256,256]{2,1,0:T(8,128)(2,1)S(1)} async-done(((bf16[8,256,256]{2,1,0:T(8,128)(2,1)}), bf16[8,256,256]{2,1,0:T(8,128)(2,1)S(1)}, u32[]{:S(2)}, u32[]{:S(2)}) %all-to-all-start.3) | async-done | bytes 1048608 | tf_op jit(solution)/shard_map/all_to_all | solution.py:124
  175.2 1.3 fusion.75
  176.5 1.3 fusion.74
  177.8 1.2 fusion.36
  179.1 1.3 fusion.42
  180.3 1.2 fusion.48
  182.5 0.7 fusion.33
  183.4 1.2 fusion.39
  184.7 1.3 fusion.45
  186.0 1.2 fusion.51
  187.2 1.2 fusion.57
  188.4 1.2 fusion.63
  189.7 1.2 convolution_add_fusion.1
  191.5 21.7 %all_to_all.31 = bf16[32,8,1920]{2,1,0:T(8,128)(2,1)S(1)} all-to-all(bf16[32,8,1920]{2,1,0:T(8,128)(2,1)S(1)} %pad_maximum_fusion.1), channel_id=1, replica_groups=mesh['node'=16,'expert'=4,'slice'=8] {'expert','slice'}, dimensions={0} | all-to-all | bytes 1966080 | tf_op jit(solution)/shard_map/all_to_all | solution.py:143
  214.0 34.0 %all_to_all.32 = bf16[16,120,128]{2,1,0:T(8,128)(2,1)S(1)} all-to-all(bf16[16,120,128]{2,1,0:T(8,128)(2,1)S(1)} %bitcast.237), channel_id=1, replica_groups=mesh['node'=16,'expert'=4,'slice'=8] {'node'}, dimensions={0} | all-to-all | bytes 983040 | tf_op jit(solution)/shard_map/all_to_all | solution.py:160
  248.4 0.7 select_reduce_fusion.3
  249.1 0.7 fusion.135
  (127 shorter events, 11.6 us)
Async XLA Ops:
  56.3 42.6 %all-to-all-start.1 = ((bf16[32,8,1920]{2,1,0:T(8,128)(2,1)}), bf16[32,8,1920]{2,1,0:T(8,128)(2,1)S(1)}, u32[]{:S(2)}, u32[]{:S(2)}) async-start(bf16[32,8,1920]{2,1,0:T(8,128)(2,1)} %bitcast.13), calls=%async_computation.1 | async-start | bytes 1966080 | tf_op jit(solution)/shard_map/all_to_all | solution.py:89
  67.6 58.8 %collective-permute-start.5 = (bf16[1792,128]{1,0:T(8,128)(2,1)}, bf16[1792,128]{1,0:T(8,128)(2,1)S(1)}, u32[]{:S(2)}, u32[]{:S(2)}) collective-permute-start(bf16[1792,128]{1,0:T(8,128)(2,1)} %get-tuple-element.7), channel_id=1, source_target_pairs={{0,7},{1,6},{2,1},{3,0},{4,3},{5,2},{6,5},{7,4},{8,15},{9,14},{10,... | collective-permute-start | bytes 1376264 | tf_op jit(solution)/shard_map/ppermute | solution.py:63
  69.7 57.5 %collective-permute-start.6 = (bf16[1792,128]{1,0:T(8,128)(2,1)}, bf16[1792,128]{1,0:T(8,128)(2,1)S(1)}, u32[]{:S(2)}, u32[]{:S(2)}) collective-permute-start(bf16[1792,128]{1,0:T(8,128)(2,1)} %get-tuple-element.8), channel_id=1, source_target_pairs={{0,1},{1,0},{2,3},{3,2},{4,5},{5,4},{6,7},{7,6},{8,9},{9,8},{10,11... | collective-permute-start | bytes 1376264 | tf_op jit(solution)/shard_map/ppermute | solution.py:63
  71.8 54.0 %collective-permute-start.4 = (bf16[1792,128]{1,0:T(8,128)(2,1)}, bf16[1792,128]{1,0:T(8,128)(2,1)S(1)}, u32[]{:S(2)}, u32[]{:S(2)}) collective-permute-start(bf16[1792,128]{1,0:T(8,128)(2,1)} %get-tuple-element.9), channel_id=1, source_target_pairs={{0,3},{1,2},{2,5},{3,4},{4,7},{5,6},{6,1},{7,0},{8,11},{9,10},{10,... | collective-permute-start | bytes 1376264 | tf_op jit(solution)/shard_map/ppermute | solution.py:63
  75.3 36.2 %collective-permute-start.1 = (bf16[1792,128]{1,0:T(8,128)(2,1)}, bf16[1792,128]{1,0:T(8,128)(2,1)S(1)}, u32[]{:S(2)}, u32[]{:S(2)}) collective-permute-start(bf16[1792,128]{1,0:T(8,128)(2,1)} %get-tuple-element.12), channel_id=1, source_target_pairs={{0,5},{1,4},{2,7},{3,6},{4,1},{5,0},{6,3},{7,2},{8,13},{9,12},{10,... | collective-permute-start | bytes 1376264 | tf_op jit(solution)/shard_map/ppermute | solution.py:63
  80.4 26.7 %collective-permute-start = (bf16[1792,128]{1,0:T(8,128)(2,1)}, bf16[1792,128]{1,0:T(8,128)(2,1)S(1)}, u32[]{:S(2)}, u32[]{:S(2)}) collective-permute-start(bf16[1792,128]{1,0:T(8,128)(2,1)} %get-tuple-element.13), channel_id=1, source_target_pairs={{0,4},{1,5},{2,6},{3,7},{4,0},{5,1},{6,2},{7,3},{8,12},{9,13},{10,... | collective-permute-start | bytes 1376264 | tf_op jit(solution)/shard_map/ppermute | solution.py:63
  99.0 12.5 %copy-start.12 = (bf16[1792,128]{1,0:T(8,128)(2,1)S(1)}, bf16[1792,128]{1,0:T(8,128)(2,1)}, u32[]{:S(2)}) copy-start(bf16[1792,128]{1,0:T(8,128)(2,1)} %get-tuple-element.10) | copy-start | bytes 1376260
  107.2 25.9 %copy-start = (bf16[1792,128]{1,0:T(8,128)(2,1)}, bf16[1792,128]{1,0:T(8,128)(2,1)S(1)}, u32[]{:S(2)}) copy-start(bf16[1792,128]{1,0:T(8,128)(2,1)S(1)} %collective-permute-done) | copy-start | bytes 1376260
  107.2 15.1 %collective-permute-start.2 = (bf16[1792,128]{1,0:T(8,128)(2,1)}, bf16[1792,128]{1,0:T(8,128)(2,1)S(1)}, u32[]{:S(2)}, u32[]{:S(2)}) collective-permute-start(bf16[1792,128]{1,0:T(8,128)(2,1)} %get-tuple-element.11), channel_id=1, source_target_pairs={{0,2},{1,3},{2,4},{3,5},{4,6},{5,7},{6,0},{7,1},{8,10},{9,11},{10,... | collective-permute-start | bytes 1376264 | tf_op jit(solution)/shard_map/ppermute | solution.py:63
  111.4 15.0 %copy-start.9 = (bf16[1792,128]{1,0:T(8,128)(2,1)}, bf16[1792,128]{1,0:T(8,128)(2,1)S(1)}, u32[]{:S(2)}) copy-start(bf16[1792,128]{1,0:T(8,128)(2,1)S(1)} %collective-permute-done.1) | copy-start | bytes 1376260
  111.5 13.7 %collective-permute-start.3 = (bf16[1792,128]{1,0:T(8,128)(2,1)S(1)}, bf16[1792,128]{1,0:T(8,128)(2,1)S(1)}, u32[]{:S(2)}, u32[]{:S(2)}) collective-permute-start(bf16[1792,128]{1,0:T(8,128)(2,1)S(1)} %copy-done.12), channel_id=1, source_target_pairs={{0,6},{1,7},{2,0},{3,1},{4,2},{5,3},{6,4},{7,5},{8,14},{9,15},{10,... | collective-permute-start | bytes 1376264 | tf_op jit(solution)/shard_map/ppermute | solution.py:63
  122.3 4.8 %copy-start.5 = (bf16[1792,128]{1,0:T(8,128)(2,1)}, bf16[1792,128]{1,0:T(8,128)(2,1)S(1)}, u32[]{:S(2)}) copy-start(bf16[1792,128]{1,0:T(8,128)(2,1)S(1)} %collective-permute-done.2) | copy-start | bytes 1376260
  125.1 2.6 %copy-start.7 = (bf16[1792,128]{1,0:T(8,128)(2,1)}, bf16[1792,128]{1,0:T(8,128)(2,1)S(1)}, u32[]{:S(2)}) copy-start(bf16[1792,128]{1,0:T(8,128)(2,1)S(1)} %collective-permute-done.3) | copy-start | bytes 1376260
  125.8 5.9 %copy-start.3 = (bf16[1792,128]{1,0:T(8,128)(2,1)}, bf16[1792,128]{1,0:T(8,128)(2,1)S(1)}, u32[]{:S(2)}) copy-start(bf16[1792,128]{1,0:T(8,128)(2,1)S(1)} %collective-permute-done.4) | copy-start | bytes 1376260
  126.5 6.6 %copy-start.2 = (bf16[1792,128]{1,0:T(8,128)(2,1)}, bf16[1792,128]{1,0:T(8,128)(2,1)S(1)}, u32[]{:S(2)}) copy-start(bf16[1792,128]{1,0:T(8,128)(2,1)S(1)} %collective-permute-done.5) | copy-start | bytes 1376260
  127.1 27.3 %copy-start.4 = (bf16[1792,128]{1,0:T(8,128)(2,1)}, bf16[1792,128]{1,0:T(8,128)(2,1)S(1)}, u32[]{:S(2)}) copy-start(bf16[1792,128]{1,0:T(8,128)(2,1)S(1)} %collective-permute-done.6) | copy-start | bytes 1376260
  133.0 21.2 %all-to-all-start.2 = ((bf16[8,256,256]{1,2,0:T(8,128)(2,1)}), bf16[8,256,256]{1,2,0:T(8,128)(2,1)S(1)}, u32[]{:S(2)}, u32[]{:S(2)}) async-start(bf16[8,256,256]{1,2,0:T(8,128)(2,1)} %dynamic-slice_dynamic-update-slice_fusion), calls=%async_computation.2 | async-start | bytes 2097152 | tf_op jit(solution)/shard_map/all_to_all | solution.py:116
  155.7 19.5 %all-to-all-start.3 = ((bf16[8,256,256]{2,1,0:T(8,128)(2,1)}), bf16[8,256,256]{2,1,0:T(8,128)(2,1)S(1)}, u32[]{:S(2)}, u32[]{:S(2)}) async-start(bf16[8,256,256]{2,1,0:T(8,128)(2,1)} %broadcast_in_dim.149), calls=%async_computation.3 | async-start | bytes 2097152 | tf_op jit(solution)/shard_map/all_to_all | solution.py:124
  175.1 6.5 %copy-start.8 = (bf16[1792,128]{1,0:T(8,128)(2,1)S(1)}, bf16[1792,128]{1,0:T(8,128)(2,1)}, u32[]{:S(2)}) copy-start(bf16[1792,128]{1,0:T(8,128)(2,1)} %copy-done.7) | copy-start | bytes 1376260
  175.2 6.7 %copy-start.6 = (bf16[1792,128]{1,0:T(8,128)(2,1)S(1)}, bf16[1792,128]{1,0:T(8,128)(2,1)}, u32[]{:S(2)}) copy-start(bf16[1792,128]{1,0:T(8,128)(2,1)} %copy-done.5) | copy-start | bytes 1376260
  176.5 5.7 %copy-start.1 = (bf16[1792,128]{1,0:T(8,128)(2,1)S(1)}, bf16[1792,128]{1,0:T(8,128)(2,1)}, u32[]{:S(2)}) copy-start(bf16[1792,128]{1,0:T(8,128)(2,1)} %copy-done) | copy-start | bytes 1376260
  179.1 3.5 %copy-start.10 = (bf16[1792,128]{1,0:T(8,128)(2,1)S(1)}, bf16[1792,128]{1,0:T(8,128)(2,1)}, u32[]{:S(2)}) copy-start(bf16[1792,128]{1,0:T(8,128)(2,1)} %copy-done.9) | copy-start | bytes 1376260
  184.7 6.2 %copy-start.11 = (bf16[1792,128]{1,0:T(8,128)(2,1)S(1)}, bf16[1792,128]{1,0:T(8,128)(2,1)}, u32[]{:S(2)}) copy-start(bf16[1792,128]{1,0:T(8,128)(2,1)} %copy-done.9) | copy-start | bytes 1376260
  213.2 35.2 %copy-start.13 = (s32[4,2,2]{0,2,1:T(2,128)S(1)}, s32[4,2,2]{0,2,1:T(2,128)}, u32[]{:S(2)}) copy-start(s32[4,2,2]{0,2,1:T(2,128)} %param.10) | copy-start | bytes 196

commit v2 on v1

--- a/solution.py
+++ b/solution.py
@@ -1,6 +1,8 @@
 import jax
 import jax.numpy as jnp
 from jax import lax
+from jax.experimental import pallas as pl
+from jax.experimental.pallas import tpu as pltpu
 from jax.sharding import Mesh, PartitionSpec as P
 
 EXP_NODE = 4
@@ -9,6 +11,112 @@
 
 def dot(a, b, dims):
     return lax.dot_general(a, b, (dims, ((), ())), preferred_element_type=jnp.float32)
+
+
+def columns(own, other, core):
+    part = other.shape[0] // (2 * len(own))
+    for ref in own:
+        start = pl.multiple_of(core * part, part)
+        yield ref, start, 2 * part + start
+    for i in range(len(own)):
+        yield other, 2 * i * part, (2 * i + 1) * part
+
+
+def pack_kernel(chips, up, down, *refs):
+    outs, sems = refs[:-1], refs[-1]
+    wide = up.shape[0] // len(outs)
+    tiles = wide // LANES
+    copies = []
+    for i, out in enumerate(outs):
+        start = pl.multiple_of(chips[i] * wide, wide)
+        copies.append(
+            pltpu.make_async_copy(up.at[pl.ds(start, wide)], out.at[pl.ds(0, wide)], sems.at[i, tiles])
+        )
+        for j in range(tiles):
+            copies.append(
+                pltpu.make_async_copy(
+                    down.at[:, pl.ds(start + j * LANES, LANES)],
+                    out.at[pl.ds(wide + j * LANES, LANES)],
+                    sems.at[i, j],
+                )
+            )
+    for copy in copies:
+        copy.start()
+    for copy in copies:
+        copy.wait()
+
+
+def other_kernel(scalars, *refs):
+    blocks, out, sems = refs[:-2], refs[-2], refs[-1]
+    part = blocks[0].shape[0] // 4
+    start = pl.multiple_of((1 - scalars[0]) * part, part)
+    copies = [
+        pltpu.make_async_copy(
+            block.at[pl.ds(2 * u * part + start, part)],
+            out.at[pl.ds((2 * i + u) * part, part)],
+            sems.at[2 * i + u],
+        )
+        for i, block in enumerate(blocks)
+        for u in range(2)
+    ]
+    for copy in copies:
+        copy.start()
+    for copy in copies:
+        copy.wait()
+
+
+def partial_kernel(scalars, rows, *refs):
+    own, other, out = refs[:-2], refs[-2], refs[-1]
+    hidden = other.shape[1]
+    part = other.shape[0] // (2 * len(own))
+    x, dy = rows[:, :part], rows[:, part : 2 * part]
+    for i, (ref, up, down) in enumerate(columns(own, other, scalars[0])):
+        at = scalars[2 + i]
+        out[at, :, :hidden] = dot(x, ref[pl.ds(up, part), :], ((1,), (0,))).astype(out.dtype)
+        tiles = [ref[pl.ds(down + j, LANES), :] for j in range(0, part, LANES)]
+        out[at, :, hidden:] = dot(dy, jnp.concatenate(tiles, 1), ((1,), (1,))).astype(out.dtype)
+
+
+def output_kernel(scalars, rows, every, *refs):
+    own, other, result = refs[:-2], refs[-2], refs[-1]
+    hidden = other.shape[1]
+    part = other.shape[0] // (2 * len(own))
+    count = 2 * len(own)
+    lane = lax.broadcasted_iota(jnp.int32, (rows.shape[0], LANES), 1)
+    mine = lane == scalars[1]
+    gate = jnp.sum(
+        jnp.where(mine, rows[:, 2 * part :].astype(jnp.float32), 0.0), 1, keepdims=True
+    )
+    active = jnp.concatenate([every[scalars[2 + i], :, :hidden] for i in range(count)], 1)
+    grad_pre = jnp.concatenate([every[scalars[2 + i], :, hidden:] for i in range(count)], 1)
+    pieces = list(columns(own, other, scalars[0]))
+    inner = jnp.zeros((rows.shape[0], 1), jnp.float32)
+    for j in range(0, part, LANES):
+        down = jnp.concatenate([ref[pl.ds(d + j, LANES), :] for ref, _, d in pieces], 0)
+        up = jnp.concatenate([ref[pl.ds(u + j, LANES), :] for ref, u, _ in pieces], 1)
+        out = dot(active, down, ((1,), (0,)))
+        inner += jnp.sum(
+            out * rows[:, part + j : part + j + LANES].astype(jnp.float32), 1, keepdims=True
+        )
+        result[:, j : j + LANES] = (gate * out).astype(result.dtype)
+        result[:, part + j : part + j + LANES] = dot(grad_pre, up, ((1,), (1,))).astype(
+            result.dtype
+        )
+    inner = jnp.where(gate > 0, inner, 0.0)
+    result[:, 2 * part :] = jnp.where(mine, inner, 0.0).astype(result.dtype)
+
+
+def call(kernel, shape, scalars, *operands, space=pltpu.VMEM, scratch=()):
+    spec = pl.BlockSpec(memory_space=space)
+    one = jax.ShapeDtypeStruct(shape, jnp.bfloat16) if isinstance(shape, tuple) else shape
+    return pl.pallas_call(
+        kernel,
+        out_shape=one,
+        in_specs=[pl.BlockSpec(memory_space=pltpu.SMEM)] + [spec] * len(operands),
+        out_specs=jax.tree.map(lambda _: spec, one),
+        scratch_shapes=scratch,
+        compiler_params=pltpu.CompilerParams(vmem_limit_bytes=32 * 2**20),
+    )(scalars, *operands)
 
 
 def per_device(tokens, cotangent, groups, choices, gates, up_weight, down_weight):
@@ -40,30 +148,42 @@
         1,
     )
 
-    both_weights = jnp.concatenate(
-        [
-            up_weight.reshape(slices, part, hidden),
-            down_weight.T.reshape(slices, part, hidden),
-        ],
-        1,
-    )
-    sent, both_weights = lax.optimization_barrier((sent, both_weights))
+    chip, core = me // 2, me % 2
+    chips = slices // 2
+    block = jax.ShapeDtypeStruct((4 * part, hidden), bf16)
+    targets = jnp.stack([(chip + s) % chips for s in range(chips)]).astype(jnp.int32)
+    targets, sent = lax.optimization_barrier((targets, sent))
+    own = call(
+        pack_kernel,
+        [block] * chips,
+        targets,
+        up_weight,
+        down_weight,
+        space=pl.ANY,
+        scratch=[pltpu.SemaphoreType.DMA((chips, 2 * part // LANES + 1))],
+    )
+    own = [own[0]] + [
+        lax.ppermute(
+            own[s], "slice", [(i, ((i // 2 + s) % chips) * 2 + i % 2) for i in range(slices)]
+        )
+        for s in range(1, chips)
+    ]
     recv = lax.all_to_all(sent, "node", split_axis=0, concat_axis=0, tiled=True)
-
-    shifts = [(0, 0), (2, 0), (2, 1), (1, 0), (3, 0), (1, 1), (3, 1), (0, 1)]
-    chips = slices // 2
-
-    def moved(index, shift, sign):
-        return ((index // 2 + sign * shift[0]) % chips) * 2 + (index % 2 + shift[1]) % 2
-
-    held = []
-    for shift in shifts:
-        block = lax.dynamic_index_in_dim(both_weights, moved(me, shift, 1), 0, False)
-        if shift != (0, 0):
-            block = lax.ppermute(
-                block, "slice", [(i, moved(i, shift, 1)) for i in range(slices)]
-            )
-        held.append(block)
+    recv, own = lax.optimization_barrier((recv, own))
+
+    sources = [(chip + chips - s) % chips for s in range(chips)]
+    scalars = jnp.stack(
+        [core, expert] + [2 * s + core for s in sources] + [2 * s + 1 - core for s in sources]
+    ).astype(jnp.int32)
+    other = call(
+        other_kernel,
+        (2 * chips * part, hidden),
+        scalars,
+        *own,
+        space=pl.ANY,
+        scratch=[pltpu.SemaphoreType.DMA((2 * chips,))],
+    )
+    other = lax.ppermute(other, "slice", [(i, i + 1 - 2 * (i % 2)) for i in range(slices)])
 
     used = jnp.any(recv[:, 2 * width // LANES, :] > 0, 1)
     rank = jnp.cumsum(used.astype(jnp.int32)) - 1
@@ -89,29 +209,12 @@
     rows = lax.all_to_all(
         spread, ("expert", "slice"), split_axis=0, concat_axis=0, tiled=True
     ).reshape(experts * slices * pairs, -1)
-    x = rows[:, :part]
-    dy = rows[:, part : 2 * part]
     gate = jnp.sum(
         jnp.where(lane[None, :] == expert, rows[:, 2 * part :].astype(f32), 0.0), 1, keepdims=True
     )
 
-    partial = jnp.stack(
-        [
-            jnp.concatenate(
-                [dot(x, w[:part], ((1,), (0,))), dot(dy, w[part:], ((1,), (0,)))], 1
-            ).astype(bf16)
-            for w in held
-        ]
-    )
-    order = jnp.stack([jnp.asarray(moved(me, s, -1)) for s in shifts])
-    where_is = jnp.sum(
-        jnp.where(
-            order[None, :] == jnp.arange(slices)[:, None], jnp.arange(slices)[None, :], 0
-        ),
-        1,
-    )
-    outgoing = jnp.stack(
-        [lax.dynamic_index_in_dim(partial, where_is[m], 0, False) for m in range(slices)]
+    outgoing = call(
+        partial_kernel, (slices, rows.shape[0], 2 * hidden), scalars, rows, *own, other
     )
     incoming = lax.all_to_all(outgoing, "slice", split_axis=0, concat_axis=0, tiled=True)
     both = jnp.sum(incoming.astype(f32), 0)
@@ -120,25 +223,16 @@
     sig = jax.nn.sigmoid(pre)
     active = (pre * sig).astype(bf16)
     grad_pre = (gate * back * sig * (1.0 + pre * (1.0 - sig))).astype(bf16)
-    own = jnp.concatenate([active, grad_pre], 1)
+    units = jnp.concatenate([active, grad_pre], 1)
     every = lax.all_to_all(
-        jnp.broadcast_to(own[None], (slices,) + own.shape),
+        jnp.broadcast_to(units[None], (slices,) + units.shape),
         "slice",
         split_axis=0,
         concat_axis=0,
         tiled=True,
     )
 
-    out = jnp.zeros((x.shape[0], part), f32)
-    dx = jnp.zeros((x.shape[0], part), f32)
-    for i, w in enumerate(held):
-        units = lax.dynamic_index_in_dim(every, order[i], 0, False)
-        out = out + dot(units[:, :hidden], w[part:], ((1,), (1,)))
-        dx = dx + dot(units[:, hidden:], w[:part], ((1,), (1,)))
-    inner = jnp.where(gate > 0, jnp.sum(out * dy.astype(f32), 1, keepdims=True), 0.0)
-    result = jnp.concatenate(
-        [gate * out, dx, jnp.where(lane[None, :] == expert, inner, 0.0)], 1
-    ).astype(bf16)
+    result = call(output_kernel, rows.shape, scalars, rows, every, *own, other)
 
     parts_back = lax.all_to_all(
         result.reshape(experts * slices, pairs, -1),

time: 251 us -> 214 us (0.85)
  matrix products: 24.6 us -> 1.96 us
  between operations: 17.1 us -> 1.22 us
  Pallas kernels: 0 us -> 13.1 us
  local copies, waits for them, and re-layouts: 16.3 us -> 5.14 us
  waiting for transfers between devices: 44.1 us -> 52.2 us
  starting transfers between devices: 40.6 us -> 33.2 us
    dot_general x36 -> x4, matrix products: 24.6 us -> 1.96 us  [dot(): lax.dot_general(a, b, (dims, ((), ())), preferred_element_type=jnp.float32)]
    ppermute x7 -> x4, waiting for transfers between devices: 15.1 us -> 37.7 us  [the longest x3 37.7 us: per_device(): lax.ppermute(own[s], 'slice', [(i, (i // 2 + s) % chips * 2 + i % 2) for...]
    all_to_all x2 -> x1, waiting for transfers between devices: 14.5 us -> 0.01 us  [per_device(): recv = lax.all_to_all(sent, 'node', split_axis=0, concat_axis=0, tiled=True)]
    pallas_call x0 -> x4, Pallas kernels: none -> 13.1 us  [call(): pl.pallas_call(kernel, out_shape=one, in_specs=[pl.BlockSpec(memory_space...]
    ppermute x7 -> x4, starting transfers between devices: 21.4 us -> 12.4 us  [the longest x3 10.5 us: per_device(): lax.ppermute(own[s], 'slice', [(i, (i // 2 + s) % chips * 2 + i % 2) for...]
    all_to_all x1, blocking collectives: 34 us -> 39.9 us  [per_device(): lax.all_to_all(expanded, 'node', split_axis=0, concat_axis=0, tiled=True)]
    concatenate x3 -> x1, other arithmetic: 3.66 us -> 0.02 us  [per_device(): units = jnp.concatenate([active, grad_pre], 1)]
    squeeze x2 -> x0, local copies, waits for them, and re-layouts: 3.6 us -> none  [the longest x1 3.53 us: per_device(): lax.dynamic_index_in_dim(both_weights, moved(me, shift, 1), 0, False)]
  transfers between devices with their start and end apart: 10 -> 6, of which waited for: 5 -> 4; matrix products, arithmetic and copies ran while one was open for 4% -> 0% of each run, Pallas kernels for 0% -> 1%
where the time goes in v2:
time: 214 us
  blocking collectives  100 us (47%)
  waiting for transfers between devices  52.2 us (24%)
  starting transfers between devices  33.2 us (16%)
  Pallas kernels  13.1 us (6%)
  other arithmetic  6.55 us (3%)
  local copies, waits for them, and re-layouts  5.14 us (2%)
    all_to_all x1, blocking collectives, per_device(): lax.all_to_all(expanded, 'node', split_axis=0, concat_axis=0, tiled=True)  39.9 us
    ppermute x3, waiting for transfers between devices, per_device(): lax.ppermute(own[s], 'slice', [(i, (i // 2 + s) % chips * 2 + i % 2) for...  37.7 us
    all_to_all x1, blocking collectives, per_device(): lax.all_to_all(spread, ('expert', 'slice'), split_axis=0, concat_axis=0,...  22.2 us
    all_to_all x1, blocking collectives, per_device(): lax.all_to_all(result.reshape(experts * slices, pairs, -1), ('expert', 's...  19.6 us
    all_to_all x1, blocking collectives, per_device(): lax.all_to_all(jnp.broadcast_to(units[None], (slices,) + units.shape), 's...  18.6 us
    all_to_all x1, starting transfers between devices, per_device(): recv = lax.all_to_all(sent, 'node', split_axis=0, concat_axis=0, tiled=True)  15.2 us
    all_to_all x1, waiting for transfers between devices, per_device(): lax.all_to_all(outgoing, 'slice', split_axis=0, concat_axis=0, tiled=True)  14.5 us
    pallas_call x4, Pallas kernels, call(): pl.pallas_call(kernel, out_shape=one, in_specs=[pl.BlockSpec(memory_space...  13.1 us
  transfers between devices with their start and end apart: 6, of which 4 were waited for; matrix products, arithmetic and copies ran while one was open for 0% of the time, Pallas kernels for 1%

profile of v2, /device:TPU:2, one launch (start us, length us, event | category | flops | bytes accessed | tf_op | source)
XLA Modules:
  0.0 213.6 jit_solution(3116940946560253636)
XLA Ops:
  0.7 0.9 iota_compare_fusion.3
  1.6 1.2 fusion
  2.8 0.1 copy.25
  2.9 0.7 convert_element_type.83
  3.6 0.8 select_reduce_fusion.4
  4.4 0.1 select_reduce_fusion.2
  4.5 0.8 fusion.2
  5.3 0.1 pad_add_fusion.chips
  5.4 15.2 %all-to-all-start = ((bf16[16,120,128]{2,1,0:T(8,128)(2,1)}), bf16[16,120,128]{2,1,0:T(8,128)(2,1)S(1)}, u32[]{:S(2)}, u32[]{:S(2)}) async-start(bf16[16,120,128]{2,1,0:T(8,128)(2,1)} %fusion.2), calls=%async_computation | async-start | bytes 983040 | tf_op jit(solution)/shard_map/all_to_all | solution.py:171
  20.6 0.0 copy-start.7
  20.6 1.5 copy-done.7
  22.1 3.0 %shard_map.94 = (bf16[3584,128]{1,0:T(8,128)(2,1)S(1)}, bf16[3584,128]{1,0:T(8,128)(2,1)}, bf16[3584,128]{1,0:T(8,128)(2,1)}, bf16[3584,128]{1,0:T(8,128)(2,1)}) custom-call(s32[4]{0:T(128)S(1)} %pad_add_fusion.chips, bf16[7168,128]{1,0:T(8,128)(2,1)S(1)} %copy-done.6, bf16[128,7168]{1,0:T(8,128)(2,1)S(1)} %copy-done.7), custom_call_target="tpu_custom_call" | custom-call | tf_op jit(solution)/shard_map/pallas_call | solution.py:112
  25.2 3.4 %collective-permute-start = (bf16[3584,128]{1,0:T(8,128)(2,1)}, bf16[3584,128]{1,0:T(8,128)(2,1)S(1)}, u32[]{:S(2)}, u32[]{:S(2)}) collective-permute-start(bf16[3584,128]{1,0:T(8,128)(2,1)} %get-tuple-element.17), channel_id=1, source_target_pairs={{0,2},{1,3},{2,4},{3,5},{4,6},{5,7},{6,0},{7,1},{8,10},{9,11},{10,... | collective-permute-start | bytes 2752520 | tf_op jit(solution)/shard_map/ppermute | solution.py:166
  28.6 3.0 %collective-permute-start.1 = (bf16[3584,128]{1,0:T(8,128)(2,1)}, bf16[3584,128]{1,0:T(8,128)(2,1)S(1)}, u32[]{:S(2)}, u32[]{:S(2)}) collective-permute-start(bf16[3584,128]{1,0:T(8,128)(2,1)} %get-tuple-element.18), channel_id=1, source_target_pairs={{0,4},{1,5},{2,6},{3,7},{4,0},{5,1},{6,2},{7,3},{8,12},{9,13},{10,... | collective-permute-start | bytes 2752520 | tf_op jit(solution)/shard_map/ppermute | solution.py:166
  31.6 4.1 %collective-permute-start.2 = (bf16[3584,128]{1,0:T(8,128)(2,1)}, bf16[3584,128]{1,0:T(8,128)(2,1)}, u32[]{:S(2)}, u32[]{:S(2)}) collective-permute-start(bf16[3584,128]{1,0:T(8,128)(2,1)} %get-tuple-element.19), channel_id=1, source_target_pairs={{0,6},{1,7},{2,0},{3,1},{4,2},{5,3},{6,4},{7,5},{8,14},{9,15},{10,... | collective-permute-start | bytes 2752520 | tf_op jit(solution)/shard_map/ppermute | solution.py:166
  35.7 0.1 stack.90.scalars
  35.8 14.7 %collective-permute-done.refs_1_ = bf16[3584,128]{1,0:T(8,128)(2,1)S(1)} collective-permute-done((bf16[3584,128]{1,0:T(8,128)(2,1)}, bf16[3584,128]{1,0:T(8,128)(2,1)S(1)}, u32[]{:S(2)}, u32[]{:S(2)}) %collective-permute-start) | collective-permute-done | bytes 917536 | tf_op jit(solution)/shard_map/ppermute | solution.py:166
  50.6 5.0 %collective-permute-done.1.refs_2_ = bf16[3584,128]{1,0:T(8,128)(2,1)S(1)} collective-permute-done((bf16[3584,128]{1,0:T(8,128)(2,1)}, bf16[3584,128]{1,0:T(8,128)(2,1)S(1)}, u32[]{:S(2)}, u32[]{:S(2)}) %collective-permute-start.1) | collective-permute-done | bytes 917536 | tf_op jit(solution)/shard_map/ppermute | solution.py:166
  55.5 18.0 %collective-permute-done.2.refs_3_ = bf16[3584,128]{1,0:T(8,128)(2,1)} collective-permute-done((bf16[3584,128]{1,0:T(8,128)(2,1)}, bf16[3584,128]{1,0:T(8,128)(2,1)}, u32[]{:S(2)}, u32[]{:S(2)}) %collective-permute-start.2) | collective-permute-done | bytes 917536 | tf_op jit(solution)/shard_map/ppermute | solution.py:166
  73.5 0.4 compare_reduce_fusion
  73.9 0.1 copy.22
  74.0 0.1 add_reduce_fusion
  74.1 0.2 convolution_convert_fusion.1
  74.4 3.4 %shard_map.95 = bf16[7168,128]{1,0:T(8,128)(2,1)S(1)} custom-call(s32[10]{0:T(128)S(1)} %stack.90.scalars, bf16[3584,128]{1,0:T(8,128)(2,1)S(1)} %get-tuple-element.21.refs_0_, bf16[3584,128]{1,0:T(8,128)(2,1)S(1)} %collective-permute-done.refs_1_, bf16[3584,128]{1,0:T(8,128)(2,1)S(1)} %collective-permute-done.1.refs_2_, ...), custom_call_target="tpu_custom_call" | custom-call | tf_op jit(solution)/shard_map/pallas_call | solution.py:112
  77.9 1.9 collective-permute-start.3
  79.9 0.1 broadcast_in_dim.105
  80.0 22.2 %all_to_all.30 = bf16[32,8,1920]{2,1,0:T(8,128)(2,1)S(1)} all-to-all(bf16[32,8,1920]{2,1,0:T(8,128)(2,1)S(1)} %bitcast.142), channel_id=1, replica_groups=mesh['node'=16,'expert'=4,'slice'=8] {'expert','slice'}, dimensions={0} | all-to-all | bytes 1966080 | tf_op jit(solution)/shard_map/all_to_all | solution.py:209
  102.2 3.3 %shard_map.96 = bf16[8,256,256]{2,1,0:T(8,128)(2,1)S(1)} custom-call(s32[10]{0:T(128)S(1)} %stack.90.scalars, bf16[256,1920]{1,0:T(8,128)(2,1)S(1)} %bitcast.138, bf16[3584,128]{1,0:T(8,128)(2,1)S(1)} %get-tuple-element.21.refs_0_, bf16[3584,128]{1,0:T(8,128)(2,1)S(1)} %collective-permute-done.refs_1_, bf16[3584,128]{1,0:T(8,128)(2,1)S(1)} %copy-done.1, ...), custom_call_target="tpu_custom_call" | custom-call | tf_op jit(solution)/shard_map/pallas_call | solution.py:112
  105.5 1.2 copy-done.3
  106.7 1.0 copy-done.5
  107.7 5.6 %all-to-all-start.2 = ((bf16[8,256,256]{2,1,0:T(8,128)(2,1)}), bf16[8,256,256]{2,1,0:T(8,128)(2,1)}, u32[]{:S(2)}, u32[]{:S(2)}) async-start(bf16[8,256,256]{2,1,0:T(8,128)(2,1)} %copy-done.5), calls=%async_computation.2 | async-start | bytes 2097152 | tf_op jit(solution)/shard_map/all_to_all | solution.py:219
  113.2 0.1 select_reduce_fusion
  113.3 14.5 %all-to-all-done.2 = bf16[8,256,256]{2,1,0:T(8,128)(2,1)} async-done(((bf16[8,256,256]{2,1,0:T(8,128)(2,1)}), bf16[8,256,256]{2,1,0:T(8,128)(2,1)}, u32[]{:S(2)}, u32[]{:S(2)}) %all-to-all-start.2) | async-done | bytes 1048608 | tf_op jit(solution)/shard_map/all_to_all | solution.py:219
  127.9 1.4 convert_reduce_fusion
  129.3 0.1 multiply_convert_fusion
  129.4 0.1 broadcast_in_dim.108
  129.5 18.6 %all_to_all.31.every = bf16[8,256,256]{2,1,0:T(8,128)(2,1)S(1)} all-to-all(bf16[8,256,256]{2,1,0:T(8,128)(2,1)S(1)} %broadcast_in_dim.108), channel_id=1, replica_groups=mesh['node'=16,'expert'=4,'slice'=8] {'slice'}, dimensions={0} | all-to-all | bytes 2097152 | tf_op jit(solution)/shard_map/all_to_all | solution.py:227
  148.1 3.3 %shard_map.97 = bf16[256,1920]{1,0:T(8,128)(2,1)S(1)} custom-call(s32[10]{0:T(128)S(1)} %stack.90.scalars, bf16[256,1920]{1,0:T(8,128)(2,1)S(1)} %bitcast.140, bf16[8,256,256]{2,1,0:T(8,128)(2,1)S(1)} %all_to_all.31.every, bf16[3584,128]{1,0:T(8,128)(2,1)S(1)} %get-tuple-element.21.refs_0_, bf16[3584,128]{1,0:T(8,128)(2,1)S(1)} %collective-permute-done.refs_1_, ...), custom_call_target="tpu_custom_call" | custom-call | tf_op jit(solution)/shard_map/pallas_call | solution.py:112
  151.5 19.6 %all_to_all.32 = bf16[32,8,1920]{2,1,0:T(8,128)(2,1)S(1)} all-to-all(bf16[32,8,1920]{2,1,0:T(8,128)(2,1)S(1)} %bitcast.141), channel_id=1, replica_groups=mesh['node'=16,'expert'=4,'slice'=8] {'expert','slice'}, dimensions={0} | all-to-all | bytes 1966080 | tf_op jit(solution)/shard_map/all_to_all | solution.py:237
  171.1 0.1 convert_reduce_fusion.1
  171.5 0.3 convolution_convert_fusion
  171.9 0.0 copy-start.8
  171.9 0.1 copy.27
  172.0 39.9 %all_to_all.33 = bf16[16,120,128]{2,1,0:T(8,128)(2,1)S(1)} all-to-all(bf16[16,120,128]{2,1,0:T(8,128)(2,1)S(1)} %bitcast.145), channel_id=1, replica_groups=mesh['node'=16,'expert'=4,'slice'=8] {'node'}, dimensions={0} | all-to-all | bytes 983040 | tf_op jit(solution)/shard_map/all_to_all | solution.py:254
  211.9 0.2 convolution_convert_fusion.3
  212.1 0.7 fusion.30
  212.8 0.1 select_reduce_fusion.1
  212.9 0.7 select_reduce_fusion.3
  (56 shorter events, 0.5 us)
Async XLA Ops:
  0.6 20.0 %copy-start.6 = (bf16[7168,128]{1,0:T(8,128)(2,1)S(1)}, bf16[7168,128]{1,0:T(8,128)(2,1)}, u32[]{:S(2)}) copy-start(bf16[7168,128]{1,0:T(8,128)(2,1)} %up.1) | copy-start | bytes 5505028
  5.4 68.1 %all-to-all-start = ((bf16[16,120,128]{2,1,0:T(8,128)(2,1)}), bf16[16,120,128]{2,1,0:T(8,128)(2,1)S(1)}, u32[]{:S(2)}, u32[]{:S(2)}) async-start(bf16[16,120,128]{2,1,0:T(8,128)(2,1)} %fusion.2), calls=%async_computation | async-start | bytes 983040 | tf_op jit(solution)/shard_map/all_to_all | solution.py:171
  20.6 1.5 copy-start.7
  25.2 25.4 %collective-permute-start = (bf16[3584,128]{1,0:T(8,128)(2,1)}, bf16[3584,128]{1,0:T(8,128)(2,1)S(1)}, u32[]{:S(2)}, u32[]{:S(2)}) collective-permute-start(bf16[3584,128]{1,0:T(8,128)(2,1)} %get-tuple-element.17), channel_id=1, source_target_pairs={{0,2},{1,3},{2,4},{3,5},{4,6},{5,7},{6,0},{7,1},{8,10},{9,11},{10,... | collective-permute-start | bytes 2752520 | tf_op jit(solution)/shard_map/ppermute | solution.py:166
  28.6 26.9 %collective-permute-start.1 = (bf16[3584,128]{1,0:T(8,128)(2,1)}, bf16[3584,128]{1,0:T(8,128)(2,1)S(1)}, u32[]{:S(2)}, u32[]{:S(2)}) collective-permute-start(bf16[3584,128]{1,0:T(8,128)(2,1)} %get-tuple-element.18), channel_id=1, source_target_pairs={{0,4},{1,5},{2,6},{3,7},{4,0},{5,1},{6,2},{7,3},{8,12},{9,13},{10,... | collective-permute-start | bytes 2752520 | tf_op jit(solution)/shard_map/ppermute | solution.py:166
  31.6 41.9 %collective-permute-start.2 = (bf16[3584,128]{1,0:T(8,128)(2,1)}, bf16[3584,128]{1,0:T(8,128)(2,1)}, u32[]{:S(2)}, u32[]{:S(2)}) collective-permute-start(bf16[3584,128]{1,0:T(8,128)(2,1)} %get-tuple-element.19), channel_id=1, source_target_pairs={{0,6},{1,7},{2,0},{3,1},{4,2},{5,3},{6,4},{7,5},{8,14},{9,15},{10,... | collective-permute-start | bytes 2752520 | tf_op jit(solution)/shard_map/ppermute | solution.py:166
  55.5 22.3 %copy-start = (bf16[3584,128]{1,0:T(8,128)(2,1)}, bf16[3584,128]{1,0:T(8,128)(2,1)S(1)}, u32[]{:S(2)}) copy-start(bf16[3584,128]{1,0:T(8,128)(2,1)S(1)} %collective-permute-done.1.refs_2_) | copy-start | bytes 2752516
  77.9 24.3 %collective-permute-start.3 = (bf16[7168,128]{1,0:T(8,128)(2,1)S(1)}, bf16[7168,128]{1,0:T(8,128)(2,1)S(1)}, u32[]{:S(2)}, u32[]{:S(2)}) collective-permute-start(bf16[7168,128]{1,0:T(8,128)(2,1)S(1)} %shard_map.95), channel_id=1, source_target_pairs={{0,1},{1,0},{2,3},{3,2},{4,5},{5,4},{6,7},{7,6},{8,9},{9,8},{10,11... | collective-permute-start | bytes 5505032 | tf_op jit(solution)/shard_map/ppermute | solution.py:186
  79.8 22.4 %copy-start.1 = (bf16[3584,128]{1,0:T(8,128)(2,1)S(1)}, bf16[3584,128]{1,0:T(8,128)(2,1)}, u32[]{:S(2)}) copy-start(bf16[3584,128]{1,0:T(8,128)(2,1)} %copy-done) | copy-start | bytes 2752516
  105.4 1.3 copy-start.3
  106.7 1.0 copy-start.5
  107.7 20.2 %all-to-all-start.2 = ((bf16[8,256,256]{2,1,0:T(8,128)(2,1)}), bf16[8,256,256]{2,1,0:T(8,128)(2,1)}, u32[]{:S(2)}, u32[]{:S(2)}) async-start(bf16[8,256,256]{2,1,0:T(8,128)(2,1)} %copy-done.5), calls=%async_computation.2 | async-start | bytes 2097152 | tf_op jit(solution)/shard_map/all_to_all | solution.py:219
  129.4 18.8 %copy-start.2 = (bf16[3584,128]{1,0:T(8,128)(2,1)S(1)}, bf16[3584,128]{1,0:T(8,128)(2,1)}, u32[]{:S(2)}) copy-start(bf16[3584,128]{1,0:T(8,128)(2,1)} %copy-done) | copy-start | bytes 2752516
  129.4 18.8 %copy-start.4 = (bf16[7168,128]{1,0:T(8,128)(2,1)S(1)}, bf16[7168,128]{1,0:T(8,128)(2,1)}, u32[]{:S(2)}) copy-start(bf16[7168,128]{1,0:T(8,128)(2,1)} %copy-done.3) | copy-start | bytes 5505028
  171.9 41.0 %copy-start.8 = (s32[4,2,2]{0,2,1:T(2,128)S(1)}, s32[4,2,2]{0,2,1:T(2,128)}, u32[]{:S(2)}) copy-start(s32[4,2,2]{0,2,1:T(2,128)} %param.10) | copy-start | bytes 196

commit v3 on v1

v3 whole, which is shorter than its diff:
```python
import jax
import jax.numpy as jnp
from jax import lax
from jax.experimental import pallas as pl
from jax.experimental.pallas import tpu as pltpu
from jax.sharding import Mesh, PartitionSpec as P

EXPERTS = 4
CORES = 2
LANES = 128


def dot(a, b, dims):
    return lax.dot_general(a, b, (dims, ((), ())), preferred_element_type=jnp.float32)


def pack_kernel(chips, up, down, here, ahead, behind, sems):
    wide = here.shape[0] // 2
    tiles = wide // LANES
    copies = []

    def rows(chip, out, at):
        start = pl.multiple_of(chips[chip] * wide, wide)
        copies.append(
            pltpu.make_async_copy(
                up.at[pl.ds(start, wide)], out.at[pl.ds(at, wide)], sems.at[len(copies)]
            )
        )

    def columns(chip, out, at):
        start = pl.multiple_of(chips[chip] * wide, wide)
        for j in range(0, wide, LANES):
            copies.append(
                pltpu.make_async_copy(
                    down.at[:, pl.ds(start + j, LANES)],
                    out.at[pl.ds(at + j, LANES)],
                    sems.at[len(copies)],
                )
            )

    for chip, out in ((1, ahead), (3, behind), (0, here)):
        rows(chip, out, 0)
        columns(chip, out, wide)
    rows(2, ahead, 2 * wide)
    columns(2, behind, 2 * wide)
    for copy in copies:
        copy.start()
    for copy in copies:
        copy.wait()


def partial_kernel(scalars, rows, *refs):
    blocks, out = refs[:-1], refs[-1]
    hidden = blocks[0].shape[1]
    wide = (rows.shape[1] - LANES) // 2
    x, dy = rows[:, :wide], rows[:, wide : 2 * wide]
    for i in range(len(blocks) // CORES):
        pair = blocks[CORES * i : CORES * (i + 1)]
        at = scalars[1 + i]
        up = jnp.concatenate([ref[:wide, :] for ref in pair], 1)
        out[at, :, : CORES * hidden] = dot(x, up, ((1,), (0,))).astype(out.dtype)
        down = jnp.concatenate(
            [
                jnp.concatenate([ref[wide + j : wide + j + LANES, :] for ref in pair], 0)
                for j in range(0, wide, LANES)
            ],
            1,
        )
        out[at, :, CORES * hidden :] = dot(dy, down, ((1,), (1,))).astype(out.dtype)


def output_kernel(scalars, rows, every, *refs):
    blocks, result = refs[:-1], refs[-1]
    hidden = blocks[0].shape[1]
    wide = (rows.shape[1] - LANES) // 2
    chips = len(blocks) // CORES
    count = rows.shape[0]
    lane = lax.broadcasted_iota(jnp.int32, (count, LANES), 1)
    mine = lane == scalars[0]
    gate = jnp.sum(
        jnp.where(mine, rows[:, 2 * wide :].astype(jnp.float32), 0.0), 1, keepdims=True
    )
    active = jnp.concatenate(
        [every[scalars[1 + i], :, : CORES * hidden] for i in range(chips)], 1
    )
    grad_pre = jnp.concatenate(
        [every[scalars[1 + i], :, CORES * hidden :] for i in range(chips)], 1
    )
    inner = jnp.zeros((count, 1), jnp.float32)
    step = 2 * LANES
    for j in range(0, wide, step):
        down = jnp.concatenate(
            [
                jnp.concatenate([ref[wide + j + k : wide + j + k + LANES, :] for ref in blocks], 0)
                for k in range(0, step, LANES)
            ],
            1,
        )
        up = jnp.concatenate([ref[j : j + step, :] for ref in blocks], 1)
        out = dot(active, down, ((1,), (0,)))
        inner += jnp.sum(
            out * rows[:, wide + j : wide + j + step].astype(jnp.float32), 1, keepdims=True
        )
        result[:, j : j + step] = (gate * out).astype(result.dtype)
        result[:, wide + j : wide + j + step] = dot(grad_pre, up, ((1,), (1,))).astype(
            result.dtype
        )
    inner = jnp.where(gate > 0, inner, 0.0)
    result[:, 2 * wide :] = jnp.where(mine, inner, 0.0).astype(result.dtype)


def call(kernel, shapes, scalars, *operands, space=pltpu.VMEM, scratch=()):
    spec = pl.BlockSpec(memory_space=space)
    out = [jax.ShapeDtypeStruct(shape, jnp.bfloat16) for shape in shapes]
    return pl.pallas_call(
        kernel,
        out_shape=out,
        in_specs=[pl.BlockSpec(memory_space=pltpu.SMEM)] + [spec] * len(operands),
        out_specs=[spec] * len(out),
        scratch_shapes=scratch,
        compiler_params=pltpu.CompilerParams(vmem_limit_bytes=40 * 2**20),
    )(scalars, *operands)


def per_device(tokens, cotangent, groups, choices, gates, up_weight, down_weight):
    f32, bf16 = jnp.float32, jnp.bfloat16
    tok_count, width = tokens.shape
    nodes = lax.axis_size("node")
    experts = lax.axis_size("expert")
    chips = lax.axis_size("chip")
    hidden = up_weight.shape[1]
    pairs = 2 * tok_count
    wide = width // chips
    expert = lax.axis_index("expert")
    chip = lax.axis_index("chip")
    lane = jnp.arange(LANES, dtype=jnp.int32)
    node_ids = jnp.arange(nodes, dtype=jnp.int32)

    place = node_ids[:, None, None] == groups[None]
    token_at = jnp.any(place, 2).astype(bf16)
    dense = jnp.sum(
        jnp.where(choices[..., None] == lane, gates[..., None].astype(f32), 0.0), 2
    )
    table = jnp.sum(jnp.where(place[..., None], dense[None], 0.0), (1, 2)).astype(bf16)
    packed = jnp.concatenate([tokens, cotangent], 1)
    sent = jnp.concatenate(
        [
            dot(token_at, packed, ((1,), (0,))).astype(bf16).reshape(nodes, -1, LANES),
            jnp.pad(table[:, None, :], ((0, 0), (0, 7), (0, 0))),
        ],
        1,
    )

    ahead_of = [(i, (i + 1) % chips) for i in range(chips)]
    behind_of = [(i, (i - 1) % chips) for i in range(chips)]
    targets = jnp.stack([(chip + s) % chips for s in range(chips)]).astype(jnp.int32)
    targets, sent = lax.optimization_barrier((targets, sent))
    here, ahead, behind = call(
        pack_kernel,
        [(2 * wide, hidden), (3 * wide, hidden), (3 * wide, hidden)],
        targets,
        up_weight,
        down_weight,
        space=pl.ANY,
        scratch=[pltpu.SemaphoreType.DMA((chips * (wide // LANES + 1),))],
    )
    ahead = lax.ppermute(ahead, "chip", ahead_of)
    behind = lax.ppermute(behind, "chip", behind_of)
    recv = lax.all_to_all(sent, "node", split_axis=0, concat_axis=0, tiled=True)
    recv, ahead, behind = lax.optimization_barrier((recv, ahead, behind))
    swap = [(0, 1), (1, 0)]
    blocks = []
    for block in (here, ahead, behind):
        blocks += [block, lax.ppermute(block, "core", swap)]
    far_up = lax.ppermute(ahead[2 * wide :], "chip", ahead_of)
    far_down = lax.ppermute(behind[2 * wide :], "chip", behind_of)
    scalars = jnp.stack(
        [expert, chip, (chip + chips - 1) % chips, (chip + 1) % chips, (chip + 2) % chips]
    ).astype(jnp.int32)

    used = jnp.any(recv[:, 2 * width // LANES, :] > 0, 1)
    rank = jnp.cumsum(used.astype(jnp.int32)) - 1
    slot = jnp.arange(pairs, dtype=jnp.int32)
    pick = ((rank[None, :] == slot[:, None]) & used[None, :]).astype(bf16)
    mine = dot(pick, recv.reshape(nodes, -1), ((1,), (0,))).astype(bf16)
    parts = jnp.stack(
        [
            jnp.concatenate(
                [
                    mine[:, m * wide : (m + 1) * wide],
                    mine[:, width + m * wide : width + (m + 1) * wide],
                    mine[:, 2 * width : 2 * width + LANES],
                ],
                1,
            )
            for m in range(chips)
        ]
    )
    spread = jnp.broadcast_to(parts[None], (experts,) + parts.shape).reshape(
        experts * chips, pairs, -1
    )
    rows = lax.all_to_all(
        spread, ("expert", "chip"), split_axis=0, concat_axis=0, tiled=True
    ).reshape(experts * chips * pairs, -1)
    rows, far_up, far_down = lax.optimization_barrier((rows, far_up, far_down))
    far = jnp.concatenate([far_up, far_down], 0)
    blocks += [far, lax.ppermute(far, "core", swap)]
    gate = jnp.sum(
        jnp.where(lane[None, :] == expert, rows[:, 2 * wide :].astype(f32), 0.0), 1, keepdims=True
    )

    units = CORES * hidden
    (outgoing,) = call(
        partial_kernel, [(chips, rows.shape[0], 2 * units)], scalars, rows, *blocks
    )
    incoming = lax.all_to_all(outgoing, "chip", split_axis=0, concat_axis=0, tiled=True)
    both = jnp.sum(incoming.astype(f32), 0)
    pre = both[:, :units]
    back = both[:, units:]
    sig = jax.nn.sigmoid(pre)
    active = (pre * sig).astype(bf16)
    grad_pre = (gate * back * sig * (1.0 + pre * (1.0 - sig))).astype(bf16)
    every = lax.all_gather(jnp.concatenate([active, grad_pre], 1), "chip", axis=0)

    (result,) = call(output_kernel, [rows.shape], scalars, rows, every, *blocks)

    parts_back = lax.all_to_all(
        result.reshape(experts * chips, pairs, -1),
        ("expert", "chip"),
        split_axis=0,
        concat_axis=0,
        tiled=True,
    ).reshape(experts, chips, pairs, -1)
    summed = jnp.sum(parts_back.astype(f32), 0)
    inner_all = jnp.sum(summed[:, :, 2 * wide :], 0)
    full = jnp.concatenate(
        [summed[m, :, :wide] for m in range(chips)]
        + [summed[m, :, wide : 2 * wide] for m in range(chips)]
        + [inner_all],
        1,
    ).astype(bf16)
    expanded = dot(pick, full, ((0,), (0,))).astype(bf16)
    expanded = jnp.pad(expanded, ((0, 0), (0, 7 * LANES))).reshape(nodes, -1, LANES)
    home = lax.all_to_all(expanded, "node", split_axis=0, concat_axis=0, tiled=True)

    home_rows = home[:, : 2 * width // LANES].reshape(nodes, -1)
    total = dot(token_at, home_rows, ((0,), (0,))).astype(bf16)
    inner_rows = home[:, 2 * width // LANES].astype(f32)
    pair_inner = jnp.sum(jnp.where(place[..., None], inner_rows[:, None, None, :], 0.0), 0)
    grad_gates = jnp.sum(
        jnp.where(choices[..., None] == lane, pair_inner[:, :, None, :], 0.0), -1
    ).astype(bf16)
    return (total[:, :width], total[:, width:], grad_gates)


def solution(mesh):
    nodes, members = mesh.devices.shape
    axes = ("node", "expert", "chip", "core")
    fine = Mesh(
        mesh.devices.reshape(nodes, EXPERTS, members // (EXPERTS * CORES), CORES), axes
    )
    placed = (
        P(axes, None),
        P(axes, None),
        P(axes, None),
        P(axes, None, None),
        P(axes, None, None),
        P(None, axes),
        P(axes, None),
    )
    return jax.shard_map(
        per_device,
        mesh=fine,
        in_specs=placed,
        out_specs=(P(axes, None), P(axes, None), P(axes, None, None)),
        check_vma=False,
    )
```

time: 251 us -> 195 us (0.78)
  the two profiles are of different devices: /device:TPU:2 before, /device:TPU:64 now
where the time goes in v3:
time: 195 us; the launch traced here: 194 us
  blocking collectives  66.8 us (34%)
  waiting for transfers between devices  48.6 us (25%)
  starting transfers between devices  48.1 us (25%)
  Pallas kernels  12.5 us (6%)
  local copies, waits for them, and re-layouts  8.38 us (4%)
  other arithmetic  6.17 us (3%)
  matrix products  1.96 us (1%)
    all_to_all x1, blocking collectives, per_device(): lax.all_to_all(expanded, 'node', split_axis=0, concat_axis=0, tiled=True)  35.1 us
    ppermute x1, waiting for transfers between devices, per_device(): ahead = lax.ppermute(ahead, 'chip', ahead_of)  27.4 us
    all_to_all x1, blocking collectives, per_device(): lax.all_to_all(result.reshape(experts * chips, pairs, -1), ('expert', 'ch...  18.3 us
    all_to_all x1, starting transfers between devices, per_device(): recv = lax.all_to_all(sent, 'node', split_axis=0, concat_axis=0, tiled=True)  14.8 us
    all_gather x1, blocking collectives, per_device(): lax.all_gather(jnp.concatenate([active, grad_pre], 1), 'chip', axis=0)  13.4 us
    pallas_call x3, Pallas kernels, call(): pl.pallas_call(kernel, out_shape=out, in_specs=[pl.BlockSpec(memory_space...  12.5 us
    all_to_all x1, waiting for transfers between devices, per_device(): lax.all_to_all(outgoing, 'chip', split_axis=0, concat_axis=0, tiled=True)  9.98 us
    all_to_all x1, starting transfers between devices, per_device(): lax.all_to_all(spread, ('expert', 'chip'), split_axis=0, concat_axis=0, t...  6.97 us
  transfers between devices with their start and end apart: 11, of which 6 were waited for; matrix products, arithmetic and copies ran while one was open for 2% of the time, Pallas kernels for 2%

profile of v3, /device:TPU:64, one launch (start us, length us, event | category | flops | bytes accessed | tf_op | source)
XLA Modules:
  0.0 193.5 jit_solution(4759248723472470018)
XLA Ops:
  0.7 0.8 iota_compare_fusion.3
  1.4 0.7 convert_element_type.83
  2.1 0.8 select_reduce_fusion.4
  2.9 0.1 select_reduce_fusion.2
  3.0 1.2 fusion
  4.3 0.8 fusion.2
  5.3 14.8 %all-to-all-start = ((bf16[16,120,128]{2,1,0:T(8,128)(2,1)}), bf16[16,120,128]{2,1,0:T(8,128)(2,1)S(1)}, u32[]{:S(2)}, u32[]{:S(2)}) async-start(bf16[16,120,128]{2,1,0:T(8,128)(2,1)} %fusion.2), calls=%async_computation | async-start | bytes 983040 | tf_op jit(solution)/shard_map/all_to_all | solution.py:169
  20.0 1.5 copy-done.2
  21.5 2.9 %shard_map.94 = (bf16[3584,128]{1,0:T(8,128)(2,1)}, bf16[5376,128]{1,0:T(8,128)(2,1)S(1)}, bf16[5376,128]{1,0:T(8,128)(2,1)S(1)}) custom-call(s32[4]{0:T(128)S(1)} %pad_add_fusion.chips, bf16[7168,128]{1,0:T(8,128)(2,1)S(1)} %copy-done.1, bf16[128,7168]{1,0:T(8,128)(2,1)S(1)} %copy-done.2), custom_call_target="tpu_custom_call" | custom-call | tf_op jit(solution)/shard_map/pallas_call | solution.py:115
  24.4 3.4 %collective-permute-start = (bf16[5376,128]{1,0:T(8,128)(2,1)S(1)}, bf16[5376,128]{1,0:T(8,128)(2,1)S(1)}, u32[]{:S(2)}, u32[]{:S(2)}) collective-permute-start(bf16[5376,128]{1,0:T(8,128)(2,1)S(1)} %get-tuple-element.16), channel_id=1, source_target_pairs={{0,2},{2,4},{4,6},{6,0},{1,3},{3,5},{5,7},{7,1},{8,10},{10,12},{12... | collective-permute-start | bytes 4128776 | tf_op jit(solution)/shard_map/ppermute | solution.py:167
  27.9 3.7 %collective-permute-start.1 = (bf16[5376,128]{1,0:T(8,128)(2,1)S(1)}, bf16[5376,128]{1,0:T(8,128)(2,1)}, u32[]{:S(2)}, u32[]{:S(2)}) collective-permute-start(bf16[5376,128]{1,0:T(8,128)(2,1)S(1)} %get-tuple-element.17), channel_id=1, source_target_pairs={{0,6},{2,0},{4,2},{6,4},{1,7},{3,1},{5,3},{7,5},{8,14},{10,8},{12,... | collective-permute-start | bytes 4128776 | tf_op jit(solution)/shard_map/ppermute | solution.py:168
  31.5 27.4 %collective-permute-done.refs_2_ = bf16[5376,128]{1,0:T(8,128)(2,1)S(1)} collective-permute-done((bf16[5376,128]{1,0:T(8,128)(2,1)S(1)}, bf16[5376,128]{1,0:T(8,128)(2,1)S(1)}, u32[]{:S(2)}, u32[]{:S(2)}) %collective-permute-start) | collective-permute-done | bytes 1376288 | tf_op jit(solution)/shard_map/ppermute | solution.py:167
  58.9 2.0 %collective-permute-done.1.refs_4_ = bf16[5376,128]{1,0:T(8,128)(2,1)} collective-permute-done((bf16[5376,128]{1,0:T(8,128)(2,1)S(1)}, bf16[5376,128]{1,0:T(8,128)(2,1)}, u32[]{:S(2)}, u32[]{:S(2)}) %collective-permute-start.1) | collective-permute-done | bytes 1376288 | tf_op jit(solution)/shard_map/ppermute | solution.py:168
  60.9 0.4 compare_reduce_fusion
  61.4 0.1 add_reduce_fusion
  61.6 0.2 convolution_convert_fusion.1
  61.9 1.0 broadcast_in_dim.99
  62.9 7.0 %all-to-all-start.1 = ((bf16[16,8,3712]{2,1,0:T(8,128)(2,1)}), bf16[16,8,3712]{2,1,0:T(8,128)(2,1)S(1)}, u32[]{:S(2)}, u32[]{:S(2)}) async-start(bf16[16,8,3712]{2,1,0:T(8,128)(2,1)} %bitcast.12), calls=%async_computation.1 | async-start | bytes 1900544 | tf_op jit(solution)/shard_map/all_to_all | solution.py:202
  69.9 1.1 slice.107
  71.0 5.0 %collective-permute-start.3 = (bf16[1792,128]{1,0:T(8,128)(2,1)S(1)}, bf16[1792,128]{1,0:T(8,128)(2,1)S(1)}, u32[]{:S(2)}, u32[]{:S(2)}) collective-permute-start(bf16[1792,128]{1,0:T(8,128)(2,1)S(1)} %slice.107), channel_id=1, source_target_pairs={{0,6},{2,0},{4,2},{6,4},{1,7},{3,1},{5,3},{7,5},{8,14},{10,8},{12,... | collective-permute-start | bytes 1376264 | tf_op jit(solution)/shard_map/ppermute | solution.py:176
  76.0 1.9 collective-permute-start.2
  78.0 1.9 collective-permute-start.4
  79.9 2.4 %collective-permute-start.5 = (bf16[5376,128]{1,0:T(8,128)(2,1)S(1)}, bf16[5376,128]{1,0:T(8,128)(2,1)}, u32[]{:S(2)}, u32[]{:S(2)}) collective-permute-start(bf16[5376,128]{1,0:T(8,128)(2,1)S(1)} %collective-permute-done.refs_2_), channel_id=1, source_target_pairs={{0,1},{1,0},{2,3},{3,2},{4,5},{5,4},{6,7},{7,6},{8,9},{9,8},{10,11... | collective-permute-start | bytes 4128776 | tf_op jit(solution)/shard_map/ppermute | solution.py:174
  82.3 1.9 collective-permute-start.6
  84.2 6.5 %collective-permute-done.3 = bf16[1792,128]{1,0:T(8,128)(2,1)S(1)} collective-permute-done((bf16[1792,128]{1,0:T(8,128)(2,1)S(1)}, bf16[1792,128]{1,0:T(8,128)(2,1)S(1)}, u32[]{:S(2)}, u32[]{:S(2)}) %collective-permute-start.3) | collective-permute-done | bytes 458784 | tf_op jit(solution)/shard_map/ppermute | solution.py:176
  90.7 0.8 copy-done.3
  91.5 0.2 collective-permute-done.2
  91.7 1.0 constant_dynamic-update-slice_fusion.1
  92.8 1.1 constant_dynamic-update-slice_fusion.refs_6_
  93.8 1.9 collective-permute-start.7
  95.9 2.5 %collective-permute-done.7.refs_7_ = bf16[3584,128]{1,0:T(8,128)(2,1)} collective-permute-done((bf16[3584,128]{1,0:T(8,128)(2,1)S(1)}, bf16[3584,128]{1,0:T(8,128)(2,1)}, u32[]{:S(2)}, u32[]{:S(2)}) %collective-permute-start.7) | collective-permute-done | bytes 917536 | tf_op jit(solution)/shard_map/ppermute | solution.py:207
  98.3 4.8 %shard_map.95 = bf16[4,128,512]{2,1,0:T(8,128)(2,1)S(1)} custom-call(s32[5]{0:T(128)S(1)} %stack.49.scalars, bf16[128,3712]{1,0:T(8,128)(2,1)S(1)} %bitcast.75, bf16[3584,128]{1,0:T(8,128)(2,1)} %get-tuple-element.22.refs_0_, bf16[3584,128]{1,0:T(8,128)(2,1)} %collective-permute-done.4.refs_1_, bf16[5376,128]{1,0:T(8,128)(2,1)S(1)} %collective-permute-done.refs_2_, ...), custom_call_target="tpu_custom_call" | custom-call | tf_op jit(solution)/shard_map/pallas_call | solution.py:115
  103.1 0.8 copy-done
  103.9 4.2 %all-to-all-start.2 = ((bf16[4,128,512]{2,1,0:T(8,128)(2,1)}), bf16[4,128,512]{2,1,0:T(8,128)(2,1)}, u32[]{:S(2)}, u32[]{:S(2)}) async-start(bf16[4,128,512]{2,1,0:T(8,128)(2,1)} %copy-done), calls=%async_computation.2 | async-start | bytes 1048576 | tf_op jit(solution)/shard_map/all_to_all | solution.py:216
  108.1 0.1 select_reduce_fusion.1
  108.2 10.0 %all-to-all-done.2 = bf16[4,128,512]{2,1,0:T(8,128)(2,1)} async-done(((bf16[4,128,512]{2,1,0:T(8,128)(2,1)}), bf16[4,128,512]{2,1,0:T(8,128)(2,1)}, u32[]{:S(2)}, u32[]{:S(2)}) %all-to-all-start.2) | async-done | bytes 524320 | tf_op jit(solution)/shard_map/all_to_all | solution.py:216
  118.2 1.1 convert_reduce_fusion.1
  119.3 0.1 multiply_convert_fusion
  119.4 13.4 %all-gather = bf16[512,512]{1,0:T(8,128)(2,1)S(1)} all-gather(bf16[128,512]{1,0:T(8,128)(2,1)S(1)} %pad_maximum_fusion.1), channel_id=2, replica_groups=mesh['node'=16,'expert'=4,'chip'=4,'core'=2] {'chip'}, dimensions={0}, use_global_device_ids=true | all-gather | bytes 655360 | tf_op jit(solution)/shard_map/all_gather | solution.py:223
  132.8 4.8 %shard_map.96 = bf16[128,3712]{1,0:T(8,128)(2,1)S(1)} custom-call(s32[5]{0:T(128)S(1)} %stack.49.scalars, bf16[128,3712]{1,0:T(8,128)(2,1)S(1)} %bitcast.77, bf16[4,128,512]{2,1,0:T(8,128)(2,1)S(1)} %bitcast.79, bf16[3584,128]{1,0:T(8,128)(2,1)} %get-tuple-element.22.refs_0_, bf16[3584,128]{1,0:T(8,128)(2,1)} %collective-permute-done.4.refs_1_, ...), custom_call_target="tpu_custom_call" | custom-call | tf_op jit(solution)/shard_map/pallas_call | solution.py:115
  137.6 18.3 %all_to_all.25 = bf16[16,8,3712]{2,1,0:T(8,128)(2,1)S(1)} all-to-all(bf16[16,8,3712]{2,1,0:T(8,128)(2,1)S(1)} %bitcast.78), channel_id=1, replica_groups=mesh['node'=16,'expert'=4,'chip'=4,'core'=2] {'expert','chip'}, dimensions={0} | all-to-all | bytes 1900544 | tf_op jit(solution)/shard_map/all_to_all | solution.py:227
  155.9 0.1 convert_reduce_fusion
  156.2 0.3 convolution_convert_fusion
  156.7 35.1 %all_to_all.26 = bf16[16,120,128]{2,1,0:T(8,128)(2,1)S(1)} all-to-all(bf16[16,120,128]{2,1,0:T(8,128)(2,1)S(1)} %bitcast.82), channel_id=1, replica_groups=mesh['node'=16,'expert'=4,'chip'=4,'core'=2] {'node'}, dimensions={0} | all-to-all | bytes 983040 | tf_op jit(solution)/shard_map/all_to_all | solution.py:244
  191.8 0.2 convolution_convert_fusion.3
  192.0 0.1 select_reduce_fusion
  192.1 0.7 select_reduce_fusion.3
  192.9 0.7 fusion.34
  (45 shorter events, 0.8 us)
Async XLA Ops:
  4.2 15.8 %copy-start.1 = (bf16[7168,128]{1,0:T(8,128)(2,1)S(1)}, bf16[7168,128]{1,0:T(8,128)(2,1)}, u32[]{:S(2)}) copy-start(bf16[7168,128]{1,0:T(8,128)(2,1)} %up.1) | copy-start | bytes 5505028
  5.3 55.7 %all-to-all-start = ((bf16[16,120,128]{2,1,0:T(8,128)(2,1)}), bf16[16,120,128]{2,1,0:T(8,128)(2,1)S(1)}, u32[]{:S(2)}, u32[]{:S(2)}) async-start(bf16[16,120,128]{2,1,0:T(8,128)(2,1)} %fusion.2), calls=%async_computation | async-start | bytes 983040 | tf_op jit(solution)/shard_map/all_to_all | solution.py:169
  20.0 1.5 copy-start.2
  24.4 34.5 %collective-permute-start = (bf16[5376,128]{1,0:T(8,128)(2,1)S(1)}, bf16[5376,128]{1,0:T(8,128)(2,1)S(1)}, u32[]{:S(2)}, u32[]{:S(2)}) collective-permute-start(bf16[5376,128]{1,0:T(8,128)(2,1)S(1)} %get-tuple-element.16), channel_id=1, source_target_pairs={{0,2},{2,4},{4,6},{6,0},{1,3},{3,5},{5,7},{7,1},{8,10},{10,12},{12... | collective-permute-start | bytes 4128776 | tf_op jit(solution)/shard_map/ppermute | solution.py:167
  27.9 33.1 %collective-permute-start.1 = (bf16[5376,128]{1,0:T(8,128)(2,1)S(1)}, bf16[5376,128]{1,0:T(8,128)(2,1)}, u32[]{:S(2)}, u32[]{:S(2)}) collective-permute-start(bf16[5376,128]{1,0:T(8,128)(2,1)S(1)} %get-tuple-element.17), channel_id=1, source_target_pairs={{0,6},{2,0},{4,2},{6,4},{1,7},{3,1},{5,3},{7,5},{8,14},{10,8},{12,... | collective-permute-start | bytes 4128776 | tf_op jit(solution)/shard_map/ppermute | solution.py:168
  62.9 28.8 %all-to-all-start.1 = ((bf16[16,8,3712]{2,1,0:T(8,128)(2,1)}), bf16[16,8,3712]{2,1,0:T(8,128)(2,1)S(1)}, u32[]{:S(2)}, u32[]{:S(2)}) async-start(bf16[16,8,3712]{2,1,0:T(8,128)(2,1)} %bitcast.12), calls=%async_computation.1 | async-start | bytes 1900544 | tf_op jit(solution)/shard_map/all_to_all | solution.py:202
  71.0 19.7 %collective-permute-start.3 = (bf16[1792,128]{1,0:T(8,128)(2,1)S(1)}, bf16[1792,128]{1,0:T(8,128)(2,1)S(1)}, u32[]{:S(2)}, u32[]{:S(2)}) collective-permute-start(bf16[1792,128]{1,0:T(8,128)(2,1)S(1)} %slice.107), channel_id=1, source_target_pairs={{0,6},{2,0},{4,2},{6,4},{1,7},{3,1},{5,3},{7,5},{8,14},{10,8},{12,... | collective-permute-start | bytes 1376264 | tf_op jit(solution)/shard_map/ppermute | solution.py:176
  76.0 15.7 %collective-permute-start.2 = (bf16[1792,128]{1,0:T(8,128)(2,1)S(1)}, bf16[1792,128]{1,0:T(8,128)(2,1)}, u32[]{:S(2)}, u32[]{:S(2)}) collective-permute-start(bf16[1792,128]{1,0:T(8,128)(2,1)S(1)} %slice.106), channel_id=1, source_target_pairs={{0,2},{2,4},{4,6},{6,0},{1,3},{3,5},{5,7},{7,1},{8,10},{10,12},{12... | collective-permute-start | bytes 1376264 | tf_op jit(solution)/shard_map/ppermute | solution.py:175
  78.0 17.9 %collective-permute-start.4 = (bf16[3584,128]{1,0:T(8,128)(2,1)}, bf16[3584,128]{1,0:T(8,128)(2,1)}, u32[]{:S(2)}, u32[]{:S(2)}) collective-permute-start(bf16[3584,128]{1,0:T(8,128)(2,1)} %get-tuple-element.22.refs_0_), channel_id=1, source_target_pairs={{0,1},{1,0},{2,3},{3,2},{4,5},{5,4},{6,7},{7,6},{8,9},{9,8},{10,11... | collective-permute-start | bytes 2752520 | tf_op jit(solution)/shard_map/ppermute | solution.py:174
  79.9 16.0 %collective-permute-start.5 = (bf16[5376,128]{1,0:T(8,128)(2,1)S(1)}, bf16[5376,128]{1,0:T(8,128)(2,1)}, u32[]{:S(2)}, u32[]{:S(2)}) collective-permute-start(bf16[5376,128]{1,0:T(8,128)(2,1)S(1)} %collective-permute-done.refs_2_), channel_id=1, source_target_pairs={{0,1},{1,0},{2,3},{3,2},{4,5},{5,4},{6,7},{7,6},{8,9},{9,8},{10,11... | collective-permute-start | bytes 4128776 | tf_op jit(solution)/shard_map/ppermute | solution.py:174
  82.3 13.6 %collective-permute-start.6 = (bf16[5376,128]{1,0:T(8,128)(2,1)}, bf16[5376,128]{1,0:T(8,128)(2,1)}, u32[]{:S(2)}, u32[]{:S(2)}) collective-permute-start(bf16[5376,128]{1,0:T(8,128)(2,1)} %collective-permute-done.1.refs_4_), channel_id=1, source_target_pairs={{0,1},{1,0},{2,3},{3,2},{4,5},{5,4},{6,7},{7,6},{8,9},{9,8},{10,11... | collective-permute-start | bytes 4128776 | tf_op jit(solution)/shard_map/ppermute | solution.py:174
  90.7 0.8 copy-start.3
  93.8 4.5 %collective-permute-start.7 = (bf16[3584,128]{1,0:T(8,128)(2,1)S(1)}, bf16[3584,128]{1,0:T(8,128)(2,1)}, u32[]{:S(2)}, u32[]{:S(2)}) collective-permute-start(bf16[3584,128]{1,0:T(8,128)(2,1)S(1)} %constant_dynamic-update-slice_fusion.refs_6_), channel_id=1, source_target_pairs={{0,1},{1,0},{2,3},{3,2},{4,5},{5,4},{6,7},{7,6},{8,9},{9,8},{10,11... | collective-permute-start | bytes 2752520 | tf_op jit(solution)/shard_map/ppermute | solution.py:207
  103.1 0.8 copy-start
  103.9 14.3 %all-to-all-start.2 = ((bf16[4,128,512]{2,1,0:T(8,128)(2,1)}), bf16[4,128,512]{2,1,0:T(8,128)(2,1)}, u32[]{:S(2)}, u32[]{:S(2)}) async-start(bf16[4,128,512]{2,1,0:T(8,128)(2,1)} %copy-done), calls=%async_computation.2 | async-start | bytes 1048576 | tf_op jit(solution)/shard_map/all_to_all | solution.py:216
  156.7 35.4 %copy-start.4 = (s32[4,2,2]{0,2,1:T(2,128)S(1)}, s32[4,2,2]{0,2,1:T(2,128)}, u32[]{:S(2)}) copy-start(s32[4,2,2]{0,2,1:T(2,128)} %param.10) | copy-start | bytes 196

commit v4 on v3

--- a/solution.py
+++ b/solution.py
@@ -12,6 +12,56 @@
 
 def dot(a, b, dims):
     return lax.dot_general(a, b, (dims, ((), ())), preferred_element_type=jnp.float32)
+
+
+def send_kernel(groups, choices, gates, tokens, cotangent, out, wide):
+    count, width = tokens.shape
+    chunks = width // LANES
+    for j in range(chunks):
+        at = pl.ds(j * LANES, LANES)
+        wide[:, j, :] = tokens[:, at].astype(jnp.float32)
+        wide[:, chunks + j, :] = cotangent[:, at].astype(jnp.float32)
+    out[...] = jnp.zeros_like(out)
+    every_gate = gates[...].astype(jnp.float32)
+    row = lax.broadcasted_iota(jnp.int32, (8, LANES), 0)
+    lane = lax.broadcasted_iota(jnp.int32, (8, LANES), 1)
+    i, j = (lax.broadcasted_iota(jnp.int32, (2, 2), d) for d in range(2))
+    for t in range(count):
+        rows = wide[t].astype(out.dtype)
+        for c in range(2):
+            node = groups[t, c]
+            out[node, : 2 * chunks, :] = rows
+            table = jnp.zeros((8, LANES), jnp.float32)
+            for k in range(2):
+                gate = jnp.sum(jnp.where((i == c) & (j == k), every_gate[t], 0.0), keepdims=True)
+                table += jnp.where((row == 0) & (lane == choices[t, c, k]), gate, 0.0)
+            out[node, 2 * chunks :, :] = table.astype(out.dtype)
+
+
+def home_kernel(groups, choices, home, mixed, grad_tokens, grad_gates, wide):
+    count, width = mixed.shape
+    chunks = width // LANES
+    row = lax.broadcasted_iota(jnp.int32, (8, LANES), 0)
+    lane = lax.broadcasted_iota(jnp.int32, (8, LANES), 1)
+    i, j = (lax.broadcasted_iota(jnp.int32, (2, 2), d) for d in range(2))
+    for t in range(count):
+        total = jnp.zeros((2 * chunks, LANES), jnp.float32)
+        inner = jnp.zeros((2, 2), jnp.float32)
+        for c in range(2):
+            node = groups[t, c]
+            total += home[node, : 2 * chunks, :].astype(jnp.float32)
+            table = home[node, 2 * chunks :, :].astype(jnp.float32)
+            for k in range(2):
+                value = jnp.sum(
+                    jnp.where((row == 0) & (lane == choices[t, c, k]), table, 0.0), keepdims=True
+                )
+                inner = jnp.where((i == c) & (j == k), value, inner)
+        wide[t] = total
+        grad_gates[t] = inner.astype(grad_gates.dtype)
+    for j in range(chunks):
+        at = pl.ds(j * LANES, LANES)
+        mixed[:, at] = wide[:, j, :].astype(mixed.dtype)
+        grad_tokens[:, at] = wide[:, chunks + j, :].astype(grad_tokens.dtype)
 
 
 def pack_kernel(chips, up, down, here, ahead, behind, sems):
@@ -111,15 +161,16 @@
 
 def call(kernel, shapes, scalars, *operands, space=pltpu.VMEM, scratch=()):
     spec = pl.BlockSpec(memory_space=space)
+    scalars = scalars if isinstance(scalars, tuple) else (scalars,)
     out = [jax.ShapeDtypeStruct(shape, jnp.bfloat16) for shape in shapes]
     return pl.pallas_call(
         kernel,
         out_shape=out,
-        in_specs=[pl.BlockSpec(memory_space=pltpu.SMEM)] + [spec] * len(operands),
+        in_specs=[pl.BlockSpec(memory_space=pltpu.SMEM)] * len(scalars) + [spec] * len(operands),
         out_specs=[spec] * len(out),
         scratch_shapes=scratch,
         compiler_params=pltpu.CompilerParams(vmem_limit_bytes=40 * 2**20),
-    )(scalars, *operands)
+    )(*scalars, *operands)
 
 
 def per_device(tokens, cotangent, groups, choices, gates, up_weight, down_weight):
@@ -134,27 +185,22 @@
     expert = lax.axis_index("expert")
     chip = lax.axis_index("chip")
     lane = jnp.arange(LANES, dtype=jnp.int32)
-    node_ids = jnp.arange(nodes, dtype=jnp.int32)
-
-    place = node_ids[:, None, None] == groups[None]
-    token_at = jnp.any(place, 2).astype(bf16)
-    dense = jnp.sum(
-        jnp.where(choices[..., None] == lane, gates[..., None].astype(f32), 0.0), 2
-    )
-    table = jnp.sum(jnp.where(place[..., None], dense[None], 0.0), (1, 2)).astype(bf16)
-    packed = jnp.concatenate([tokens, cotangent], 1)
-    sent = jnp.concatenate(
-        [
-            dot(token_at, packed, ((1,), (0,))).astype(bf16).reshape(nodes, -1, LANES),
-            jnp.pad(table[:, None, :], ((0, 0), (0, 7), (0, 0))),
-        ],
-        1,
+
+    slot_rows = 2 * width // LANES
+    wide_rows = pltpu.VMEM((tok_count, slot_rows, LANES), f32)
+    (sent,) = call(
+        send_kernel,
+        [(nodes, slot_rows + 8, LANES)],
+        (groups, choices),
+        gates,
+        tokens,
+        cotangent,
+        scratch=[wide_rows],
     )
 
     ahead_of = [(i, (i + 1) % chips) for i in range(chips)]
     behind_of = [(i, (i - 1) % chips) for i in range(chips)]
     targets = jnp.stack([(chip + s) % chips for s in range(chips)]).astype(jnp.int32)
-    targets, sent = lax.optimization_barrier((targets, sent))
     here, ahead, behind = call(
         pack_kernel,
         [(2 * wide, hidden), (3 * wide, hidden), (3 * wide, hidden)],
@@ -167,13 +213,15 @@
     ahead = lax.ppermute(ahead, "chip", ahead_of)
     behind = lax.ppermute(behind, "chip", behind_of)
     recv = lax.all_to_all(sent, "node", split_axis=0, concat_axis=0, tiled=True)
-    recv, ahead, behind = lax.optimization_barrier((recv, ahead, behind))
     swap = [(0, 1), (1, 0)]
     blocks = []
     for block in (here, ahead, behind):
         blocks += [block, lax.ppermute(block, "core", swap)]
     far_up = lax.ppermute(ahead[2 * wide :], "chip", ahead_of)
     far_down = lax.ppermute(behind[2 * wide :], "chip", behind_of)
+    recv, far_up, far_down = lax.optimization_barrier((recv, far_up, far_down))
+    far = jnp.concatenate([far_up, far_down], 0)
+    blocks += [far, lax.ppermute(far, "core", swap)]
     scalars = jnp.stack(
         [expert, chip, (chip + chips - 1) % chips, (chip + 1) % chips, (chip + 2) % chips]
     ).astype(jnp.int32)
@@ -202,9 +250,6 @@
     rows = lax.all_to_all(
         spread, ("expert", "chip"), split_axis=0, concat_axis=0, tiled=True
     ).reshape(experts * chips * pairs, -1)
-    rows, far_up, far_down = lax.optimization_barrier((rows, far_up, far_down))
-    far = jnp.concatenate([far_up, far_down], 0)
-    blocks += [far, lax.ppermute(far, "core", swap)]
     gate = jnp.sum(
         jnp.where(lane[None, :] == expert, rows[:, 2 * wide :].astype(f32), 0.0), 1, keepdims=True
     )
@@ -243,14 +288,13 @@
     expanded = jnp.pad(expanded, ((0, 0), (0, 7 * LANES))).reshape(nodes, -1, LANES)
     home = lax.all_to_all(expanded, "node", split_axis=0, concat_axis=0, tiled=True)
 
-    home_rows = home[:, : 2 * width // LANES].reshape(nodes, -1)
-    total = dot(token_at, home_rows, ((0,), (0,))).astype(bf16)
-    inner_rows = home[:, 2 * width // LANES].astype(f32)
-    pair_inner = jnp.sum(jnp.where(place[..., None], inner_rows[:, None, None, :], 0.0), 0)
-    grad_gates = jnp.sum(
-        jnp.where(choices[..., None] == lane, pair_inner[:, :, None, :], 0.0), -1
-    ).astype(bf16)
-    return (total[:, :width], total[:, width:], grad_gates)
+    return call(
+        home_kernel,
+        [tokens.shape, tokens.shape, gates.shape],
+        (groups, choices),
+        home,
+        scratch=[wide_rows],
+    )
 
 
 def solution(mesh):

time: 195 us -> 198 us (1.015)
  waiting for transfers between devices: 48.6 us -> 55 us
  blocking collectives: 66.8 us -> 62.5 us
  other arithmetic: 6.17 us -> 2.2 us
  Pallas kernels: 12.5 us -> 15.8 us
  local copies, waits for them, and re-layouts: 8.38 us -> 10.9 us
    all_to_all x1, waiting for transfers between devices: 0.01 us -> 17 us  [per_device(): lax.all_to_all(spread, ('expert', 'chip'), split_axis=0, concat_axis=0, t...]
    ppermute x1, waiting for transfers between devices: 6.49 us -> 1.7 us  [per_device(): far_down = lax.ppermute(behind[2 * wide:], 'chip', behind_of)]
    unnamed x23 -> x24, local copies, waits for them, and re-layouts: 4.29 us -> 7.9 us
    pallas_call x3 -> x5, Pallas kernels: 12.5 us -> 15.8 us  [call(): pl.pallas_call(kernel, out_shape=out, in_specs=[pl.BlockSpec(memory_space...]
    all_to_all x1, blocking collectives: 18.3 us -> 15.6 us  [per_device(): lax.all_to_all(result.reshape(experts * chips, pairs, -1), ('expert', 'ch...]
    ppermute x1, waiting for transfers between devices: 2.46 us -> 0.01 us  [per_device(): blocks += [far, lax.ppermute(far, 'core', swap)]]
    ppermute x1, waiting for transfers between devices: 2.02 us -> 0.01 us  [per_device(): behind = lax.ppermute(behind, 'chip', behind_of)]
  transfers between devices with their start and end apart: 11 -> 11, of which waited for: 6 -> 4; matrix products, arithmetic and copies ran while one was open for 2% -> 2% of each run, Pallas kernels for 2% -> 1%
where the time goes in v4:
time: 198 us; the launch traced here: 197 us
  blocking collectives  62.5 us (32%)
  waiting for transfers between devices  55 us (28%)
  starting transfers between devices  48.9 us (25%)
  Pallas kernels  15.8 us (8%)
  local copies, waits for them, and re-layouts  10.9 us (6%)
  other arithmetic  2.2 us (1%)
    all_to_all x1, blocking collectives, per_device(): lax.all_to_all(expanded, 'node', split_axis=0, concat_axis=0, tiled=True)  34.1 us
    ppermute x1, waiting for transfers between devices, per_device(): ahead = lax.ppermute(ahead, 'chip', ahead_of)  27.4 us
    all_to_all x1, waiting for transfers between devices, per_device(): lax.all_to_all(spread, ('expert', 'chip'), split_axis=0, concat_axis=0, t...  17 us
    pallas_call x5, Pallas kernels, call(): pl.pallas_call(kernel, out_shape=out, in_specs=[pl.BlockSpec(memory_space...  15.8 us
    all_to_all x1, blocking collectives, per_device(): lax.all_to_all(result.reshape(experts * chips, pairs, -1), ('expert', 'ch...  15.6 us
    all_to_all x1, starting transfers between devices, per_device(): recv = lax.all_to_all(sent, 'node', split_axis=0, concat_axis=0, tiled=True)  14.8 us
    all_gather x1, blocking collectives, per_device(): lax.all_gather(jnp.concatenate([active, grad_pre], 1), 'chip', axis=0)  12.8 us
    all_to_all x1, waiting for transfers between devices, per_device(): lax.all_to_all(outgoing, 'chip', split_axis=0, concat_axis=0, tiled=True)  8.89 us
  transfers between devices with their start and end apart: 11, of which 4 were waited for; matrix products, arithmetic and copies ran while one was open for 2% of the time, Pallas kernels for 1%

profile of v4, /device:TPU:64, one launch (start us, length us, event | category | flops | bytes accessed | tf_op | source)
XLA Modules:
  0.0 196.8 jit_solution(7976245112415879957)
XLA Ops:
  0.6 0.8 copy.28.groups
  1.4 0.8 copy.26.gates
  2.2 0.8 copy.29.choices
  3.0 0.8 copy-done.3
  3.8 0.8 copy-done.4
  4.6 1.7 shard_map.94
  6.3 14.8 %all-to-all-start = ((bf16[16,120,128]{2,1,0:T(8,128)(2,1)}), bf16[16,120,128]{2,1,0:T(8,128)(2,1)S(1)}, u32[]{:S(2)}, u32[]{:S(2)}) async-start(bf16[16,120,128]{2,1,0:T(8,128)(2,1)} %shard_map.94), calls=%async_computation | async-start | bytes 983040 | tf_op jit(solution)/shard_map/all_to_all | solution.py:215
  21.0 0.1 pad_add_fusion.chips
  21.1 1.5 copy-done.1
  22.6 1.5 copy-done.2
  24.1 2.9 %shard_map.95 = (bf16[3584,128]{1,0:T(8,128)(2,1)}, bf16[5376,128]{1,0:T(8,128)(2,1)S(1)}, bf16[5376,128]{1,0:T(8,128)(2,1)S(1)}) custom-call(s32[4]{0:T(128)S(1)} %pad_add_fusion.chips, bf16[7168,128]{1,0:T(8,128)(2,1)S(1)} %copy-done.1, bf16[128,7168]{1,0:T(8,128)(2,1)S(1)} %copy-done.2), custom_call_target="tpu_custom_call" | custom-call | tf_op jit(solution)/shard_map/pallas_call | solution.py:166
  27.0 3.4 %collective-permute-start = (bf16[5376,128]{1,0:T(8,128)(2,1)S(1)}, bf16[5376,128]{1,0:T(8,128)(2,1)S(1)}, u32[]{:S(2)}, u32[]{:S(2)}) collective-permute-start(bf16[5376,128]{1,0:T(8,128)(2,1)S(1)} %get-tuple-element.9), channel_id=1, source_target_pairs={{0,2},{2,4},{4,6},{6,0},{1,3},{3,5},{5,7},{7,1},{8,10},{10,12},{12... | collective-permute-start | bytes 4128776 | tf_op jit(solution)/shard_map/ppermute | solution.py:213
  30.4 3.7 %collective-permute-start.2 = (bf16[5376,128]{1,0:T(8,128)(2,1)S(1)}, bf16[5376,128]{1,0:T(8,128)(2,1)}, u32[]{:S(2)}, u32[]{:S(2)}) collective-permute-start(bf16[5376,128]{1,0:T(8,128)(2,1)S(1)} %get-tuple-element.10), channel_id=1, source_target_pairs={{0,6},{2,0},{4,2},{6,4},{1,7},{3,1},{5,3},{7,5},{8,14},{10,8},{12,... | collective-permute-start | bytes 4128776 | tf_op jit(solution)/shard_map/ppermute | solution.py:214
  34.1 27.4 %collective-permute-done.refs_2_ = bf16[5376,128]{1,0:T(8,128)(2,1)S(1)} collective-permute-done((bf16[5376,128]{1,0:T(8,128)(2,1)S(1)}, bf16[5376,128]{1,0:T(8,128)(2,1)S(1)}, u32[]{:S(2)}, u32[]{:S(2)}) %collective-permute-start) | collective-permute-done | bytes 1376288 | tf_op jit(solution)/shard_map/ppermute | solution.py:213
  61.5 2.2 %collective-permute-start.1 = (bf16[1792,128]{1,0:T(8,128)(2,1)S(1)}, bf16[1792,128]{1,0:T(8,128)(2,1)S(1)}, u32[]{:S(2)}, u32[]{:S(2)}) collective-permute-start(bf16[1792,128]{1,0:T(8,128)(2,1)S(1)} %slice.108), channel_id=1, source_target_pairs={{0,2},{2,4},{4,6},{6,0},{1,3},{3,5},{5,7},{7,1},{8,10},{10,12},{12... | collective-permute-start | bytes 1376264 | tf_op jit(solution)/shard_map/ppermute | solution.py:220
  63.7 1.1 slice.109
  64.8 4.9 %collective-permute-start.3 = (bf16[1792,128]{1,0:T(8,128)(2,1)S(1)}, bf16[1792,128]{1,0:T(8,128)(2,1)S(1)}, u32[]{:S(2)}, u32[]{:S(2)}) collective-permute-start(bf16[1792,128]{1,0:T(8,128)(2,1)S(1)} %slice.109), channel_id=1, source_target_pairs={{0,6},{2,0},{4,2},{6,4},{1,7},{3,1},{5,3},{7,5},{8,14},{10,8},{12,... | collective-permute-start | bytes 1376264 | tf_op jit(solution)/shard_map/ppermute | solution.py:221
  69.7 1.9 collective-permute-start.4
  71.6 2.4 %collective-permute-start.5 = (bf16[5376,128]{1,0:T(8,128)(2,1)S(1)}, bf16[5376,128]{1,0:T(8,128)(2,1)}, u32[]{:S(2)}, u32[]{:S(2)}) collective-permute-start(bf16[5376,128]{1,0:T(8,128)(2,1)S(1)} %collective-permute-done.refs_2_), channel_id=1, source_target_pairs={{0,1},{1,0},{2,3},{3,2},{4,5},{5,4},{6,7},{7,6},{8,9},{9,8},{10,11... | collective-permute-start | bytes 4128776 | tf_op jit(solution)/shard_map/ppermute | solution.py:219
  74.0 1.9 collective-permute-start.6
  75.9 1.7 collective-permute-done.3
  77.6 0.0 all-to-all-done
  77.6 0.4 compare_reduce_fusion
  78.0 0.1 copy.27
  78.2 0.1 add_reduce_fusion
  78.3 0.2 convolution_convert_fusion.1
  78.6 0.1 constant_dynamic-update-slice_fusion.refs_6_
  78.6 1.9 collective-permute-start.7
  80.7 1.0 broadcast_in_dim.10
  81.7 7.7 %all-to-all-start.1 = ((bf16[16,8,3712]{2,1,0:T(8,128)(2,1)}), bf16[16,8,3712]{2,1,0:T(8,128)(2,1)S(1)}, u32[]{:S(2)}, u32[]{:S(2)}) async-start(bf16[16,8,3712]{2,1,0:T(8,128)(2,1)} %bitcast.67), calls=%async_computation.1 | async-start | bytes 1900544 | tf_op jit(solution)/shard_map/all_to_all | solution.py:250
  89.4 0.1 stack.49.scalars
  89.5 17.0 %all-to-all-done.1 = bf16[16,8,3712]{2,1,0:T(8,128)(2,1)S(1)} async-done(((bf16[16,8,3712]{2,1,0:T(8,128)(2,1)}), bf16[16,8,3712]{2,1,0:T(8,128)(2,1)S(1)}, u32[]{:S(2)}, u32[]{:S(2)}) %all-to-all-start.1) | async-done | bytes 950304 | tf_op jit(solution)/shard_map/all_to_all | solution.py:250
  106.5 4.8 %shard_map.96 = bf16[4,128,512]{2,1,0:T(8,128)(2,1)S(1)} custom-call(s32[5]{0:T(128)S(1)} %stack.49.scalars, bf16[128,3712]{1,0:T(8,128)(2,1)S(1)} %bitcast.62, bf16[3584,128]{1,0:T(8,128)(2,1)} %get-tuple-element.12.refs_0_, bf16[3584,128]{1,0:T(8,128)(2,1)} %collective-permute-done.4.refs_1_, bf16[5376,128]{1,0:T(8,128)(2,1)S(1)} %collective-permute-done.refs_2_, ...), custom_call_target="tpu_custom_call" | custom-call | tf_op jit(solution)/shard_map/pallas_call | solution.py:166
  111.3 0.8 copy-done
  112.1 4.1 %all-to-all-start.2 = ((bf16[4,128,512]{2,1,0:T(8,128)(2,1)}), bf16[4,128,512]{2,1,0:T(8,128)(2,1)}, u32[]{:S(2)}, u32[]{:S(2)}) async-start(bf16[4,128,512]{2,1,0:T(8,128)(2,1)} %copy-done), calls=%async_computation.2 | async-start | bytes 1048576 | tf_op jit(solution)/shard_map/all_to_all | solution.py:261
  116.2 0.1 select_reduce_fusion
  116.4 8.9 %all-to-all-done.2 = bf16[4,128,512]{2,1,0:T(8,128)(2,1)} async-done(((bf16[4,128,512]{2,1,0:T(8,128)(2,1)}), bf16[4,128,512]{2,1,0:T(8,128)(2,1)}, u32[]{:S(2)}, u32[]{:S(2)}) %all-to-all-start.2) | async-done | bytes 524320 | tf_op jit(solution)/shard_map/all_to_all | solution.py:261
  125.2 1.1 convert_reduce_fusion.1
  126.4 0.1 multiply_convert_fusion
  126.5 12.8 %all-gather = bf16[512,512]{1,0:T(8,128)(2,1)S(1)} all-gather(bf16[128,512]{1,0:T(8,128)(2,1)S(1)} %pad_maximum_fusion.1), channel_id=2, replica_groups=mesh['node'=16,'expert'=4,'chip'=4,'core'=2] {'chip'}, dimensions={0}, use_global_device_ids=true | all-gather | bytes 655360 | tf_op jit(solution)/shard_map/all_gather | solution.py:268
  139.3 4.8 %shard_map.97 = bf16[128,3712]{1,0:T(8,128)(2,1)S(1)} custom-call(s32[5]{0:T(128)S(1)} %stack.49.scalars, bf16[128,3712]{1,0:T(8,128)(2,1)S(1)} %bitcast.64, bf16[4,128,512]{2,1,0:T(8,128)(2,1)S(1)} %bitcast.66, bf16[3584,128]{1,0:T(8,128)(2,1)} %get-tuple-element.12.refs_0_, bf16[3584,128]{1,0:T(8,128)(2,1)} %collective-permute-done.4.refs_1_, ...), custom_call_target="tpu_custom_call" | custom-call | tf_op jit(solution)/shard_map/pallas_call | solution.py:166
  144.1 15.6 %all_to_all.25 = bf16[16,8,3712]{2,1,0:T(8,128)(2,1)S(1)} all-to-all(bf16[16,8,3712]{2,1,0:T(8,128)(2,1)S(1)} %bitcast.65), channel_id=1, replica_groups=mesh['node'=16,'expert'=4,'chip'=4,'core'=2] {'expert','chip'}, dimensions={0} | all-to-all | bytes 1900544 | tf_op jit(solution)/shard_map/all_to_all | solution.py:272
  159.7 0.1 convert_reduce_fusion
  160.0 0.3 convolution_convert_fusion
  160.4 0.1 copy.32
  160.5 34.1 %all_to_all.26.home = bf16[16,120,128]{2,1,0:T(8,128)(2,1)S(1)} all-to-all(bf16[16,120,128]{2,1,0:T(8,128)(2,1)S(1)} %bitcast.70), channel_id=1, replica_groups=mesh['node'=16,'expert'=4,'chip'=4,'core'=2] {'node'}, dimensions={0} | all-to-all | bytes 983040 | tf_op jit(solution)/shard_map/all_to_all | solution.py:289
  194.6 1.6 shard_map.98
  196.2 0.7 copy.30
  (34 shorter events, 0.3 us)
Async XLA Ops:
  3.0 0.8 copy-start.3
  3.8 0.8 copy-start.4
  6.3 71.4 %all-to-all-start = ((bf16[16,120,128]{2,1,0:T(8,128)(2,1)}), bf16[16,120,128]{2,1,0:T(8,128)(2,1)S(1)}, u32[]{:S(2)}, u32[]{:S(2)}) async-start(bf16[16,120,128]{2,1,0:T(8,128)(2,1)} %shard_map.94), calls=%async_computation | async-start | bytes 983040 | tf_op jit(solution)/shard_map/all_to_all | solution.py:215
  21.1 1.5 copy-start.1
  22.6 1.5 copy-start.2
  27.0 34.5 %collective-permute-start = (bf16[5376,128]{1,0:T(8,128)(2,1)S(1)}, bf16[5376,128]{1,0:T(8,128)(2,1)S(1)}, u32[]{:S(2)}, u32[]{:S(2)}) collective-permute-start(bf16[5376,128]{1,0:T(8,128)(2,1)S(1)} %get-tuple-element.9), channel_id=1, source_target_pairs={{0,2},{2,4},{4,6},{6,0},{1,3},{3,5},{5,7},{7,1},{8,10},{10,12},{12... | collective-permute-start | bytes 4128776 | tf_op jit(solution)/shard_map/ppermute | solution.py:213
  30.4 33.3 %collective-permute-start.2 = (bf16[5376,128]{1,0:T(8,128)(2,1)S(1)}, bf16[5376,128]{1,0:T(8,128)(2,1)}, u32[]{:S(2)}, u32[]{:S(2)}) collective-permute-start(bf16[5376,128]{1,0:T(8,128)(2,1)S(1)} %get-tuple-element.10), channel_id=1, source_target_pairs={{0,6},{2,0},{4,2},{6,4},{1,7},{3,1},{5,3},{7,5},{8,14},{10,8},{12,... | collective-permute-start | bytes 4128776 | tf_op jit(solution)/shard_map/ppermute | solution.py:214
  61.5 14.4 %collective-permute-start.1 = (bf16[1792,128]{1,0:T(8,128)(2,1)S(1)}, bf16[1792,128]{1,0:T(8,128)(2,1)S(1)}, u32[]{:S(2)}, u32[]{:S(2)}) collective-permute-start(bf16[1792,128]{1,0:T(8,128)(2,1)S(1)} %slice.108), channel_id=1, source_target_pairs={{0,2},{2,4},{4,6},{6,0},{1,3},{3,5},{5,7},{7,1},{8,10},{10,12},{12... | collective-permute-start | bytes 1376264 | tf_op jit(solution)/shard_map/ppermute | solution.py:220
  64.8 12.9 %collective-permute-start.3 = (bf16[1792,128]{1,0:T(8,128)(2,1)S(1)}, bf16[1792,128]{1,0:T(8,128)(2,1)S(1)}, u32[]{:S(2)}, u32[]{:S(2)}) collective-permute-start(bf16[1792,128]{1,0:T(8,128)(2,1)S(1)} %slice.109), channel_id=1, source_target_pairs={{0,6},{2,0},{4,2},{6,4},{1,7},{3,1},{5,3},{7,5},{8,14},{10,8},{12,... | collective-permute-start | bytes 1376264 | tf_op jit(solution)/shard_map/ppermute | solution.py:221
  69.7 19.8 %collective-permute-start.4 = (bf16[3584,128]{1,0:T(8,128)(2,1)}, bf16[3584,128]{1,0:T(8,128)(2,1)}, u32[]{:S(2)}, u32[]{:S(2)}) collective-permute-start(bf16[3584,128]{1,0:T(8,128)(2,1)} %get-tuple-element.12.refs_0_), channel_id=1, source_target_pairs={{0,1},{1,0},{2,3},{3,2},{4,5},{5,4},{6,7},{7,6},{8,9},{9,8},{10,11... | collective-permute-start | bytes 2752520 | tf_op jit(solution)/shard_map/ppermute | solution.py:219
  71.6 34.9 %collective-permute-start.5 = (bf16[5376,128]{1,0:T(8,128)(2,1)S(1)}, bf16[5376,128]{1,0:T(8,128)(2,1)}, u32[]{:S(2)}, u32[]{:S(2)}) collective-permute-start(bf16[5376,128]{1,0:T(8,128)(2,1)S(1)} %collective-permute-done.refs_2_), channel_id=1, source_target_pairs={{0,1},{1,0},{2,3},{3,2},{4,5},{5,4},{6,7},{7,6},{8,9},{9,8},{10,11... | collective-permute-start | bytes 4128776 | tf_op jit(solution)/shard_map/ppermute | solution.py:219
  74.0 32.5 %collective-permute-start.6 = (bf16[5376,128]{1,0:T(8,128)(2,1)}, bf16[5376,128]{1,0:T(8,128)(2,1)}, u32[]{:S(2)}, u32[]{:S(2)}) collective-permute-start(bf16[5376,128]{1,0:T(8,128)(2,1)} %collective-permute-done.2.refs_4_), channel_id=1, source_target_pairs={{0,1},{1,0},{2,3},{3,2},{4,5},{5,4},{6,7},{7,6},{8,9},{9,8},{10,11... | collective-permute-start | bytes 4128776 | tf_op jit(solution)/shard_map/ppermute | solution.py:219
  78.6 27.8 %collective-permute-start.7 = (bf16[3584,128]{1,0:T(8,128)(2,1)S(1)}, bf16[3584,128]{1,0:T(8,128)(2,1)}, u32[]{:S(2)}, u32[]{:S(2)}) collective-permute-start(bf16[3584,128]{1,0:T(8,128)(2,1)S(1)} %constant_dynamic-update-slice_fusion.refs_6_), channel_id=1, source_target_pairs={{0,1},{1,0},{2,3},{3,2},{4,5},{5,4},{6,7},{7,6},{8,9},{9,8},{10,11... | collective-permute-start | bytes 2752520 | tf_op jit(solution)/shard_map/ppermute | solution.py:224
  81.7 24.8 %all-to-all-start.1 = ((bf16[16,8,3712]{2,1,0:T(8,128)(2,1)}), bf16[16,8,3712]{2,1,0:T(8,128)(2,1)S(1)}, u32[]{:S(2)}, u32[]{:S(2)}) async-start(bf16[16,8,3712]{2,1,0:T(8,128)(2,1)} %bitcast.67), calls=%async_computation.1 | async-start | bytes 1900544 | tf_op jit(solution)/shard_map/all_to_all | solution.py:250
  111.3 0.8 copy-start
  112.1 13.2 %all-to-all-start.2 = ((bf16[4,128,512]{2,1,0:T(8,128)(2,1)}), bf16[4,128,512]{2,1,0:T(8,128)(2,1)}, u32[]{:S(2)}, u32[]{:S(2)}) async-start(bf16[4,128,512]{2,1,0:T(8,128)(2,1)} %copy-done), calls=%async_computation.2 | async-start | bytes 1048576 | tf_op jit(solution)/shard_map/all_to_all | solution.py:261

commit v5 on v4

--- a/solution.py
+++ b/solution.py
@@ -14,28 +14,37 @@
     return lax.dot_general(a, b, (dims, ((), ())), preferred_element_type=jnp.float32)
 
 
-def send_kernel(groups, choices, gates, tokens, cotangent, out, wide):
+def send_kernel(groups, choices, gates, tokens, cotangent, out, narrow, wide, sems):
     count, width = tokens.shape
     chunks = width // LANES
-    for j in range(chunks):
-        at = pl.ds(j * LANES, LANES)
-        wide[:, j, :] = tokens[:, at].astype(jnp.float32)
-        wide[:, chunks + j, :] = cotangent[:, at].astype(jnp.float32)
+    copies = [
+        pltpu.make_async_copy(ref, narrow.at[i], sems.at[i])
+        for i, ref in enumerate((tokens, cotangent))
+    ]
+    for copy in copies:
+        copy.start()
     out[...] = jnp.zeros_like(out)
     every_gate = gates[...].astype(jnp.float32)
     row = lax.broadcasted_iota(jnp.int32, (8, LANES), 0)
     lane = lax.broadcasted_iota(jnp.int32, (8, LANES), 1)
-    i, j = (lax.broadcasted_iota(jnp.int32, (2, 2), d) for d in range(2))
+    i, j = (lax.broadcasted_iota(jnp.int32, (2, count), d) for d in range(2))
+    for t in range(count):
+        for c in range(2):
+            table = jnp.zeros((8, LANES), jnp.float32)
+            for k in range(2):
+                gate = jnp.sum(jnp.where((i == k) & (j == t), every_gate[c], 0.0), keepdims=True)
+                table += jnp.where((row == 0) & (lane == choices[c, k, t]), gate, 0.0)
+            out[groups[c, t], 2 * chunks :, :] = table.astype(out.dtype)
+    for i, copy in enumerate(copies):
+        copy.wait()
+        for j in range(chunks):
+            wide[:, i * chunks + j, :] = narrow[i, :, j * LANES : (j + 1) * LANES].astype(
+                jnp.float32
+            )
     for t in range(count):
         rows = wide[t].astype(out.dtype)
         for c in range(2):
-            node = groups[t, c]
-            out[node, : 2 * chunks, :] = rows
-            table = jnp.zeros((8, LANES), jnp.float32)
-            for k in range(2):
-                gate = jnp.sum(jnp.where((i == c) & (j == k), every_gate[t], 0.0), keepdims=True)
-                table += jnp.where((row == 0) & (lane == choices[t, c, k]), gate, 0.0)
-            out[node, 2 * chunks :, :] = table.astype(out.dtype)
+            out[groups[c, t], : 2 * chunks, :] = rows
 
 
 def home_kernel(groups, choices, home, mixed, grad_tokens, grad_gates, wide):
@@ -43,30 +52,30 @@
     chunks = width // LANES
     row = lax.broadcasted_iota(jnp.int32, (8, LANES), 0)
     lane = lax.broadcasted_iota(jnp.int32, (8, LANES), 1)
-    i, j = (lax.broadcasted_iota(jnp.int32, (2, 2), d) for d in range(2))
+    i, j = (lax.broadcasted_iota(jnp.int32, (2, count), d) for d in range(2))
+    inner = [jnp.zeros((2, count), jnp.float32) for c in range(2)]
     for t in range(count):
         total = jnp.zeros((2 * chunks, LANES), jnp.float32)
-        inner = jnp.zeros((2, 2), jnp.float32)
         for c in range(2):
-            node = groups[t, c]
+            node = groups[c, t]
             total += home[node, : 2 * chunks, :].astype(jnp.float32)
             table = home[node, 2 * chunks :, :].astype(jnp.float32)
             for k in range(2):
                 value = jnp.sum(
-                    jnp.where((row == 0) & (lane == choices[t, c, k]), table, 0.0), keepdims=True
+                    jnp.where((row == 0) & (lane == choices[c, k, t]), table, 0.0), keepdims=True
                 )
-                inner = jnp.where((i == c) & (j == k), value, inner)
+                inner[c] = jnp.where((i == k) & (j == t), value, inner[c])
         wide[t] = total
-        grad_gates[t] = inner.astype(grad_gates.dtype)
+    for c in range(2):
+        grad_gates[c] = inner[c].astype(grad_gates.dtype)
     for j in range(chunks):
         at = pl.ds(j * LANES, LANES)
         mixed[:, at] = wide[:, j, :].astype(mixed.dtype)
         grad_tokens[:, at] = wide[:, chunks + j, :].astype(grad_tokens.dtype)
 
 
-def pack_kernel(chips, up, down, here, ahead, behind, sems):
-    wide = here.shape[0] // 2
-    tiles = wide // LANES
+def pack_kernel(chips, up, down, here, ahead, behind, far_up, far_down, sems):
+    wide = far_up.shape[0]
     copies = []
 
     def rows(chip, out, at):
@@ -91,27 +100,33 @@
     for chip, out in ((1, ahead), (3, behind), (0, here)):
         rows(chip, out, 0)
         columns(chip, out, wide)
-    rows(2, ahead, 2 * wide)
-    columns(2, behind, 2 * wide)
+    rows(2, far_up, 0)
+    columns(2, far_down, 0)
     for copy in copies:
         copy.start()
     for copy in copies:
         copy.wait()
 
 
+def pieces(refs, wide):
+    whole = [(ref.at[pl.ds(0, wide)], ref.at[pl.ds(wide, wide)]) for ref in refs[:-4]]
+    return whole + [(refs[-4], refs[-2]), (refs[-3], refs[-1])]
+
+
 def partial_kernel(scalars, rows, *refs):
-    blocks, out = refs[:-1], refs[-1]
-    hidden = blocks[0].shape[1]
+    out = refs[-1]
+    hidden = refs[0].shape[1]
     wide = (rows.shape[1] - LANES) // 2
+    blocks = pieces(refs[:-1], wide)
     x, dy = rows[:, :wide], rows[:, wide : 2 * wide]
     for i in range(len(blocks) // CORES):
         pair = blocks[CORES * i : CORES * (i + 1)]
         at = scalars[1 + i]
-        up = jnp.concatenate([ref[:wide, :] for ref in pair], 1)
+        up = jnp.concatenate([u[...] for u, _ in pair], 1)
         out[at, :, : CORES * hidden] = dot(x, up, ((1,), (0,))).astype(out.dtype)
         down = jnp.concatenate(
             [
-                jnp.concatenate([ref[wide + j : wide + j + LANES, :] for ref in pair], 0)
+                jnp.concatenate([d[j : j + LANES, :] for _, d in pair], 0)
                 for j in range(0, wide, LANES)
             ],
             1,
@@ -120,9 +135,10 @@
 
 
 def output_kernel(scalars, rows, every, *refs):
-    blocks, result = refs[:-1], refs[-1]
-    hidden = blocks[0].shape[1]
+    result = refs[-1]
+    hidden = refs[0].shape[1]
     wide = (rows.shape[1] - LANES) // 2
+    blocks = pieces(refs[:-1], wide)
     chips = len(blocks) // CORES
     count = rows.shape[0]
     lane = lax.broadcasted_iota(jnp.int32, (count, LANES), 1)
@@ -141,12 +157,12 @@
     for j in range(0, wide, step):
         down = jnp.concatenate(
             [
-                jnp.concatenate([ref[wide + j + k : wide + j + k + LANES, :] for ref in blocks], 0)
+                jnp.concatenate([d[j + k : j + k + LANES, :] for _, d in blocks], 0)
                 for k in range(0, step, LANES)
             ],
             1,
         )
-        up = jnp.concatenate([ref[j : j + step, :] for ref in blocks], 1)
+        up = jnp.concatenate([u[j : j + step, :] for u, _ in blocks], 1)
         out = dot(active, down, ((1,), (0,)))
         inner += jnp.sum(
             out * rows[:, wide + j : wide + j + step].astype(jnp.float32), 1, keepdims=True
@@ -159,14 +175,17 @@
     result[:, 2 * wide :] = jnp.where(mine, inner, 0.0).astype(result.dtype)
 
 
-def call(kernel, shapes, scalars, *operands, space=pltpu.VMEM, scratch=()):
-    spec = pl.BlockSpec(memory_space=space)
+def call(kernel, shapes, scalars, *operands, hbm=0, scratch=()):
+    spec = pl.BlockSpec(memory_space=pltpu.VMEM)
+    far = pl.BlockSpec(memory_space=pltpu.HBM)
     scalars = scalars if isinstance(scalars, tuple) else (scalars,)
     out = [jax.ShapeDtypeStruct(shape, jnp.bfloat16) for shape in shapes]
     return pl.pallas_call(
         kernel,
         out_shape=out,
-        in_specs=[pl.BlockSpec(memory_space=pltpu.SMEM)] * len(scalars) + [spec] * len(operands),
+        in_specs=[pl.BlockSpec(memory_space=pltpu.SMEM)] * len(scalars)
+        + [spec] * (len(operands) - hbm)
+        + [far] * hbm,
         out_specs=[spec] * len(out),
         scratch_shapes=scratch,
         compiler_params=pltpu.CompilerParams(vmem_limit_bytes=40 * 2**20),
@@ -187,41 +206,50 @@
     lane = jnp.arange(LANES, dtype=jnp.int32)
 
     slot_rows = 2 * width // LANES
+    groups, choices = groups.T, choices.transpose(1, 2, 0)
     wide_rows = pltpu.VMEM((tok_count, slot_rows, LANES), f32)
     (sent,) = call(
         send_kernel,
         [(nodes, slot_rows + 8, LANES)],
         (groups, choices),
-        gates,
+        gates.transpose(1, 2, 0),
         tokens,
         cotangent,
-        scratch=[wide_rows],
+        hbm=2,
+        scratch=[
+            pltpu.VMEM((2,) + tokens.shape, bf16),
+            wide_rows,
+            pltpu.SemaphoreType.DMA((2,)),
+        ],
     )
 
     ahead_of = [(i, (i + 1) % chips) for i in range(chips)]
     behind_of = [(i, (i - 1) % chips) for i in range(chips)]
     targets = jnp.stack([(chip + s) % chips for s in range(chips)]).astype(jnp.int32)
-    here, ahead, behind = call(
+    here, ahead, behind, far_up, far_down = call(
         pack_kernel,
-        [(2 * wide, hidden), (3 * wide, hidden), (3 * wide, hidden)],
+        [(2 * wide, hidden)] * 3 + [(wide, hidden)] * 2,
         targets,
         up_weight,
         down_weight,
-        space=pl.ANY,
+        hbm=2,
         scratch=[pltpu.SemaphoreType.DMA((chips * (wide // LANES + 1),))],
     )
+    swap = [(0, 1), (1, 0)]
+    far_up = lax.ppermute(far_up, "chip", ahead_of)
+    far_down = lax.ppermute(far_down, "chip", behind_of)
     ahead = lax.ppermute(ahead, "chip", ahead_of)
     behind = lax.ppermute(behind, "chip", behind_of)
+    here_too = lax.ppermute(here, "core", swap)
     recv = lax.all_to_all(sent, "node", split_axis=0, concat_axis=0, tiled=True)
-    swap = [(0, 1), (1, 0)]
-    blocks = []
-    for block in (here, ahead, behind):
+    recv, here_too, ahead, behind, far_up, far_down = lax.optimization_barrier(
+        (recv, here_too, ahead, behind, far_up, far_down)
+    )
+    far_up = lax.ppermute(far_up, "chip", ahead_of)
+    far_down = lax.ppermute(far_down, "chip", behind_of)
+    blocks = [here, here_too]
+    for block in (ahead, behind, far_up, far_down):
         blocks += [block, lax.ppermute(block, "core", swap)]
-    far_up = lax.ppermute(ahead[2 * wide :], "chip", ahead_of)
-    far_down = lax.ppermute(behind[2 * wide :], "chip", behind_of)
-    recv, far_up, far_down = lax.optimization_barrier((recv, far_up, far_down))
-    far = jnp.concatenate([far_up, far_down], 0)
-    blocks += [far, lax.ppermute(far, "core", swap)]
     scalars = jnp.stack(
         [expert, chip, (chip + chips - 1) % chips, (chip + 1) % chips, (chip + 2) % chips]
     ).astype(jnp.int32)
@@ -288,13 +316,14 @@
     expanded = jnp.pad(expanded, ((0, 0), (0, 7 * LANES))).reshape(nodes, -1, LANES)
     home = lax.all_to_all(expanded, "node", split_axis=0, concat_axis=0, tiled=True)
 
-    return call(
+    mixed, grad_tokens, grad_gates = call(
         home_kernel,
-        [tokens.shape, tokens.shape, gates.shape],
+        [tokens.shape, tokens.shape, choices.shape],
         (groups, choices),
         home,
         scratch=[wide_rows],
     )
+    return mixed, grad_tokens, grad_gates.transpose(2, 0, 1)
 
 
 def solution(mesh):

time: 198 us -> 188 us (0.949)
  the two profiles are of different devices: /device:TPU:64 before, /device:TPU:32 now
where the time goes in v5:
time: 188 us; the launch traced here: 187 us
  blocking collectives  60.7 us (32%)
  starting transfers between devices  56.8 us (30%)
  waiting for transfers between devices  40.7 us (22%)
  Pallas kernels  14.9 us (8%)
  local copies, waits for them, and re-layouts  10.2 us (5%)
  other arithmetic  2.27 us (1%)
    all_to_all x1, blocking collectives, per_device(): lax.all_to_all(expanded, 'node', split_axis=0, concat_axis=0, tiled=True)  32.5 us
    ppermute x2, waiting for transfers between devices, per_device(): far_up = lax.ppermute(far_up, 'chip', ahead_of)  18.5 us
    all_to_all x1, blocking collectives, per_device(): lax.all_to_all(result.reshape(experts * chips, pairs, -1), ('expert', 'ch...  15.4 us
    all_to_all x1, starting transfers between devices, per_device(): recv = lax.all_to_all(sent, 'node', split_axis=0, concat_axis=0, tiled=True)  15.2 us
    pallas_call x5, Pallas kernels, call(): pl.pallas_call(kernel, out_shape=out, in_specs=[pl.BlockSpec(memory_space...  14.9 us
    all_gather x1, blocking collectives, per_device(): lax.all_gather(jnp.concatenate([active, grad_pre], 1), 'chip', axis=0)  12.8 us
    all_to_all x1, waiting for transfers between devices, per_device(): lax.all_to_all(spread, ('expert', 'chip'), split_axis=0, concat_axis=0, t...  12.2 us
    unnamed x34, local copies, waits for them, and re-layouts  8.97 us
  transfers between devices with their start and end apart: 14, of which 4 were waited for; matrix products, arithmetic and copies ran while one was open for 1% of the time, Pallas kernels for 2%

profile of v5, /device:TPU:32, one launch (start us, length us, event | category | flops | bytes accessed | tf_op | source)
XLA Modules:
  0.0 187.2 jit_solution(3040233233889764108)
XLA Ops:
  0.6 0.8 copy-done.5
  1.5 0.8 copy-done.6
  2.3 0.7 copy-done.7
  3.0 0.7 copy-done.9
  3.6 0.7 copy-done.11
  4.3 1.8 shard_map.94
  6.1 15.2 %all-to-all-start = ((bf16[16,120,128]{2,1,0:T(8,128)(2,1)}), bf16[16,120,128]{2,1,0:T(8,128)(2,1)S(1)}, u32[]{:S(2)}, u32[]{:S(2)}) async-start(bf16[16,120,128]{2,1,0:T(8,128)(2,1)} %shard_map.94), calls=%async_computation | async-start | bytes 983040 | tf_op jit(solution)/shard_map/all_to_all | solution.py:244
  21.4 0.1 pad_add_fusion.chips
  21.4 1.5 copy-done.3
  22.9 1.5 copy-done.4
  24.4 2.9 %shard_map.95 = (bf16[3584,128]{1,0:T(8,128)(2,1)S(1)}, bf16[3584,128]{1,0:T(8,128)(2,1)S(1)}, bf16[3584,128]{1,0:T(8,128)(2,1)S(1)}, bf16[1792,128]{1,0:T(8,128)(2,1)S(1)}, bf16[1792,128]{1,0:T(8,128)(2,1)S(1)}) custom-call(s32[4]{0:T(128)S(1)} %pad_add_fusion.chips, bf16[7168,128]{1,0:T(8,128)(2,1)S(1)} %copy-done.3, bf16[128,7168]{1,0:T(8,128)(2,1)S(1)} %copy-done.4), custom_call_target="tpu_custom_call" | custom-call | tf_op jit(solution)/shard_map/pallas_call | solution.py:183
  27.3 3.4 %collective-permute-start.1 = (bf16[3584,128]{1,0:T(8,128)(2,1)S(1)}, bf16[3584,128]{1,0:T(8,128)(2,1)S(1)}, u32[]{:S(2)}, u32[]{:S(2)}) collective-permute-start(bf16[3584,128]{1,0:T(8,128)(2,1)S(1)} %get-tuple-element.18), channel_id=1, source_target_pairs={{0,2},{2,4},{4,6},{6,0},{1,3},{3,5},{5,7},{7,1},{8,10},{10,12},{12... | collective-permute-start | bytes 2752520 | tf_op jit(solution)/shard_map/ppermute | solution.py:241
  30.7 3.7 %collective-permute-start.2 = (bf16[3584,128]{1,0:T(8,128)(2,1)S(1)}, bf16[3584,128]{1,0:T(8,128)(2,1)}, u32[]{:S(2)}, u32[]{:S(2)}) collective-permute-start(bf16[3584,128]{1,0:T(8,128)(2,1)S(1)} %get-tuple-element.19), channel_id=1, source_target_pairs={{0,6},{2,0},{4,2},{6,4},{1,7},{3,1},{5,3},{7,5},{8,14},{10,8},{12,... | collective-permute-start | bytes 2752520 | tf_op jit(solution)/shard_map/ppermute | solution.py:242
  34.4 1.9 %collective-permute-start = (bf16[3584,128]{1,0:T(8,128)(2,1)S(1)}, bf16[3584,128]{1,0:T(8,128)(2,1)S(1)}, u32[]{:S(2)}, u32[]{:S(2)}) collective-permute-start(bf16[3584,128]{1,0:T(8,128)(2,1)S(1)} %get-tuple-element.17.refs_0_), channel_id=1, source_target_pairs={{0,1},{1,0},{2,3},{3,2},{4,5},{5,4},{6,7},{7,6},{8,9},{9,8},{10,11... | collective-permute-start | bytes 2752520 | tf_op jit(solution)/shard_map/ppermute | solution.py:243
  36.3 2.2 %collective-permute-start.3 = (bf16[1792,128]{1,0:T(8,128)(2,1)S(1)}, bf16[1792,128]{1,0:T(8,128)(2,1)}, u32[]{:S(2)}, u32[]{:S(2)}) collective-permute-start(bf16[1792,128]{1,0:T(8,128)(2,1)S(1)} %get-tuple-element.20), channel_id=1, source_target_pairs={{0,2},{2,4},{4,6},{6,0},{1,3},{3,5},{5,7},{7,1},{8,10},{10,12},{12... | collective-permute-start | bytes 1376264 | tf_op jit(solution)/shard_map/ppermute | solution.py:239
  38.5 4.9 %collective-permute-start.4 = (bf16[1792,128]{1,0:T(8,128)(2,1)S(1)}, bf16[1792,128]{1,0:T(8,128)(2,1)}, u32[]{:S(2)}, u32[]{:S(2)}) collective-permute-start(bf16[1792,128]{1,0:T(8,128)(2,1)S(1)} %get-tuple-element.21), channel_id=1, source_target_pairs={{0,6},{2,0},{4,2},{6,4},{1,7},{3,1},{5,3},{7,5},{8,14},{10,8},{12,... | collective-permute-start | bytes 1376264 | tf_op jit(solution)/shard_map/ppermute | solution.py:240
  43.4 18.5 %collective-permute-done.3 = bf16[1792,128]{1,0:T(8,128)(2,1)} collective-permute-done((bf16[1792,128]{1,0:T(8,128)(2,1)S(1)}, bf16[1792,128]{1,0:T(8,128)(2,1)}, u32[]{:S(2)}, u32[]{:S(2)}) %collective-permute-start.3) | collective-permute-done | bytes 458784 | tf_op jit(solution)/shard_map/ppermute | solution.py:239
  61.9 1.9 %collective-permute-done.4 = bf16[1792,128]{1,0:T(8,128)(2,1)} collective-permute-done((bf16[1792,128]{1,0:T(8,128)(2,1)S(1)}, bf16[1792,128]{1,0:T(8,128)(2,1)}, u32[]{:S(2)}, u32[]{:S(2)}) %collective-permute-start.4) | collective-permute-done | bytes 458784 | tf_op jit(solution)/shard_map/ppermute | solution.py:240
  63.8 1.0 copy-done
  64.8 0.4 compare_reduce_fusion
  65.2 0.1 copy.12
  65.3 0.1 add_reduce_fusion
  65.4 0.2 convolution_convert_fusion.1
  65.7 3.4 %collective-permute-start.7 = (bf16[1792,128]{1,0:T(8,128)(2,1)}, bf16[1792,128]{1,0:T(8,128)(2,1)S(1)}, u32[]{:S(2)}, u32[]{:S(2)}) collective-permute-start(bf16[1792,128]{1,0:T(8,128)(2,1)} %collective-permute-done.3), channel_id=1, source_target_pairs={{0,2},{2,4},{4,6},{6,0},{1,3},{3,5},{5,7},{7,1},{8,10},{10,12},{12... | collective-permute-start | bytes 1376264 | tf_op jit(solution)/shard_map/ppermute | solution.py:248
  69.1 3.7 %collective-permute-start.9 = (bf16[1792,128]{1,0:T(8,128)(2,1)}, bf16[1792,128]{1,0:T(8,128)(2,1)}, u32[]{:S(2)}, u32[]{:S(2)}) collective-permute-start(bf16[1792,128]{1,0:T(8,128)(2,1)} %collective-permute-done.4), channel_id=1, source_target_pairs={{0,6},{2,0},{4,2},{6,4},{1,7},{3,1},{5,3},{7,5},{8,14},{10,8},{12,... | collective-permute-start | bytes 1376264 | tf_op jit(solution)/shard_map/ppermute | solution.py:249
  72.8 1.9 %collective-permute-start.5 = (bf16[3584,128]{1,0:T(8,128)(2,1)S(1)}, bf16[3584,128]{1,0:T(8,128)(2,1)}, u32[]{:S(2)}, u32[]{:S(2)}) collective-permute-start(bf16[3584,128]{1,0:T(8,128)(2,1)S(1)} %collective-permute-done.1.refs_2_), channel_id=1, source_target_pairs={{0,1},{1,0},{2,3},{3,2},{4,5},{5,4},{6,7},{7,6},{8,9},{9,8},{10,11... | collective-permute-start | bytes 2752520 | tf_op jit(solution)/shard_map/ppermute | solution.py:252
  74.7 2.4 %collective-permute-start.6 = (bf16[3584,128]{1,0:T(8,128)(2,1)}, bf16[3584,128]{1,0:T(8,128)(2,1)}, u32[]{:S(2)}, u32[]{:S(2)}) collective-permute-start(bf16[3584,128]{1,0:T(8,128)(2,1)} %collective-permute-done.2.refs_4_), channel_id=1, source_target_pairs={{0,1},{1,0},{2,3},{3,2},{4,5},{5,4},{6,7},{7,6},{8,9},{9,8},{10,11... | collective-permute-start | bytes 2752520 | tf_op jit(solution)/shard_map/ppermute | solution.py:252
  77.2 1.0 broadcast_in_dim.10
  78.3 5.8 %all-to-all-start.1 = ((bf16[16,8,3712]{2,1,0:T(8,128)(2,1)}), bf16[16,8,3712]{2,1,0:T(8,128)(2,1)S(1)}, u32[]{:S(2)}, u32[]{:S(2)}) async-start(bf16[16,8,3712]{2,1,0:T(8,128)(2,1)} %bitcast.76), calls=%async_computation.1 | async-start | bytes 1900544 | tf_op jit(solution)/shard_map/all_to_all | solution.py:278
  84.0 1.9 %collective-permute-start.8 = (bf16[1792,128]{1,0:T(8,128)(2,1)S(1)}, bf16[1792,128]{1,0:T(8,128)(2,1)}, u32[]{:S(2)}, u32[]{:S(2)}) collective-permute-start(bf16[1792,128]{1,0:T(8,128)(2,1)S(1)} %collective-permute-done.7.refs_6_), channel_id=1, source_target_pairs={{0,1},{1,0},{2,3},{3,2},{4,5},{5,4},{6,7},{7,6},{8,9},{9,8},{10,11... | collective-permute-start | bytes 1376264 | tf_op jit(solution)/shard_map/ppermute | solution.py:252
  86.0 2.4 %collective-permute-start.10 = (bf16[1792,128]{1,0:T(8,128)(2,1)}, bf16[1792,128]{1,0:T(8,128)(2,1)}, u32[]{:S(2)}, u32[]{:S(2)}) collective-permute-start(bf16[1792,128]{1,0:T(8,128)(2,1)} %collective-permute-done.9.refs_8_), channel_id=1, source_target_pairs={{0,1},{1,0},{2,3},{3,2},{4,5},{5,4},{6,7},{7,6},{8,9},{9,8},{10,11... | collective-permute-start | bytes 1376264 | tf_op jit(solution)/shard_map/ppermute | solution.py:252
  88.4 0.1 stack.49.scalars
  88.5 12.2 %all-to-all-done.1 = bf16[16,8,3712]{2,1,0:T(8,128)(2,1)S(1)} async-done(((bf16[16,8,3712]{2,1,0:T(8,128)(2,1)}), bf16[16,8,3712]{2,1,0:T(8,128)(2,1)S(1)}, u32[]{:S(2)}, u32[]{:S(2)}) %all-to-all-start.1) | async-done | bytes 950304 | tf_op jit(solution)/shard_map/all_to_all | solution.py:278
  100.7 1.2 copy-done.1
  101.8 4.7 %shard_map.96 = bf16[4,128,512]{2,1,0:T(8,128)(2,1)} custom-call(s32[5]{0:T(128)S(1)} %stack.49.scalars, bf16[128,3712]{1,0:T(8,128)(2,1)S(1)} %bitcast.66, bf16[3584,128]{1,0:T(8,128)(2,1)S(1)} %get-tuple-element.17.refs_0_, bf16[3584,128]{1,0:T(8,128)(2,1)S(1)} %copy-done.1, bf16[3584,128]{1,0:T(8,128)(2,1)S(1)} %collective-permute-done.1.refs_2_, ...), custom_call_target="tpu_custom_call" | custom-call | tf_op jit(solution)/shard_map/pallas_call | solution.py:183
  106.5 4.1 %all-to-all-start.2 = ((bf16[4,128,512]{2,1,0:T(8,128)(2,1)}), bf16[4,128,512]{2,1,0:T(8,128)(2,1)}, u32[]{:S(2)}, u32[]{:S(2)}) async-start(bf16[4,128,512]{2,1,0:T(8,128)(2,1)} %shard_map.96), calls=%async_computation.2 | async-start | bytes 1048576 | tf_op jit(solution)/shard_map/all_to_all | solution.py:289
  110.7 0.1 select_reduce_fusion
  110.8 8.1 %all-to-all-done.2 = bf16[4,128,512]{2,1,0:T(8,128)(2,1)} async-done(((bf16[4,128,512]{2,1,0:T(8,128)(2,1)}), bf16[4,128,512]{2,1,0:T(8,128)(2,1)}, u32[]{:S(2)}, u32[]{:S(2)}) %all-to-all-start.2) | async-done | bytes 524320 | tf_op jit(solution)/shard_map/all_to_all | solution.py:289
  118.9 1.2 convert_reduce_fusion.1
  120.1 0.1 multiply_convert_fusion
  120.2 12.8 %all-gather = bf16[512,512]{1,0:T(8,128)(2,1)S(1)} all-gather(bf16[128,512]{1,0:T(8,128)(2,1)S(1)} %pad_maximum_fusion.1), channel_id=2, replica_groups=mesh['node'=16,'expert'=4,'chip'=4,'core'=2] {'chip'}, dimensions={0}, use_global_device_ids=true | all-gather | bytes 655360 | tf_op jit(solution)/shard_map/all_gather | solution.py:296
  133.0 4.0 %shard_map.97 = bf16[128,3712]{1,0:T(8,128)(2,1)S(1)} custom-call(s32[5]{0:T(128)S(1)} %stack.49.scalars, bf16[128,3712]{1,0:T(8,128)(2,1)S(1)} %bitcast.68, bf16[4,128,512]{2,1,0:T(8,128)(2,1)S(1)} %bitcast.70, bf16[3584,128]{1,0:T(8,128)(2,1)S(1)} %get-tuple-element.17.refs_0_, bf16[3584,128]{1,0:T(8,128)(2,1)S(1)} %copy-done.2, ...), custom_call_target="tpu_custom_call" | custom-call | tf_op jit(solution)/shard_map/pallas_call | solution.py:183
  137.0 15.4 %all_to_all.25 = bf16[16,8,3712]{2,1,0:T(8,128)(2,1)S(1)} all-to-all(bf16[16,8,3712]{2,1,0:T(8,128)(2,1)S(1)} %bitcast.69), channel_id=1, replica_groups=mesh['node'=16,'expert'=4,'chip'=4,'core'=2] {'expert','chip'}, dimensions={0} | all-to-all | bytes 1900544 | tf_op jit(solution)/shard_map/all_to_all | solution.py:300
  152.4 0.1 convert_reduce_fusion
  152.7 0.3 convolution_convert_fusion
  153.1 0.1 copy.14
  153.2 32.5 %all_to_all.26.home = bf16[16,120,128]{2,1,0:T(8,128)(2,1)S(1)} all-to-all(bf16[16,120,128]{2,1,0:T(8,128)(2,1)S(1)} %bitcast.79), channel_id=1, replica_groups=mesh['node'=16,'expert'=4,'chip'=4,'core'=2] {'node'}, dimensions={0} | all-to-all | bytes 983040 | tf_op jit(solution)/shard_map/all_to_all | solution.py:317
  185.7 1.5 shard_map.98
  (46 shorter events, 0.3 us)
Async XLA Ops:
  0.6 0.8 copy-start.5
  1.5 0.8 copy-start.6
  2.3 0.7 copy-start.7
  3.0 0.7 copy-start.9
  3.6 0.7 copy-start.11
  6.1 58.7 %all-to-all-start = ((bf16[16,120,128]{2,1,0:T(8,128)(2,1)}), bf16[16,120,128]{2,1,0:T(8,128)(2,1)S(1)}, u32[]{:S(2)}, u32[]{:S(2)}) async-start(bf16[16,120,128]{2,1,0:T(8,128)(2,1)} %shard_map.94), calls=%async_computation | async-start | bytes 983040 | tf_op jit(solution)/shard_map/all_to_all | solution.py:244
  21.4 1.5 copy-start.3
  22.9 1.5 copy-start.4
  27.3 36.5 %collective-permute-start.1 = (bf16[3584,128]{1,0:T(8,128)(2,1)S(1)}, bf16[3584,128]{1,0:T(8,128)(2,1)S(1)}, u32[]{:S(2)}, u32[]{:S(2)}) collective-permute-start(bf16[3584,128]{1,0:T(8,128)(2,1)S(1)} %get-tuple-element.18), channel_id=1, source_target_pairs={{0,2},{2,4},{4,6},{6,0},{1,3},{3,5},{5,7},{7,1},{8,10},{10,12},{12... | collective-permute-start | bytes 2752520 | tf_op jit(solution)/shard_map/ppermute | solution.py:241
  30.7 33.1 %collective-permute-start.2 = (bf16[3584,128]{1,0:T(8,128)(2,1)S(1)}, bf16[3584,128]{1,0:T(8,128)(2,1)}, u32[]{:S(2)}, u32[]{:S(2)}) collective-permute-start(bf16[3584,128]{1,0:T(8,128)(2,1)S(1)} %get-tuple-element.19), channel_id=1, source_target_pairs={{0,6},{2,0},{4,2},{6,4},{1,7},{3,1},{5,3},{7,5},{8,14},{10,8},{12,... | collective-permute-start | bytes 2752520 | tf_op jit(solution)/shard_map/ppermute | solution.py:242
  34.4 29.4 %collective-permute-start = (bf16[3584,128]{1,0:T(8,128)(2,1)S(1)}, bf16[3584,128]{1,0:T(8,128)(2,1)S(1)}, u32[]{:S(2)}, u32[]{:S(2)}) collective-permute-start(bf16[3584,128]{1,0:T(8,128)(2,1)S(1)} %get-tuple-element.17.refs_0_), channel_id=1, source_target_pairs={{0,1},{1,0},{2,3},{3,2},{4,5},{5,4},{6,7},{7,6},{8,9},{9,8},{10,11... | collective-permute-start | bytes 2752520 | tf_op jit(solution)/shard_map/ppermute | solution.py:243
  36.3 25.6 %collective-permute-start.3 = (bf16[1792,128]{1,0:T(8,128)(2,1)S(1)}, bf16[1792,128]{1,0:T(8,128)(2,1)}, u32[]{:S(2)}, u32[]{:S(2)}) collective-permute-start(bf16[1792,128]{1,0:T(8,128)(2,1)S(1)} %get-tuple-element.20), channel_id=1, source_target_pairs={{0,2},{2,4},{4,6},{6,0},{1,3},{3,5},{5,7},{7,1},{8,10},{10,12},{12... | collective-permute-start | bytes 1376264 | tf_op jit(solution)/shard_map/ppermute | solution.py:239
  38.5 25.3 %collective-permute-start.4 = (bf16[1792,128]{1,0:T(8,128)(2,1)S(1)}, bf16[1792,128]{1,0:T(8,128)(2,1)}, u32[]{:S(2)}, u32[]{:S(2)}) collective-permute-start(bf16[1792,128]{1,0:T(8,128)(2,1)S(1)} %get-tuple-element.21), channel_id=1, source_target_pairs={{0,6},{2,0},{4,2},{6,4},{1,7},{3,1},{5,3},{7,5},{8,14},{10,8},{12,... | collective-permute-start | bytes 1376264 | tf_op jit(solution)/shard_map/ppermute | solution.py:240
  63.8 1.0 copy-start
  65.7 18.3 %collective-permute-start.7 = (bf16[1792,128]{1,0:T(8,128)(2,1)}, bf16[1792,128]{1,0:T(8,128)(2,1)S(1)}, u32[]{:S(2)}, u32[]{:S(2)}) collective-permute-start(bf16[1792,128]{1,0:T(8,128)(2,1)} %collective-permute-done.3), channel_id=1, source_target_pairs={{0,2},{2,4},{4,6},{6,0},{1,3},{3,5},{5,7},{7,1},{8,10},{10,12},{12... | collective-permute-start | bytes 1376264 | tf_op jit(solution)/shard_map/ppermute | solution.py:248
  69.1 16.8 %collective-permute-start.9 = (bf16[1792,128]{1,0:T(8,128)(2,1)}, bf16[1792,128]{1,0:T(8,128)(2,1)}, u32[]{:S(2)}, u32[]{:S(2)}) collective-permute-start(bf16[1792,128]{1,0:T(8,128)(2,1)} %collective-permute-done.4), channel_id=1, source_target_pairs={{0,6},{2,0},{4,2},{6,4},{1,7},{3,1},{5,3},{7,5},{8,14},{10,8},{12,... | collective-permute-start | bytes 1376264 | tf_op jit(solution)/shard_map/ppermute | solution.py:249
  72.8 27.9 %collective-permute-start.5 = (bf16[3584,128]{1,0:T(8,128)(2,1)S(1)}, bf16[3584,128]{1,0:T(8,128)(2,1)}, u32[]{:S(2)}, u32[]{:S(2)}) collective-permute-start(bf16[3584,128]{1,0:T(8,128)(2,1)S(1)} %collective-permute-done.1.refs_2_), channel_id=1, source_target_pairs={{0,1},{1,0},{2,3},{3,2},{4,5},{5,4},{6,7},{7,6},{8,9},{9,8},{10,11... | collective-permute-start | bytes 2752520 | tf_op jit(solution)/shard_map/ppermute | solution.py:252
  74.7 25.9 %collective-permute-start.6 = (bf16[3584,128]{1,0:T(8,128)(2,1)}, bf16[3584,128]{1,0:T(8,128)(2,1)}, u32[]{:S(2)}, u32[]{:S(2)}) collective-permute-start(bf16[3584,128]{1,0:T(8,128)(2,1)} %collective-permute-done.2.refs_4_), channel_id=1, source_target_pairs={{0,1},{1,0},{2,3},{3,2},{4,5},{5,4},{6,7},{7,6},{8,9},{9,8},{10,11... | collective-permute-start | bytes 2752520 | tf_op jit(solution)/shard_map/ppermute | solution.py:252
  78.3 22.4 %all-to-all-start.1 = ((bf16[16,8,3712]{2,1,0:T(8,128)(2,1)}), bf16[16,8,3712]{2,1,0:T(8,128)(2,1)S(1)}, u32[]{:S(2)}, u32[]{:S(2)}) async-start(bf16[16,8,3712]{2,1,0:T(8,128)(2,1)} %bitcast.76), calls=%async_computation.1 | async-start | bytes 1900544 | tf_op jit(solution)/shard_map/all_to_all | solution.py:278
  84.0 16.6 %collective-permute-start.8 = (bf16[1792,128]{1,0:T(8,128)(2,1)S(1)}, bf16[1792,128]{1,0:T(8,128)(2,1)}, u32[]{:S(2)}, u32[]{:S(2)}) collective-permute-start(bf16[1792,128]{1,0:T(8,128)(2,1)S(1)} %collective-permute-done.7.refs_6_), channel_id=1, source_target_pairs={{0,1},{1,0},{2,3},{3,2},{4,5},{5,4},{6,7},{7,6},{8,9},{9,8},{10,11... | collective-permute-start | bytes 1376264 | tf_op jit(solution)/shard_map/ppermute | solution.py:252
  86.0 14.7 %collective-permute-start.10 = (bf16[1792,128]{1,0:T(8,128)(2,1)}, bf16[1792,128]{1,0:T(8,128)(2,1)}, u32[]{:S(2)}, u32[]{:S(2)}) collective-permute-start(bf16[1792,128]{1,0:T(8,128)(2,1)} %collective-permute-done.9.refs_8_), channel_id=1, source_target_pairs={{0,1},{1,0},{2,3},{3,2},{4,5},{5,4},{6,7},{7,6},{8,9},{9,8},{10,11... | collective-permute-start | bytes 1376264 | tf_op jit(solution)/shard_map/ppermute | solution.py:252
  100.7 1.2 copy-start.1
  106.5 12.4 %all-to-all-start.2 = ((bf16[4,128,512]{2,1,0:T(8,128)(2,1)}), bf16[4,128,512]{2,1,0:T(8,128)(2,1)}, u32[]{:S(2)}, u32[]{:S(2)}) async-start(bf16[4,128,512]{2,1,0:T(8,128)(2,1)} %shard_map.96), calls=%async_computation.2 | async-start | bytes 1048576 | tf_op jit(solution)/shard_map/all_to_all | solution.py:289
  118.9 14.1 %copy-start.2 = (bf16[3584,128]{1,0:T(8,128)(2,1)S(1)}, bf16[3584,128]{1,0:T(8,128)(2,1)}, u32[]{:S(2)}) copy-start(bf16[3584,128]{1,0:T(8,128)(2,1)} %copy-done) | copy-start | bytes 2752516
  152.7 33.0 %copy-start.8 = (s32[4,2,2]{0,2,1:T(2,128)S(1)}, s32[4,2,2]{0,2,1:T(2,128)}, u32[]{:S(2)}) copy-start(s32[4,2,2]{0,2,1:T(2,128)} %param.10) | copy-start | bytes 196
  152.7 33.0 %copy-start.10 = (s32[4,2]{0,1:T(2,128)S(1)}, s32[4,2]{0,1:T(2,128)}, u32[]{:S(2)}) copy-start(s32[4,2]{0,1:T(2,128)} %param.9) | copy-start | bytes 100

commit v6 on v5

--- a/solution.py
+++ b/solution.py
@@ -14,16 +14,30 @@
     return lax.dot_general(a, b, (dims, ((), ())), preferred_element_type=jnp.float32)
 
 
-def send_kernel(groups, choices, gates, tokens, cotangent, out, narrow, wide, sems):
+def small_copies(pairs, sems):
+    copies = [pltpu.make_async_copy(a, b, sems.at[i]) for i, (a, b) in enumerate(pairs)]
+    for copy in copies:
+        copy.start()
+    return copies
+
+
+def send_kernel(
+    gates, groups_at, choices_at, tokens, cotangent, out, groups, choices, narrow, wide, sems
+):
     count, width = tokens.shape
     chunks = width // LANES
-    copies = [
-        pltpu.make_async_copy(ref, narrow.at[i], sems.at[i])
-        for i, ref in enumerate((tokens, cotangent))
-    ]
-    for copy in copies:
-        copy.start()
+    first, second, *copies = small_copies(
+        [
+            (groups_at, groups),
+            (choices_at, choices),
+            (tokens, narrow.at[0]),
+            (cotangent, narrow.at[1]),
+        ],
+        sems,
+    )
     out[...] = jnp.zeros_like(out)
+    first.wait()
+    second.wait()
     every_gate = gates[...].astype(jnp.float32)
     row = lax.broadcasted_iota(jnp.int32, (8, LANES), 0)
     lane = lax.broadcasted_iota(jnp.int32, (8, LANES), 1)
@@ -47,13 +61,17 @@
             out[groups[c, t], : 2 * chunks, :] = rows
 
 
-def home_kernel(groups, choices, home, mixed, grad_tokens, grad_gates, wide):
+def home_kernel(
+    home, groups_at, choices_at, mixed, grad_tokens, grad_gates, groups, choices, wide, sems
+):
     count, width = mixed.shape
     chunks = width // LANES
     row = lax.broadcasted_iota(jnp.int32, (8, LANES), 0)
     lane = lax.broadcasted_iota(jnp.int32, (8, LANES), 1)
     i, j = (lax.broadcasted_iota(jnp.int32, (2, count), d) for d in range(2))
     inner = [jnp.zeros((2, count), jnp.float32) for c in range(2)]
+    for copy in small_copies([(groups_at, groups), (choices_at, choices)], sems):
+        copy.wait()
     for t in range(count):
         total = jnp.zeros((2 * chunks, LANES), jnp.float32)
         for c in range(2):
@@ -113,25 +131,39 @@
     return whole + [(refs[-4], refs[-2]), (refs[-3], refs[-1])]
 
 
-def partial_kernel(scalars, rows, *refs):
-    out = refs[-1]
-    hidden = refs[0].shape[1]
+def chip_sums(rows, pair, out):
+    wide = pair[0][0].shape[0]
+    units = out.shape[1] // 2
+    up = jnp.concatenate([u[...] for u, _ in pair], 1)
+    out[:, :units] = dot(rows[:, :wide], up, ((1,), (0,))).astype(out.dtype)
+    down = jnp.concatenate(
+        [
+            jnp.concatenate([d[j : j + LANES, :] for _, d in pair], 0)
+            for j in range(0, wide, LANES)
+        ],
+        1,
+    )
+    out[:, units:] = dot(rows[:, wide : 2 * wide], down, ((1,), (1,))).astype(out.dtype)
+
+
+def near_kernel(scalars, rows, *refs):
+    blocks, (out, sums, sems) = refs[:-3], refs[-3:]
     wide = (rows.shape[1] - LANES) // 2
-    blocks = pieces(refs[:-1], wide)
-    x, dy = rows[:, :wide], rows[:, wide : 2 * wide]
+    halves = [(ref.at[pl.ds(0, wide)], ref.at[pl.ds(wide, wide)]) for ref in blocks]
+    copies = []
     for i in range(len(blocks) // CORES):
-        pair = blocks[CORES * i : CORES * (i + 1)]
-        at = scalars[1 + i]
-        up = jnp.concatenate([u[...] for u, _ in pair], 1)
-        out[at, :, : CORES * hidden] = dot(x, up, ((1,), (0,))).astype(out.dtype)
-        down = jnp.concatenate(
-            [
-                jnp.concatenate([d[j : j + LANES, :] for _, d in pair], 0)
-                for j in range(0, wide, LANES)
-            ],
-            1,
-        )
-        out[at, :, CORES * hidden :] = dot(dy, down, ((1,), (1,))).astype(out.dtype)
+        chip_sums(rows, halves[CORES * i : CORES * (i + 1)], sums.at[i])
+        copies.append(pltpu.make_async_copy(sums.at[i], out.at[scalars[1 + i]], sems.at[i]))
+        copies[-1].start()
+    for copy in copies:
+        copy.wait()
+
+
+def far_kernel(scalars, rows, up, up_too, down, down_too, sums, out, block, sem):
+    chip_sums(rows, [(up, down), (up_too, down_too)], block)
+    copy = pltpu.make_async_copy(block, out.at[scalars[4]], sem)
+    copy.start()
+    copy.wait()
 
 
 def output_kernel(scalars, rows, every, *refs):
@@ -175,21 +207,27 @@
     result[:, 2 * wide :] = jnp.where(mine, inner, 0.0).astype(result.dtype)
 
 
-def call(kernel, shapes, scalars, *operands, hbm=0, scratch=()):
-    spec = pl.BlockSpec(memory_space=pltpu.VMEM)
-    far = pl.BlockSpec(memory_space=pltpu.HBM)
+def call(kernel, shapes, scalars, *operands, hbm=0, scratch=(), aliases=None, out_any=False):
+    small, near, far = (
+        pl.BlockSpec(memory_space=space) for space in (pltpu.SMEM, pltpu.VMEM, pltpu.HBM)
+    )
+    count = len(operands) - hbm
     scalars = scalars if isinstance(scalars, tuple) else (scalars,)
-    out = [jax.ShapeDtypeStruct(shape, jnp.bfloat16) for shape in shapes]
+    scalars = [pltpu.with_memory_space_constraint(v, pltpu.SMEM) for v in scalars]
+    held = operands[count:]
+    if out_any:
+        far = pl.BlockSpec(memory_space=pl.ANY)
+    else:
+        held = [pltpu.with_memory_space_constraint(v, pltpu.HBM) for v in held]
     return pl.pallas_call(
         kernel,
-        out_shape=out,
-        in_specs=[pl.BlockSpec(memory_space=pltpu.SMEM)] * len(scalars)
-        + [spec] * (len(operands) - hbm)
-        + [far] * hbm,
-        out_specs=[spec] * len(out),
+        out_shape=[jax.ShapeDtypeStruct(shape, jnp.bfloat16) for shape in shapes],
+        in_specs=[small] * len(scalars) + [near] * count + [far] * hbm,
+        out_specs=[far if out_any else near] * len(shapes),
         scratch_shapes=scratch,
-        compiler_params=pltpu.CompilerParams(vmem_limit_bytes=40 * 2**20),
-    )(*scalars, *operands)
+        input_output_aliases=aliases or {},
+        compiler_params=pltpu.CompilerParams(vmem_limit_bytes=20 * 2**20),
+    )(*scalars, *operands[:count], *held)
 
 
 def per_device(tokens, cotangent, groups, choices, gates, up_weight, down_weight):
@@ -207,19 +245,23 @@
 
     slot_rows = 2 * width // LANES
     groups, choices = groups.T, choices.transpose(1, 2, 0)
+    tables = [pltpu.SMEM(v.shape, jnp.int32) for v in (groups, choices)]
     wide_rows = pltpu.VMEM((tok_count, slot_rows, LANES), f32)
     (sent,) = call(
         send_kernel,
         [(nodes, slot_rows + 8, LANES)],
-        (groups, choices),
+        (),
         gates.transpose(1, 2, 0),
+        groups,
+        choices,
         tokens,
         cotangent,
-        hbm=2,
+        hbm=4,
         scratch=[
+            *tables,
             pltpu.VMEM((2,) + tokens.shape, bf16),
             wide_rows,
-            pltpu.SemaphoreType.DMA((2,)),
+            pltpu.SemaphoreType.DMA((4,)),
         ],
     )
 
@@ -247,9 +289,9 @@
     )
     far_up = lax.ppermute(far_up, "chip", ahead_of)
     far_down = lax.ppermute(far_down, "chip", behind_of)
-    blocks = [here, here_too]
-    for block in (ahead, behind, far_up, far_down):
-        blocks += [block, lax.ppermute(block, "core", swap)]
+    near = [here, here_too]
+    for block in (ahead, behind):
+        near += [block, lax.ppermute(block, "core", swap)]
     scalars = jnp.stack(
         [expert, chip, (chip + chips - 1) % chips, (chip + 1) % chips, (chip + 2) % chips]
     ).astype(jnp.int32)
@@ -278,13 +320,38 @@
     rows = lax.all_to_all(
         spread, ("expert", "chip"), split_axis=0, concat_axis=0, tiled=True
     ).reshape(experts * chips * pairs, -1)
+    rows, far_up, far_down = lax.optimization_barrier((rows, far_up, far_down))
+    far = []
+    for block in (far_up, far_down):
+        far += [block, lax.ppermute(block, "core", swap)]
     gate = jnp.sum(
         jnp.where(lane[None, :] == expert, rows[:, 2 * wide :].astype(f32), 0.0), 1, keepdims=True
     )
 
     units = CORES * hidden
     (outgoing,) = call(
-        partial_kernel, [(chips, rows.shape[0], 2 * units)], scalars, rows, *blocks
+        near_kernel,
+        [(chips, rows.shape[0], 2 * units)],
+        scalars,
+        rows,
+        *near,
+        scratch=[
+            pltpu.VMEM((chips - 1, rows.shape[0], 2 * units), bf16),
+            pltpu.SemaphoreType.DMA((chips - 1,)),
+        ],
+        out_any=True,
+    )
+    (outgoing,) = call(
+        far_kernel,
+        [outgoing.shape],
+        scalars,
+        rows,
+        *far,
+        outgoing,
+        hbm=1,
+        scratch=[pltpu.VMEM(outgoing.shape[1:], bf16), pltpu.SemaphoreType.DMA],
+        aliases={6: 0},
+        out_any=True,
     )
     incoming = lax.all_to_all(outgoing, "chip", split_axis=0, concat_axis=0, tiled=True)
     both = jnp.sum(incoming.astype(f32), 0)
@@ -295,7 +362,7 @@
     grad_pre = (gate * back * sig * (1.0 + pre * (1.0 - sig))).astype(bf16)
     every = lax.all_gather(jnp.concatenate([active, grad_pre], 1), "chip", axis=0)
 
-    (result,) = call(output_kernel, [rows.shape], scalars, rows, every, *blocks)
+    (result,) = call(output_kernel, [rows.shape], scalars, rows, every, *near, *far)
 
     parts_back = lax.all_to_all(
         result.reshape(experts * chips, pairs, -1),
@@ -319,9 +386,12 @@
     mixed, grad_tokens, grad_gates = call(
         home_kernel,
         [tokens.shape, tokens.shape, choices.shape],
-        (groups, choices),
+        (),
         home,
-        scratch=[wide_rows],
+        groups,
+        choices,
+        hbm=2,
+        scratch=[*tables, wide_rows, pltpu.SemaphoreType.DMA((2,))],
     )
     return mixed, grad_tokens, grad_gates.transpose(2, 0, 1)
 

time: 188 us -> 191 us (1.016)
  the two profiles are of different devices: /device:TPU:32 before, /device:TPU:64 now
where the time goes in v6:
time: 191 us; the launch traced here: 190 us
  blocking collectives  66.5 us (35%)
  starting transfers between devices  57.6 us (30%)
  waiting for transfers between devices  40.5 us (21%)
  Pallas kernels  16.9 us (9%)
  local copies, waits for them, and re-layouts  4.95 us (3%)
  other arithmetic  2.29 us (1%)
    all_to_all x1, blocking collectives, per_device(): lax.all_to_all(expanded, 'node', split_axis=0, concat_axis=0, tiled=True)  35 us
    ppermute x2, waiting for transfers between devices, per_device(): far_up = lax.ppermute(far_up, 'chip', ahead_of)  28.7 us
    all_to_all x1, blocking collectives, per_device(): lax.all_to_all(result.reshape(experts * chips, pairs, -1), ('expert', 'ch...  18.2 us
    pallas_call x6, Pallas kernels, call(): pl.pallas_call(kernel, out_shape=[jax.ShapeDtypeStruct(shape, jnp.bfloat1...  16.9 us
    all_to_all x1, starting transfers between devices, per_device(): recv = lax.all_to_all(sent, 'node', split_axis=0, concat_axis=0, tiled=True)  14.8 us
    all_gather x1, blocking collectives, per_device(): lax.all_gather(jnp.concatenate([active, grad_pre], 1), 'chip', axis=0)  13.3 us
    all_to_all x1, waiting for transfers between devices, per_device(): lax.all_to_all(outgoing, 'chip', split_axis=0, concat_axis=0, tiled=True)  9.87 us
    ppermute x2, starting transfers between devices, per_device(): far_down = lax.ppermute(far_down, 'chip', behind_of)  8.1 us
  transfers between devices with their start and end apart: 14, of which 4 were waited for; matrix products, arithmetic and copies ran while one was open for 0% of the time, Pallas kernels for 4%

profile of v6, /device:TPU:64, one launch (start us, length us, event | category | flops | bytes accessed | tf_op | source)
XLA Modules:
  0.0 190.3 jit_solution(9364968153403299575)
XLA Ops:
  0.6 0.7 copy-done.3
  1.3 1.9 shard_map.94
  3.2 14.8 %all-to-all-start = ((bf16[16,120,128]{2,1,0:T(8,128)(2,1)}), bf16[16,120,128]{2,1,0:T(8,128)(2,1)S(1)}, u32[]{:S(2)}, u32[]{:S(2)}) async-start(bf16[16,120,128]{2,1,0:T(8,128)(2,1)} %shard_map.94), calls=%async_computation | async-start | bytes 983040 | tf_op jit(solution)/shard_map/all_to_all | solution.py:286
  17.9 0.1 pad_add_fusion.chips
  18.0 3.1 %shard_map.95 = (bf16[3584,128]{1,0:T(8,128)(2,1)S(1)}, bf16[3584,128]{1,0:T(8,128)(2,1)S(1)}, bf16[3584,128]{1,0:T(8,128)(2,1)S(1)}, bf16[1792,128]{1,0:T(8,128)(2,1)S(1)}, bf16[1792,128]{1,0:T(8,128)(2,1)S(1)}) custom-call(s32[4]{0:T(128)S(1)} %pad_add_fusion.chips, bf16[7168,128]{1,0:T(8,128)(2,1)} %up.1, bf16[128,7168]{1,0:T(8,128)(2,1)} %down.1), custom_call_target="tpu_custom_call" | custom-call | tf_op jit(solution)/shard_map/pallas_call | solution.py:222
  21.1 3.4 %collective-permute-start.1 = (bf16[3584,128]{1,0:T(8,128)(2,1)S(1)}, bf16[3584,128]{1,0:T(8,128)(2,1)S(1)}, u32[]{:S(2)}, u32[]{:S(2)}) collective-permute-start(bf16[3584,128]{1,0:T(8,128)(2,1)S(1)} %get-tuple-element.21), channel_id=1, source_target_pairs={{0,2},{2,4},{4,6},{6,0},{1,3},{3,5},{5,7},{7,1},{8,10},{10,12},{12... | collective-permute-start | bytes 2752520 | tf_op jit(solution)/shard_map/ppermute | solution.py:283
  24.5 3.7 %collective-permute-start.2 = (bf16[3584,128]{1,0:T(8,128)(2,1)S(1)}, bf16[3584,128]{1,0:T(8,128)(2,1)}, u32[]{:S(2)}, u32[]{:S(2)}) collective-permute-start(bf16[3584,128]{1,0:T(8,128)(2,1)S(1)} %get-tuple-element.22), channel_id=1, source_target_pairs={{0,6},{2,0},{4,2},{6,4},{1,7},{3,1},{5,3},{7,5},{8,14},{10,8},{12,... | collective-permute-start | bytes 2752520 | tf_op jit(solution)/shard_map/ppermute | solution.py:284
  28.2 1.9 %collective-permute-start = (bf16[3584,128]{1,0:T(8,128)(2,1)S(1)}, bf16[3584,128]{1,0:T(8,128)(2,1)S(1)}, u32[]{:S(2)}, u32[]{:S(2)}) collective-permute-start(bf16[3584,128]{1,0:T(8,128)(2,1)S(1)} %get-tuple-element.20.refs_0_), channel_id=1, source_target_pairs={{0,1},{1,0},{2,3},{3,2},{4,5},{5,4},{6,7},{7,6},{8,9},{9,8},{10,11... | collective-permute-start | bytes 2752520 | tf_op jit(solution)/shard_map/ppermute | solution.py:285
  30.1 2.2 %collective-permute-start.3 = (bf16[1792,128]{1,0:T(8,128)(2,1)S(1)}, bf16[1792,128]{1,0:T(8,128)(2,1)S(1)}, u32[]{:S(2)}, u32[]{:S(2)}) collective-permute-start(bf16[1792,128]{1,0:T(8,128)(2,1)S(1)} %get-tuple-element.23), channel_id=1, source_target_pairs={{0,2},{2,4},{4,6},{6,0},{1,3},{3,5},{5,7},{7,1},{8,10},{10,12},{12... | collective-permute-start | bytes 1376264 | tf_op jit(solution)/shard_map/ppermute | solution.py:281
  32.3 4.9 %collective-permute-start.4 = (bf16[1792,128]{1,0:T(8,128)(2,1)S(1)}, bf16[1792,128]{1,0:T(8,128)(2,1)S(1)}, u32[]{:S(2)}, u32[]{:S(2)}) collective-permute-start(bf16[1792,128]{1,0:T(8,128)(2,1)S(1)} %get-tuple-element.24), channel_id=1, source_target_pairs={{0,6},{2,0},{4,2},{6,4},{1,7},{3,1},{5,3},{7,5},{8,14},{10,8},{12,... | collective-permute-start | bytes 1376264 | tf_op jit(solution)/shard_map/ppermute | solution.py:282
  37.2 18.4 %collective-permute-done.3 = bf16[1792,128]{1,0:T(8,128)(2,1)S(1)} collective-permute-done((bf16[1792,128]{1,0:T(8,128)(2,1)S(1)}, bf16[1792,128]{1,0:T(8,128)(2,1)S(1)}, u32[]{:S(2)}, u32[]{:S(2)}) %collective-permute-start.3) | collective-permute-done | bytes 458784 | tf_op jit(solution)/shard_map/ppermute | solution.py:281
  55.6 1.9 %collective-permute-done.4 = bf16[1792,128]{1,0:T(8,128)(2,1)S(1)} collective-permute-done((bf16[1792,128]{1,0:T(8,128)(2,1)S(1)}, bf16[1792,128]{1,0:T(8,128)(2,1)S(1)}, u32[]{:S(2)}, u32[]{:S(2)}) %collective-permute-start.4) | collective-permute-done | bytes 458784 | tf_op jit(solution)/shard_map/ppermute | solution.py:282
  57.5 0.0 collective-permute-done.2.refs_4_
  57.5 0.8 copy-done.5
  58.3 0.0 collective-permute-done.refs_1_
  58.3 1.0 copy-done
  59.3 0.4 compare_reduce_fusion
  59.7 0.1 copy.13
  59.8 0.1 add_reduce_fusion
  59.9 0.2 convolution_convert_fusion.1
  60.2 1.0 broadcast_in_dim.10
  61.3 7.0 %all-to-all-start.1 = ((bf16[16,8,3712]{2,1,0:T(8,128)(2,1)}), bf16[16,8,3712]{2,1,0:T(8,128)(2,1)S(1)}, u32[]{:S(2)}, u32[]{:S(2)}) async-start(bf16[16,8,3712]{2,1,0:T(8,128)(2,1)} %bitcast.73), calls=%async_computation.1 | async-start | bytes 1900544 | tf_op jit(solution)/shard_map/all_to_all | solution.py:320
  68.2 3.8 %collective-permute-start.5 = (bf16[1792,128]{1,0:T(8,128)(2,1)}, bf16[1792,128]{1,0:T(8,128)(2,1)S(1)}, u32[]{:S(2)}, u32[]{:S(2)}) collective-permute-start(bf16[1792,128]{1,0:T(8,128)(2,1)} %copy-done.4), channel_id=1, source_target_pairs={{0,2},{2,4},{4,6},{6,0},{1,3},{3,5},{5,7},{7,1},{8,10},{10,12},{12... | collective-permute-start | bytes 1376264 | tf_op jit(solution)/shard_map/ppermute | solution.py:290
  72.1 3.2 %collective-permute-start.6 = (bf16[1792,128]{1,0:T(8,128)(2,1)}, bf16[1792,128]{1,0:T(8,128)(2,1)}, u32[]{:S(2)}, u32[]{:S(2)}) collective-permute-start(bf16[1792,128]{1,0:T(8,128)(2,1)} %copy-done.5), channel_id=1, source_target_pairs={{0,6},{2,0},{4,2},{6,4},{1,7},{3,1},{5,3},{7,5},{8,14},{10,8},{12,... | collective-permute-start | bytes 1376264 | tf_op jit(solution)/shard_map/ppermute | solution.py:291
  75.3 1.9 %collective-permute-start.9 = (bf16[3584,128]{1,0:T(8,128)(2,1)S(1)}, bf16[3584,128]{1,0:T(8,128)(2,1)}, u32[]{:S(2)}, u32[]{:S(2)}) collective-permute-start(bf16[3584,128]{1,0:T(8,128)(2,1)S(1)} %collective-permute-done.1.refs_2_), channel_id=1, source_target_pairs={{0,1},{1,0},{2,3},{3,2},{4,5},{5,4},{6,7},{7,6},{8,9},{9,8},{10,11... | collective-permute-start | bytes 2752520 | tf_op jit(solution)/shard_map/ppermute | solution.py:294
  77.2 2.4 %collective-permute-start.10 = (bf16[3584,128]{1,0:T(8,128)(2,1)}, bf16[3584,128]{1,0:T(8,128)(2,1)}, u32[]{:S(2)}, u32[]{:S(2)}) collective-permute-start(bf16[3584,128]{1,0:T(8,128)(2,1)} %collective-permute-done.2.refs_4_), channel_id=1, source_target_pairs={{0,1},{1,0},{2,3},{3,2},{4,5},{5,4},{6,7},{7,6},{8,9},{9,8},{10,11... | collective-permute-start | bytes 2752520 | tf_op jit(solution)/shard_map/ppermute | solution.py:294
  79.7 10.3 %collective-permute-done.5.up.refs_6_ = bf16[1792,128]{1,0:T(8,128)(2,1)S(1)} collective-permute-done((bf16[1792,128]{1,0:T(8,128)(2,1)}, bf16[1792,128]{1,0:T(8,128)(2,1)S(1)}, u32[]{:S(2)}, u32[]{:S(2)}) %collective-permute-start.5) | collective-permute-done | bytes 458784 | tf_op jit(solution)/shard_map/ppermute | solution.py:290
  90.0 0.0 collective-permute-done.6.down.refs_8_
  90.0 0.0 all-to-all-done.1
  90.0 1.9 %collective-permute-start.7 = (bf16[1792,128]{1,0:T(8,128)(2,1)S(1)}, bf16[1792,128]{1,0:T(8,128)(2,1)}, u32[]{:S(2)}, u32[]{:S(2)}) collective-permute-start(bf16[1792,128]{1,0:T(8,128)(2,1)S(1)} %collective-permute-done.5.up.refs_6_), channel_id=1, source_target_pairs={{0,1},{1,0},{2,3},{3,2},{4,5},{5,4},{6,7},{7,6},{8,9},{9,8},{10,11... | collective-permute-start | bytes 1376264 | tf_op jit(solution)/shard_map/ppermute | solution.py:326
  91.9 2.4 %collective-permute-start.8 = (bf16[1792,128]{1,0:T(8,128)(2,1)}, bf16[1792,128]{1,0:T(8,128)(2,1)}, u32[]{:S(2)}, u32[]{:S(2)}) collective-permute-start(bf16[1792,128]{1,0:T(8,128)(2,1)} %collective-permute-done.6.down.refs_8_), channel_id=1, source_target_pairs={{0,1},{1,0},{2,3},{3,2},{4,5},{5,4},{6,7},{7,6},{8,9},{9,8},{10,11... | collective-permute-start | bytes 1376264 | tf_op jit(solution)/shard_map/ppermute | solution.py:326
  94.3 0.1 stack.49.scalars
  94.4 1.2 copy-done.1
  95.6 3.7 %shard_map.96.sums = bf16[4,128,512]{2,1,0:T(8,128)(2,1)} custom-call(s32[5]{0:T(128)S(1)} %stack.49.scalars, bf16[128,3712]{1,0:T(8,128)(2,1)S(1)} %bitcast.66, bf16[3584,128]{1,0:T(8,128)(2,1)S(1)} %get-tuple-element.20.refs_0_, bf16[3584,128]{1,0:T(8,128)(2,1)S(1)} %copy-done.1, bf16[3584,128]{1,0:T(8,128)(2,1)S(1)} %collective-permute-done.1.refs_2_, ...), custom_call_target="tpu_custom_call" | custom-call | tf_op jit(solution)/shard_map/pallas_call | solution.py:222
  99.3 2.5 %shard_map.97 = bf16[4,128,512]{2,1,0:T(8,128)(2,1)} custom-call(s32[5]{0:T(128)S(1)} %stack.49.scalars, bf16[128,3712]{1,0:T(8,128)(2,1)S(1)} %bitcast.67, bf16[1792,128]{1,0:T(8,128)(2,1)S(1)} %collective-permute-done.5.up.refs_6_, bf16[1792,128]{1,0:T(8,128)(2,1)} %collective-permute-done.7.up_too.refs_7_, ...), custom_call_target="tpu_custom_call", output_to_operand_aliasing={{}: (6, {})} | custom-call | tf_op jit(solution)/shard_map/pallas_call | solution.py:222
  101.9 4.2 %all-to-all-start.2 = ((bf16[4,128,512]{2,1,0:T(8,128)(2,1)}), bf16[4,128,512]{2,1,0:T(8,128)(2,1)}, u32[]{:S(2)}, u32[]{:S(2)}) async-start(bf16[4,128,512]{2,1,0:T(8,128)(2,1)} %shard_map.97), calls=%async_computation.2 | async-start | bytes 1048576 | tf_op jit(solution)/shard_map/all_to_all | solution.py:356
  106.0 0.1 select_reduce_fusion
  106.1 9.9 %all-to-all-done.2 = bf16[4,128,512]{2,1,0:T(8,128)(2,1)} async-done(((bf16[4,128,512]{2,1,0:T(8,128)(2,1)}), bf16[4,128,512]{2,1,0:T(8,128)(2,1)}, u32[]{:S(2)}, u32[]{:S(2)}) %all-to-all-start.2) | async-done | bytes 524320 | tf_op jit(solution)/shard_map/all_to_all | solution.py:356
  116.0 1.2 convert_reduce_fusion.1
  117.3 0.1 multiply_convert_fusion
  117.4 13.3 %all-gather = bf16[512,512]{1,0:T(8,128)(2,1)S(1)} all-gather(bf16[128,512]{1,0:T(8,128)(2,1)S(1)} %pad_maximum_fusion.1), channel_id=2, replica_groups=mesh['node'=16,'expert'=4,'chip'=4,'core'=2] {'chip'}, dimensions={0}, use_global_device_ids=true | all-gather | bytes 655360 | tf_op jit(solution)/shard_map/all_gather | solution.py:363
  130.7 4.0 %shard_map.98 = bf16[128,3712]{1,0:T(8,128)(2,1)S(1)} custom-call(s32[5]{0:T(128)S(1)} %stack.49.scalars, bf16[128,3712]{1,0:T(8,128)(2,1)S(1)} %bitcast.69, bf16[4,128,512]{2,1,0:T(8,128)(2,1)S(1)} %bitcast.71, bf16[3584,128]{1,0:T(8,128)(2,1)S(1)} %get-tuple-element.20.refs_0_, bf16[3584,128]{1,0:T(8,128)(2,1)S(1)} %copy-done.2, ...), custom_call_target="tpu_custom_call" | custom-call | tf_op jit(solution)/shard_map/pallas_call | solution.py:222
  134.7 18.2 %all_to_all.25 = bf16[16,8,3712]{2,1,0:T(8,128)(2,1)S(1)} all-to-all(bf16[16,8,3712]{2,1,0:T(8,128)(2,1)S(1)} %bitcast.70), channel_id=1, replica_groups=mesh['node'=16,'expert'=4,'chip'=4,'core'=2] {'expert','chip'}, dimensions={0} | all-to-all | bytes 1900544 | tf_op jit(solution)/shard_map/all_to_all | solution.py:367
  152.9 0.1 convert_reduce_fusion
  153.2 0.3 convolution_convert_fusion
  153.5 0.1 copy.15
  153.6 35.0 %all_to_all.26.home = bf16[16,120,128]{2,1,0:T(8,128)(2,1)S(1)} all-to-all(bf16[16,120,128]{2,1,0:T(8,128)(2,1)S(1)} %bitcast.76), channel_id=1, replica_groups=mesh['node'=16,'expert'=4,'chip'=4,'core'=2] {'node'}, dimensions={0} | all-to-all | bytes 983040 | tf_op jit(solution)/shard_map/all_to_all | solution.py:384
  188.6 1.7 shard_map.99
  (35 shorter events, 0.3 us)
Async XLA Ops:
  0.6 0.7 copy-start.3
  3.2 56.1 %all-to-all-start = ((bf16[16,120,128]{2,1,0:T(8,128)(2,1)}), bf16[16,120,128]{2,1,0:T(8,128)(2,1)S(1)}, u32[]{:S(2)}, u32[]{:S(2)}) async-start(bf16[16,120,128]{2,1,0:T(8,128)(2,1)} %shard_map.94), calls=%async_computation | async-start | bytes 983040 | tf_op jit(solution)/shard_map/all_to_all | solution.py:286
  21.1 36.4 %collective-permute-start.1 = (bf16[3584,128]{1,0:T(8,128)(2,1)S(1)}, bf16[3584,128]{1,0:T(8,128)(2,1)S(1)}, u32[]{:S(2)}, u32[]{:S(2)}) collective-permute-start(bf16[3584,128]{1,0:T(8,128)(2,1)S(1)} %get-tuple-element.21), channel_id=1, source_target_pairs={{0,2},{2,4},{4,6},{6,0},{1,3},{3,5},{5,7},{7,1},{8,10},{10,12},{12... | collective-permute-start | bytes 2752520 | tf_op jit(solution)/shard_map/ppermute | solution.py:283
  24.5 33.0 %collective-permute-start.2 = (bf16[3584,128]{1,0:T(8,128)(2,1)S(1)}, bf16[3584,128]{1,0:T(8,128)(2,1)}, u32[]{:S(2)}, u32[]{:S(2)}) collective-permute-start(bf16[3584,128]{1,0:T(8,128)(2,1)S(1)} %get-tuple-element.22), channel_id=1, source_target_pairs={{0,6},{2,0},{4,2},{6,4},{1,7},{3,1},{5,3},{7,5},{8,14},{10,8},{12,... | collective-permute-start | bytes 2752520 | tf_op jit(solution)/shard_map/ppermute | solution.py:284
  28.2 30.1 %collective-permute-start = (bf16[3584,128]{1,0:T(8,128)(2,1)S(1)}, bf16[3584,128]{1,0:T(8,128)(2,1)S(1)}, u32[]{:S(2)}, u32[]{:S(2)}) collective-permute-start(bf16[3584,128]{1,0:T(8,128)(2,1)S(1)} %get-tuple-element.20.refs_0_), channel_id=1, source_target_pairs={{0,1},{1,0},{2,3},{3,2},{4,5},{5,4},{6,7},{7,6},{8,9},{9,8},{10,11... | collective-permute-start | bytes 2752520 | tf_op jit(solution)/shard_map/ppermute | solution.py:285
  30.1 25.5 %collective-permute-start.3 = (bf16[1792,128]{1,0:T(8,128)(2,1)S(1)}, bf16[1792,128]{1,0:T(8,128)(2,1)S(1)}, u32[]{:S(2)}, u32[]{:S(2)}) collective-permute-start(bf16[1792,128]{1,0:T(8,128)(2,1)S(1)} %get-tuple-element.23), channel_id=1, source_target_pairs={{0,2},{2,4},{4,6},{6,0},{1,3},{3,5},{5,7},{7,1},{8,10},{10,12},{12... | collective-permute-start | bytes 1376264 | tf_op jit(solution)/shard_map/ppermute | solution.py:281
  32.3 25.2 %collective-permute-start.4 = (bf16[1792,128]{1,0:T(8,128)(2,1)S(1)}, bf16[1792,128]{1,0:T(8,128)(2,1)S(1)}, u32[]{:S(2)}, u32[]{:S(2)}) collective-permute-start(bf16[1792,128]{1,0:T(8,128)(2,1)S(1)} %get-tuple-element.24), channel_id=1, source_target_pairs={{0,6},{2,0},{4,2},{6,4},{1,7},{3,1},{5,3},{7,5},{8,14},{10,8},{12,... | collective-permute-start | bytes 1376264 | tf_op jit(solution)/shard_map/ppermute | solution.py:282
  55.6 1.9 %copy-start.4 = (bf16[1792,128]{1,0:T(8,128)(2,1)}, bf16[1792,128]{1,0:T(8,128)(2,1)S(1)}, u32[]{:S(2)}) copy-start(bf16[1792,128]{1,0:T(8,128)(2,1)S(1)} %collective-permute-done.3) | copy-start | bytes 1376260
  57.5 0.8 copy-start.5
  58.3 1.0 copy-start
  61.3 28.7 %all-to-all-start.1 = ((bf16[16,8,3712]{2,1,0:T(8,128)(2,1)}), bf16[16,8,3712]{2,1,0:T(8,128)(2,1)S(1)}, u32[]{:S(2)}, u32[]{:S(2)}) async-start(bf16[16,8,3712]{2,1,0:T(8,128)(2,1)} %bitcast.73), calls=%async_computation.1 | async-start | bytes 1900544 | tf_op jit(solution)/shard_map/all_to_all | solution.py:320
  68.2 21.7 %collective-permute-start.5 = (bf16[1792,128]{1,0:T(8,128)(2,1)}, bf16[1792,128]{1,0:T(8,128)(2,1)S(1)}, u32[]{:S(2)}, u32[]{:S(2)}) collective-permute-start(bf16[1792,128]{1,0:T(8,128)(2,1)} %copy-done.4), channel_id=1, source_target_pairs={{0,2},{2,4},{4,6},{6,0},{1,3},{3,5},{5,7},{7,1},{8,10},{10,12},{12... | collective-permute-start | bytes 1376264 | tf_op jit(solution)/shard_map/ppermute | solution.py:290
  72.1 17.9 %collective-permute-start.6 = (bf16[1792,128]{1,0:T(8,128)(2,1)}, bf16[1792,128]{1,0:T(8,128)(2,1)}, u32[]{:S(2)}, u32[]{:S(2)}) collective-permute-start(bf16[1792,128]{1,0:T(8,128)(2,1)} %copy-done.5), channel_id=1, source_target_pairs={{0,6},{2,0},{4,2},{6,4},{1,7},{3,1},{5,3},{7,5},{8,14},{10,8},{12,... | collective-permute-start | bytes 1376264 | tf_op jit(solution)/shard_map/ppermute | solution.py:291
  75.3 19.1 %collective-permute-start.9 = (bf16[3584,128]{1,0:T(8,128)(2,1)S(1)}, bf16[3584,128]{1,0:T(8,128)(2,1)}, u32[]{:S(2)}, u32[]{:S(2)}) collective-permute-start(bf16[3584,128]{1,0:T(8,128)(2,1)S(1)} %collective-permute-done.1.refs_2_), channel_id=1, source_target_pairs={{0,1},{1,0},{2,3},{3,2},{4,5},{5,4},{6,7},{7,6},{8,9},{9,8},{10,11... | collective-permute-start | bytes 2752520 | tf_op jit(solution)/shard_map/ppermute | solution.py:294
  77.2 17.2 %collective-permute-start.10 = (bf16[3584,128]{1,0:T(8,128)(2,1)}, bf16[3584,128]{1,0:T(8,128)(2,1)}, u32[]{:S(2)}, u32[]{:S(2)}) collective-permute-start(bf16[3584,128]{1,0:T(8,128)(2,1)} %collective-permute-done.2.refs_4_), channel_id=1, source_target_pairs={{0,1},{1,0},{2,3},{3,2},{4,5},{5,4},{6,7},{7,6},{8,9},{9,8},{10,11... | collective-permute-start | bytes 2752520 | tf_op jit(solution)/shard_map/ppermute | solution.py:294
  90.0 9.4 %collective-permute-start.7 = (bf16[1792,128]{1,0:T(8,128)(2,1)S(1)}, bf16[1792,128]{1,0:T(8,128)(2,1)}, u32[]{:S(2)}, u32[]{:S(2)}) collective-permute-start(bf16[1792,128]{1,0:T(8,128)(2,1)S(1)} %collective-permute-done.5.up.refs_6_), channel_id=1, source_target_pairs={{0,1},{1,0},{2,3},{3,2},{4,5},{5,4},{6,7},{7,6},{8,9},{9,8},{10,11... | collective-permute-start | bytes 1376264 | tf_op jit(solution)/shard_map/ppermute | solution.py:326
  91.9 7.5 %collective-permute-start.8 = (bf16[1792,128]{1,0:T(8,128)(2,1)}, bf16[1792,128]{1,0:T(8,128)(2,1)}, u32[]{:S(2)}, u32[]{:S(2)}) collective-permute-start(bf16[1792,128]{1,0:T(8,128)(2,1)} %collective-permute-done.6.down.refs_8_), channel_id=1, source_target_pairs={{0,1},{1,0},{2,3},{3,2},{4,5},{5,4},{6,7},{7,6},{8,9},{9,8},{10,11... | collective-permute-start | bytes 1376264 | tf_op jit(solution)/shard_map/ppermute | solution.py:326
  94.4 1.2 copy-start.1
  101.9 14.2 %all-to-all-start.2 = ((bf16[4,128,512]{2,1,0:T(8,128)(2,1)}), bf16[4,128,512]{2,1,0:T(8,128)(2,1)}, u32[]{:S(2)}, u32[]{:S(2)}) async-start(bf16[4,128,512]{2,1,0:T(8,128)(2,1)} %shard_map.97), calls=%async_computation.2 | async-start | bytes 1048576 | tf_op jit(solution)/shard_map/all_to_all | solution.py:356
  116.0 14.7 %copy-start.2 = (bf16[3584,128]{1,0:T(8,128)(2,1)S(1)}, bf16[3584,128]{1,0:T(8,128)(2,1)}, u32[]{:S(2)}) copy-start(bf16[3584,128]{1,0:T(8,128)(2,1)} %copy-done) | copy-start | bytes 2752516

commit v7 on v6

v7 whole, which is shorter than its diff:
```python
import jax
import jax.numpy as jnp
from jax import lax
from jax.experimental import pallas as pl
from jax.experimental.pallas import tpu as pltpu
from jax.sharding import Mesh, PartitionSpec as P

EXPERTS = 4
CORES = 2
SIDES = 2
LANES = 128


def dot(a, b, dims):
    return lax.dot_general(a, b, (dims, ((), ())), preferred_element_type=jnp.float32)


def small_copies(pairs, sems):
    copies = [pltpu.make_async_copy(a, b, sems.at[i]) for i, (a, b) in enumerate(pairs)]
    for copy in copies:
        copy.start()
    return copies


def send_kernel(
    gates, groups_at, choices_at, tokens, cotangent, out, groups, choices, narrow, wide, sems
):
    count, width = tokens.shape
    chunks = width // LANES
    first, second, *copies = small_copies(
        [
            (groups_at, groups),
            (choices_at, choices),
            (tokens, narrow.at[0]),
            (cotangent, narrow.at[1]),
        ],
        sems,
    )
    out[...] = jnp.zeros_like(out)
    first.wait()
    second.wait()
    every_gate = gates[...].astype(jnp.float32)
    row = lax.broadcasted_iota(jnp.int32, (8, LANES), 0)
    lane = lax.broadcasted_iota(jnp.int32, (8, LANES), 1)
    i, j = (lax.broadcasted_iota(jnp.int32, (2, count), d) for d in range(2))
    for t in range(count):
        for c in range(2):
            table = jnp.zeros((8, LANES), jnp.float32)
            for k in range(2):
                gate = jnp.sum(jnp.where((i == k) & (j == t), every_gate[c], 0.0), keepdims=True)
                table += jnp.where((row == 0) & (lane == choices[c, k, t]), gate, 0.0)
            out[groups[c, t], 2 * chunks :, :] = table.astype(out.dtype)
    for i, copy in enumerate(copies):
        copy.wait()
        for j in range(chunks):
            wide[:, i * chunks + j, :] = narrow[i, :, j * LANES : (j + 1) * LANES].astype(
                jnp.float32
            )
    for t in range(count):
        rows = wide[t].astype(out.dtype)
        for c in range(2):
            out[groups[c, t], : 2 * chunks, :] = rows


def home_kernel(
    home, groups_at, choices_at, mixed, grad_tokens, grad_gates, groups, choices, wide, sems
):
    count, width = mixed.shape
    chunks = width // LANES
    row = lax.broadcasted_iota(jnp.int32, (8, LANES), 0)
    lane = lax.broadcasted_iota(jnp.int32, (8, LANES), 1)
    i, j = (lax.broadcasted_iota(jnp.int32, (2, count), d) for d in range(2))
    inner = [jnp.zeros((2, count), jnp.float32) for c in range(2)]
    for copy in small_copies([(groups_at, groups), (choices_at, choices)], sems):
        copy.wait()
    for t in range(count):
        total = jnp.zeros((2 * chunks, LANES), jnp.float32)
        for c in range(2):
            node = groups[c, t]
            total += home[node, : 2 * chunks, :].astype(jnp.float32)
            table = home[node, 2 * chunks :, :].astype(jnp.float32)
            for k in range(2):
                value = jnp.sum(
                    jnp.where((row == 0) & (lane == choices[c, k, t]), table, 0.0), keepdims=True
                )
                inner[c] = jnp.where((i == k) & (j == t), value, inner[c])
        wide[t] = total
    for c in range(2):
        grad_gates[c] = inner[c].astype(grad_gates.dtype)
    for j in range(chunks):
        at = pl.ds(j * LANES, LANES)
        mixed[:, at] = wide[:, j, :].astype(mixed.dtype)
        grad_tokens[:, at] = wide[:, chunks + j, :].astype(grad_tokens.dtype)


def pack_kernel(sides, up, down, here, give_up, give_down, sems):
    half = give_up.shape[0]
    copies = []
    for i, (rows, tiles) in enumerate(
        ((give_up, give_down), (here.at[pl.ds(0, half)], here.at[pl.ds(half, half)]))
    ):
        start = pl.multiple_of(sides[1 - i] * half, half)
        copies.append((up.at[pl.ds(start, half)], rows))
        for j in range(0, half, LANES):
            copies.append((down.at[:, pl.ds(start + j, LANES)], tiles.at[pl.ds(j, LANES)]))
    for copy in small_copies(copies, sems):
        copy.wait()


def chip_sums(rows, pair, out):
    half = pair[0][0].shape[0]
    units = out.shape[1] // 2
    up = jnp.concatenate([u[...] for u, _ in pair], 1)
    out[:, :units] = dot(rows[:, :half], up, ((1,), (0,))).astype(out.dtype)
    down = jnp.concatenate(
        [
            jnp.concatenate([d[j : j + LANES, :] for _, d in pair], 0)
            for j in range(0, half, LANES)
        ],
        1,
    )
    out[:, units:] = dot(rows[:, half : 2 * half], down, ((1,), (1,))).astype(out.dtype)


def halves(refs):
    half = refs[0].shape[0] // 2
    return [(ref.at[pl.ds(0, half)], ref.at[pl.ds(half, half)]) for ref in refs]


def own_kernel(rows, here, here_too, out):
    chip_sums(rows, halves((here, here_too)), out)


def partner_kernel(rows, up, up_too, down, down_too, out):
    chip_sums(rows, [(up, down), (up_too, down_too)], out)


def output_kernel(scalars, rows, own, partner, here, here_too, up, up_too, down, down_too, result):
    blocks = halves((here, here_too)) + [(up, down), (up_too, down_too)]
    half = up.shape[0]
    units = own.shape[1] // 2
    count = rows.shape[0]
    lane = lax.broadcasted_iota(jnp.int32, (count, LANES), 1)
    mine = lane == scalars[0]
    gate = jnp.sum(
        jnp.where(mine, rows[:, 2 * half :].astype(jnp.float32), 0.0), 1, keepdims=True
    )
    active = jnp.concatenate([own[:, :units], partner[:, :units]], 1)
    grad_pre = jnp.concatenate([own[:, units:], partner[:, units:]], 1)
    inner = jnp.zeros((count, 1), jnp.float32)
    step = 2 * LANES
    for j in range(0, half, step):
        tiles = jnp.concatenate(
            [
                jnp.concatenate([d[j + k : j + k + LANES, :] for _, d in blocks], 0)
                for k in range(0, step, LANES)
            ],
            1,
        )
        ups = jnp.concatenate([u[j : j + step, :] for u, _ in blocks], 1)
        out = dot(active, tiles, ((1,), (0,)))
        inner += jnp.sum(
            out * rows[:, half + j : half + j + step].astype(jnp.float32), 1, keepdims=True
        )
        result[:, j : j + step] = (gate * out).astype(result.dtype)
        result[:, half + j : half + j + step] = dot(grad_pre, ups, ((1,), (1,))).astype(
            result.dtype
        )
    inner = jnp.where(gate > 0, inner, 0.0)
    result[:, 2 * half :] = jnp.where(mine, inner, 0.0).astype(result.dtype)


def call(kernel, shapes, scalars, *operands, hbm=0, scratch=(), dtype=jnp.bfloat16):
    small, near, far = (
        pl.BlockSpec(memory_space=space) for space in (pltpu.SMEM, pltpu.VMEM, pltpu.HBM)
    )
    count = len(operands) - hbm
    held = [pltpu.with_memory_space_constraint(v, pltpu.HBM) for v in operands[count:]]
    return pl.pallas_call(
        kernel,
        out_shape=[jax.ShapeDtypeStruct(shape, dtype) for shape in shapes],
        in_specs=[small] * len(scalars) + [near] * count + [far] * hbm,
        out_specs=[near] * len(shapes),
        scratch_shapes=scratch,
        compiler_params=pltpu.CompilerParams(vmem_limit_bytes=24 * 2**20),
    )(*scalars, *operands[:count], *held)


def per_device(tokens, cotangent, groups, choices, gates, up_weight, down_weight):
    f32, bf16 = jnp.float32, jnp.bfloat16
    tok_count, width = tokens.shape
    nodes = lax.axis_size("node")
    experts = lax.axis_size("expert")
    couples = lax.axis_size("pair")
    sides = lax.axis_size("side")
    group = ("expert", "pair", "side")
    hidden = up_weight.shape[1]
    pairs = 2 * tok_count
    half = width // sides
    expert = lax.axis_index("expert")
    side = lax.axis_index("side")
    lane = jnp.arange(LANES, dtype=jnp.int32)

    slot_rows = 2 * width // LANES
    groups, choices = groups.T, choices.transpose(1, 2, 0)
    tables = [pltpu.SMEM(v.shape, jnp.int32) for v in (groups, choices)]
    wide_rows = pltpu.VMEM((tok_count, slot_rows, LANES), f32)
    (sent,) = call(
        send_kernel,
        [(nodes, slot_rows + 8, LANES)],
        (),
        gates.transpose(1, 2, 0),
        groups,
        choices,
        tokens,
        cotangent,
        hbm=4,
        scratch=[
            *tables,
            pltpu.VMEM((2,) + tokens.shape, bf16),
            wide_rows,
            pltpu.SemaphoreType.DMA((4,)),
        ],
    )

    swap = [(0, 1), (1, 0)]
    here, give_up, give_down = call(
        pack_kernel,
        [(2 * half, hidden), (half, hidden), (half, hidden)],
        (jnp.stack([side, 1 - side]).astype(jnp.int32),),
        up_weight,
        down_weight,
        hbm=2,
        scratch=[pltpu.SemaphoreType.DMA((sides * (half // LANES + 1),))],
    )
    up = lax.ppermute(give_up, "side", swap)
    here_too = lax.ppermute(here, "core", swap)
    recv = lax.all_to_all(sent, "node", split_axis=0, concat_axis=0, tiled=True)
    recv, up, here_too = lax.optimization_barrier((recv, up, here_too))
    down = lax.ppermute(give_down, "side", swap)
    up_too = lax.ppermute(up, "core", swap)

    used = jnp.any(recv[:, 2 * width // LANES, :] > 0, 1)
    rank = jnp.cumsum(used.astype(jnp.int32)) - 1
    slot = jnp.arange(pairs, dtype=jnp.int32)
    pick = ((rank[None, :] == slot[:, None]) & used[None, :]).astype(bf16)
    mine = dot(pick, recv.reshape(nodes, -1), ((1,), (0,))).astype(bf16)
    parts = jnp.stack(
        [
            jnp.concatenate(
                [
                    mine[:, m * half : (m + 1) * half],
                    mine[:, width + m * half : width + (m + 1) * half],
                    mine[:, 2 * width : 2 * width + LANES],
                ],
                1,
            )
            for m in range(sides)
        ]
    )
    spread = jnp.broadcast_to(parts[None], (experts * couples,) + parts.shape).reshape(
        experts * couples * sides, pairs, -1
    )
    rows = lax.all_to_all(spread, group, split_axis=0, concat_axis=0, tiled=True)
    rows, down = lax.optimization_barrier((rows, down))
    down_too = lax.ppermute(down, "core", swap)
    rows = rows.reshape(experts * couples * sides * pairs, -1)
    gate = jnp.sum(
        jnp.where(lane[None, :] == expert, rows[:, 2 * half :].astype(f32), 0.0), 1, keepdims=True
    )

    units = CORES * hidden
    sums_shape = (rows.shape[0], 2 * units)
    (outgoing,) = call(partner_kernel, [sums_shape], (), rows, up, up_too, down, down_too)
    incoming = lax.ppermute(outgoing, "side", swap)
    (both,) = call(own_kernel, [sums_shape], (), rows, here, here_too, dtype=f32)
    both = both + incoming.astype(f32)
    pre = both[:, :units]
    back = both[:, units:]
    sig = jax.nn.sigmoid(pre)
    active = (pre * sig).astype(bf16)
    grad_pre = (gate * back * sig * (1.0 + pre * (1.0 - sig))).astype(bf16)
    own = jnp.concatenate([active, grad_pre], 1)
    partner = lax.ppermute(own, "side", swap)

    (result,) = call(
        output_kernel,
        [rows.shape],
        (expert.astype(jnp.int32).reshape(1),),
        rows,
        own,
        partner,
        here,
        here_too,
        up,
        up_too,
        down,
        down_too,
    )

    parts_back = lax.all_to_all(
        result.reshape(experts * couples * sides, pairs, -1),
        group,
        split_axis=0,
        concat_axis=0,
        tiled=True,
    ).reshape(experts * couples, sides, pairs, -1)
    summed = jnp.sum(parts_back.astype(f32), 0)
    inner_all = jnp.sum(summed[:, :, 2 * half :], 0)
    full = jnp.concatenate(
        [summed[m, :, :half] for m in range(sides)]
        + [summed[m, :, half : 2 * half] for m in range(sides)]
        + [inner_all],
        1,
    ).astype(bf16)
    expanded = dot(pick, full, ((0,), (0,))).astype(bf16)
    expanded = jnp.pad(expanded, ((0, 0), (0, 7 * LANES))).reshape(nodes, -1, LANES)
    home = lax.all_to_all(expanded, "node", split_axis=0, concat_axis=0, tiled=True)

    mixed, grad_tokens, grad_gates = call(
        home_kernel,
        [tokens.shape, tokens.shape, choices.shape],
        (),
        home,
        groups,
        choices,
        hbm=2,
        scratch=[*tables, wide_rows, pltpu.SemaphoreType.DMA((2,))],
    )
    return mixed, grad_tokens, grad_gates.transpose(2, 0, 1)


def solution(mesh):
    nodes, members = mesh.devices.shape
    axes = ("node", "expert", "pair", "side", "core")
    couples = members // (EXPERTS * SIDES * CORES)
    fine = Mesh(mesh.devices.reshape(nodes, EXPERTS, couples, SIDES, CORES), axes)
    placed = (
        P(axes, None),
        P(axes, None),
        P(axes, None),
        P(axes, None, None),
        P(axes, None, None),
        P(None, axes),
        P(axes, None),
    )
    return jax.shard_map(
        per_device,
        mesh=fine,
        in_specs=placed,
        out_specs=(P(axes, None), P(axes, None), P(axes, None, None)),
        check_vma=False,
    )
```

time: 191 us -> 202 us (1.058)
  waiting for transfers between devices: 40.5 us -> 69.8 us
  starting transfers between devices: 57.6 us -> 40.2 us
  Pallas kernels: 16.9 us -> 13.9 us
  blocking collectives: 66.5 us -> 68.6 us
    ppermute x10 -> x6, waiting for transfers between devices: 30.6 us -> 69.8 us  [the longest x1 38.1 us: per_device(): down = lax.ppermute(give_down, 'side', swap)]
    all_to_all x1, blocking collectives: 18.2 us -> 31.7 us  [per_device(): lax.all_to_all(result.reshape(experts * couples * sides, pairs, -1), grou...]
    all_gather x1 -> x0, blocking collectives: 13.3 us -> none  [per_device(): lax.all_gather(jnp.concatenate([active, grad_pre], 1), 'chip', axis=0)]
    ppermute x10 -> x6, starting transfers between devices: 29.8 us -> 16.5 us  [the longest x1 3.82 us: per_device(): down = lax.ppermute(give_down, 'side', swap)]
    all_to_all x2 -> x1, waiting for transfers between devices: 9.87 us -> 0.01 us  [per_device(): lax.all_to_all(spread, group, split_axis=0, concat_axis=0, tiled=True)]
    all_to_all x2 -> x1, starting transfers between devices: 11.1 us -> 7.03 us  [per_device(): lax.all_to_all(spread, group, split_axis=0, concat_axis=0, tiled=True)]
    pallas_call x6, Pallas kernels: 16.9 us -> 13.9 us  [call(): pl.pallas_call(kernel, out_shape=[jax.ShapeDtypeStruct(shape, dtype) for...]
    unnamed x22 -> x18, local copies, waits for them, and re-layouts: 3.72 us -> 4.22 us
  transfers between devices with their start and end apart: 14 -> 9, of which waited for: 4 -> 5; matrix products, arithmetic and copies ran while one was open for 0% -> 0% of each run, Pallas kernels for 4% -> 2%
where the time goes in v7:
time: 202 us; the launch traced here: 201 us
  waiting for transfers between devices  69.8 us (35%)
  blocking collectives  68.6 us (34%)
  starting transfers between devices  40.2 us (20%)
  Pallas kernels  13.9 us (7%)
  local copies, waits for them, and re-layouts  5.72 us (3%)
    ppermute x1, waiting for transfers between devices, per_device(): down = lax.ppermute(give_down, 'side', swap)  38.1 us
    all_to_all x1, blocking collectives, per_device(): lax.all_to_all(expanded, 'node', split_axis=0, concat_axis=0, tiled=True)  36.9 us
    all_to_all x1, blocking collectives, per_device(): lax.all_to_all(result.reshape(experts * couples * sides, pairs, -1), grou...  31.7 us
    ppermute x1, waiting for transfers between devices, per_device(): up = lax.ppermute(give_up, 'side', swap)  21.2 us
    all_to_all x1, starting transfers between devices, per_device(): recv = lax.all_to_all(sent, 'node', split_axis=0, concat_axis=0, tiled=True)  14.8 us
    pallas_call x6, Pallas kernels, call(): pl.pallas_call(kernel, out_shape=[jax.ShapeDtypeStruct(shape, dtype) for...  13.9 us
    all_to_all x1, starting transfers between devices, per_device(): lax.all_to_all(spread, group, split_axis=0, concat_axis=0, tiled=True)  7.03 us
    unnamed x18, local copies, waits for them, and re-layouts  4.22 us
  transfers between devices with their start and end apart: 9, of which 5 were waited for; matrix products, arithmetic and copies ran while one was open for 0% of the time, Pallas kernels for 2%

profile of v7, /device:TPU:64, one launch (start us, length us, event | category | flops | bytes accessed | tf_op | source)
XLA Modules:
  0.0 201.0 jit_solution(4191836716364504249)
XLA Ops:
  0.6 0.0 copy-start.4
  0.6 0.7 copy-done.4
  1.3 1.8 shard_map.94
  3.2 14.8 %all-to-all-start = ((bf16[16,120,128]{2,1,0:T(8,128)(2,1)}), bf16[16,120,128]{2,1,0:T(8,128)(2,1)S(1)}, u32[]{:S(2)}, u32[]{:S(2)}) async-start(bf16[16,120,128]{2,1,0:T(8,128)(2,1)} %shard_map.94), calls=%async_computation | async-start | bytes 983040 | tf_op jit(solution)/shard_map/all_to_all | solution.py:238
  17.9 0.1 pad_add_fusion.sides
  18.0 3.0 %shard_map.95 = (bf16[7168,128]{1,0:T(8,128)(2,1)S(1)}, bf16[3584,128]{1,0:T(8,128)(2,1)S(1)}, bf16[3584,128]{1,0:T(8,128)(2,1)S(1)}) custom-call(s32[2]{0:T(128)S(1)} %pad_add_fusion.sides, bf16[7168,128]{1,0:T(8,128)(2,1)} %up.1, bf16[128,7168]{1,0:T(8,128)(2,1)} %down.1), custom_call_target="tpu_custom_call" | custom-call | tf_op jit(solution)/shard_map/pallas_call | solution.py:179
  21.0 0.0 copy-start.5
  21.0 0.9 copy-done.5
  22.0 1.9 collective-permute-start.1
  23.9 0.0 copy-start
  23.9 1.2 copy-done
  25.1 3.4 %collective-permute-start = (bf16[3584,128]{1,0:T(8,128)(2,1)S(1)}, bf16[3584,128]{1,0:T(8,128)(2,1)S(1)}, u32[]{:S(2)}, u32[]{:S(2)}) collective-permute-start(bf16[3584,128]{1,0:T(8,128)(2,1)S(1)} %get-tuple-element.14), channel_id=1, source_target_pairs={{0,2},{2,0},{1,3},{3,1},{4,6},{6,4},{5,7},{7,5},{8,10},{10,8},{9,1... | collective-permute-start | bytes 2752520 | tf_op jit(solution)/shard_map/ppermute | solution.py:236
  28.5 21.2 %collective-permute-done.up = bf16[3584,128]{1,0:T(8,128)(2,1)S(1)} collective-permute-done((bf16[3584,128]{1,0:T(8,128)(2,1)S(1)}, bf16[3584,128]{1,0:T(8,128)(2,1)S(1)}, u32[]{:S(2)}, u32[]{:S(2)}) %collective-permute-start) | collective-permute-done | bytes 917536 | tf_op jit(solution)/shard_map/ppermute | solution.py:236
  49.7 0.0 collective-permute-done.1.here_too
  49.7 0.0 copy-start.2
  49.7 1.2 copy-done.2
  51.0 0.0 all-to-all-done
  51.0 0.4 compare_reduce_fusion
  51.4 0.1 copy.12
  51.5 0.1 add_reduce_fusion
  51.6 0.2 convolution_convert_fusion.1
  52.0 1.4 broadcast_in_dim.10
  53.3 7.0 %all-to-all-start.1 = ((bf16[16,8,7296]{2,1,0:T(8,128)(2,1)}), bf16[16,8,7296]{2,1,0:T(8,128)(2,1)S(1)}, u32[]{:S(2)}, u32[]{:S(2)}) async-start(bf16[16,8,7296]{2,1,0:T(8,128)(2,1)} %bitcast.48), calls=%async_computation.1 | async-start | bytes 3735552 | tf_op jit(solution)/shard_map/all_to_all | solution.py:264
  60.4 3.8 %collective-permute-start.2 = (bf16[3584,128]{1,0:T(8,128)(2,1)}, bf16[3584,128]{1,0:T(8,128)(2,1)}, u32[]{:S(2)}, u32[]{:S(2)}) collective-permute-start(bf16[3584,128]{1,0:T(8,128)(2,1)} %copy-done.5), channel_id=1, source_target_pairs={{0,2},{2,0},{1,3},{3,1},{4,6},{6,4},{5,7},{7,5},{8,10},{10,8},{9,1... | collective-permute-start | bytes 2752520 | tf_op jit(solution)/shard_map/ppermute | solution.py:240
  64.2 1.9 collective-permute-start.3
  66.1 38.1 %collective-permute-done.2.down = bf16[3584,128]{1,0:T(8,128)(2,1)} collective-permute-done((bf16[3584,128]{1,0:T(8,128)(2,1)}, bf16[3584,128]{1,0:T(8,128)(2,1)}, u32[]{:S(2)}, u32[]{:S(2)}) %collective-permute-start.2) | collective-permute-done | bytes 917536 | tf_op jit(solution)/shard_map/ppermute | solution.py:240
  104.2 0.0 all-to-all-done.1
  104.2 1.9 collective-permute-start.4
  106.2 0.0 collective-permute-done.3.up_too
  106.2 2.8 %collective-permute-done.4.down_too = bf16[3584,128]{1,0:T(8,128)(2,1)} collective-permute-done((bf16[3584,128]{1,0:T(8,128)(2,1)}, bf16[3584,128]{1,0:T(8,128)(2,1)}, u32[]{:S(2)}, u32[]{:S(2)}) %collective-permute-start.4) | collective-permute-done | bytes 917536 | tf_op jit(solution)/shard_map/ppermute | solution.py:266
  108.9 0.0 copy-start.1
  108.9 2.8 %shard_map.97 = bf16[128,512]{1,0:T(8,128)(2,1)S(1)} custom-call(bf16[128,7296]{1,0:T(8,128)(2,1)S(1)} %bitcast.42, bf16[3584,128]{1,0:T(8,128)(2,1)S(1)} %collective-permute-done.up, bf16[3584,128]{1,0:T(8,128)(2,1)} %collective-permute-done.3.up_too, bf16[3584,128]{1,0:T(8,128)(2,1)} %collective-permute-done.2.down, ...), custom_call_target="tpu_custom_call" | custom-call | tf_op jit(solution)/shard_map/pallas_call | solution.py:179
  111.8 2.7 %collective-permute-start.5 = (bf16[128,512]{1,0:T(8,128)(2,1)S(1)}, bf16[128,512]{1,0:T(8,128)(2,1)S(1)}, u32[]{:S(2)}, u32[]{:S(2)}) collective-permute-start(bf16[128,512]{1,0:T(8,128)(2,1)S(1)} %shard_map.97), channel_id=1, source_target_pairs={{0,2},{2,0},{1,3},{3,1},{4,6},{6,4},{5,7},{7,5},{8,10},{10,8},{9,1... | collective-permute-start | bytes 393224 | tf_op jit(solution)/shard_map/ppermute | solution.py:275
  114.5 0.0 copy-done.1
  114.6 0.0 copy-done.3
  114.6 1.0 shard_map.96
  115.5 0.1 select_reduce_fusion
  115.6 3.6 %collective-permute-done.5 = bf16[128,512]{1,0:T(8,128)(2,1)S(1)} collective-permute-done((bf16[128,512]{1,0:T(8,128)(2,1)S(1)}, bf16[128,512]{1,0:T(8,128)(2,1)S(1)}, u32[]{:S(2)}, u32[]{:S(2)}) %collective-permute-start.5) | collective-permute-done | bytes 131104 | tf_op jit(solution)/shard_map/ppermute | solution.py:275
  119.2 0.1 multiply_convert_fusion
  119.4 2.7 %collective-permute-start.6 = (bf16[128,512]{1,0:T(8,128)(2,1)S(1)}, bf16[128,512]{1,0:T(8,128)(2,1)S(1)}, u32[]{:S(2)}, u32[]{:S(2)}) collective-permute-start(bf16[128,512]{1,0:T(8,128)(2,1)S(1)} %pad_maximum_fusion.1.own), channel_id=1, source_target_pairs={{0,2},{2,0},{1,3},{3,1},{4,6},{6,4},{5,7},{7,5},{8,10},{10,8},{9,1... | collective-permute-start | bytes 393224 | tf_op jit(solution)/shard_map/ppermute | solution.py:284
  122.1 4.1 %collective-permute-done.6.partner = bf16[128,512]{1,0:T(8,128)(2,1)S(1)} collective-permute-done((bf16[128,512]{1,0:T(8,128)(2,1)S(1)}, bf16[128,512]{1,0:T(8,128)(2,1)S(1)}, u32[]{:S(2)}, u32[]{:S(2)}) %collective-permute-start.6) | collective-permute-done | bytes 131104 | tf_op jit(solution)/shard_map/ppermute | solution.py:284
  126.2 3.6 %shard_map.98 = bf16[128,7296]{1,0:T(8,128)(2,1)S(1)} custom-call(s32[1]{0:T(128)} %bitcast.6.scalars, bf16[128,7296]{1,0:T(8,128)(2,1)S(1)} %bitcast.45, bf16[128,512]{1,0:T(8,128)(2,1)S(1)} %pad_maximum_fusion.1.own, bf16[128,512]{1,0:T(8,128)(2,1)S(1)} %collective-permute-done.6.partner, bf16[7168,128]{1,0:T(8,128)(2,1)S(1)} %copy-done.1, ...), custom_call_target="tpu_custom_call" | custom-call | tf_op jit(solution)/shard_map/pallas_call | solution.py:179
  129.8 31.7 %all_to_all.20 = bf16[16,8,7296]{2,1,0:T(8,128)(2,1)S(1)} all-to-all(bf16[16,8,7296]{2,1,0:T(8,128)(2,1)S(1)} %bitcast.46), channel_id=1, replica_groups=mesh['node'=16,'expert'=4,'pair'=2,'side'=2,'core'=2] {'expert','pair','..., dimensions={0} | all-to-all | bytes 3735552 | tf_op jit(solution)/shard_map/all_to_all | solution.py:301
  161.5 0.3 convert_reduce_fusion
  161.9 0.3 convolution_convert_fusion
  162.3 0.1 copy.14
  162.4 36.9 %all_to_all.21.home = bf16[16,120,128]{2,1,0:T(8,128)(2,1)S(1)} all-to-all(bf16[16,120,128]{2,1,0:T(8,128)(2,1)S(1)} %bitcast.51), channel_id=1, replica_groups=mesh['node'=16,'expert'=4,'pair'=2,'side'=2,'core'=2] {'node'}, dimensions={0} | all-to-all | bytes 983040 | tf_op jit(solution)/shard_map/all_to_all | solution.py:318
  199.3 1.7 shard_map.99
  (19 shorter events, 0.3 us)
Async XLA Ops:
  0.6 0.7 copy-start.4
  3.2 47.8 %all-to-all-start = ((bf16[16,120,128]{2,1,0:T(8,128)(2,1)}), bf16[16,120,128]{2,1,0:T(8,128)(2,1)S(1)}, u32[]{:S(2)}, u32[]{:S(2)}) async-start(bf16[16,120,128]{2,1,0:T(8,128)(2,1)} %shard_map.94), calls=%async_computation | async-start | bytes 983040 | tf_op jit(solution)/shard_map/all_to_all | solution.py:238
  21.0 1.0 copy-start.5
  22.0 27.8 %collective-permute-start.1 = (bf16[7168,128]{1,0:T(8,128)(2,1)S(1)}, bf16[7168,128]{1,0:T(8,128)(2,1)S(1)}, u32[]{:S(2)}, u32[]{:S(2)}) collective-permute-start(bf16[7168,128]{1,0:T(8,128)(2,1)S(1)} %get-tuple-element.15.here), channel_id=1, source_target_pairs={{0,1},{1,0},{2,3},{3,2},{4,5},{5,4},{6,7},{7,6},{8,9},{9,8},{10,11... | collective-permute-start | bytes 5505032 | tf_op jit(solution)/shard_map/ppermute | solution.py:237
  23.9 1.2 copy-start
  25.1 24.6 %collective-permute-start = (bf16[3584,128]{1,0:T(8,128)(2,1)S(1)}, bf16[3584,128]{1,0:T(8,128)(2,1)S(1)}, u32[]{:S(2)}, u32[]{:S(2)}) collective-permute-start(bf16[3584,128]{1,0:T(8,128)(2,1)S(1)} %get-tuple-element.14), channel_id=1, source_target_pairs={{0,2},{2,0},{1,3},{3,1},{4,6},{6,4},{5,7},{7,5},{8,10},{10,8},{9,1... | collective-permute-start | bytes 2752520 | tf_op jit(solution)/shard_map/ppermute | solution.py:236
  49.7 1.3 copy-start.2
  53.3 50.9 %all-to-all-start.1 = ((bf16[16,8,7296]{2,1,0:T(8,128)(2,1)}), bf16[16,8,7296]{2,1,0:T(8,128)(2,1)S(1)}, u32[]{:S(2)}, u32[]{:S(2)}) async-start(bf16[16,8,7296]{2,1,0:T(8,128)(2,1)} %bitcast.48), calls=%async_computation.1 | async-start | bytes 3735552 | tf_op jit(solution)/shard_map/all_to_all | solution.py:264
  60.4 43.9 %collective-permute-start.2 = (bf16[3584,128]{1,0:T(8,128)(2,1)}, bf16[3584,128]{1,0:T(8,128)(2,1)}, u32[]{:S(2)}, u32[]{:S(2)}) collective-permute-start(bf16[3584,128]{1,0:T(8,128)(2,1)} %copy-done.5), channel_id=1, source_target_pairs={{0,2},{2,0},{1,3},{3,1},{4,6},{6,4},{5,7},{7,5},{8,10},{10,8},{9,1... | collective-permute-start | bytes 2752520 | tf_op jit(solution)/shard_map/ppermute | solution.py:240
  64.2 42.0 %collective-permute-start.3 = (bf16[3584,128]{1,0:T(8,128)(2,1)S(1)}, bf16[3584,128]{1,0:T(8,128)(2,1)}, u32[]{:S(2)}, u32[]{:S(2)}) collective-permute-start(bf16[3584,128]{1,0:T(8,128)(2,1)S(1)} %collective-permute-done.up), channel_id=1, source_target_pairs={{0,1},{1,0},{2,3},{3,2},{4,5},{5,4},{6,7},{7,6},{8,9},{9,8},{10,11... | collective-permute-start | bytes 2752520 | tf_op jit(solution)/shard_map/ppermute | solution.py:241
  104.2 4.7 %collective-permute-start.4 = (bf16[3584,128]{1,0:T(8,128)(2,1)}, bf16[3584,128]{1,0:T(8,128)(2,1)}, u32[]{:S(2)}, u32[]{:S(2)}) collective-permute-start(bf16[3584,128]{1,0:T(8,128)(2,1)} %collective-permute-done.2.down), channel_id=1, source_target_pairs={{0,1},{1,0},{2,3},{3,2},{4,5},{5,4},{6,7},{7,6},{8,9},{9,8},{10,11... | collective-permute-start | bytes 2752520 | tf_op jit(solution)/shard_map/ppermute | solution.py:266
  108.9 5.6 %copy-start.1 = (bf16[7168,128]{1,0:T(8,128)(2,1)S(1)}, bf16[7168,128]{1,0:T(8,128)(2,1)}, u32[]{:S(2)}) copy-start(bf16[7168,128]{1,0:T(8,128)(2,1)} %copy-done) | copy-start | bytes 5505028
  108.9 5.6 %copy-start.3 = (bf16[7168,128]{1,0:T(8,128)(2,1)S(1)}, bf16[7168,128]{1,0:T(8,128)(2,1)}, u32[]{:S(2)}) copy-start(bf16[7168,128]{1,0:T(8,128)(2,1)} %copy-done.2) | copy-start | bytes 5505028
  111.8 7.4 %collective-permute-start.5 = (bf16[128,512]{1,0:T(8,128)(2,1)S(1)}, bf16[128,512]{1,0:T(8,128)(2,1)S(1)}, u32[]{:S(2)}, u32[]{:S(2)}) collective-permute-start(bf16[128,512]{1,0:T(8,128)(2,1)S(1)} %shard_map.97), channel_id=1, source_target_pairs={{0,2},{2,0},{1,3},{3,1},{4,6},{6,4},{5,7},{7,5},{8,10},{10,8},{9,1... | collective-permute-start | bytes 393224 | tf_op jit(solution)/shard_map/ppermute | solution.py:275
  119.4 6.9 %collective-permute-start.6 = (bf16[128,512]{1,0:T(8,128)(2,1)S(1)}, bf16[128,512]{1,0:T(8,128)(2,1)S(1)}, u32[]{:S(2)}, u32[]{:S(2)}) collective-permute-start(bf16[128,512]{1,0:T(8,128)(2,1)S(1)} %pad_maximum_fusion.1.own), channel_id=1, source_target_pairs={{0,2},{2,0},{1,3},{3,1},{4,6},{6,4},{5,7},{7,5},{8,10},{10,8},{9,1... | collective-permute-start | bytes 393224 | tf_op jit(solution)/shard_map/ppermute | solution.py:284

commit v8 on v5

--- a/solution.py
+++ b/solution.py
@@ -14,16 +14,30 @@
     return lax.dot_general(a, b, (dims, ((), ())), preferred_element_type=jnp.float32)
 
 
-def send_kernel(groups, choices, gates, tokens, cotangent, out, narrow, wide, sems):
+def small_copies(pairs, sems):
+    copies = [pltpu.make_async_copy(a, b, sems.at[i]) for i, (a, b) in enumerate(pairs)]
+    for copy in copies:
+        copy.start()
+    return copies
+
+
+def send_kernel(
+    gates, groups_at, choices_at, tokens, cotangent, out, groups, choices, narrow, wide, sems
+):
     count, width = tokens.shape
     chunks = width // LANES
-    copies = [
-        pltpu.make_async_copy(ref, narrow.at[i], sems.at[i])
-        for i, ref in enumerate((tokens, cotangent))
-    ]
-    for copy in copies:
-        copy.start()
+    first, second, *copies = small_copies(
+        [
+            (groups_at, groups),
+            (choices_at, choices),
+            (tokens, narrow.at[0]),
+            (cotangent, narrow.at[1]),
+        ],
+        sems,
+    )
     out[...] = jnp.zeros_like(out)
+    first.wait()
+    second.wait()
     every_gate = gates[...].astype(jnp.float32)
     row = lax.broadcasted_iota(jnp.int32, (8, LANES), 0)
     lane = lax.broadcasted_iota(jnp.int32, (8, LANES), 1)
@@ -47,13 +61,17 @@
             out[groups[c, t], : 2 * chunks, :] = rows
 
 
-def home_kernel(groups, choices, home, mixed, grad_tokens, grad_gates, wide):
+def home_kernel(
+    home, groups_at, choices_at, mixed, grad_tokens, grad_gates, groups, choices, wide, sems
+):
     count, width = mixed.shape
     chunks = width // LANES
     row = lax.broadcasted_iota(jnp.int32, (8, LANES), 0)
     lane = lax.broadcasted_iota(jnp.int32, (8, LANES), 1)
     i, j = (lax.broadcasted_iota(jnp.int32, (2, count), d) for d in range(2))
     inner = [jnp.zeros((2, count), jnp.float32) for c in range(2)]
+    for copy in small_copies([(groups_at, groups), (choices_at, choices)], sems):
+        copy.wait()
     for t in range(count):
         total = jnp.zeros((2 * chunks, LANES), jnp.float32)
         for c in range(2):
@@ -108,16 +126,33 @@
         copy.wait()
 
 
-def pieces(refs, wide):
-    whole = [(ref.at[pl.ds(0, wide)], ref.at[pl.ds(wide, wide)]) for ref in refs[:-4]]
-    return whole + [(refs[-4], refs[-2]), (refs[-3], refs[-1])]
+def merge_kernel(ahead, behind, far_up, far_down, out, sems):
+    at = 0
+    copies = []
+    for ref in (ahead, behind, far_up, far_down):
+        copies.append((ref, out.at[pl.ds(at, ref.shape[0])]))
+        at += ref.shape[0]
+    for copy in small_copies(copies, sems):
+        copy.wait()
+
+
+def pieces(refs):
+    here, here_too, ahead, behind, far_up, far_down, merged = refs
+    wide = far_up.shape[0]
+    found = []
+    for i, own in enumerate((here, ahead, behind, None)):
+        other, start = (merged, 2 * (i - 1) * wide) if i else (here_too, 0)
+        found += [
+            (own.at[pl.ds(0, wide)], own.at[pl.ds(wide, wide)]) if own is not None else (far_up, far_down),
+            (other.at[pl.ds(start, wide)], other.at[pl.ds(start + wide, wide)]),
+        ]
+    return found
 
 
 def partial_kernel(scalars, rows, *refs):
-    out = refs[-1]
+    blocks, out = pieces(refs[:-1]), refs[-1]
     hidden = refs[0].shape[1]
     wide = (rows.shape[1] - LANES) // 2
-    blocks = pieces(refs[:-1], wide)
     x, dy = rows[:, :wide], rows[:, wide : 2 * wide]
     for i in range(len(blocks) // CORES):
         pair = blocks[CORES * i : CORES * (i + 1)]
@@ -138,7 +173,7 @@
     result = refs[-1]
     hidden = refs[0].shape[1]
     wide = (rows.shape[1] - LANES) // 2
-    blocks = pieces(refs[:-1], wide)
+    blocks = pieces(refs[:-1])
     chips = len(blocks) // CORES
     count = rows.shape[0]
     lane = lax.broadcasted_iota(jnp.int32, (count, LANES), 1)
@@ -176,20 +211,19 @@
 
 
 def call(kernel, shapes, scalars, *operands, hbm=0, scratch=()):
-    spec = pl.BlockSpec(memory_space=pltpu.VMEM)
-    far = pl.BlockSpec(memory_space=pltpu.HBM)
-    scalars = scalars if isinstance(scalars, tuple) else (scalars,)
-    out = [jax.ShapeDtypeStruct(shape, jnp.bfloat16) for shape in shapes]
+    small, near, far = (
+        pl.BlockSpec(memory_space=space) for space in (pltpu.SMEM, pltpu.VMEM, pltpu.HBM)
+    )
+    count = len(operands) - hbm
+    held = [pltpu.with_memory_space_constraint(v, pltpu.HBM) for v in operands[count:]]
     return pl.pallas_call(
         kernel,
-        out_shape=out,
-        in_specs=[pl.BlockSpec(memory_space=pltpu.SMEM)] * len(scalars)
-        + [spec] * (len(operands) - hbm)
-        + [far] * hbm,
-        out_specs=[spec] * len(out),
+        out_shape=[jax.ShapeDtypeStruct(shape, jnp.bfloat16) for shape in shapes],
+        in_specs=[small] * len(scalars) + [near] * count + [far] * hbm,
+        out_specs=[near] * len(shapes),
         scratch_shapes=scratch,
-        compiler_params=pltpu.CompilerParams(vmem_limit_bytes=40 * 2**20),
-    )(*scalars, *operands)
+        compiler_params=pltpu.CompilerParams(vmem_limit_bytes=24 * 2**20),
+    )(*scalars, *operands[:count], *held)
 
 
 def per_device(tokens, cotangent, groups, choices, gates, up_weight, down_weight):
@@ -207,19 +241,23 @@
 
     slot_rows = 2 * width // LANES
     groups, choices = groups.T, choices.transpose(1, 2, 0)
+    tables = [pltpu.SMEM(v.shape, jnp.int32) for v in (groups, choices)]
     wide_rows = pltpu.VMEM((tok_count, slot_rows, LANES), f32)
     (sent,) = call(
         send_kernel,
         [(nodes, slot_rows + 8, LANES)],
-        (groups, choices),
+        (),
         gates.transpose(1, 2, 0),
+        groups,
+        choices,
         tokens,
         cotangent,
-        hbm=2,
+        hbm=4,
         scratch=[
+            *tables,
             pltpu.VMEM((2,) + tokens.shape, bf16),
             wide_rows,
-            pltpu.SemaphoreType.DMA((2,)),
+            pltpu.SemaphoreType.DMA((4,)),
         ],
     )
 
@@ -229,7 +267,7 @@
     here, ahead, behind, far_up, far_down = call(
         pack_kernel,
         [(2 * wide, hidden)] * 3 + [(wide, hidden)] * 2,
-        targets,
+        (targets,),
         up_weight,
         down_weight,
         hbm=2,
@@ -242,14 +280,23 @@
     behind = lax.ppermute(behind, "chip", behind_of)
     here_too = lax.ppermute(here, "core", swap)
     recv = lax.all_to_all(sent, "node", split_axis=0, concat_axis=0, tiled=True)
+    far_up = lax.ppermute(far_up, "chip", ahead_of)
+    far_down = lax.ppermute(far_down, "chip", behind_of)
     recv, here_too, ahead, behind, far_up, far_down = lax.optimization_barrier(
         (recv, here_too, ahead, behind, far_up, far_down)
     )
-    far_up = lax.ppermute(far_up, "chip", ahead_of)
-    far_down = lax.ppermute(far_down, "chip", behind_of)
-    blocks = [here, here_too]
-    for block in (ahead, behind, far_up, far_down):
-        blocks += [block, lax.ppermute(block, "core", swap)]
+    (merged,) = call(
+        merge_kernel,
+        [(2 * (chips - 1) * wide, hidden)],
+        (),
+        ahead,
+        behind,
+        far_up,
+        far_down,
+        scratch=[pltpu.SemaphoreType.DMA((4,))],
+    )
+    merged = lax.ppermute(merged, "core", swap)
+    blocks = (here, here_too, ahead, behind, far_up, far_down, merged)
     scalars = jnp.stack(
         [expert, chip, (chip + chips - 1) % chips, (chip + 1) % chips, (chip + 2) % chips]
     ).astype(jnp.int32)
@@ -284,7 +331,7 @@
 
     units = CORES * hidden
     (outgoing,) = call(
-        partial_kernel, [(chips, rows.shape[0], 2 * units)], scalars, rows, *blocks
+        partial_kernel, [(chips, rows.shape[0], 2 * units)], (scalars,), rows, *blocks
     )
     incoming = lax.all_to_all(outgoing, "chip", split_axis=0, concat_axis=0, tiled=True)
     both = jnp.sum(incoming.astype(f32), 0)
@@ -295,7 +342,7 @@
     grad_pre = (gate * back * sig * (1.0 + pre * (1.0 - sig))).astype(bf16)
     every = lax.all_gather(jnp.concatenate([active, grad_pre], 1), "chip", axis=0)
 
-    (result,) = call(output_kernel, [rows.shape], scalars, rows, every, *blocks)
+    (result,) = call(output_kernel, [rows.shape], (scalars,), rows, every, *blocks)
 
     parts_back = lax.all_to_all(
         result.reshape(experts * chips, pairs, -1),
@@ -319,9 +366,12 @@
     mixed, grad_tokens, grad_gates = call(
         home_kernel,
         [tokens.shape, tokens.shape, choices.shape],
-        (groups, choices),
+        (),
         home,
-        scratch=[wide_rows],
+        groups,
+        choices,
+        hbm=2,
+        scratch=[*tables, wide_rows, pltpu.SemaphoreType.DMA((2,))],
     )
     return mixed, grad_tokens, grad_gates.transpose(2, 0, 1)
 

time: 188 us -> 202 us (1.074)
  the two profiles are of different devices: /device:TPU:32 before, /device:TPU:64 now
where the time goes in v8:
time: 202 us; the launch traced here: 201 us
  blocking collectives  62.5 us (31%)
  starting transfers between devices  51.6 us (26%)
  waiting for transfers between devices  48 us (24%)
  local copies, waits for them, and re-layouts  17.3 us (9%)
  Pallas kernels  15.2 us (8%)
  other arithmetic  3.85 us (2%)
    all_to_all x1, blocking collectives, per_device(): lax.all_to_all(expanded, 'node', split_axis=0, concat_axis=0, tiled=True)  34.1 us
    ppermute x2, waiting for transfers between devices, per_device(): far_up = lax.ppermute(far_up, 'chip', ahead_of)  21.5 us
    all_to_all x1, waiting for transfers between devices, per_device(): lax.all_to_all(spread, ('expert', 'chip'), split_axis=0, concat_axis=0, t...  17.1 us
    unnamed x46, local copies, waits for them, and re-layouts  16.1 us
    all_to_all x1, blocking collectives, per_device(): lax.all_to_all(result.reshape(experts * chips, pairs, -1), ('expert', 'ch...  15.6 us
    pallas_call x6, Pallas kernels, call(): pl.pallas_call(kernel, out_shape=[jax.ShapeDtypeStruct(shape, jnp.bfloat1...  15.2 us
    all_to_all x1, starting transfers between devices, per_device(): recv = lax.all_to_all(sent, 'node', split_axis=0, concat_axis=0, tiled=True)  14.8 us
    all_gather x1, blocking collectives, per_device(): lax.all_gather(jnp.concatenate([active, grad_pre], 1), 'chip', axis=0)  12.8 us
  transfers between devices with their start and end apart: 11, of which 4 were waited for; matrix products, arithmetic and copies ran while one was open for 2% of the time, Pallas kernels for 2%

profile of v8, /device:TPU:64, one launch (start us, length us, event | category | flops | bytes accessed | tf_op | source)
XLA Modules:
  0.0 201.0 jit_solution(11145431868749778950)
XLA Ops:
  0.6 0.7 copy-done.16
  1.3 1.8 shard_map.94
  3.1 14.8 %all-to-all-start = ((bf16[16,120,128]{2,1,0:T(8,128)(2,1)}), bf16[16,120,128]{2,1,0:T(8,128)(2,1)S(1)}, u32[]{:S(2)}, u32[]{:S(2)}) async-start(bf16[16,120,128]{2,1,0:T(8,128)(2,1)} %shard_map.94), calls=%async_computation | async-start | bytes 983040 | tf_op jit(solution)/shard_map/all_to_all | solution.py:282
  18.0 3.1 %shard_map.95 = (bf16[3584,128]{1,0:T(8,128)(2,1)S(1)}, bf16[3584,128]{1,0:T(8,128)(2,1)S(1)}, bf16[3584,128]{1,0:T(8,128)(2,1)S(1)}, bf16[1792,128]{1,0:T(8,128)(2,1)S(1)}, bf16[1792,128]{1,0:T(8,128)(2,1)S(1)}) custom-call(s32[4]{0:T(128)S(1)} %pad_add_fusion.chips, bf16[7168,128]{1,0:T(8,128)(2,1)} %up.1, bf16[128,7168]{1,0:T(8,128)(2,1)} %down.1), custom_call_target="tpu_custom_call" | custom-call | tf_op jit(solution)/shard_map/pallas_call | solution.py:219
  21.0 3.4 %collective-permute-start.3 = (bf16[1792,128]{1,0:T(8,128)(2,1)S(1)}, bf16[1792,128]{1,0:T(8,128)(2,1)S(1)}, u32[]{:S(2)}, u32[]{:S(2)}) collective-permute-start(bf16[1792,128]{1,0:T(8,128)(2,1)S(1)} %get-tuple-element.20), channel_id=1, source_target_pairs={{0,2},{2,4},{4,6},{6,0},{1,3},{3,5},{5,7},{7,1},{8,10},{10,12},{12... | collective-permute-start | bytes 1376264 | tf_op jit(solution)/shard_map/ppermute | solution.py:277
  24.5 3.6 %collective-permute-start.5 = (bf16[1792,128]{1,0:T(8,128)(2,1)S(1)}, bf16[1792,128]{1,0:T(8,128)(2,1)S(1)}, u32[]{:S(2)}, u32[]{:S(2)}) collective-permute-start(bf16[1792,128]{1,0:T(8,128)(2,1)S(1)} %get-tuple-element.21), channel_id=1, source_target_pairs={{0,6},{2,0},{4,2},{6,4},{1,7},{3,1},{5,3},{7,5},{8,14},{10,8},{12,... | collective-permute-start | bytes 1376264 | tf_op jit(solution)/shard_map/ppermute | solution.py:278
  28.1 1.9 collective-permute-start
  30.1 1.0 copy-done.9
  31.0 2.2 %collective-permute-start.1 = (bf16[3584,128]{1,0:T(8,128)(2,1)S(1)}, bf16[3584,128]{1,0:T(8,128)(2,1)S(1)}, u32[]{:S(2)}, u32[]{:S(2)}) collective-permute-start(bf16[3584,128]{1,0:T(8,128)(2,1)S(1)} %get-tuple-element.18), channel_id=1, source_target_pairs={{0,2},{2,4},{4,6},{6,0},{1,3},{3,5},{5,7},{7,1},{8,10},{10,12},{12... | collective-permute-start | bytes 2752520 | tf_op jit(solution)/shard_map/ppermute | solution.py:279
  33.2 4.9 %collective-permute-start.2 = (bf16[3584,128]{1,0:T(8,128)(2,1)S(1)}, bf16[3584,128]{1,0:T(8,128)(2,1)S(1)}, u32[]{:S(2)}, u32[]{:S(2)}) collective-permute-start(bf16[3584,128]{1,0:T(8,128)(2,1)S(1)} %get-tuple-element.19), channel_id=1, source_target_pairs={{0,6},{2,0},{4,2},{6,4},{1,7},{3,1},{5,3},{7,5},{8,14},{10,8},{12,... | collective-permute-start | bytes 2752520 | tf_op jit(solution)/shard_map/ppermute | solution.py:280
  38.1 1.9 collective-permute-start.4
  40.0 5.1 %collective-permute-start.6 = (bf16[1792,128]{1,0:T(8,128)(2,1)S(1)}, bf16[1792,128]{1,0:T(8,128)(2,1)S(1)}, u32[]{:S(2)}, u32[]{:S(2)}) collective-permute-start(bf16[1792,128]{1,0:T(8,128)(2,1)S(1)} %collective-permute-done.5), channel_id=1, source_target_pairs={{0,6},{2,0},{4,2},{6,4},{1,7},{3,1},{5,3},{7,5},{8,14},{10,8},{12,... | collective-permute-start | bytes 1376264 | tf_op jit(solution)/shard_map/ppermute | solution.py:284
  45.2 21.5 %collective-permute-done.4.far_up.refs_4_ = bf16[1792,128]{1,0:T(8,128)(2,1)S(1)} collective-permute-done((bf16[1792,128]{1,0:T(8,128)(2,1)S(1)}, bf16[1792,128]{1,0:T(8,128)(2,1)S(1)}, u32[]{:S(2)}, u32[]{:S(2)}) %collective-permute-start.4) | collective-permute-done | bytes 458784 | tf_op jit(solution)/shard_map/ppermute | solution.py:283
  66.7 1.2 collective-permute-done.6.far_down.refs_5_
  67.9 0.9 copy-done.12
  68.8 0.8 copy-done.17
  69.6 2.6 %shard_map.96 = bf16[10752,128]{1,0:T(8,128)(2,1)} custom-call(bf16[3584,128]{1,0:T(8,128)(2,1)S(1)} %collective-permute-done.1.ahead.refs_2_, bf16[3584,128]{1,0:T(8,128)(2,1)S(1)} %collective-permute-done.2.behind.refs_3_, bf16[1792,128]{1,0:T(8,128)(2,1)S(1)} %collective-permute-done.4.far_up.refs_4_, ...), custom_call_target="tpu_custom_call" | custom-call | tf_op jit(solution)/shard_map/pallas_call | solution.py:219
  72.2 0.9 copy-done
  73.1 1.0 copy-done.3
  74.1 0.8 copy-done.6
  74.9 1.9 collective-permute-start.7
  76.8 1.1 compare_reduce_fusion
  78.1 0.1 add_reduce_fusion
  78.2 1.2 convolution_convert_fusion.1
  79.6 1.0 broadcast_in_dim.10
  80.6 7.7 %all-to-all-start.1 = ((bf16[16,8,3712]{2,1,0:T(8,128)(2,1)}), bf16[16,8,3712]{2,1,0:T(8,128)(2,1)}, u32[]{:S(2)}, u32[]{:S(2)}) async-start(bf16[16,8,3712]{2,1,0:T(8,128)(2,1)} %bitcast.69), calls=%async_computation.1 | async-start | bytes 1900544 | tf_op jit(solution)/shard_map/all_to_all | solution.py:325
  88.4 17.1 %all-to-all-done.1 = bf16[16,8,3712]{2,1,0:T(8,128)(2,1)} async-done(((bf16[16,8,3712]{2,1,0:T(8,128)(2,1)}), bf16[16,8,3712]{2,1,0:T(8,128)(2,1)}, u32[]{:S(2)}, u32[]{:S(2)}) %all-to-all-start.1) | async-done | bytes 950304 | tf_op jit(solution)/shard_map/all_to_all | solution.py:325
  105.5 1.2 copy-done.1
  106.7 1.2 copy-done.4
  107.9 1.0 copy-done.7
  108.9 1.2 copy-done.10
  110.1 1.2 copy-done.13
  111.2 3.0 %shard_map.97 = bf16[4,128,512]{2,1,0:T(8,128)(2,1)S(1)} custom-call(s32[5]{0:T(128)S(1)} %stack.49.scalars, bf16[128,3712]{1,0:T(8,128)(2,1)} %bitcast.15.rows, bf16[3584,128]{1,0:T(8,128)(2,1)S(1)} %copy-done.10, bf16[3584,128]{1,0:T(8,128)(2,1)S(1)} %copy-done.13, bf16[3584,128]{1,0:T(8,128)(2,1)S(1)} %copy-done.1, bf16[3584,128]{1,0:T(8,128)(2,1)S(1)} %copy-done.4, ...), custom_call_target="tpu_custom_call" | custom-call | tf_op jit(solution)/shard_map/pallas_call | solution.py:219
  114.2 0.8 copy-done.15
  115.0 4.2 %all-to-all-start.2 = ((bf16[4,128,512]{2,1,0:T(8,128)(2,1)}), bf16[4,128,512]{2,1,0:T(8,128)(2,1)}, u32[]{:S(2)}, u32[]{:S(2)}) async-start(bf16[4,128,512]{2,1,0:T(8,128)(2,1)} %copy-done.15), calls=%async_computation.2 | async-start | bytes 1048576 | tf_op jit(solution)/shard_map/all_to_all | solution.py:336
  119.2 0.9 select_reduce_fusion
  120.1 8.1 %all-to-all-done.2 = bf16[4,128,512]{2,1,0:T(8,128)(2,1)} async-done(((bf16[4,128,512]{2,1,0:T(8,128)(2,1)}), bf16[4,128,512]{2,1,0:T(8,128)(2,1)}, u32[]{:S(2)}, u32[]{:S(2)}) %all-to-all-start.2) | async-done | bytes 524320 | tf_op jit(solution)/shard_map/all_to_all | solution.py:336
  128.2 1.3 convert_reduce_fusion.1
  129.6 12.8 %all-gather = bf16[512,512]{1,0:T(8,128)(2,1)S(1)} all-gather(bf16[128,512]{1,0:T(8,128)(2,1)S(1)} %pad_maximum_fusion.1), channel_id=2, replica_groups=mesh['node'=16,'expert'=4,'chip'=4,'core'=2] {'chip'}, dimensions={0}, use_global_device_ids=true | all-gather | bytes 655360 | tf_op jit(solution)/shard_map/all_gather | solution.py:343
  142.4 1.0 copy-done.8
  143.4 1.2 copy-done.11
  144.6 1.2 copy-done.14
  145.8 3.0 %shard_map.98 = bf16[128,3712]{1,0:T(8,128)(2,1)S(1)} custom-call(s32[5]{0:T(128)S(1)} %stack.49.scalars, bf16[128,3712]{1,0:T(8,128)(2,1)} %bitcast.15.rows, bf16[4,128,512]{2,1,0:T(8,128)(2,1)S(1)} %bitcast.67, bf16[3584,128]{1,0:T(8,128)(2,1)S(1)} %copy-done.11, bf16[3584,128]{1,0:T(8,128)(2,1)S(1)} %copy-done.14, bf16[3584,128]{1,0:T(8,128)(2,1)S(1)} %copy-done.2, ...), custom_call_target="tpu_custom_call" | custom-call | tf_op jit(solution)/shard_map/pallas_call | solution.py:219
  148.8 15.6 %all_to_all.25 = bf16[16,8,3712]{2,1,0:T(8,128)(2,1)S(1)} all-to-all(bf16[16,8,3712]{2,1,0:T(8,128)(2,1)S(1)} %bitcast.66), channel_id=1, replica_groups=mesh['node'=16,'expert'=4,'chip'=4,'core'=2] {'expert','chip'}, dimensions={0} | all-to-all | bytes 1900544 | tf_op jit(solution)/shard_map/all_to_all | solution.py:347
  164.4 0.1 convert_reduce_fusion
  164.7 0.3 convolution_convert_fusion
  165.2 34.1 %all_to_all.26.home = bf16[16,120,128]{2,1,0:T(8,128)(2,1)S(1)} all-to-all(bf16[16,120,128]{2,1,0:T(8,128)(2,1)S(1)} %bitcast.72), channel_id=1, replica_groups=mesh['node'=16,'expert'=4,'chip'=4,'core'=2] {'node'}, dimensions={0} | all-to-all | bytes 983040 | tf_op jit(solution)/shard_map/all_to_all | solution.py:364
  199.3 1.7 shard_map.99
  (53 shorter events, 0.7 us)
Async XLA Ops:
  0.6 0.7 copy-start.16
  3.1 65.7 %all-to-all-start = ((bf16[16,120,128]{2,1,0:T(8,128)(2,1)}), bf16[16,120,128]{2,1,0:T(8,128)(2,1)S(1)}, u32[]{:S(2)}, u32[]{:S(2)}) async-start(bf16[16,120,128]{2,1,0:T(8,128)(2,1)} %shard_map.94), calls=%async_computation | async-start | bytes 983040 | tf_op jit(solution)/shard_map/all_to_all | solution.py:282
  21.0 17.0 %collective-permute-start.3 = (bf16[1792,128]{1,0:T(8,128)(2,1)S(1)}, bf16[1792,128]{1,0:T(8,128)(2,1)S(1)}, u32[]{:S(2)}, u32[]{:S(2)}) collective-permute-start(bf16[1792,128]{1,0:T(8,128)(2,1)S(1)} %get-tuple-element.20), channel_id=1, source_target_pairs={{0,2},{2,4},{4,6},{6,0},{1,3},{3,5},{5,7},{7,1},{8,10},{10,12},{12... | collective-permute-start | bytes 1376264 | tf_op jit(solution)/shard_map/ppermute | solution.py:277
  24.5 15.6 %collective-permute-start.5 = (bf16[1792,128]{1,0:T(8,128)(2,1)S(1)}, bf16[1792,128]{1,0:T(8,128)(2,1)S(1)}, u32[]{:S(2)}, u32[]{:S(2)}) collective-permute-start(bf16[1792,128]{1,0:T(8,128)(2,1)S(1)} %get-tuple-element.21), channel_id=1, source_target_pairs={{0,6},{2,0},{4,2},{6,4},{1,7},{3,1},{5,3},{7,5},{8,14},{10,8},{12,... | collective-permute-start | bytes 1376264 | tf_op jit(solution)/shard_map/ppermute | solution.py:278
  28.1 39.8 %collective-permute-start = (bf16[3584,128]{1,0:T(8,128)(2,1)S(1)}, bf16[3584,128]{1,0:T(8,128)(2,1)S(1)}, u32[]{:S(2)}, u32[]{:S(2)}) collective-permute-start(bf16[3584,128]{1,0:T(8,128)(2,1)S(1)} %get-tuple-element.17.refs_0_), channel_id=1, source_target_pairs={{0,1},{1,0},{2,3},{3,2},{4,5},{5,4},{6,7},{7,6},{8,9},{9,8},{10,11... | collective-permute-start | bytes 2752520 | tf_op jit(solution)/shard_map/ppermute | solution.py:281
  30.0 1.0 copy-start.9
  31.0 37.8 %collective-permute-start.1 = (bf16[3584,128]{1,0:T(8,128)(2,1)S(1)}, bf16[3584,128]{1,0:T(8,128)(2,1)S(1)}, u32[]{:S(2)}, u32[]{:S(2)}) collective-permute-start(bf16[3584,128]{1,0:T(8,128)(2,1)S(1)} %get-tuple-element.18), channel_id=1, source_target_pairs={{0,2},{2,4},{4,6},{6,0},{1,3},{3,5},{5,7},{7,1},{8,10},{10,12},{12... | collective-permute-start | bytes 2752520 | tf_op jit(solution)/shard_map/ppermute | solution.py:279
  33.2 35.6 %collective-permute-start.2 = (bf16[3584,128]{1,0:T(8,128)(2,1)S(1)}, bf16[3584,128]{1,0:T(8,128)(2,1)S(1)}, u32[]{:S(2)}, u32[]{:S(2)}) collective-permute-start(bf16[3584,128]{1,0:T(8,128)(2,1)S(1)} %get-tuple-element.19), channel_id=1, source_target_pairs={{0,6},{2,0},{4,2},{6,4},{1,7},{3,1},{5,3},{7,5},{8,14},{10,8},{12,... | collective-permute-start | bytes 2752520 | tf_op jit(solution)/shard_map/ppermute | solution.py:280
  38.1 28.6 %collective-permute-start.4 = (bf16[1792,128]{1,0:T(8,128)(2,1)S(1)}, bf16[1792,128]{1,0:T(8,128)(2,1)S(1)}, u32[]{:S(2)}, u32[]{:S(2)}) collective-permute-start(bf16[1792,128]{1,0:T(8,128)(2,1)S(1)} %collective-permute-done.3), channel_id=1, source_target_pairs={{0,2},{2,4},{4,6},{6,0},{1,3},{3,5},{5,7},{7,1},{8,10},{10,12},{12... | collective-permute-start | bytes 1376264 | tf_op jit(solution)/shard_map/ppermute | solution.py:283
  40.0 27.9 %collective-permute-start.6 = (bf16[1792,128]{1,0:T(8,128)(2,1)S(1)}, bf16[1792,128]{1,0:T(8,128)(2,1)S(1)}, u32[]{:S(2)}, u32[]{:S(2)}) collective-permute-start(bf16[1792,128]{1,0:T(8,128)(2,1)S(1)} %collective-permute-done.5), channel_id=1, source_target_pairs={{0,6},{2,0},{4,2},{6,4},{1,7},{3,1},{5,3},{7,5},{8,14},{10,8},{12,... | collective-permute-start | bytes 1376264 | tf_op jit(solution)/shard_map/ppermute | solution.py:284
  67.9 0.9 copy-start.12
  68.8 0.8 copy-start.17
  72.2 0.9 copy-start
  73.1 1.0 copy-start.3
  74.1 0.8 copy-start.6
  74.9 30.6 %collective-permute-start.7 = (bf16[10752,128]{1,0:T(8,128)(2,1)}, bf16[10752,128]{1,0:T(8,128)(2,1)S(1)}, u32[]{:S(2)}, u32[]{:S(2)}) collective-permute-start(bf16[10752,128]{1,0:T(8,128)(2,1)} %shard_map.96), channel_id=1, source_target_pairs={{0,1},{1,0},{2,3},{3,2},{4,5},{5,4},{6,7},{7,6},{8,9},{9,8},{10,11... | collective-permute-start | bytes 8257544 | tf_op jit(solution)/shard_map/ppermute | solution.py:298
  80.6 24.9 %all-to-all-start.1 = ((bf16[16,8,3712]{2,1,0:T(8,128)(2,1)}), bf16[16,8,3712]{2,1,0:T(8,128)(2,1)}, u32[]{:S(2)}, u32[]{:S(2)}) async-start(bf16[16,8,3712]{2,1,0:T(8,128)(2,1)} %bitcast.69), calls=%async_computation.1 | async-start | bytes 1900544 | tf_op jit(solution)/shard_map/all_to_all | solution.py:325
  105.5 1.2 copy-start.1
  106.7 1.2 copy-start.4
  107.9 1.0 copy-start.7
  108.9 1.2 copy-start.10
  110.1 1.2 copy-start.13
  114.2 0.8 copy-start.15
  115.0 13.2 %all-to-all-start.2 = ((bf16[4,128,512]{2,1,0:T(8,128)(2,1)}), bf16[4,128,512]{2,1,0:T(8,128)(2,1)}, u32[]{:S(2)}, u32[]{:S(2)}) async-start(bf16[4,128,512]{2,1,0:T(8,128)(2,1)} %copy-done.15), calls=%async_computation.2 | async-start | bytes 1048576 | tf_op jit(solution)/shard_map/all_to_all | solution.py:336
  128.2 14.2 %copy-start.2 = (bf16[3584,128]{1,0:T(8,128)(2,1)S(1)}, bf16[3584,128]{1,0:T(8,128)(2,1)}, u32[]{:S(2)}) copy-start(bf16[3584,128]{1,0:T(8,128)(2,1)} %copy-done) | copy-start | bytes 2752516
  128.2 14.2 %copy-start.5 = (bf16[3584,128]{1,0:T(8,128)(2,1)S(1)}, bf16[3584,128]{1,0:T(8,128)(2,1)}, u32[]{:S(2)}) copy-start(bf16[3584,128]{1,0:T(8,128)(2,1)} %copy-done.3) | copy-start | bytes 2752516
  142.4 1.0 copy-start.8
  143.4 1.2 copy-start.11
  144.6 1.2 copy-start.14

commit v9 on v8

--- a/solution.py
+++ b/solution.py
@@ -126,42 +126,50 @@
         copy.wait()
 
 
-def merge_kernel(ahead, behind, far_up, far_down, out, sems):
-    at = 0
-    copies = []
-    for ref in (ahead, behind, far_up, far_down):
-        copies.append((ref, out.at[pl.ds(at, ref.shape[0])]))
-        at += ref.shape[0]
-    for copy in small_copies(copies, sems):
-        copy.wait()
-
-
-def pieces(refs):
-    here, here_too, ahead, behind, far_up, far_down, merged = refs
-    wide = far_up.shape[0]
+def fetch(refs, held, sems, cuts):
+    wide = held.shape[1] // 2
+    halves = [(ref.at[pl.ds(0, wide)], ref.at[pl.ds(wide, wide)]) for ref in refs[:-4]]
+    halves += [(refs[-4], refs[-3]), (refs[-2], refs[-1])]
     found = []
-    for i, own in enumerate((here, ahead, behind, None)):
-        other, start = (merged, 2 * (i - 1) * wide) if i else (here_too, 0)
-        found += [
-            (own.at[pl.ds(0, wide)], own.at[pl.ds(wide, wide)]) if own is not None else (far_up, far_down),
-            (other.at[pl.ds(start, wide)], other.at[pl.ds(start + wide, wide)]),
-        ]
+    for k, (low, high) in enumerate(zip((0,) + cuts, cuts + (wide,))):
+        at = pl.ds(low, high - low)
+        found.append(
+            [
+                [
+                    pltpu.make_async_copy(
+                        ref.at[at],
+                        held.at[i, pl.ds(half * wide + low, high - low)],
+                        sems.at[k, i, half],
+                    )
+                    for half, ref in enumerate(pair)
+                ]
+                for i, pair in enumerate(halves)
+            ]
+        )
+    for cut in found:
+        for pair in cut:
+            for copy in pair:
+                copy.start()
     return found
 
 
 def partial_kernel(scalars, rows, *refs):
-    blocks, out = pieces(refs[:-1]), refs[-1]
-    hidden = refs[0].shape[1]
-    wide = (rows.shape[1] - LANES) // 2
+    *blocks, out, held, sems = refs
+    count, _, hidden = held.shape
+    wide = held.shape[1] // 2
+    (copies,) = fetch(blocks, held, sems, ())
     x, dy = rows[:, :wide], rows[:, wide : 2 * wide]
-    for i in range(len(blocks) // CORES):
-        pair = blocks[CORES * i : CORES * (i + 1)]
+    for i in range(count // CORES):
+        pair = range(CORES * i, CORES * (i + 1))
+        for m in pair:
+            for copy in copies[m]:
+                copy.wait()
         at = scalars[1 + i]
-        up = jnp.concatenate([u[...] for u, _ in pair], 1)
+        up = jnp.concatenate([held[m, :wide, :] for m in pair], 1)
         out[at, :, : CORES * hidden] = dot(x, up, ((1,), (0,))).astype(out.dtype)
         down = jnp.concatenate(
             [
-                jnp.concatenate([d[j : j + LANES, :] for _, d in pair], 0)
+                jnp.concatenate([held[m, wide + j : wide + j + LANES, :] for m in pair], 0)
                 for j in range(0, wide, LANES)
             ],
             1,
@@ -170,11 +178,13 @@
 
 
 def output_kernel(scalars, rows, every, *refs):
-    result = refs[-1]
-    hidden = refs[0].shape[1]
-    wide = (rows.shape[1] - LANES) // 2
-    blocks = pieces(refs[:-1])
-    chips = len(blocks) // CORES
+    *blocks, result, held, sems = refs
+    many, _, hidden = held.shape
+    wide = held.shape[1] // 2
+    step = 2 * LANES
+    cut = (wide // step // 2 + 1) * step
+    copies = fetch(blocks, held, sems, (cut,))
+    chips = many // CORES
     count = rows.shape[0]
     lane = lax.broadcasted_iota(jnp.int32, (count, LANES), 1)
     mine = lane == scalars[0]
@@ -188,16 +198,21 @@
         [every[scalars[1 + i], :, CORES * hidden :] for i in range(chips)], 1
     )
     inner = jnp.zeros((count, 1), jnp.float32)
-    step = 2 * LANES
     for j in range(0, wide, step):
+        if j in (0, cut):
+            for pair in copies[j // cut]:
+                for copy in pair:
+                    copy.wait()
         down = jnp.concatenate(
             [
-                jnp.concatenate([d[j + k : j + k + LANES, :] for _, d in blocks], 0)
+                jnp.concatenate(
+                    [held[m, wide + j + k : wide + j + k + LANES, :] for m in range(many)], 0
+                )
                 for k in range(0, step, LANES)
             ],
             1,
         )
-        up = jnp.concatenate([u[j : j + step, :] for u, _ in blocks], 1)
+        up = jnp.concatenate([held[m, j : j + step, :] for m in range(many)], 1)
         out = dot(active, down, ((1,), (0,)))
         inner += jnp.sum(
             out * rows[:, wide + j : wide + j + step].astype(jnp.float32), 1, keepdims=True
@@ -210,17 +225,20 @@
     result[:, 2 * wide :] = jnp.where(mine, inner, 0.0).astype(result.dtype)
 
 
-def call(kernel, shapes, scalars, *operands, hbm=0, scratch=()):
+def call(kernel, shapes, scalars, *operands, hbm=0, scratch=(), out_hbm=False, loose=0):
     small, near, far = (
         pl.BlockSpec(memory_space=space) for space in (pltpu.SMEM, pltpu.VMEM, pltpu.HBM)
     )
     count = len(operands) - hbm
-    held = [pltpu.with_memory_space_constraint(v, pltpu.HBM) for v in operands[count:]]
+    fixed = len(operands) - loose
+    held = [pltpu.with_memory_space_constraint(v, pltpu.HBM) for v in operands[count:fixed]]
+    held += operands[fixed:]
+    anywhere = pl.BlockSpec(memory_space=pl.ANY)
     return pl.pallas_call(
         kernel,
         out_shape=[jax.ShapeDtypeStruct(shape, jnp.bfloat16) for shape in shapes],
-        in_specs=[small] * len(scalars) + [near] * count + [far] * hbm,
-        out_specs=[near] * len(shapes),
+        in_specs=[small] * len(scalars) + [near] * count + [far] * (hbm - loose) + [anywhere] * loose,
+        out_specs=[far if out_hbm else near] * len(shapes),
         scratch_shapes=scratch,
         compiler_params=pltpu.CompilerParams(vmem_limit_bytes=24 * 2**20),
     )(*scalars, *operands[:count], *held)
@@ -272,6 +290,10 @@
         down_weight,
         hbm=2,
         scratch=[pltpu.SemaphoreType.DMA((chips * (wide // LANES + 1),))],
+        out_hbm=True,
+    )
+    here, ahead, behind, far_up, far_down, sent = lax.optimization_barrier(
+        (here, ahead, behind, far_up, far_down, sent)
     )
     swap = [(0, 1), (1, 0)]
     far_up = lax.ppermute(far_up, "chip", ahead_of)
@@ -279,24 +301,20 @@
     ahead = lax.ppermute(ahead, "chip", ahead_of)
     behind = lax.ppermute(behind, "chip", behind_of)
     here_too = lax.ppermute(here, "core", swap)
-    recv = lax.all_to_all(sent, "node", split_axis=0, concat_axis=0, tiled=True)
     far_up = lax.ppermute(far_up, "chip", ahead_of)
     far_down = lax.ppermute(far_down, "chip", behind_of)
-    recv, here_too, ahead, behind, far_up, far_down = lax.optimization_barrier(
-        (recv, here_too, ahead, behind, far_up, far_down)
-    )
-    (merged,) = call(
-        merge_kernel,
-        [(2 * (chips - 1) * wide, hidden)],
-        (),
-        ahead,
-        behind,
-        far_up,
-        far_down,
-        scratch=[pltpu.SemaphoreType.DMA((4,))],
-    )
-    merged = lax.ppermute(merged, "core", swap)
-    blocks = (here, here_too, ahead, behind, far_up, far_down, merged)
+    near = (here, here_too)
+    for block in (ahead, behind):
+        near += (block, lax.ppermute(block, "core", swap))
+    recv = lax.all_to_all(sent, "node", split_axis=0, concat_axis=0, tiled=True)
+    recv, near, far_up, far_down = lax.optimization_barrier((recv, near, far_up, far_down))
+    blocks = near + (far_up, far_down)
+    for block in (far_up, far_down):
+        blocks += (lax.ppermute(block, "core", swap),)
+    held = [
+        pltpu.VMEM((chips * CORES, 2 * wide, hidden), bf16),
+        pltpu.SemaphoreType.DMA((2, chips * CORES, 2)),
+    ]
     scalars = jnp.stack(
         [expert, chip, (chip + chips - 1) % chips, (chip + 1) % chips, (chip + 2) % chips]
     ).astype(jnp.int32)
@@ -331,7 +349,14 @@
 
     units = CORES * hidden
     (outgoing,) = call(
-        partial_kernel, [(chips, rows.shape[0], 2 * units)], (scalars,), rows, *blocks
+        partial_kernel,
+        [(chips, rows.shape[0], 2 * units)],
+        (scalars,),
+        rows,
+        *blocks,
+        hbm=len(blocks),
+        loose=2,
+        scratch=held,
     )
     incoming = lax.all_to_all(outgoing, "chip", split_axis=0, concat_axis=0, tiled=True)
     both = jnp.sum(incoming.astype(f32), 0)
@@ -342,7 +367,17 @@
     grad_pre = (gate * back * sig * (1.0 + pre * (1.0 - sig))).astype(bf16)
     every = lax.all_gather(jnp.concatenate([active, grad_pre], 1), "chip", axis=0)
 
-    (result,) = call(output_kernel, [rows.shape], (scalars,), rows, every, *blocks)
+    (result,) = call(
+        output_kernel,
+        [rows.shape],
+        (scalars,),
+        rows,
+        every,
+        *blocks,
+        hbm=len(blocks),
+        loose=2,
+        scratch=held,
+    )
 
     parts_back = lax.all_to_all(
         result.reshape(experts * chips, pairs, -1),

time: 202 us -> 184 us (0.911)
  the two profiles are of different devices: /device:TPU:64 before, /device:TPU:32 now
where the time goes in v9:
time: 184 us; the launch traced here: 183 us
  blocking collectives  59.2 us (32%)
  starting transfers between devices  58 us (32%)
  waiting for transfers between devices  40.3 us (22%)
  Pallas kernels  18 us (10%)
  local copies, waits for them, and re-layouts  3.1 us (2%)
  other arithmetic  1.93 us (1%)
    all_to_all x1, blocking collectives, per_device(): lax.all_to_all(expanded, 'node', split_axis=0, concat_axis=0, tiled=True)  30.8 us
    pallas_call x5, Pallas kernels, call(): pl.pallas_call(kernel, out_shape=[jax.ShapeDtypeStruct(shape, jnp.bfloat1...  18 us
    all_to_all x1, blocking collectives, per_device(): lax.all_to_all(result.reshape(experts * chips, pairs, -1), ('expert', 'ch...  15.7 us
    all_to_all x1, starting transfers between devices, per_device(): recv = lax.all_to_all(sent, 'node', split_axis=0, concat_axis=0, tiled=True)  15.2 us
    all_gather x1, blocking collectives, per_device(): lax.all_gather(jnp.concatenate([active, grad_pre], 1), 'chip', axis=0)  12.8 us
    ppermute x2, waiting for transfers between devices, per_device(): far_up = lax.ppermute(far_up, 'chip', ahead_of)  10.6 us
    ppermute x1, waiting for transfers between devices, per_device(): ahead = lax.ppermute(ahead, 'chip', ahead_of)  10.3 us
    ppermute x2, starting transfers between devices, per_device(): far_down = lax.ppermute(far_down, 'chip', behind_of)  9.73 us
  transfers between devices with their start and end apart: 14, of which 8 were waited for; matrix products, arithmetic and copies ran while one was open for 0% of the time, Pallas kernels for 0%

profile of v9, /device:TPU:32, one launch (start us, length us, event | category | flops | bytes accessed | tf_op | source)
XLA Modules:
  0.0 183.2 jit_solution(18259529992689902310)
XLA Ops:
  0.7 0.1 pad_add_fusion.chips
  0.8 3.1 %shard_map.94 = (bf16[3584,128]{1,0:T(8,128)(2,1)S(1)}, bf16[3584,128]{1,0:T(8,128)(2,1)S(1)}, bf16[3584,128]{1,0:T(8,128)(2,1)S(1)}, bf16[1792,128]{1,0:T(8,128)(2,1)S(1)}, bf16[1792,128]{1,0:T(8,128)(2,1)S(1)}) custom-call(s32[4]{0:T(128)S(1)} %pad_add_fusion.chips, bf16[7168,128]{1,0:T(8,128)(2,1)} %up.1, bf16[128,7168]{1,0:T(8,128)(2,1)} %down.1), custom_call_target="tpu_custom_call" | custom-call | tf_op jit(solution)/shard_map/pallas_call | solution.py:237
  3.8 0.8 copy-done.2
  4.6 1.9 %shard_map.95 = bf16[16,120,128]{2,1,0:T(8,128)(2,1)} custom-call(bf16[2,2,4]{2,1,0:T(2,128)(2,1)S(1)} %bitcast.71, s32[2,4]{1,0:T(2,128)} %bitcast.76, s32[2,2,4]{2,1,0:T(2,128)} %bitcast.74, bf16[4,7168]{1,0:T(4,128)(2,1)} %tokens.1, bf16[4,7168]{1,0:T(4,128)(2,1)} %cotangent.1), custom_call_target="tpu_custom_call" | custom-call | tf_op jit(solution)/shard_map/pallas_call | solution.py:237
  6.5 15.2 %all-to-all-start = ((bf16[16,120,128]{2,1,0:T(8,128)(2,1)}), bf16[16,120,128]{2,1,0:T(8,128)(2,1)}, u32[]{:S(2)}, u32[]{:S(2)}) async-start(bf16[16,120,128]{2,1,0:T(8,128)(2,1)} %shard_map.95), calls=%async_computation | async-start | bytes 983040 | tf_op jit(solution)/shard_map/all_to_all | solution.py:309
  21.7 3.4 %collective-permute-start.1 = (bf16[3584,128]{1,0:T(8,128)(2,1)S(1)}, bf16[3584,128]{1,0:T(8,128)(2,1)S(1)}, u32[]{:S(2)}, u32[]{:S(2)}) collective-permute-start(bf16[3584,128]{1,0:T(8,128)(2,1)S(1)} %get-tuple-element.33), channel_id=1, source_target_pairs={{0,2},{2,4},{4,6},{6,0},{1,3},{3,5},{5,7},{7,1},{8,10},{10,12},{12... | collective-permute-start | bytes 2752520 | tf_op jit(solution)/shard_map/ppermute | solution.py:301
  25.1 3.7 %collective-permute-start.3 = (bf16[3584,128]{1,0:T(8,128)(2,1)S(1)}, bf16[3584,128]{1,0:T(8,128)(2,1)S(1)}, u32[]{:S(2)}, u32[]{:S(2)}) collective-permute-start(bf16[3584,128]{1,0:T(8,128)(2,1)S(1)} %get-tuple-element.34), channel_id=1, source_target_pairs={{0,6},{2,0},{4,2},{6,4},{1,7},{3,1},{5,3},{7,5},{8,14},{10,8},{12,... | collective-permute-start | bytes 2752520 | tf_op jit(solution)/shard_map/ppermute | solution.py:302
  28.8 2.2 %collective-permute-start.5 = (bf16[1792,128]{1,0:T(8,128)(2,1)}, bf16[1792,128]{1,0:T(8,128)(2,1)S(1)}, u32[]{:S(2)}, u32[]{:S(2)}) collective-permute-start(bf16[1792,128]{1,0:T(8,128)(2,1)} %copy-done.2), channel_id=1, source_target_pairs={{0,2},{2,4},{4,6},{6,0},{1,3},{3,5},{5,7},{7,1},{8,10},{10,12},{12... | collective-permute-start | bytes 1376264 | tf_op jit(solution)/shard_map/ppermute | solution.py:299
  31.0 4.9 %collective-permute-start.7 = (bf16[1792,128]{1,0:T(8,128)(2,1)S(1)}, bf16[1792,128]{1,0:T(8,128)(2,1)S(1)}, u32[]{:S(2)}, u32[]{:S(2)}) collective-permute-start(bf16[1792,128]{1,0:T(8,128)(2,1)S(1)} %get-tuple-element.36), channel_id=1, source_target_pairs={{0,6},{2,0},{4,2},{6,4},{1,7},{3,1},{5,3},{7,5},{8,14},{10,8},{12,... | collective-permute-start | bytes 1376264 | tf_op jit(solution)/shard_map/ppermute | solution.py:300
  35.8 1.9 %collective-permute-start = (bf16[3584,128]{1,0:T(8,128)(2,1)S(1)}, bf16[3584,128]{1,0:T(8,128)(2,1)S(1)}, u32[]{:S(2)}, u32[]{:S(2)}) collective-permute-start(bf16[3584,128]{1,0:T(8,128)(2,1)S(1)} %get-tuple-element.38.refs_0_), channel_id=1, source_target_pairs={{0,1},{1,0},{2,3},{3,2},{4,5},{5,4},{6,7},{7,6},{8,9},{9,8},{10,11... | collective-permute-start | bytes 2752520 | tf_op jit(solution)/shard_map/ppermute | solution.py:303
  37.8 10.3 %collective-permute-done.1.refs_2_ = bf16[3584,128]{1,0:T(8,128)(2,1)S(1)} collective-permute-done((bf16[3584,128]{1,0:T(8,128)(2,1)S(1)}, bf16[3584,128]{1,0:T(8,128)(2,1)S(1)}, u32[]{:S(2)}, u32[]{:S(2)}) %collective-permute-start.1) | collective-permute-done | bytes 917536 | tf_op jit(solution)/shard_map/ppermute | solution.py:301
  48.1 1.9 %collective-permute-start.2 = (bf16[3584,128]{1,0:T(8,128)(2,1)S(1)}, bf16[3584,128]{1,0:T(8,128)(2,1)S(1)}, u32[]{:S(2)}, u32[]{:S(2)}) collective-permute-start(bf16[3584,128]{1,0:T(8,128)(2,1)S(1)} %collective-permute-done.1.refs_2_), channel_id=1, source_target_pairs={{0,1},{1,0},{2,3},{3,2},{4,5},{5,4},{6,7},{7,6},{8,9},{9,8},{10,11... | collective-permute-start | bytes 2752520 | tf_op jit(solution)/shard_map/ppermute | solution.py:308
  50.0 0.3 collective-permute-done.3.refs_4_
  50.3 2.1 %collective-permute-start.4 = (bf16[3584,128]{1,0:T(8,128)(2,1)S(1)}, bf16[3584,128]{1,0:T(8,128)(2,1)S(1)}, u32[]{:S(2)}, u32[]{:S(2)}) collective-permute-start(bf16[3584,128]{1,0:T(8,128)(2,1)S(1)} %collective-permute-done.3.refs_4_), channel_id=1, source_target_pairs={{0,1},{1,0},{2,3},{3,2},{4,5},{5,4},{6,7},{7,6},{8,9},{9,8},{10,11... | collective-permute-start | bytes 2752520 | tf_op jit(solution)/shard_map/ppermute | solution.py:308
  52.5 3.7 %collective-permute-done.5 = bf16[1792,128]{1,0:T(8,128)(2,1)S(1)} collective-permute-done((bf16[1792,128]{1,0:T(8,128)(2,1)}, bf16[1792,128]{1,0:T(8,128)(2,1)S(1)}, u32[]{:S(2)}, u32[]{:S(2)}) %collective-permute-start.5) | collective-permute-done | bytes 458784 | tf_op jit(solution)/shard_map/ppermute | solution.py:299
  56.2 2.2 %collective-permute-start.6 = (bf16[1792,128]{1,0:T(8,128)(2,1)S(1)}, bf16[1792,128]{1,0:T(8,128)(2,1)}, u32[]{:S(2)}, u32[]{:S(2)}) collective-permute-start(bf16[1792,128]{1,0:T(8,128)(2,1)S(1)} %collective-permute-done.5), channel_id=1, source_target_pairs={{0,2},{2,4},{4,6},{6,0},{1,3},{3,5},{5,7},{7,1},{8,10},{10,12},{12... | collective-permute-start | bytes 1376264 | tf_op jit(solution)/shard_map/ppermute | solution.py:304
  58.4 4.9 %collective-permute-start.8 = (bf16[1792,128]{1,0:T(8,128)(2,1)S(1)}, bf16[1792,128]{1,0:T(8,128)(2,1)}, u32[]{:S(2)}, u32[]{:S(2)}) collective-permute-start(bf16[1792,128]{1,0:T(8,128)(2,1)S(1)} %collective-permute-done.7), channel_id=1, source_target_pairs={{0,6},{2,0},{4,2},{6,4},{1,7},{3,1},{5,3},{7,5},{8,14},{10,8},{12,... | collective-permute-start | bytes 1376264 | tf_op jit(solution)/shard_map/ppermute | solution.py:305
  63.2 6.9 %collective-permute-done.6.refs_6_ = bf16[1792,128]{1,0:T(8,128)(2,1)} collective-permute-done((bf16[1792,128]{1,0:T(8,128)(2,1)S(1)}, bf16[1792,128]{1,0:T(8,128)(2,1)}, u32[]{:S(2)}, u32[]{:S(2)}) %collective-permute-start.6) | collective-permute-done | bytes 458784 | tf_op jit(solution)/shard_map/ppermute | solution.py:304
  70.2 1.1 collective-permute-done.8.refs_7_
  71.2 0.0 collective-permute-done.refs_1_
  71.3 0.9 copy-done.5
  72.2 0.0 collective-permute-done.4.refs_5_
  72.2 0.0 all-to-all-done
  72.2 1.2 compare_reduce_fusion
  73.4 0.1 copy.12
  73.5 0.1 add_reduce_fusion
  73.6 1.2 convolution_convert_fusion.1
  75.0 1.0 broadcast_in_dim.10
  76.0 7.8 %all-to-all-start.1 = ((bf16[16,8,3712]{2,1,0:T(8,128)(2,1)}), bf16[16,8,3712]{2,1,0:T(8,128)(2,1)S(1)}, u32[]{:S(2)}, u32[]{:S(2)}) async-start(bf16[16,8,3712]{2,1,0:T(8,128)(2,1)} %bitcast.14), calls=%async_computation.1 | async-start | bytes 1900544 | tf_op jit(solution)/shard_map/all_to_all | solution.py:343
  83.9 1.9 %collective-permute-start.9 = (bf16[1792,128]{1,0:T(8,128)(2,1)}, bf16[1792,128]{1,0:T(8,128)(2,1)S(1)}, u32[]{:S(2)}, u32[]{:S(2)}) collective-permute-start(bf16[1792,128]{1,0:T(8,128)(2,1)} %collective-permute-done.6.refs_6_), channel_id=1, source_target_pairs={{0,1},{1,0},{2,3},{3,2},{4,5},{5,4},{6,7},{7,6},{8,9},{9,8},{10,11... | collective-permute-start | bytes 1376264 | tf_op jit(solution)/shard_map/ppermute | solution.py:313
  85.8 2.4 %collective-permute-start.10 = (bf16[1792,128]{1,0:T(8,128)(2,1)}, bf16[1792,128]{1,0:T(8,128)(2,1)S(1)}, u32[]{:S(2)}, u32[]{:S(2)}) collective-permute-start(bf16[1792,128]{1,0:T(8,128)(2,1)} %collective-permute-done.8.refs_7_), channel_id=1, source_target_pairs={{0,1},{1,0},{2,3},{3,2},{4,5},{5,4},{6,7},{7,6},{8,9},{9,8},{10,11... | collective-permute-start | bytes 1376264 | tf_op jit(solution)/shard_map/ppermute | solution.py:313
  88.2 0.1 stack.49.scalars
  88.3 1.5 collective-permute-done.10.refs_9_
  89.8 7.7 %all-to-all-done.1 = bf16[16,8,3712]{2,1,0:T(8,128)(2,1)S(1)} async-done(((bf16[16,8,3712]{2,1,0:T(8,128)(2,1)}), bf16[16,8,3712]{2,1,0:T(8,128)(2,1)S(1)}, u32[]{:S(2)}, u32[]{:S(2)}) %all-to-all-start.1) | async-done | bytes 950304 | tf_op jit(solution)/shard_map/all_to_all | solution.py:343
  97.6 6.2 %shard_map.96 = bf16[4,128,512]{2,1,0:T(8,128)(2,1)} custom-call(s32[5]{0:T(128)S(1)} %stack.49.scalars, bf16[128,3712]{1,0:T(8,128)(2,1)S(1)} %bitcast.66, bf16[3584,128]{1,0:T(8,128)(2,1)} %copy-done, bf16[3584,128]{1,0:T(8,128)(2,1)} %copy-done.5, bf16[3584,128]{1,0:T(8,128)(2,1)} %copy-done.3, bf16[3584,128]{1,0:T(8,128)(2,1)} %copy-done.6, ...), custom_call_target="tpu_custom_call" | custom-call | tf_op jit(solution)/shard_map/pallas_call | solution.py:237
  103.8 3.5 %all-to-all-start.2 = ((bf16[4,128,512]{2,1,0:T(8,128)(2,1)}), bf16[4,128,512]{2,1,0:T(8,128)(2,1)S(1)}, u32[]{:S(2)}, u32[]{:S(2)}) async-start(bf16[4,128,512]{2,1,0:T(8,128)(2,1)} %shard_map.96), calls=%async_computation.2 | async-start | bytes 1048576 | tf_op jit(solution)/shard_map/all_to_all | solution.py:361
  107.3 0.1 select_reduce_fusion
  107.4 8.7 %all-to-all-done.2 = bf16[4,128,512]{2,1,0:T(8,128)(2,1)S(1)} async-done(((bf16[4,128,512]{2,1,0:T(8,128)(2,1)}), bf16[4,128,512]{2,1,0:T(8,128)(2,1)S(1)}, u32[]{:S(2)}, u32[]{:S(2)}) %all-to-all-start.2) | async-done | bytes 524320 | tf_op jit(solution)/shard_map/all_to_all | solution.py:361
  116.1 0.1 convert_reduce_fusion.1
  116.2 0.1 multiply_convert_fusion
  116.3 12.8 %all-gather = bf16[512,512]{1,0:T(8,128)(2,1)S(1)} all-gather(bf16[128,512]{1,0:T(8,128)(2,1)S(1)} %pad_maximum_fusion.1), channel_id=2, replica_groups=mesh['node'=16,'expert'=4,'chip'=4,'core'=2] {'chip'}, dimensions={0}, use_global_device_ids=true | all-gather | bytes 655360 | tf_op jit(solution)/shard_map/all_gather | solution.py:368
  129.1 5.1 %shard_map.97 = bf16[128,3712]{1,0:T(8,128)(2,1)S(1)} custom-call(s32[5]{0:T(128)S(1)} %stack.49.scalars, bf16[128,3712]{1,0:T(8,128)(2,1)S(1)} %bitcast.68, bf16[4,128,512]{2,1,0:T(8,128)(2,1)S(1)} %bitcast.70, bf16[3584,128]{1,0:T(8,128)(2,1)} %copy-done, bf16[3584,128]{1,0:T(8,128)(2,1)} %copy-done.5, bf16[3584,128]{1,0:T(8,128)(2,1)} %copy-done.3, ...), custom_call_target="tpu_custom_call" | custom-call | tf_op jit(solution)/shard_map/pallas_call | solution.py:237
  134.3 15.7 %all_to_all.25 = bf16[16,8,3712]{2,1,0:T(8,128)(2,1)S(1)} all-to-all(bf16[16,8,3712]{2,1,0:T(8,128)(2,1)S(1)} %bitcast.69), channel_id=1, replica_groups=mesh['node'=16,'expert'=4,'chip'=4,'core'=2] {'expert','chip'}, dimensions={0} | all-to-all | bytes 1900544 | tf_op jit(solution)/shard_map/all_to_all | solution.py:382
  149.9 0.1 convert_reduce_fusion
  150.2 0.3 convolution_convert_fusion
  150.6 0.1 copy.14
  150.7 30.8 %all_to_all.26.home = bf16[16,120,128]{2,1,0:T(8,128)(2,1)S(1)} all-to-all(bf16[16,120,128]{2,1,0:T(8,128)(2,1)S(1)} %bitcast.73), channel_id=1, replica_groups=mesh['node'=16,'expert'=4,'chip'=4,'core'=2] {'node'}, dimensions={0} | all-to-all | bytes 983040 | tf_op jit(solution)/shard_map/all_to_all | solution.py:399
  181.4 1.7 shard_map.98
  (38 shorter events, 0.3 us)
Async XLA Ops:
  0.7 3.9 %copy-start.1 = (bf16[4,2,2]{0,2,1:T(2,128)(2,1)S(1)}, bf16[4,2,2]{0,2,1:T(2,128)(2,1)}, u32[]{:S(2)}) copy-start(bf16[4,2,2]{0,2,1:T(2,128)(2,1)} %param.11) | copy-start | bytes 100
  3.8 0.8 copy-start.2
  4.6 70.4 %copy-start = (bf16[3584,128]{1,0:T(8,128)(2,1)}, bf16[3584,128]{1,0:T(8,128)(2,1)S(1)}, u32[]{:S(2)}) copy-start(bf16[3584,128]{1,0:T(8,128)(2,1)S(1)} %get-tuple-element.38.refs_0_) | copy-start | bytes 2752516
  6.5 65.7 %all-to-all-start = ((bf16[16,120,128]{2,1,0:T(8,128)(2,1)}), bf16[16,120,128]{2,1,0:T(8,128)(2,1)}, u32[]{:S(2)}, u32[]{:S(2)}) async-start(bf16[16,120,128]{2,1,0:T(8,128)(2,1)} %shard_map.95), calls=%async_computation | async-start | bytes 983040 | tf_op jit(solution)/shard_map/all_to_all | solution.py:309
  21.7 26.4 %collective-permute-start.1 = (bf16[3584,128]{1,0:T(8,128)(2,1)S(1)}, bf16[3584,128]{1,0:T(8,128)(2,1)S(1)}, u32[]{:S(2)}, u32[]{:S(2)}) collective-permute-start(bf16[3584,128]{1,0:T(8,128)(2,1)S(1)} %get-tuple-element.33), channel_id=1, source_target_pairs={{0,2},{2,4},{4,6},{6,0},{1,3},{3,5},{5,7},{7,1},{8,10},{10,12},{12... | collective-permute-start | bytes 2752520 | tf_op jit(solution)/shard_map/ppermute | solution.py:301
  25.1 25.2 %collective-permute-start.3 = (bf16[3584,128]{1,0:T(8,128)(2,1)S(1)}, bf16[3584,128]{1,0:T(8,128)(2,1)S(1)}, u32[]{:S(2)}, u32[]{:S(2)}) collective-permute-start(bf16[3584,128]{1,0:T(8,128)(2,1)S(1)} %get-tuple-element.34), channel_id=1, source_target_pairs={{0,6},{2,0},{4,2},{6,4},{1,7},{3,1},{5,3},{7,5},{8,14},{10,8},{12,... | collective-permute-start | bytes 2752520 | tf_op jit(solution)/shard_map/ppermute | solution.py:302
  28.8 27.4 %collective-permute-start.5 = (bf16[1792,128]{1,0:T(8,128)(2,1)}, bf16[1792,128]{1,0:T(8,128)(2,1)S(1)}, u32[]{:S(2)}, u32[]{:S(2)}) collective-permute-start(bf16[1792,128]{1,0:T(8,128)(2,1)} %copy-done.2), channel_id=1, source_target_pairs={{0,2},{2,4},{4,6},{6,0},{1,3},{3,5},{5,7},{7,1},{8,10},{10,12},{12... | collective-permute-start | bytes 1376264 | tf_op jit(solution)/shard_map/ppermute | solution.py:299
  31.0 27.4 %collective-permute-start.7 = (bf16[1792,128]{1,0:T(8,128)(2,1)S(1)}, bf16[1792,128]{1,0:T(8,128)(2,1)S(1)}, u32[]{:S(2)}, u32[]{:S(2)}) collective-permute-start(bf16[1792,128]{1,0:T(8,128)(2,1)S(1)} %get-tuple-element.36), channel_id=1, source_target_pairs={{0,6},{2,0},{4,2},{6,4},{1,7},{3,1},{5,3},{7,5},{8,14},{10,8},{12,... | collective-permute-start | bytes 1376264 | tf_op jit(solution)/shard_map/ppermute | solution.py:300
  35.8 35.4 %collective-permute-start = (bf16[3584,128]{1,0:T(8,128)(2,1)S(1)}, bf16[3584,128]{1,0:T(8,128)(2,1)S(1)}, u32[]{:S(2)}, u32[]{:S(2)}) collective-permute-start(bf16[3584,128]{1,0:T(8,128)(2,1)S(1)} %get-tuple-element.38.refs_0_), channel_id=1, source_target_pairs={{0,1},{1,0},{2,3},{3,2},{4,5},{5,4},{6,7},{7,6},{8,9},{9,8},{10,11... | collective-permute-start | bytes 2752520 | tf_op jit(solution)/shard_map/ppermute | solution.py:303
  48.1 23.1 %copy-start.3 = (bf16[3584,128]{1,0:T(8,128)(2,1)}, bf16[3584,128]{1,0:T(8,128)(2,1)S(1)}, u32[]{:S(2)}) copy-start(bf16[3584,128]{1,0:T(8,128)(2,1)S(1)} %collective-permute-done.1.refs_2_) | copy-start | bytes 2752516
  48.1 23.1 %collective-permute-start.2 = (bf16[3584,128]{1,0:T(8,128)(2,1)S(1)}, bf16[3584,128]{1,0:T(8,128)(2,1)S(1)}, u32[]{:S(2)}, u32[]{:S(2)}) collective-permute-start(bf16[3584,128]{1,0:T(8,128)(2,1)S(1)} %collective-permute-done.1.refs_2_), channel_id=1, source_target_pairs={{0,1},{1,0},{2,3},{3,2},{4,5},{5,4},{6,7},{7,6},{8,9},{9,8},{10,11... | collective-permute-start | bytes 2752520 | tf_op jit(solution)/shard_map/ppermute | solution.py:308
  50.3 20.9 %copy-start.4 = (bf16[3584,128]{1,0:T(8,128)(2,1)}, bf16[3584,128]{1,0:T(8,128)(2,1)S(1)}, u32[]{:S(2)}) copy-start(bf16[3584,128]{1,0:T(8,128)(2,1)S(1)} %collective-permute-done.3.refs_4_) | copy-start | bytes 2752516
  50.3 21.9 %collective-permute-start.4 = (bf16[3584,128]{1,0:T(8,128)(2,1)S(1)}, bf16[3584,128]{1,0:T(8,128)(2,1)S(1)}, u32[]{:S(2)}, u32[]{:S(2)}) collective-permute-start(bf16[3584,128]{1,0:T(8,128)(2,1)S(1)} %collective-permute-done.3.refs_4_), channel_id=1, source_target_pairs={{0,1},{1,0},{2,3},{3,2},{4,5},{5,4},{6,7},{7,6},{8,9},{9,8},{10,11... | collective-permute-start | bytes 2752520 | tf_op jit(solution)/shard_map/ppermute | solution.py:308
  56.2 14.0 %collective-permute-start.6 = (bf16[1792,128]{1,0:T(8,128)(2,1)S(1)}, bf16[1792,128]{1,0:T(8,128)(2,1)}, u32[]{:S(2)}, u32[]{:S(2)}) collective-permute-start(bf16[1792,128]{1,0:T(8,128)(2,1)S(1)} %collective-permute-done.5), channel_id=1, source_target_pairs={{0,2},{2,4},{4,6},{6,0},{1,3},{3,5},{5,7},{7,1},{8,10},{10,12},{12... | collective-permute-start | bytes 1376264 | tf_op jit(solution)/shard_map/ppermute | solution.py:304
  58.4 12.9 %collective-permute-start.8 = (bf16[1792,128]{1,0:T(8,128)(2,1)S(1)}, bf16[1792,128]{1,0:T(8,128)(2,1)}, u32[]{:S(2)}, u32[]{:S(2)}) collective-permute-start(bf16[1792,128]{1,0:T(8,128)(2,1)S(1)} %collective-permute-done.7), channel_id=1, source_target_pairs={{0,6},{2,0},{4,2},{6,4},{1,7},{3,1},{5,3},{7,5},{8,14},{10,8},{12,... | collective-permute-start | bytes 1376264 | tf_op jit(solution)/shard_map/ppermute | solution.py:305
  71.2 0.9 copy-start.5
  72.2 3.9 %copy-start.6 = (bf16[3584,128]{1,0:T(8,128)(2,1)}, bf16[3584,128]{1,0:T(8,128)(2,1)S(1)}, u32[]{:S(2)}) copy-start(bf16[3584,128]{1,0:T(8,128)(2,1)S(1)} %collective-permute-done.2.refs_3_) | copy-start | bytes 2752516
  72.2 3.9 %copy-start.7 = (bf16[3584,128]{1,0:T(8,128)(2,1)}, bf16[3584,128]{1,0:T(8,128)(2,1)S(1)}, u32[]{:S(2)}) copy-start(bf16[3584,128]{1,0:T(8,128)(2,1)S(1)} %collective-permute-done.4.refs_5_) | copy-start | bytes 2752516
  76.0 21.5 %all-to-all-start.1 = ((bf16[16,8,3712]{2,1,0:T(8,128)(2,1)}), bf16[16,8,3712]{2,1,0:T(8,128)(2,1)S(1)}, u32[]{:S(2)}, u32[]{:S(2)}) async-start(bf16[16,8,3712]{2,1,0:T(8,128)(2,1)} %bitcast.14), calls=%async_computation.1 | async-start | bytes 1900544 | tf_op jit(solution)/shard_map/all_to_all | solution.py:343
  83.9 4.4 %collective-permute-start.9 = (bf16[1792,128]{1,0:T(8,128)(2,1)}, bf16[1792,128]{1,0:T(8,128)(2,1)S(1)}, u32[]{:S(2)}, u32[]{:S(2)}) collective-permute-start(bf16[1792,128]{1,0:T(8,128)(2,1)} %collective-permute-done.6.refs_6_), channel_id=1, source_target_pairs={{0,1},{1,0},{2,3},{3,2},{4,5},{5,4},{6,7},{7,6},{8,9},{9,8},{10,11... | collective-permute-start | bytes 1376264 | tf_op jit(solution)/shard_map/ppermute | solution.py:313
  85.8 4.0 %collective-permute-start.10 = (bf16[1792,128]{1,0:T(8,128)(2,1)}, bf16[1792,128]{1,0:T(8,128)(2,1)S(1)}, u32[]{:S(2)}, u32[]{:S(2)}) collective-permute-start(bf16[1792,128]{1,0:T(8,128)(2,1)} %collective-permute-done.8.refs_7_), channel_id=1, source_target_pairs={{0,1},{1,0},{2,3},{3,2},{4,5},{5,4},{6,7},{7,6},{8,9},{9,8},{10,11... | collective-permute-start | bytes 1376264 | tf_op jit(solution)/shard_map/ppermute | solution.py:313
  103.8 12.3 %all-to-all-start.2 = ((bf16[4,128,512]{2,1,0:T(8,128)(2,1)}), bf16[4,128,512]{2,1,0:T(8,128)(2,1)S(1)}, u32[]{:S(2)}, u32[]{:S(2)}) async-start(bf16[4,128,512]{2,1,0:T(8,128)(2,1)} %shard_map.96), calls=%async_computation.2 | async-start | bytes 1048576 | tf_op jit(solution)/shard_map/all_to_all | solution.py:361

commit v10 on v9

--- a/solution.py
+++ b/solution.py
@@ -146,11 +146,40 @@
                 for i, pair in enumerate(halves)
             ]
         )
-    for cut in found:
-        for pair in cut:
-            for copy in pair:
+    return found
+
+
+def run_ahead(groups):
+    for group in groups[:2]:
+        for copy in group:
+            copy.start()
+    for i, group in enumerate(groups):
+        for copy in group:
+            copy.wait()
+        if i + 2 < len(groups):
+            for copy in groups[i + 2]:
                 copy.start()
-    return found
+        yield
+
+
+def flat(lists):
+    return [item for items in lists for item in items]
+
+
+def mark_kernel(scalars, *refs):
+    for i in range(scalars.shape[0]):
+        refs[-1][i] = scalars[i]
+
+
+def mark(scalars, *arrays):
+    small = pl.BlockSpec(memory_space=pltpu.SMEM)
+    return pl.pallas_call(
+        mark_kernel,
+        out_shape=jax.ShapeDtypeStruct(scalars.shape, scalars.dtype),
+        in_specs=[small] + [pl.BlockSpec(memory_space=pl.ANY)] * len(arrays),
+        out_specs=small,
+        cost_estimate=pl.CostEstimate(flops=10**11, bytes_accessed=4096, transcendentals=0),
+    )(scalars, *arrays)
 
 
 def partial_kernel(scalars, rows, *refs):
@@ -158,12 +187,11 @@
     count, _, hidden = held.shape
     wide = held.shape[1] // 2
     (copies,) = fetch(blocks, held, sems, ())
+    arrived = run_ahead([flat(copies[i : i + CORES]) for i in range(0, count, CORES)])
     x, dy = rows[:, :wide], rows[:, wide : 2 * wide]
     for i in range(count // CORES):
         pair = range(CORES * i, CORES * (i + 1))
-        for m in pair:
-            for copy in copies[m]:
-                copy.wait()
+        next(arrived)
         at = scalars[1 + i]
         up = jnp.concatenate([held[m, :wide, :] for m in pair], 1)
         out[at, :, : CORES * hidden] = dot(x, up, ((1,), (0,))).astype(out.dtype)
@@ -182,8 +210,8 @@
     many, _, hidden = held.shape
     wide = held.shape[1] // 2
     step = 2 * LANES
-    cut = (wide // step // 2 + 1) * step
-    copies = fetch(blocks, held, sems, (cut,))
+    cuts = tuple(range(2 * step, wide, 2 * step))
+    arrived = run_ahead([flat(cut) for cut in fetch(blocks, held, sems, cuts)])
     chips = many // CORES
     count = rows.shape[0]
     lane = lax.broadcasted_iota(jnp.int32, (count, LANES), 1)
@@ -199,10 +227,8 @@
     )
     inner = jnp.zeros((count, 1), jnp.float32)
     for j in range(0, wide, step):
-        if j in (0, cut):
-            for pair in copies[j // cut]:
-                for copy in pair:
-                    copy.wait()
+        if j == 0 or j in cuts:
+            next(arrived)
         down = jnp.concatenate(
             [
                 jnp.concatenate(
@@ -301,6 +327,13 @@
     ahead = lax.ppermute(ahead, "chip", ahead_of)
     behind = lax.ppermute(behind, "chip", behind_of)
     here_too = lax.ppermute(here, "core", swap)
+    scalars = jnp.stack(
+        [expert, chip, (chip + chips - 1) % chips, (chip + 1) % chips, (chip + 2) % chips]
+    ).astype(jnp.int32)
+    scalars = mark(scalars, ahead, behind, far_up, far_down)
+    ahead, behind, far_up, far_down, scalars = lax.optimization_barrier(
+        (ahead, behind, far_up, far_down, scalars)
+    )
     far_up = lax.ppermute(far_up, "chip", ahead_of)
     far_down = lax.ppermute(far_down, "chip", behind_of)
     near = (here, here_too)
@@ -313,12 +346,8 @@
         blocks += (lax.ppermute(block, "core", swap),)
     held = [
         pltpu.VMEM((chips * CORES, 2 * wide, hidden), bf16),
-        pltpu.SemaphoreType.DMA((2, chips * CORES, 2)),
+        pltpu.SemaphoreType.DMA((4, chips * CORES, 2)),
     ]
-    scalars = jnp.stack(
-        [expert, chip, (chip + chips - 1) % chips, (chip + 1) % chips, (chip + 2) % chips]
-    ).astype(jnp.int32)
-
     used = jnp.any(recv[:, 2 * width // LANES, :] > 0, 1)
     rank = jnp.cumsum(used.astype(jnp.int32)) - 1
     slot = jnp.arange(pairs, dtype=jnp.int32)

time: 184 us -> 197 us (1.071)
  Pallas kernels: 18 us -> 34 us
  waiting for transfers between devices: 40.3 us -> 34.6 us
  blocking collectives: 59.2 us -> 63.7 us
    pallas_call x5, Pallas kernels: 18 us -> 32.8 us  [call(): pl.pallas_call(kernel, out_shape=[jax.ShapeDtypeStruct(shape, jnp.bfloat1...]
    ppermute x1, waiting for transfers between devices: 10.3 us -> 0.01 us  [per_device(): ahead = lax.ppermute(ahead, 'chip', ahead_of)]
    all_to_all x1, blocking collectives: 30.8 us -> 35.3 us  [per_device(): lax.all_to_all(expanded, 'node', split_axis=0, concat_axis=0, tiled=True)]
    ppermute x2, waiting for transfers between devices: 1.09 us -> 3.82 us  [per_device(): far_down = lax.ppermute(far_down, 'chip', behind_of)]
  transfers between devices with their start and end apart: 14 -> 14, of which waited for: 8 -> 7; matrix products, arithmetic and copies ran while one was open for 0% -> 0% of each run, Pallas kernels for 0% -> 1%
where the time goes in v10:
time: 197 us; the launch traced here: 196 us
  blocking collectives  63.7 us (32%)
  starting transfers between devices  57.4 us (29%)
  waiting for transfers between devices  34.6 us (18%)
  Pallas kernels  34 us (17%)
    all_to_all x1, blocking collectives, per_device(): lax.all_to_all(expanded, 'node', split_axis=0, concat_axis=0, tiled=True)  35.3 us
    pallas_call x5, Pallas kernels, call(): pl.pallas_call(kernel, out_shape=[jax.ShapeDtypeStruct(shape, jnp.bfloat1...  32.8 us
    all_to_all x1, starting transfers between devices, per_device(): recv = lax.all_to_all(sent, 'node', split_axis=0, concat_axis=0, tiled=True)  15.2 us
    all_to_all x1, blocking collectives, per_device(): lax.all_to_all(result.reshape(experts * chips, pairs, -1), ('expert', 'ch...  15.1 us
    all_gather x1, blocking collectives, per_device(): lax.all_gather(jnp.concatenate([active, grad_pre], 1), 'chip', axis=0)  13.3 us
    ppermute x2, waiting for transfers between devices, per_device(): far_up = lax.ppermute(far_up, 'chip', ahead_of)  11.9 us
    all_to_all x1, waiting for transfers between devices, per_device(): lax.all_to_all(spread, ('expert', 'chip'), split_axis=0, concat_axis=0, t...  9.55 us
    ppermute x2, starting transfers between devices, per_device(): far_down = lax.ppermute(far_down, 'chip', behind_of)  8.52 us
  transfers between devices with their start and end apart: 14, of which 7 were waited for; matrix products, arithmetic and copies ran while one was open for 0% of the time, Pallas kernels for 1%

profile of v10, /device:TPU:32, one launch (start us, length us, event | category | flops | bytes accessed | tf_op | source)
XLA Modules:
  0.0 196.2 jit_solution(6035171174662280137)
XLA Ops:
  0.7 0.1 pad_add_fusion.chips
  0.8 16.2 %shard_map.94 = (bf16[3584,128]{1,0:T(8,128)(2,1)S(1)}, bf16[3584,128]{1,0:T(8,128)(2,1)S(1)}, bf16[3584,128]{1,0:T(8,128)(2,1)S(1)}, bf16[1792,128]{1,0:T(8,128)(2,1)}, bf16[1792,128]{1,0:T(8,128)(2,1)S(1)}) custom-call(s32[4]{0:T(128)S(1)} %pad_add_fusion.chips, bf16[7168,128]{1,0:T(8,128)(2,1)} %up.1, bf16[128,7168]{1,0:T(8,128)(2,1)} %down.1), custom_call_target="tpu_custom_call" | custom-call | tf_op jit(solution)/shard_map/pallas_call | solution.py:263
  17.0 1.9 shard_map.95
  18.9 3.4 %collective-permute-start.1 = (bf16[3584,128]{1,0:T(8,128)(2,1)S(1)}, bf16[3584,128]{1,0:T(8,128)(2,1)}, u32[]{:S(2)}, u32[]{:S(2)}) collective-permute-start(bf16[3584,128]{1,0:T(8,128)(2,1)S(1)} %get-tuple-element.38), channel_id=1, source_target_pairs={{0,2},{2,4},{4,6},{6,0},{1,3},{3,5},{5,7},{7,1},{8,10},{10,12},{12... | collective-permute-start | bytes 2752520 | tf_op jit(solution)/shard_map/ppermute | solution.py:327
  22.3 3.7 %collective-permute-start.2 = (bf16[3584,128]{1,0:T(8,128)(2,1)S(1)}, bf16[3584,128]{1,0:T(8,128)(2,1)}, u32[]{:S(2)}, u32[]{:S(2)}) collective-permute-start(bf16[3584,128]{1,0:T(8,128)(2,1)S(1)} %get-tuple-element.39), channel_id=1, source_target_pairs={{0,6},{2,0},{4,2},{6,4},{1,7},{3,1},{5,3},{7,5},{8,14},{10,8},{12,... | collective-permute-start | bytes 2752520 | tf_op jit(solution)/shard_map/ppermute | solution.py:328
  25.9 2.2 %collective-permute-start.3 = (bf16[1792,128]{1,0:T(8,128)(2,1)}, bf16[1792,128]{1,0:T(8,128)(2,1)}, u32[]{:S(2)}, u32[]{:S(2)}) collective-permute-start(bf16[1792,128]{1,0:T(8,128)(2,1)} %get-tuple-element.40), channel_id=1, source_target_pairs={{0,2},{2,4},{4,6},{6,0},{1,3},{3,5},{5,7},{7,1},{8,10},{10,12},{12... | collective-permute-start | bytes 1376264 | tf_op jit(solution)/shard_map/ppermute | solution.py:325
  28.1 4.9 %collective-permute-start.4 = (bf16[1792,128]{1,0:T(8,128)(2,1)S(1)}, bf16[1792,128]{1,0:T(8,128)(2,1)}, u32[]{:S(2)}, u32[]{:S(2)}) collective-permute-start(bf16[1792,128]{1,0:T(8,128)(2,1)S(1)} %get-tuple-element.41), channel_id=1, source_target_pairs={{0,6},{2,0},{4,2},{6,4},{1,7},{3,1},{5,3},{7,5},{8,14},{10,8},{12,... | collective-permute-start | bytes 1376264 | tf_op jit(solution)/shard_map/ppermute | solution.py:326
  33.0 15.2 %all-to-all-start = ((bf16[16,120,128]{2,1,0:T(8,128)(2,1)}), bf16[16,120,128]{2,1,0:T(8,128)(2,1)}, u32[]{:S(2)}, u32[]{:S(2)}) async-start(bf16[16,120,128]{2,1,0:T(8,128)(2,1)} %shard_map.95), calls=%async_computation | async-start | bytes 983040 | tf_op jit(solution)/shard_map/all_to_all | solution.py:342
  48.2 1.9 collective-permute-start
  50.2 0.7 stack.49.scalars
  50.8 3.2 %collective-permute-done.3.refs_2_ = bf16[1792,128]{1,0:T(8,128)(2,1)} collective-permute-done((bf16[1792,128]{1,0:T(8,128)(2,1)}, bf16[1792,128]{1,0:T(8,128)(2,1)}, u32[]{:S(2)}, u32[]{:S(2)}) %collective-permute-start.3) | collective-permute-done | bytes 458784 | tf_op jit(solution)/shard_map/ppermute | solution.py:325
  54.0 1.9 collective-permute-done.4.refs_3_
  55.9 0.0 collective-permute-done.1.refs_0_.refs_2_
  55.9 0.0 collective-permute-done.2.refs_1_.refs_4_
  55.9 1.2 shard_map.96.scalars
  57.1 1.9 collective-permute-start.5
  59.1 2.4 %collective-permute-start.6 = (bf16[3584,128]{1,0:T(8,128)(2,1)}, bf16[3584,128]{1,0:T(8,128)(2,1)}, u32[]{:S(2)}, u32[]{:S(2)}) collective-permute-start(bf16[3584,128]{1,0:T(8,128)(2,1)} %collective-permute-done.2.refs_1_.refs_4_), channel_id=1, source_target_pairs={{0,1},{1,0},{2,3},{3,2},{4,5},{5,4},{6,7},{7,6},{8,9},{9,8},{10,11... | collective-permute-start | bytes 2752520 | tf_op jit(solution)/shard_map/ppermute | solution.py:341
  61.5 3.4 %collective-permute-start.7 = (bf16[1792,128]{1,0:T(8,128)(2,1)}, bf16[1792,128]{1,0:T(8,128)(2,1)S(1)}, u32[]{:S(2)}, u32[]{:S(2)}) collective-permute-start(bf16[1792,128]{1,0:T(8,128)(2,1)} %collective-permute-done.3.refs_2_), channel_id=1, source_target_pairs={{0,2},{2,4},{4,6},{6,0},{1,3},{3,5},{5,7},{7,1},{8,10},{10,12},{12... | collective-permute-start | bytes 1376264 | tf_op jit(solution)/shard_map/ppermute | solution.py:337
  64.9 3.7 %collective-permute-start.8 = (bf16[1792,128]{1,0:T(8,128)(2,1)}, bf16[1792,128]{1,0:T(8,128)(2,1)S(1)}, u32[]{:S(2)}, u32[]{:S(2)}) collective-permute-start(bf16[1792,128]{1,0:T(8,128)(2,1)} %collective-permute-done.4.refs_3_), channel_id=1, source_target_pairs={{0,6},{2,0},{4,2},{6,4},{1,7},{3,1},{5,3},{7,5},{8,14},{10,8},{12,... | collective-permute-start | bytes 1376264 | tf_op jit(solution)/shard_map/ppermute | solution.py:338
  68.5 0.0 collective-permute-done.refs_1_
  68.6 8.7 %collective-permute-done.7.refs_6_ = bf16[1792,128]{1,0:T(8,128)(2,1)S(1)} collective-permute-done((bf16[1792,128]{1,0:T(8,128)(2,1)}, bf16[1792,128]{1,0:T(8,128)(2,1)S(1)}, u32[]{:S(2)}, u32[]{:S(2)}) %collective-permute-start.7) | collective-permute-done | bytes 458784 | tf_op jit(solution)/shard_map/ppermute | solution.py:337
  77.2 1.9 collective-permute-done.8.refs_7_
  79.1 0.0 collective-permute-done.5.refs_3_
  79.2 1.2 compare_reduce_fusion
  80.4 0.1 copy.12
  80.5 0.1 add_reduce_fusion
  80.6 1.2 convolution_convert_fusion.1
  81.9 0.0 copy-start.1
  82.0 1.0 broadcast_in_dim.10
  83.0 7.0 %all-to-all-start.1 = ((bf16[16,8,3712]{2,1,0:T(8,128)(2,1)}), bf16[16,8,3712]{2,1,0:T(8,128)(2,1)S(1)}, u32[]{:S(2)}, u32[]{:S(2)}) async-start(bf16[16,8,3712]{2,1,0:T(8,128)(2,1)} %bitcast.14), calls=%async_computation.1 | async-start | bytes 1900544 | tf_op jit(solution)/shard_map/all_to_all | solution.py:372
  90.0 1.9 collective-permute-start.9
  91.9 2.4 %collective-permute-start.10 = (bf16[1792,128]{1,0:T(8,128)(2,1)S(1)}, bf16[1792,128]{1,0:T(8,128)(2,1)S(1)}, u32[]{:S(2)}, u32[]{:S(2)}) collective-permute-start(bf16[1792,128]{1,0:T(8,128)(2,1)S(1)} %collective-permute-done.8.refs_7_), channel_id=1, source_target_pairs={{0,1},{1,0},{2,3},{3,2},{4,5},{5,4},{6,7},{7,6},{8,9},{9,8},{10,11... | collective-permute-start | bytes 1376264 | tf_op jit(solution)/shard_map/ppermute | solution.py:346
  94.3 1.4 collective-permute-done.10.refs_9_
  95.8 9.6 %all-to-all-done.1 = bf16[16,8,3712]{2,1,0:T(8,128)(2,1)S(1)} async-done(((bf16[16,8,3712]{2,1,0:T(8,128)(2,1)}), bf16[16,8,3712]{2,1,0:T(8,128)(2,1)S(1)}, u32[]{:S(2)}, u32[]{:S(2)}) %all-to-all-start.1) | async-done | bytes 950304 | tf_op jit(solution)/shard_map/all_to_all | solution.py:372
  105.3 7.0 %shard_map.97 = bf16[4,128,512]{2,1,0:T(8,128)(2,1)} custom-call(s32[5]{0:T(128)S(1)} %copy-done.1, bf16[128,3712]{1,0:T(8,128)(2,1)S(1)} %bitcast.66, bf16[3584,128]{1,0:T(8,128)(2,1)} %copy-done, bf16[3584,128]{1,0:T(8,128)(2,1)} %collective-permute-done.refs_1_, bf16[3584,128]{1,0:T(8,128)(2,1)} %collective-permute-done.1.refs_0_.refs_2_, ...), custom_call_target="tpu_custom_call" | custom-call | tf_op jit(solution)/shard_map/pallas_call | solution.py:263
  112.3 3.5 %all-to-all-start.2 = ((bf16[4,128,512]{2,1,0:T(8,128)(2,1)}), bf16[4,128,512]{2,1,0:T(8,128)(2,1)S(1)}, u32[]{:S(2)}, u32[]{:S(2)}) async-start(bf16[4,128,512]{2,1,0:T(8,128)(2,1)} %shard_map.97), calls=%async_computation.2 | async-start | bytes 1048576 | tf_op jit(solution)/shard_map/all_to_all | solution.py:390
  115.8 0.1 select_reduce_fusion
  116.0 7.9 %all-to-all-done.2 = bf16[4,128,512]{2,1,0:T(8,128)(2,1)S(1)} async-done(((bf16[4,128,512]{2,1,0:T(8,128)(2,1)}), bf16[4,128,512]{2,1,0:T(8,128)(2,1)S(1)}, u32[]{:S(2)}, u32[]{:S(2)}) %all-to-all-start.2) | async-done | bytes 524320 | tf_op jit(solution)/shard_map/all_to_all | solution.py:390
  123.9 0.1 convert_reduce_fusion.1
  124.0 0.1 multiply_convert_fusion
  124.1 13.3 %all-gather = bf16[512,512]{1,0:T(8,128)(2,1)S(1)} all-gather(bf16[128,512]{1,0:T(8,128)(2,1)S(1)} %pad_maximum_fusion.1), channel_id=2, replica_groups=mesh['node'=16,'expert'=4,'chip'=4,'core'=2] {'chip'}, dimensions={0}, use_global_device_ids=true | all-gather | bytes 655360 | tf_op jit(solution)/shard_map/all_gather | solution.py:397
  137.4 6.0 %shard_map.98 = bf16[128,3712]{1,0:T(8,128)(2,1)S(1)} custom-call(s32[5]{0:T(128)S(1)} %copy-done.1, bf16[128,3712]{1,0:T(8,128)(2,1)S(1)} %bitcast.68, bf16[4,128,512]{2,1,0:T(8,128)(2,1)S(1)} %bitcast.70, bf16[3584,128]{1,0:T(8,128)(2,1)} %copy-done, bf16[3584,128]{1,0:T(8,128)(2,1)} %collective-permute-done.refs_1_, ...), custom_call_target="tpu_custom_call" | custom-call | tf_op jit(solution)/shard_map/pallas_call | solution.py:263
  143.4 15.1 %all_to_all.25 = bf16[16,8,3712]{2,1,0:T(8,128)(2,1)S(1)} all-to-all(bf16[16,8,3712]{2,1,0:T(8,128)(2,1)S(1)} %bitcast.69), channel_id=1, replica_groups=mesh['node'=16,'expert'=4,'chip'=4,'core'=2] {'expert','chip'}, dimensions={0} | all-to-all | bytes 1900544 | tf_op jit(solution)/shard_map/all_to_all | solution.py:411
  158.5 0.1 convert_reduce_fusion
  158.8 0.3 convolution_convert_fusion
  159.2 0.1 copy.14
  159.3 35.3 %all_to_all.26.home = bf16[16,120,128]{2,1,0:T(8,128)(2,1)S(1)} all-to-all(bf16[16,120,128]{2,1,0:T(8,128)(2,1)S(1)} %bitcast.73), channel_id=1, replica_groups=mesh['node'=16,'expert'=4,'chip'=4,'core'=2] {'node'}, dimensions={0} | all-to-all | bytes 983040 | tf_op jit(solution)/shard_map/all_to_all | solution.py:428
  194.5 1.7 shard_map.99
  (35 shorter events, 0.3 us)
Async XLA Ops:
  0.7 16.2 %copy-start.2 = (bf16[4,2,2]{0,2,1:T(2,128)(2,1)S(1)}, bf16[4,2,2]{0,2,1:T(2,128)(2,1)}, u32[]{:S(2)}) copy-start(bf16[4,2,2]{0,2,1:T(2,128)(2,1)} %param.11) | copy-start | bytes 100
  17.0 40.2 %copy-start = (bf16[3584,128]{1,0:T(8,128)(2,1)}, bf16[3584,128]{1,0:T(8,128)(2,1)S(1)}, u32[]{:S(2)}) copy-start(bf16[3584,128]{1,0:T(8,128)(2,1)S(1)} %get-tuple-element.48.refs_0_) | copy-start | bytes 2752516
  18.9 37.1 %collective-permute-start.1 = (bf16[3584,128]{1,0:T(8,128)(2,1)S(1)}, bf16[3584,128]{1,0:T(8,128)(2,1)}, u32[]{:S(2)}, u32[]{:S(2)}) collective-permute-start(bf16[3584,128]{1,0:T(8,128)(2,1)S(1)} %get-tuple-element.38), channel_id=1, source_target_pairs={{0,2},{2,4},{4,6},{6,0},{1,3},{3,5},{5,7},{7,1},{8,10},{10,12},{12... | collective-permute-start | bytes 2752520 | tf_op jit(solution)/shard_map/ppermute | solution.py:327
  22.3 33.6 %collective-permute-start.2 = (bf16[3584,128]{1,0:T(8,128)(2,1)S(1)}, bf16[3584,128]{1,0:T(8,128)(2,1)}, u32[]{:S(2)}, u32[]{:S(2)}) collective-permute-start(bf16[3584,128]{1,0:T(8,128)(2,1)S(1)} %get-tuple-element.39), channel_id=1, source_target_pairs={{0,6},{2,0},{4,2},{6,4},{1,7},{3,1},{5,3},{7,5},{8,14},{10,8},{12,... | collective-permute-start | bytes 2752520 | tf_op jit(solution)/shard_map/ppermute | solution.py:328
  25.9 28.1 %collective-permute-start.3 = (bf16[1792,128]{1,0:T(8,128)(2,1)}, bf16[1792,128]{1,0:T(8,128)(2,1)}, u32[]{:S(2)}, u32[]{:S(2)}) collective-permute-start(bf16[1792,128]{1,0:T(8,128)(2,1)} %get-tuple-element.40), channel_id=1, source_target_pairs={{0,2},{2,4},{4,6},{6,0},{1,3},{3,5},{5,7},{7,1},{8,10},{10,12},{12... | collective-permute-start | bytes 1376264 | tf_op jit(solution)/shard_map/ppermute | solution.py:325
  28.1 27.8 %collective-permute-start.4 = (bf16[1792,128]{1,0:T(8,128)(2,1)S(1)}, bf16[1792,128]{1,0:T(8,128)(2,1)}, u32[]{:S(2)}, u32[]{:S(2)}) collective-permute-start(bf16[1792,128]{1,0:T(8,128)(2,1)S(1)} %get-tuple-element.41), channel_id=1, source_target_pairs={{0,6},{2,0},{4,2},{6,4},{1,7},{3,1},{5,3},{7,5},{8,14},{10,8},{12,... | collective-permute-start | bytes 1376264 | tf_op jit(solution)/shard_map/ppermute | solution.py:326
  33.0 46.1 %all-to-all-start = ((bf16[16,120,128]{2,1,0:T(8,128)(2,1)}), bf16[16,120,128]{2,1,0:T(8,128)(2,1)}, u32[]{:S(2)}, u32[]{:S(2)}) async-start(bf16[16,120,128]{2,1,0:T(8,128)(2,1)} %shard_map.95), calls=%async_computation | async-start | bytes 983040 | tf_op jit(solution)/shard_map/all_to_all | solution.py:342
  48.2 20.3 %collective-permute-start = (bf16[3584,128]{1,0:T(8,128)(2,1)S(1)}, bf16[3584,128]{1,0:T(8,128)(2,1)}, u32[]{:S(2)}, u32[]{:S(2)}) collective-permute-start(bf16[3584,128]{1,0:T(8,128)(2,1)S(1)} %get-tuple-element.48.refs_0_), channel_id=1, source_target_pairs={{0,1},{1,0},{2,3},{3,2},{4,5},{5,4},{6,7},{7,6},{8,9},{9,8},{10,11... | collective-permute-start | bytes 2752520 | tf_op jit(solution)/shard_map/ppermute | solution.py:329
  57.1 22.0 %collective-permute-start.5 = (bf16[3584,128]{1,0:T(8,128)(2,1)}, bf16[3584,128]{1,0:T(8,128)(2,1)S(1)}, u32[]{:S(2)}, u32[]{:S(2)}) collective-permute-start(bf16[3584,128]{1,0:T(8,128)(2,1)} %collective-permute-done.1.refs_0_.refs_2_), channel_id=1, source_target_pairs={{0,1},{1,0},{2,3},{3,2},{4,5},{5,4},{6,7},{7,6},{8,9},{9,8},{10,11... | collective-permute-start | bytes 2752520 | tf_op jit(solution)/shard_map/ppermute | solution.py:341
  59.1 20.1 %collective-permute-start.6 = (bf16[3584,128]{1,0:T(8,128)(2,1)}, bf16[3584,128]{1,0:T(8,128)(2,1)}, u32[]{:S(2)}, u32[]{:S(2)}) collective-permute-start(bf16[3584,128]{1,0:T(8,128)(2,1)} %collective-permute-done.2.refs_1_.refs_4_), channel_id=1, source_target_pairs={{0,1},{1,0},{2,3},{3,2},{4,5},{5,4},{6,7},{7,6},{8,9},{9,8},{10,11... | collective-permute-start | bytes 2752520 | tf_op jit(solution)/shard_map/ppermute | solution.py:341
  61.5 15.8 %collective-permute-start.7 = (bf16[1792,128]{1,0:T(8,128)(2,1)}, bf16[1792,128]{1,0:T(8,128)(2,1)S(1)}, u32[]{:S(2)}, u32[]{:S(2)}) collective-permute-start(bf16[1792,128]{1,0:T(8,128)(2,1)} %collective-permute-done.3.refs_2_), channel_id=1, source_target_pairs={{0,2},{2,4},{4,6},{6,0},{1,3},{3,5},{5,7},{7,1},{8,10},{10,12},{12... | collective-permute-start | bytes 1376264 | tf_op jit(solution)/shard_map/ppermute | solution.py:337
  64.9 14.3 %collective-permute-start.8 = (bf16[1792,128]{1,0:T(8,128)(2,1)}, bf16[1792,128]{1,0:T(8,128)(2,1)S(1)}, u32[]{:S(2)}, u32[]{:S(2)}) collective-permute-start(bf16[1792,128]{1,0:T(8,128)(2,1)} %collective-permute-done.4.refs_3_), channel_id=1, source_target_pairs={{0,6},{2,0},{4,2},{6,4},{1,7},{3,1},{5,3},{7,5},{8,14},{10,8},{12,... | collective-permute-start | bytes 1376264 | tf_op jit(solution)/shard_map/ppermute | solution.py:338
  77.2 12.7 %copy-start.4 = (bf16[1792,128]{1,0:T(8,128)(2,1)}, bf16[1792,128]{1,0:T(8,128)(2,1)S(1)}, u32[]{:S(2)}) copy-start(bf16[1792,128]{1,0:T(8,128)(2,1)S(1)} %collective-permute-done.7.refs_6_) | copy-start | bytes 1376260
  79.1 26.2 %copy-start.5 = (bf16[1792,128]{1,0:T(8,128)(2,1)}, bf16[1792,128]{1,0:T(8,128)(2,1)S(1)}, u32[]{:S(2)}) copy-start(bf16[1792,128]{1,0:T(8,128)(2,1)S(1)} %collective-permute-done.8.refs_7_) | copy-start | bytes 1376260
  79.1 3.8 %copy-start.3 = (bf16[3584,128]{1,0:T(8,128)(2,1)}, bf16[3584,128]{1,0:T(8,128)(2,1)S(1)}, u32[]{:S(2)}) copy-start(bf16[3584,128]{1,0:T(8,128)(2,1)S(1)} %collective-permute-done.5.refs_3_) | copy-start | bytes 2752516
  81.9 23.4 %copy-start.1 = (s32[5]{0:T(128)S(1)}, s32[5]{0:T(128)}, u32[]{:S(2)}) copy-start(s32[5]{0:T(128)} %shard_map.96.scalars) | copy-start | bytes 64
  83.0 22.3 %all-to-all-start.1 = ((bf16[16,8,3712]{2,1,0:T(8,128)(2,1)}), bf16[16,8,3712]{2,1,0:T(8,128)(2,1)S(1)}, u32[]{:S(2)}, u32[]{:S(2)}) async-start(bf16[16,8,3712]{2,1,0:T(8,128)(2,1)} %bitcast.14), calls=%async_computation.1 | async-start | bytes 1900544 | tf_op jit(solution)/shard_map/all_to_all | solution.py:372
  90.0 4.3 %collective-permute-start.9 = (bf16[1792,128]{1,0:T(8,128)(2,1)S(1)}, bf16[1792,128]{1,0:T(8,128)(2,1)S(1)}, u32[]{:S(2)}, u32[]{:S(2)}) collective-permute-start(bf16[1792,128]{1,0:T(8,128)(2,1)S(1)} %collective-permute-done.7.refs_6_), channel_id=1, source_target_pairs={{0,1},{1,0},{2,3},{3,2},{4,5},{5,4},{6,7},{7,6},{8,9},{9,8},{10,11... | collective-permute-start | bytes 1376264 | tf_op jit(solution)/shard_map/ppermute | solution.py:346
  91.9 3.8 %collective-permute-start.10 = (bf16[1792,128]{1,0:T(8,128)(2,1)S(1)}, bf16[1792,128]{1,0:T(8,128)(2,1)S(1)}, u32[]{:S(2)}, u32[]{:S(2)}) collective-permute-start(bf16[1792,128]{1,0:T(8,128)(2,1)S(1)} %collective-permute-done.8.refs_7_), channel_id=1, source_target_pairs={{0,1},{1,0},{2,3},{3,2},{4,5},{5,4},{6,7},{7,6},{8,9},{9,8},{10,11... | collective-permute-start | bytes 1376264 | tf_op jit(solution)/shard_map/ppermute | solution.py:346
  112.3 11.5 %all-to-all-start.2 = ((bf16[4,128,512]{2,1,0:T(8,128)(2,1)}), bf16[4,128,512]{2,1,0:T(8,128)(2,1)S(1)}, u32[]{:S(2)}, u32[]{:S(2)}) async-start(bf16[4,128,512]{2,1,0:T(8,128)(2,1)} %shard_map.97), calls=%async_computation.2 | async-start | bytes 1048576 | tf_op jit(solution)/shard_map/all_to_all | solution.py:390

commit v11 on v10

--- a/solution.py
+++ b/solution.py
@@ -149,16 +149,13 @@
     return found
 
 
-def run_ahead(groups):
-    for group in groups[:2]:
+def arrivals(groups):
+    for group in groups:
         for copy in group:
             copy.start()
-    for i, group in enumerate(groups):
+    for group in groups:
         for copy in group:
             copy.wait()
-        if i + 2 < len(groups):
-            for copy in groups[i + 2]:
-                copy.start()
         yield
 
 
@@ -187,7 +184,7 @@
     count, _, hidden = held.shape
     wide = held.shape[1] // 2
     (copies,) = fetch(blocks, held, sems, ())
-    arrived = run_ahead([flat(copies[i : i + CORES]) for i in range(0, count, CORES)])
+    arrived = arrivals([flat(copies[i : i + CORES]) for i in range(0, count, CORES)])
     x, dy = rows[:, :wide], rows[:, wide : 2 * wide]
     for i in range(count // CORES):
         pair = range(CORES * i, CORES * (i + 1))
@@ -211,7 +208,7 @@
     wide = held.shape[1] // 2
     step = 2 * LANES
     cuts = tuple(range(2 * step, wide, 2 * step))
-    arrived = run_ahead([flat(cut) for cut in fetch(blocks, held, sems, cuts)])
+    arrived = arrivals([flat(cut) for cut in fetch(blocks, held, sems, cuts)])
     chips = many // CORES
     count = rows.shape[0]
     lane = lax.broadcasted_iota(jnp.int32, (count, LANES), 1)
@@ -251,7 +248,7 @@
     result[:, 2 * wide :] = jnp.where(mine, inner, 0.0).astype(result.dtype)
 
 
-def call(kernel, shapes, scalars, *operands, hbm=0, scratch=(), out_hbm=False, loose=0):
+def call(kernel, shapes, scalars, *operands, hbm=0, scratch=(), loose=0):
     small, near, far = (
         pl.BlockSpec(memory_space=space) for space in (pltpu.SMEM, pltpu.VMEM, pltpu.HBM)
     )
@@ -264,7 +261,7 @@
         kernel,
         out_shape=[jax.ShapeDtypeStruct(shape, jnp.bfloat16) for shape in shapes],
         in_specs=[small] * len(scalars) + [near] * count + [far] * (hbm - loose) + [anywhere] * loose,
-        out_specs=[far if out_hbm else near] * len(shapes),
+        out_specs=[near] * len(shapes),
         scratch_shapes=scratch,
         compiler_params=pltpu.CompilerParams(vmem_limit_bytes=24 * 2**20),
     )(*scalars, *operands[:count], *held)
@@ -316,7 +313,6 @@
         down_weight,
         hbm=2,
         scratch=[pltpu.SemaphoreType.DMA((chips * (wide // LANES + 1),))],
-        out_hbm=True,
     )
     here, ahead, behind, far_up, far_down, sent = lax.optimization_barrier(
         (here, ahead, behind, far_up, far_down, sent)
@@ -330,18 +326,17 @@
     scalars = jnp.stack(
         [expert, chip, (chip + chips - 1) % chips, (chip + 1) % chips, (chip + 2) % chips]
     ).astype(jnp.int32)
-    scalars = mark(scalars, ahead, behind, far_up, far_down)
-    ahead, behind, far_up, far_down, scalars = lax.optimization_barrier(
-        (ahead, behind, far_up, far_down, scalars)
-    )
     far_up = lax.ppermute(far_up, "chip", ahead_of)
     far_down = lax.ppermute(far_down, "chip", behind_of)
-    near = (here, here_too)
+    scalars = mark(scalars, ahead, behind, far_up, far_down)
+    recv = lax.all_to_all(sent, "node", split_axis=0, concat_axis=0, tiled=True)
+    recv, here_too, ahead, behind, far_up, far_down, scalars = lax.optimization_barrier(
+        (recv, here_too, ahead, behind, far_up, far_down, scalars)
+    )
+    blocks = (here, here_too)
     for block in (ahead, behind):
-        near += (block, lax.ppermute(block, "core", swap))
-    recv = lax.all_to_all(sent, "node", split_axis=0, concat_axis=0, tiled=True)
-    recv, near, far_up, far_down = lax.optimization_barrier((recv, near, far_up, far_down))
-    blocks = near + (far_up, far_down)
+        blocks += (block, lax.ppermute(block, "core", swap))
+    blocks += (far_up, far_down)
     for block in (far_up, far_down):
         blocks += (lax.ppermute(block, "core", swap),)
     held = [

time: 197 us -> 182 us (0.924)
  the two profiles are of different devices: /device:TPU:32 before, /device:TPU:64 now
where the time goes in v11:
time: 182 us; the launch traced here: 181 us
  blocking collectives  57.6 us (32%)
  starting transfers between devices  54.6 us (30%)
  waiting for transfers between devices  43.6 us (24%)
  Pallas kernels  19.8 us (11%)
  local copies, waits for them, and re-layouts  2.91 us (2%)
    all_to_all x1, blocking collectives, per_device(): lax.all_to_all(expanded, 'node', split_axis=0, concat_axis=0, tiled=True)  29.3 us
    pallas_call x5, Pallas kernels, call(): pl.pallas_call(kernel, out_shape=[jax.ShapeDtypeStruct(shape, jnp.bfloat1...  18.6 us
    all_to_all x1, blocking collectives, per_device(): lax.all_to_all(result.reshape(experts * chips, pairs, -1), ('expert', 'ch...  15.6 us
    all_to_all x1, waiting for transfers between devices, per_device(): recv = lax.all_to_all(sent, 'node', split_axis=0, concat_axis=0, tiled=True)  15 us
    all_to_all x1, starting transfers between devices, per_device(): recv = lax.all_to_all(sent, 'node', split_axis=0, concat_axis=0, tiled=True)  14.8 us
    all_gather x1, blocking collectives, per_device(): lax.all_gather(jnp.concatenate([active, grad_pre], 1), 'chip', axis=0)  12.8 us
    all_to_all x1, waiting for transfers between devices, per_device(): lax.all_to_all(spread, ('expert', 'chip'), split_axis=0, concat_axis=0, t...  10.6 us
    ppermute x2, starting transfers between devices, per_device(): far_down = lax.ppermute(far_down, 'chip', behind_of)  8.5 us
  transfers between devices with their start and end apart: 14, of which 7 were waited for; matrix products, arithmetic and copies ran while one was open for 1% of the time, Pallas kernels for 1%

profile of v11, /device:TPU:64, one launch (start us, length us, event | category | flops | bytes accessed | tf_op | source)
XLA Modules:
  0.0 181.2 jit_solution(7718817584284943113)
XLA Ops:
  0.7 0.1 pad_add_fusion.chips
  0.8 3.1 %shard_map.94 = (bf16[3584,128]{1,0:T(8,128)(2,1)S(1)}, bf16[3584,128]{1,0:T(8,128)(2,1)S(1)}, bf16[3584,128]{1,0:T(8,128)(2,1)S(1)}, bf16[1792,128]{1,0:T(8,128)(2,1)S(1)}, bf16[1792,128]{1,0:T(8,128)(2,1)S(1)}) custom-call(s32[4]{0:T(128)S(1)} %pad_add_fusion.chips, bf16[7168,128]{1,0:T(8,128)(2,1)} %up.1, bf16[128,7168]{1,0:T(8,128)(2,1)} %down.1), custom_call_target="tpu_custom_call" | custom-call | tf_op jit(solution)/shard_map/pallas_call | solution.py:260
  3.8 1.9 %shard_map.95 = bf16[16,120,128]{2,1,0:T(8,128)(2,1)} custom-call(bf16[2,2,4]{2,1,0:T(2,128)(2,1)S(1)} %bitcast.71, s32[2,4]{1,0:T(2,128)} %bitcast.77, s32[2,2,4]{2,1,0:T(2,128)} %bitcast.75, bf16[4,7168]{1,0:T(4,128)(2,1)} %tokens.1, bf16[4,7168]{1,0:T(4,128)(2,1)} %cotangent.1), custom_call_target="tpu_custom_call" | custom-call | tf_op jit(solution)/shard_map/pallas_call | solution.py:260
  5.8 3.4 %collective-permute-start.3 = (bf16[1792,128]{1,0:T(8,128)(2,1)S(1)}, bf16[1792,128]{1,0:T(8,128)(2,1)}, u32[]{:S(2)}, u32[]{:S(2)}) collective-permute-start(bf16[1792,128]{1,0:T(8,128)(2,1)S(1)} %get-tuple-element.33), channel_id=1, source_target_pairs={{0,2},{2,4},{4,6},{6,0},{1,3},{3,5},{5,7},{7,1},{8,10},{10,12},{12... | collective-permute-start | bytes 1376264 | tf_op jit(solution)/shard_map/ppermute | solution.py:321
  9.2 3.7 %collective-permute-start.5 = (bf16[1792,128]{1,0:T(8,128)(2,1)S(1)}, bf16[1792,128]{1,0:T(8,128)(2,1)}, u32[]{:S(2)}, u32[]{:S(2)}) collective-permute-start(bf16[1792,128]{1,0:T(8,128)(2,1)S(1)} %get-tuple-element.34), channel_id=1, source_target_pairs={{0,6},{2,0},{4,2},{6,4},{1,7},{3,1},{5,3},{7,5},{8,14},{10,8},{12,... | collective-permute-start | bytes 1376264 | tf_op jit(solution)/shard_map/ppermute | solution.py:322
  12.8 2.2 %collective-permute-start.1 = (bf16[3584,128]{1,0:T(8,128)(2,1)S(1)}, bf16[3584,128]{1,0:T(8,128)(2,1)}, u32[]{:S(2)}, u32[]{:S(2)}) collective-permute-start(bf16[3584,128]{1,0:T(8,128)(2,1)S(1)} %get-tuple-element.31), channel_id=1, source_target_pairs={{0,2},{2,4},{4,6},{6,0},{1,3},{3,5},{5,7},{7,1},{8,10},{10,12},{12... | collective-permute-start | bytes 2752520 | tf_op jit(solution)/shard_map/ppermute | solution.py:323
  15.0 4.9 %collective-permute-start.2 = (bf16[3584,128]{1,0:T(8,128)(2,1)S(1)}, bf16[3584,128]{1,0:T(8,128)(2,1)}, u32[]{:S(2)}, u32[]{:S(2)}) collective-permute-start(bf16[3584,128]{1,0:T(8,128)(2,1)S(1)} %get-tuple-element.32), channel_id=1, source_target_pairs={{0,6},{2,0},{4,2},{6,4},{1,7},{3,1},{5,3},{7,5},{8,14},{10,8},{12,... | collective-permute-start | bytes 2752520 | tf_op jit(solution)/shard_map/ppermute | solution.py:324
  19.9 2.5 %collective-permute-done.3 = bf16[1792,128]{1,0:T(8,128)(2,1)} collective-permute-done((bf16[1792,128]{1,0:T(8,128)(2,1)S(1)}, bf16[1792,128]{1,0:T(8,128)(2,1)}, u32[]{:S(2)}, u32[]{:S(2)}) %collective-permute-start.3) | collective-permute-done | bytes 458784 | tf_op jit(solution)/shard_map/ppermute | solution.py:321
  22.4 2.2 %collective-permute-start.4 = (bf16[1792,128]{1,0:T(8,128)(2,1)}, bf16[1792,128]{1,0:T(8,128)(2,1)}, u32[]{:S(2)}, u32[]{:S(2)}) collective-permute-start(bf16[1792,128]{1,0:T(8,128)(2,1)} %collective-permute-done.3), channel_id=1, source_target_pairs={{0,2},{2,4},{4,6},{6,0},{1,3},{3,5},{5,7},{7,1},{8,10},{10,12},{12... | collective-permute-start | bytes 1376264 | tf_op jit(solution)/shard_map/ppermute | solution.py:329
  24.6 0.0 collective-permute-done.5
  24.6 4.8 %collective-permute-start.6 = (bf16[1792,128]{1,0:T(8,128)(2,1)}, bf16[1792,128]{1,0:T(8,128)(2,1)}, u32[]{:S(2)}, u32[]{:S(2)}) collective-permute-start(bf16[1792,128]{1,0:T(8,128)(2,1)} %collective-permute-done.5), channel_id=1, source_target_pairs={{0,6},{2,0},{4,2},{6,4},{1,7},{3,1},{5,3},{7,5},{8,14},{10,8},{12,... | collective-permute-start | bytes 1376264 | tf_op jit(solution)/shard_map/ppermute | solution.py:330
  29.5 14.8 %all-to-all-start = ((bf16[16,120,128]{2,1,0:T(8,128)(2,1)}), bf16[16,120,128]{2,1,0:T(8,128)(2,1)S(1)}, u32[]{:S(2)}, u32[]{:S(2)}) async-start(bf16[16,120,128]{2,1,0:T(8,128)(2,1)} %shard_map.95), calls=%async_computation | async-start | bytes 983040 | tf_op jit(solution)/shard_map/all_to_all | solution.py:332
  44.2 1.9 %collective-permute-start = (bf16[3584,128]{1,0:T(8,128)(2,1)S(1)}, bf16[3584,128]{1,0:T(8,128)(2,1)}, u32[]{:S(2)}, u32[]{:S(2)}) collective-permute-start(bf16[3584,128]{1,0:T(8,128)(2,1)S(1)} %get-tuple-element.30.refs_0_), channel_id=1, source_target_pairs={{0,1},{1,0},{2,3},{3,2},{4,5},{5,4},{6,7},{7,6},{8,9},{9,8},{10,11... | collective-permute-start | bytes 2752520 | tf_op jit(solution)/shard_map/ppermute | solution.py:325
  46.2 0.7 stack.49.scalars
  46.8 3.9 %collective-permute-done.4.refs_2_.refs_6_ = bf16[1792,128]{1,0:T(8,128)(2,1)} collective-permute-done((bf16[1792,128]{1,0:T(8,128)(2,1)}, bf16[1792,128]{1,0:T(8,128)(2,1)}, u32[]{:S(2)}, u32[]{:S(2)}) %collective-permute-start.4) | collective-permute-done | bytes 458784 | tf_op jit(solution)/shard_map/ppermute | solution.py:329
  50.7 1.9 %collective-permute-done.6.refs_3_.refs_7_ = bf16[1792,128]{1,0:T(8,128)(2,1)} collective-permute-done((bf16[1792,128]{1,0:T(8,128)(2,1)}, bf16[1792,128]{1,0:T(8,128)(2,1)}, u32[]{:S(2)}, u32[]{:S(2)}) %collective-permute-start.6) | collective-permute-done | bytes 458784 | tf_op jit(solution)/shard_map/ppermute | solution.py:330
  52.6 1.2 shard_map.96.scalars
  53.8 0.0 collective-permute-done.refs_1_
  53.9 15.0 %all-to-all-done = bf16[16,120,128]{2,1,0:T(8,128)(2,1)S(1)} async-done(((bf16[16,120,128]{2,1,0:T(8,128)(2,1)}), bf16[16,120,128]{2,1,0:T(8,128)(2,1)S(1)}, u32[]{:S(2)}, u32[]{:S(2)}) %all-to-all-start) | async-done | bytes 491552 | tf_op jit(solution)/shard_map/all_to_all | solution.py:332
  68.9 0.4 compare_reduce_fusion
  69.2 0.1 copy.12
  69.4 0.1 add_reduce_fusion
  69.5 0.2 convolution_convert_fusion.1
  69.8 1.9 %collective-permute-start.7 = (bf16[3584,128]{1,0:T(8,128)(2,1)}, bf16[3584,128]{1,0:T(8,128)(2,1)S(1)}, u32[]{:S(2)}, u32[]{:S(2)}) collective-permute-start(bf16[3584,128]{1,0:T(8,128)(2,1)} %collective-permute-done.1.refs_0_.refs_2_), channel_id=1, source_target_pairs={{0,1},{1,0},{2,3},{3,2},{4,5},{5,4},{6,7},{7,6},{8,9},{9,8},{10,11... | collective-permute-start | bytes 2752520 | tf_op jit(solution)/shard_map/ppermute | solution.py:338
  71.7 2.4 %collective-permute-start.8 = (bf16[3584,128]{1,0:T(8,128)(2,1)}, bf16[3584,128]{1,0:T(8,128)(2,1)}, u32[]{:S(2)}, u32[]{:S(2)}) collective-permute-start(bf16[3584,128]{1,0:T(8,128)(2,1)} %collective-permute-done.2.refs_1_.refs_4_), channel_id=1, source_target_pairs={{0,1},{1,0},{2,3},{3,2},{4,5},{5,4},{6,7},{7,6},{8,9},{9,8},{10,11... | collective-permute-start | bytes 2752520 | tf_op jit(solution)/shard_map/ppermute | solution.py:338
  74.1 0.0 copy-start.1
  74.2 1.0 broadcast_in_dim.10
  75.2 4.6 %all-to-all-start.1 = ((bf16[16,8,3712]{2,1,0:T(8,128)(2,1)}), bf16[16,8,3712]{2,1,0:T(8,128)(2,1)S(1)}, u32[]{:S(2)}, u32[]{:S(2)}) async-start(bf16[16,8,3712]{2,1,0:T(8,128)(2,1)} %bitcast.14), calls=%async_computation.1 | async-start | bytes 1900544 | tf_op jit(solution)/shard_map/all_to_all | solution.py:367
  79.8 1.9 %collective-permute-start.9 = (bf16[1792,128]{1,0:T(8,128)(2,1)}, bf16[1792,128]{1,0:T(8,128)(2,1)S(1)}, u32[]{:S(2)}, u32[]{:S(2)}) collective-permute-start(bf16[1792,128]{1,0:T(8,128)(2,1)} %collective-permute-done.4.refs_2_.refs_6_), channel_id=1, source_target_pairs={{0,1},{1,0},{2,3},{3,2},{4,5},{5,4},{6,7},{7,6},{8,9},{9,8},{10,11... | collective-permute-start | bytes 1376264 | tf_op jit(solution)/shard_map/ppermute | solution.py:341
  81.8 2.4 %collective-permute-start.10 = (bf16[1792,128]{1,0:T(8,128)(2,1)}, bf16[1792,128]{1,0:T(8,128)(2,1)S(1)}, u32[]{:S(2)}, u32[]{:S(2)}) collective-permute-start(bf16[1792,128]{1,0:T(8,128)(2,1)} %collective-permute-done.6.refs_3_.refs_7_), channel_id=1, source_target_pairs={{0,1},{1,0},{2,3},{3,2},{4,5},{5,4},{6,7},{7,6},{8,9},{9,8},{10,11... | collective-permute-start | bytes 1376264 | tf_op jit(solution)/shard_map/ppermute | solution.py:341
  84.2 0.0 collective-permute-done.9.refs_8_
  84.2 1.6 collective-permute-done.10.refs_9_
  85.8 10.6 %all-to-all-done.1 = bf16[16,8,3712]{2,1,0:T(8,128)(2,1)S(1)} async-done(((bf16[16,8,3712]{2,1,0:T(8,128)(2,1)}), bf16[16,8,3712]{2,1,0:T(8,128)(2,1)S(1)}, u32[]{:S(2)}, u32[]{:S(2)}) %all-to-all-start.1) | async-done | bytes 950304 | tf_op jit(solution)/shard_map/all_to_all | solution.py:367
  96.5 0.9 copy-done.3
  97.4 6.5 %shard_map.97 = bf16[4,128,512]{2,1,0:T(8,128)(2,1)} custom-call(s32[5]{0:T(128)S(1)} %copy-done.1, bf16[128,3712]{1,0:T(8,128)(2,1)S(1)} %bitcast.66, bf16[3584,128]{1,0:T(8,128)(2,1)} %copy-done, bf16[3584,128]{1,0:T(8,128)(2,1)} %collective-permute-done.refs_1_, bf16[3584,128]{1,0:T(8,128)(2,1)} %collective-permute-done.1.refs_0_.refs_2_, ...), custom_call_target="tpu_custom_call" | custom-call | tf_op jit(solution)/shard_map/pallas_call | solution.py:260
  103.9 3.5 %all-to-all-start.2 = ((bf16[4,128,512]{2,1,0:T(8,128)(2,1)}), bf16[4,128,512]{2,1,0:T(8,128)(2,1)S(1)}, u32[]{:S(2)}, u32[]{:S(2)}) async-start(bf16[4,128,512]{2,1,0:T(8,128)(2,1)} %shard_map.97), calls=%async_computation.2 | async-start | bytes 1048576 | tf_op jit(solution)/shard_map/all_to_all | solution.py:385
  107.4 0.1 select_reduce_fusion
  107.5 8.0 %all-to-all-done.2 = bf16[4,128,512]{2,1,0:T(8,128)(2,1)S(1)} async-done(((bf16[4,128,512]{2,1,0:T(8,128)(2,1)}), bf16[4,128,512]{2,1,0:T(8,128)(2,1)S(1)}, u32[]{:S(2)}, u32[]{:S(2)}) %all-to-all-start.2) | async-done | bytes 524320 | tf_op jit(solution)/shard_map/all_to_all | solution.py:385
  115.5 0.1 convert_reduce_fusion.1
  115.6 0.1 multiply_convert_fusion
  115.7 12.8 %all-gather = bf16[512,512]{1,0:T(8,128)(2,1)S(1)} all-gather(bf16[128,512]{1,0:T(8,128)(2,1)S(1)} %pad_maximum_fusion.1), channel_id=2, replica_groups=mesh['node'=16,'expert'=4,'chip'=4,'core'=2] {'chip'}, dimensions={0}, use_global_device_ids=true | all-gather | bytes 655360 | tf_op jit(solution)/shard_map/all_gather | solution.py:392
  128.5 5.4 %shard_map.98 = bf16[128,3712]{1,0:T(8,128)(2,1)S(1)} custom-call(s32[5]{0:T(128)S(1)} %copy-done.1, bf16[128,3712]{1,0:T(8,128)(2,1)S(1)} %bitcast.68, bf16[4,128,512]{2,1,0:T(8,128)(2,1)S(1)} %bitcast.70, bf16[3584,128]{1,0:T(8,128)(2,1)} %copy-done, bf16[3584,128]{1,0:T(8,128)(2,1)} %collective-permute-done.refs_1_, ...), custom_call_target="tpu_custom_call" | custom-call | tf_op jit(solution)/shard_map/pallas_call | solution.py:260
  133.9 15.6 %all_to_all.25 = bf16[16,8,3712]{2,1,0:T(8,128)(2,1)S(1)} all-to-all(bf16[16,8,3712]{2,1,0:T(8,128)(2,1)S(1)} %bitcast.69), channel_id=1, replica_groups=mesh['node'=16,'expert'=4,'chip'=4,'core'=2] {'expert','chip'}, dimensions={0} | all-to-all | bytes 1900544 | tf_op jit(solution)/shard_map/all_to_all | solution.py:406
  149.5 0.1 convert_reduce_fusion
  149.8 0.3 convolution_convert_fusion
  150.2 0.1 copy.14
  150.2 29.3 %all_to_all.26.home = bf16[16,120,128]{2,1,0:T(8,128)(2,1)S(1)} all-to-all(bf16[16,120,128]{2,1,0:T(8,128)(2,1)S(1)} %bitcast.74), channel_id=1, replica_groups=mesh['node'=16,'expert'=4,'chip'=4,'core'=2] {'node'}, dimensions={0} | all-to-all | bytes 983040 | tf_op jit(solution)/shard_map/all_to_all | solution.py:423
  179.5 1.7 shard_map.99
  (31 shorter events, 0.3 us)
Async XLA Ops:
  0.7 3.1 %copy-start.2 = (bf16[4,2,2]{0,2,1:T(2,128)(2,1)S(1)}, bf16[4,2,2]{0,2,1:T(2,128)(2,1)}, u32[]{:S(2)}) copy-start(bf16[4,2,2]{0,2,1:T(2,128)(2,1)} %param.11) | copy-start | bytes 100
  3.8 50.0 %copy-start = (bf16[3584,128]{1,0:T(8,128)(2,1)}, bf16[3584,128]{1,0:T(8,128)(2,1)S(1)}, u32[]{:S(2)}) copy-start(bf16[3584,128]{1,0:T(8,128)(2,1)S(1)} %get-tuple-element.30.refs_0_) | copy-start | bytes 2752516
  5.8 16.6 %collective-permute-start.3 = (bf16[1792,128]{1,0:T(8,128)(2,1)S(1)}, bf16[1792,128]{1,0:T(8,128)(2,1)}, u32[]{:S(2)}, u32[]{:S(2)}) collective-permute-start(bf16[1792,128]{1,0:T(8,128)(2,1)S(1)} %get-tuple-element.33), channel_id=1, source_target_pairs={{0,2},{2,4},{4,6},{6,0},{1,3},{3,5},{5,7},{7,1},{8,10},{10,12},{12... | collective-permute-start | bytes 1376264 | tf_op jit(solution)/shard_map/ppermute | solution.py:321
  9.2 15.4 %collective-permute-start.5 = (bf16[1792,128]{1,0:T(8,128)(2,1)S(1)}, bf16[1792,128]{1,0:T(8,128)(2,1)}, u32[]{:S(2)}, u32[]{:S(2)}) collective-permute-start(bf16[1792,128]{1,0:T(8,128)(2,1)S(1)} %get-tuple-element.34), channel_id=1, source_target_pairs={{0,6},{2,0},{4,2},{6,4},{1,7},{3,1},{5,3},{7,5},{8,14},{10,8},{12,... | collective-permute-start | bytes 1376264 | tf_op jit(solution)/shard_map/ppermute | solution.py:322
  12.8 39.8 %collective-permute-start.1 = (bf16[3584,128]{1,0:T(8,128)(2,1)S(1)}, bf16[3584,128]{1,0:T(8,128)(2,1)}, u32[]{:S(2)}, u32[]{:S(2)}) collective-permute-start(bf16[3584,128]{1,0:T(8,128)(2,1)S(1)} %get-tuple-element.31), channel_id=1, source_target_pairs={{0,2},{2,4},{4,6},{6,0},{1,3},{3,5},{5,7},{7,1},{8,10},{10,12},{12... | collective-permute-start | bytes 2752520 | tf_op jit(solution)/shard_map/ppermute | solution.py:323
  15.0 37.6 %collective-permute-start.2 = (bf16[3584,128]{1,0:T(8,128)(2,1)S(1)}, bf16[3584,128]{1,0:T(8,128)(2,1)}, u32[]{:S(2)}, u32[]{:S(2)}) collective-permute-start(bf16[3584,128]{1,0:T(8,128)(2,1)S(1)} %get-tuple-element.32), channel_id=1, source_target_pairs={{0,6},{2,0},{4,2},{6,4},{1,7},{3,1},{5,3},{7,5},{8,14},{10,8},{12,... | collective-permute-start | bytes 2752520 | tf_op jit(solution)/shard_map/ppermute | solution.py:324
  22.4 28.3 %collective-permute-start.4 = (bf16[1792,128]{1,0:T(8,128)(2,1)}, bf16[1792,128]{1,0:T(8,128)(2,1)}, u32[]{:S(2)}, u32[]{:S(2)}) collective-permute-start(bf16[1792,128]{1,0:T(8,128)(2,1)} %collective-permute-done.3), channel_id=1, source_target_pairs={{0,2},{2,4},{4,6},{6,0},{1,3},{3,5},{5,7},{7,1},{8,10},{10,12},{12... | collective-permute-start | bytes 1376264 | tf_op jit(solution)/shard_map/ppermute | solution.py:329
  24.6 28.0 %collective-permute-start.6 = (bf16[1792,128]{1,0:T(8,128)(2,1)}, bf16[1792,128]{1,0:T(8,128)(2,1)}, u32[]{:S(2)}, u32[]{:S(2)}) collective-permute-start(bf16[1792,128]{1,0:T(8,128)(2,1)} %collective-permute-done.5), channel_id=1, source_target_pairs={{0,6},{2,0},{4,2},{6,4},{1,7},{3,1},{5,3},{7,5},{8,14},{10,8},{12,... | collective-permute-start | bytes 1376264 | tf_op jit(solution)/shard_map/ppermute | solution.py:330
  29.5 39.4 %all-to-all-start = ((bf16[16,120,128]{2,1,0:T(8,128)(2,1)}), bf16[16,120,128]{2,1,0:T(8,128)(2,1)S(1)}, u32[]{:S(2)}, u32[]{:S(2)}) async-start(bf16[16,120,128]{2,1,0:T(8,128)(2,1)} %shard_map.95), calls=%async_computation | async-start | bytes 983040 | tf_op jit(solution)/shard_map/all_to_all | solution.py:332
  44.2 9.6 %collective-permute-start = (bf16[3584,128]{1,0:T(8,128)(2,1)S(1)}, bf16[3584,128]{1,0:T(8,128)(2,1)}, u32[]{:S(2)}, u32[]{:S(2)}) collective-permute-start(bf16[3584,128]{1,0:T(8,128)(2,1)S(1)} %get-tuple-element.30.refs_0_), channel_id=1, source_target_pairs={{0,1},{1,0},{2,3},{3,2},{4,5},{5,4},{6,7},{7,6},{8,9},{9,8},{10,11... | collective-permute-start | bytes 2752520 | tf_op jit(solution)/shard_map/ppermute | solution.py:325
  69.8 26.7 %collective-permute-start.7 = (bf16[3584,128]{1,0:T(8,128)(2,1)}, bf16[3584,128]{1,0:T(8,128)(2,1)S(1)}, u32[]{:S(2)}, u32[]{:S(2)}) collective-permute-start(bf16[3584,128]{1,0:T(8,128)(2,1)} %collective-permute-done.1.refs_0_.refs_2_), channel_id=1, source_target_pairs={{0,1},{1,0},{2,3},{3,2},{4,5},{5,4},{6,7},{7,6},{8,9},{9,8},{10,11... | collective-permute-start | bytes 2752520 | tf_op jit(solution)/shard_map/ppermute | solution.py:338
  71.7 24.8 %collective-permute-start.8 = (bf16[3584,128]{1,0:T(8,128)(2,1)}, bf16[3584,128]{1,0:T(8,128)(2,1)}, u32[]{:S(2)}, u32[]{:S(2)}) collective-permute-start(bf16[3584,128]{1,0:T(8,128)(2,1)} %collective-permute-done.2.refs_1_.refs_4_), channel_id=1, source_target_pairs={{0,1},{1,0},{2,3},{3,2},{4,5},{5,4},{6,7},{7,6},{8,9},{9,8},{10,11... | collective-permute-start | bytes 2752520 | tf_op jit(solution)/shard_map/ppermute | solution.py:338
  74.1 23.3 %copy-start.1 = (s32[5]{0:T(128)S(1)}, s32[5]{0:T(128)}, u32[]{:S(2)}) copy-start(s32[5]{0:T(128)} %shard_map.96.scalars) | copy-start | bytes 64
  75.2 21.2 %all-to-all-start.1 = ((bf16[16,8,3712]{2,1,0:T(8,128)(2,1)}), bf16[16,8,3712]{2,1,0:T(8,128)(2,1)S(1)}, u32[]{:S(2)}, u32[]{:S(2)}) async-start(bf16[16,8,3712]{2,1,0:T(8,128)(2,1)} %bitcast.14), calls=%async_computation.1 | async-start | bytes 1900544 | tf_op jit(solution)/shard_map/all_to_all | solution.py:367
  79.8 4.3 %collective-permute-start.9 = (bf16[1792,128]{1,0:T(8,128)(2,1)}, bf16[1792,128]{1,0:T(8,128)(2,1)S(1)}, u32[]{:S(2)}, u32[]{:S(2)}) collective-permute-start(bf16[1792,128]{1,0:T(8,128)(2,1)} %collective-permute-done.4.refs_2_.refs_6_), channel_id=1, source_target_pairs={{0,1},{1,0},{2,3},{3,2},{4,5},{5,4},{6,7},{7,6},{8,9},{9,8},{10,11... | collective-permute-start | bytes 1376264 | tf_op jit(solution)/shard_map/ppermute | solution.py:341
  81.8 4.0 %collective-permute-start.10 = (bf16[1792,128]{1,0:T(8,128)(2,1)}, bf16[1792,128]{1,0:T(8,128)(2,1)S(1)}, u32[]{:S(2)}, u32[]{:S(2)}) collective-permute-start(bf16[1792,128]{1,0:T(8,128)(2,1)} %collective-permute-done.6.refs_3_.refs_7_), channel_id=1, source_target_pairs={{0,1},{1,0},{2,3},{3,2},{4,5},{5,4},{6,7},{7,6},{8,9},{9,8},{10,11... | collective-permute-start | bytes 1376264 | tf_op jit(solution)/shard_map/ppermute | solution.py:341
  96.4 0.9 copy-start.3
  103.9 11.6 %all-to-all-start.2 = ((bf16[4,128,512]{2,1,0:T(8,128)(2,1)}), bf16[4,128,512]{2,1,0:T(8,128)(2,1)S(1)}, u32[]{:S(2)}, u32[]{:S(2)}) async-start(bf16[4,128,512]{2,1,0:T(8,128)(2,1)} %shard_map.97), calls=%async_computation.2 | async-start | bytes 1048576 | tf_op jit(solution)/shard_map/all_to_all | solution.py:385

commit v12 on v11

--- a/solution.py
+++ b/solution.py
@@ -175,7 +175,7 @@
         out_shape=jax.ShapeDtypeStruct(scalars.shape, scalars.dtype),
         in_specs=[small] + [pl.BlockSpec(memory_space=pl.ANY)] * len(arrays),
         out_specs=small,
-        cost_estimate=pl.CostEstimate(flops=10**11, bytes_accessed=4096, transcendentals=0),
+        cost_estimate=pl.CostEstimate(flops=25 * 10**9, bytes_accessed=4096, transcendentals=0),
     )(scalars, *arrays)
 
 
@@ -330,13 +330,13 @@
     far_down = lax.ppermute(far_down, "chip", behind_of)
     scalars = mark(scalars, ahead, behind, far_up, far_down)
     recv = lax.all_to_all(sent, "node", split_axis=0, concat_axis=0, tiled=True)
-    recv, here_too, ahead, behind, far_up, far_down, scalars = lax.optimization_barrier(
-        (recv, here_too, ahead, behind, far_up, far_down, scalars)
-    )
-    blocks = (here, here_too)
+    near = (here, here_too)
     for block in (ahead, behind):
-        blocks += (block, lax.ppermute(block, "core", swap))
-    blocks += (far_up, far_down)
+        near += (block, lax.ppermute(block, "core", swap))
+    recv, near, far_up, far_down, scalars = lax.optimization_barrier(
+        (recv, near, far_up, far_down, scalars)
+    )
+    blocks = near + (far_up, far_down)
     for block in (far_up, far_down):
         blocks += (lax.ppermute(block, "core", swap),)
     held = [

time: 182 us -> 195 us (1.071)
  waiting for transfers between devices: 43.6 us -> 56.3 us
    ppermute x2, waiting for transfers between devices: 6.35 us -> 21 us  [per_device(): far_up = lax.ppermute(far_up, 'chip', ahead_of)]
    all_to_all x1, waiting for transfers between devices: 10.6 us -> 6.71 us  [per_device(): lax.all_to_all(spread, ('expert', 'chip'), split_axis=0, concat_axis=0, t...]
    ppermute x2, waiting for transfers between devices: 1.97 us -> 0.01 us  [per_device(): far_down = lax.ppermute(far_down, 'chip', behind_of)]
  transfers between devices with their start and end apart: 14 -> 14, of which waited for: 7 -> 6; matrix products, arithmetic and copies ran while one was open for 1% -> 0% of each run, Pallas kernels for 1% -> 1%
where the time goes in v12:
time: 195 us; the launch traced here: 194 us
  blocking collectives  58.3 us (30%)
  waiting for transfers between devices  56.3 us (29%)
  starting transfers between devices  54.6 us (28%)
  Pallas kernels  19.8 us (10%)
    all_to_all x1, blocking collectives, per_device(): lax.all_to_all(expanded, 'node', split_axis=0, concat_axis=0, tiled=True)  30.3 us
    ppermute x2, waiting for transfers between devices, per_device(): far_up = lax.ppermute(far_up, 'chip', ahead_of)  21 us
    pallas_call x5, Pallas kernels, call(): pl.pallas_call(kernel, out_shape=[jax.ShapeDtypeStruct(shape, jnp.bfloat1...  18.6 us
    all_to_all x1, waiting for transfers between devices, per_device(): recv = lax.all_to_all(sent, 'node', split_axis=0, concat_axis=0, tiled=True)  16.9 us
    all_to_all x1, blocking collectives, per_device(): lax.all_to_all(result.reshape(experts * chips, pairs, -1), ('expert', 'ch...  15.2 us
    all_to_all x1, starting transfers between devices, per_device(): recv = lax.all_to_all(sent, 'node', split_axis=0, concat_axis=0, tiled=True)  14.8 us
    all_gather x1, blocking collectives, per_device(): lax.all_gather(jnp.concatenate([active, grad_pre], 1), 'chip', axis=0)  12.8 us
    ppermute x2, starting transfers between devices, per_device(): far_down = lax.ppermute(far_down, 'chip', behind_of)  9.73 us
  transfers between devices with their start and end apart: 14, of which 6 were waited for; matrix products, arithmetic and copies ran while one was open for 0% of the time, Pallas kernels for 1%

profile of v12, /device:TPU:64, one launch (start us, length us, event | category | flops | bytes accessed | tf_op | source)
XLA Modules:
  0.0 193.7 jit_solution(318242224629016384)
XLA Ops:
  0.7 0.1 pad_add_fusion.chips
  0.8 3.1 %shard_map.94 = (bf16[3584,128]{1,0:T(8,128)(2,1)S(1)}, bf16[3584,128]{1,0:T(8,128)(2,1)S(1)}, bf16[3584,128]{1,0:T(8,128)(2,1)S(1)}, bf16[1792,128]{1,0:T(8,128)(2,1)S(1)}, bf16[1792,128]{1,0:T(8,128)(2,1)S(1)}) custom-call(s32[4]{0:T(128)S(1)} %pad_add_fusion.chips, bf16[7168,128]{1,0:T(8,128)(2,1)} %up.1, bf16[128,7168]{1,0:T(8,128)(2,1)} %down.1), custom_call_target="tpu_custom_call" | custom-call | tf_op jit(solution)/shard_map/pallas_call | solution.py:260
  3.8 1.9 shard_map.95
  5.7 3.4 %collective-permute-start.1 = (bf16[3584,128]{1,0:T(8,128)(2,1)S(1)}, bf16[3584,128]{1,0:T(8,128)(2,1)}, u32[]{:S(2)}, u32[]{:S(2)}) collective-permute-start(bf16[3584,128]{1,0:T(8,128)(2,1)S(1)} %get-tuple-element.34), channel_id=1, source_target_pairs={{0,2},{2,4},{4,6},{6,0},{1,3},{3,5},{5,7},{7,1},{8,10},{10,12},{12... | collective-permute-start | bytes 2752520 | tf_op jit(solution)/shard_map/ppermute | solution.py:323
  9.1 3.7 %collective-permute-start.3 = (bf16[3584,128]{1,0:T(8,128)(2,1)S(1)}, bf16[3584,128]{1,0:T(8,128)(2,1)}, u32[]{:S(2)}, u32[]{:S(2)}) collective-permute-start(bf16[3584,128]{1,0:T(8,128)(2,1)S(1)} %get-tuple-element.35), channel_id=1, source_target_pairs={{0,6},{2,0},{4,2},{6,4},{1,7},{3,1},{5,3},{7,5},{8,14},{10,8},{12,... | collective-permute-start | bytes 2752520 | tf_op jit(solution)/shard_map/ppermute | solution.py:324
  12.8 2.2 %collective-permute-start.5 = (bf16[1792,128]{1,0:T(8,128)(2,1)S(1)}, bf16[1792,128]{1,0:T(8,128)(2,1)}, u32[]{:S(2)}, u32[]{:S(2)}) collective-permute-start(bf16[1792,128]{1,0:T(8,128)(2,1)S(1)} %get-tuple-element.36), channel_id=1, source_target_pairs={{0,2},{2,4},{4,6},{6,0},{1,3},{3,5},{5,7},{7,1},{8,10},{10,12},{12... | collective-permute-start | bytes 1376264 | tf_op jit(solution)/shard_map/ppermute | solution.py:321
  15.0 4.9 %collective-permute-start.7 = (bf16[1792,128]{1,0:T(8,128)(2,1)S(1)}, bf16[1792,128]{1,0:T(8,128)(2,1)}, u32[]{:S(2)}, u32[]{:S(2)}) collective-permute-start(bf16[1792,128]{1,0:T(8,128)(2,1)S(1)} %get-tuple-element.37), channel_id=1, source_target_pairs={{0,6},{2,0},{4,2},{6,4},{1,7},{3,1},{5,3},{7,5},{8,14},{10,8},{12,... | collective-permute-start | bytes 1376264 | tf_op jit(solution)/shard_map/ppermute | solution.py:322
  19.9 21.0 %collective-permute-done.5 = bf16[1792,128]{1,0:T(8,128)(2,1)} collective-permute-done((bf16[1792,128]{1,0:T(8,128)(2,1)S(1)}, bf16[1792,128]{1,0:T(8,128)(2,1)}, u32[]{:S(2)}, u32[]{:S(2)}) %collective-permute-start.5) | collective-permute-done | bytes 458784 | tf_op jit(solution)/shard_map/ppermute | solution.py:321
  40.9 2.2 %collective-permute-start.6 = (bf16[1792,128]{1,0:T(8,128)(2,1)}, bf16[1792,128]{1,0:T(8,128)(2,1)}, u32[]{:S(2)}, u32[]{:S(2)}) collective-permute-start(bf16[1792,128]{1,0:T(8,128)(2,1)} %collective-permute-done.5), channel_id=1, source_target_pairs={{0,2},{2,4},{4,6},{6,0},{1,3},{3,5},{5,7},{7,1},{8,10},{10,12},{12... | collective-permute-start | bytes 1376264 | tf_op jit(solution)/shard_map/ppermute | solution.py:329
  43.1 0.0 collective-permute-done.7
  43.1 4.9 %collective-permute-start.8 = (bf16[1792,128]{1,0:T(8,128)(2,1)}, bf16[1792,128]{1,0:T(8,128)(2,1)}, u32[]{:S(2)}, u32[]{:S(2)}) collective-permute-start(bf16[1792,128]{1,0:T(8,128)(2,1)} %collective-permute-done.7), channel_id=1, source_target_pairs={{0,6},{2,0},{4,2},{6,4},{1,7},{3,1},{5,3},{7,5},{8,14},{10,8},{12,... | collective-permute-start | bytes 1376264 | tf_op jit(solution)/shard_map/ppermute | solution.py:330
  47.9 14.8 %all-to-all-start = ((bf16[16,120,128]{2,1,0:T(8,128)(2,1)}), bf16[16,120,128]{2,1,0:T(8,128)(2,1)S(1)}, u32[]{:S(2)}, u32[]{:S(2)}) async-start(bf16[16,120,128]{2,1,0:T(8,128)(2,1)} %shard_map.95), calls=%async_computation | async-start | bytes 983040 | tf_op jit(solution)/shard_map/all_to_all | solution.py:332
  62.7 1.9 collective-permute-start
  64.6 0.6 stack.49.scalars
  65.3 0.0 collective-permute-done.1.refs_0_.refs_2_
  65.3 2.4 %collective-permute-start.2 = (bf16[3584,128]{1,0:T(8,128)(2,1)}, bf16[3584,128]{1,0:T(8,128)(2,1)S(1)}, u32[]{:S(2)}, u32[]{:S(2)}) collective-permute-start(bf16[3584,128]{1,0:T(8,128)(2,1)} %collective-permute-done.1.refs_0_.refs_2_), channel_id=1, source_target_pairs={{0,1},{1,0},{2,3},{3,2},{4,5},{5,4},{6,7},{7,6},{8,9},{9,8},{10,11... | collective-permute-start | bytes 2752520 | tf_op jit(solution)/shard_map/ppermute | solution.py:335
  67.7 0.0 collective-permute-done.3.refs_1_.refs_4_
  67.7 1.9 collective-permute-start.4
  69.6 0.0 collective-permute-done.6.refs_2_.refs_6_
  69.6 1.2 shard_map.96.scalars
  70.8 0.0 collective-permute-done.refs_1_
  70.9 1.4 collective-permute-done.4.refs_5_
  72.3 16.9 %all-to-all-done = bf16[16,120,128]{2,1,0:T(8,128)(2,1)S(1)} async-done(((bf16[16,120,128]{2,1,0:T(8,128)(2,1)}), bf16[16,120,128]{2,1,0:T(8,128)(2,1)S(1)}, u32[]{:S(2)}, u32[]{:S(2)}) %all-to-all-start) | async-done | bytes 491552 | tf_op jit(solution)/shard_map/all_to_all | solution.py:332
  89.1 0.4 compare_reduce_fusion
  89.5 0.1 copy.12
  89.6 0.1 add_reduce_fusion
  89.8 0.2 convolution_convert_fusion.1
  90.1 0.0 copy-start.1
  90.1 1.0 broadcast_in_dim.10
  91.1 4.6 %all-to-all-start.1 = ((bf16[16,8,3712]{2,1,0:T(8,128)(2,1)}), bf16[16,8,3712]{2,1,0:T(8,128)(2,1)S(1)}, u32[]{:S(2)}, u32[]{:S(2)}) async-start(bf16[16,8,3712]{2,1,0:T(8,128)(2,1)} %bitcast.14), calls=%async_computation.1 | async-start | bytes 1900544 | tf_op jit(solution)/shard_map/all_to_all | solution.py:367
  95.8 1.9 collective-permute-start.9
  97.7 2.4 %collective-permute-start.10 = (bf16[1792,128]{1,0:T(8,128)(2,1)}, bf16[1792,128]{1,0:T(8,128)(2,1)S(1)}, u32[]{:S(2)}, u32[]{:S(2)}) collective-permute-start(bf16[1792,128]{1,0:T(8,128)(2,1)} %collective-permute-done.8.refs_3_.refs_7_), channel_id=1, source_target_pairs={{0,1},{1,0},{2,3},{3,2},{4,5},{5,4},{6,7},{7,6},{8,9},{9,8},{10,11... | collective-permute-start | bytes 1376264 | tf_op jit(solution)/shard_map/ppermute | solution.py:341
  100.1 1.6 collective-permute-done.10.refs_9_
  101.7 6.7 %all-to-all-done.1 = bf16[16,8,3712]{2,1,0:T(8,128)(2,1)S(1)} async-done(((bf16[16,8,3712]{2,1,0:T(8,128)(2,1)}), bf16[16,8,3712]{2,1,0:T(8,128)(2,1)S(1)}, u32[]{:S(2)}, u32[]{:S(2)}) %all-to-all-start.1) | async-done | bytes 950304 | tf_op jit(solution)/shard_map/all_to_all | solution.py:367
  108.5 6.5 %shard_map.97 = bf16[4,128,512]{2,1,0:T(8,128)(2,1)} custom-call(s32[5]{0:T(128)S(1)} %copy-done.1, bf16[128,3712]{1,0:T(8,128)(2,1)S(1)} %bitcast.66, bf16[3584,128]{1,0:T(8,128)(2,1)} %copy-done, bf16[3584,128]{1,0:T(8,128)(2,1)} %collective-permute-done.refs_1_, bf16[3584,128]{1,0:T(8,128)(2,1)} %collective-permute-done.1.refs_0_.refs_2_, ...), custom_call_target="tpu_custom_call" | custom-call | tf_op jit(solution)/shard_map/pallas_call | solution.py:260
  115.0 3.5 %all-to-all-start.2 = ((bf16[4,128,512]{2,1,0:T(8,128)(2,1)}), bf16[4,128,512]{2,1,0:T(8,128)(2,1)S(1)}, u32[]{:S(2)}, u32[]{:S(2)}) async-start(bf16[4,128,512]{2,1,0:T(8,128)(2,1)} %shard_map.97), calls=%async_computation.2 | async-start | bytes 1048576 | tf_op jit(solution)/shard_map/all_to_all | solution.py:385
  118.5 0.1 select_reduce_fusion
  118.6 8.7 %all-to-all-done.2 = bf16[4,128,512]{2,1,0:T(8,128)(2,1)S(1)} async-done(((bf16[4,128,512]{2,1,0:T(8,128)(2,1)}), bf16[4,128,512]{2,1,0:T(8,128)(2,1)S(1)}, u32[]{:S(2)}, u32[]{:S(2)}) %all-to-all-start.2) | async-done | bytes 524320 | tf_op jit(solution)/shard_map/all_to_all | solution.py:385
  127.3 0.1 convert_reduce_fusion.1
  127.3 0.1 multiply_convert_fusion
  127.4 12.8 %all-gather = bf16[512,512]{1,0:T(8,128)(2,1)S(1)} all-gather(bf16[128,512]{1,0:T(8,128)(2,1)S(1)} %pad_maximum_fusion.1), channel_id=2, replica_groups=mesh['node'=16,'expert'=4,'chip'=4,'core'=2] {'chip'}, dimensions={0}, use_global_device_ids=true | all-gather | bytes 655360 | tf_op jit(solution)/shard_map/all_gather | solution.py:392
  140.2 5.4 %shard_map.98 = bf16[128,3712]{1,0:T(8,128)(2,1)S(1)} custom-call(s32[5]{0:T(128)S(1)} %copy-done.1, bf16[128,3712]{1,0:T(8,128)(2,1)S(1)} %bitcast.68, bf16[4,128,512]{2,1,0:T(8,128)(2,1)S(1)} %bitcast.70, bf16[3584,128]{1,0:T(8,128)(2,1)} %copy-done, bf16[3584,128]{1,0:T(8,128)(2,1)} %collective-permute-done.refs_1_, ...), custom_call_target="tpu_custom_call" | custom-call | tf_op jit(solution)/shard_map/pallas_call | solution.py:260
  145.7 15.2 %all_to_all.25 = bf16[16,8,3712]{2,1,0:T(8,128)(2,1)S(1)} all-to-all(bf16[16,8,3712]{2,1,0:T(8,128)(2,1)S(1)} %bitcast.69), channel_id=1, replica_groups=mesh['node'=16,'expert'=4,'chip'=4,'core'=2] {'expert','chip'}, dimensions={0} | all-to-all | bytes 1900544 | tf_op jit(solution)/shard_map/all_to_all | solution.py:406
  160.9 0.1 convert_reduce_fusion
  161.2 0.3 convolution_convert_fusion
  161.6 0.1 copy.14
  161.6 30.3 %all_to_all.26.home = bf16[16,120,128]{2,1,0:T(8,128)(2,1)S(1)} all-to-all(bf16[16,120,128]{2,1,0:T(8,128)(2,1)S(1)} %bitcast.74), channel_id=1, replica_groups=mesh['node'=16,'expert'=4,'chip'=4,'core'=2] {'node'}, dimensions={0} | all-to-all | bytes 983040 | tf_op jit(solution)/shard_map/all_to_all | solution.py:423
  192.0 1.7 shard_map.99
  (33 shorter events, 0.3 us)
Async XLA Ops:
  0.7 3.1 %copy-start.2 = (bf16[4,2,2]{0,2,1:T(2,128)(2,1)S(1)}, bf16[4,2,2]{0,2,1:T(2,128)(2,1)}, u32[]{:S(2)}) copy-start(bf16[4,2,2]{0,2,1:T(2,128)(2,1)} %param.11) | copy-start | bytes 100
  3.8 67.0 %copy-start = (bf16[3584,128]{1,0:T(8,128)(2,1)}, bf16[3584,128]{1,0:T(8,128)(2,1)S(1)}, u32[]{:S(2)}) copy-start(bf16[3584,128]{1,0:T(8,128)(2,1)S(1)} %get-tuple-element.40.refs_0_) | copy-start | bytes 2752516
  5.7 59.5 %collective-permute-start.1 = (bf16[3584,128]{1,0:T(8,128)(2,1)S(1)}, bf16[3584,128]{1,0:T(8,128)(2,1)}, u32[]{:S(2)}, u32[]{:S(2)}) collective-permute-start(bf16[3584,128]{1,0:T(8,128)(2,1)S(1)} %get-tuple-element.34), channel_id=1, source_target_pairs={{0,2},{2,4},{4,6},{6,0},{1,3},{3,5},{5,7},{7,1},{8,10},{10,12},{12... | collective-permute-start | bytes 2752520 | tf_op jit(solution)/shard_map/ppermute | solution.py:323
  9.1 58.5 %collective-permute-start.3 = (bf16[3584,128]{1,0:T(8,128)(2,1)S(1)}, bf16[3584,128]{1,0:T(8,128)(2,1)}, u32[]{:S(2)}, u32[]{:S(2)}) collective-permute-start(bf16[3584,128]{1,0:T(8,128)(2,1)S(1)} %get-tuple-element.35), channel_id=1, source_target_pairs={{0,6},{2,0},{4,2},{6,4},{1,7},{3,1},{5,3},{7,5},{8,14},{10,8},{12,... | collective-permute-start | bytes 2752520 | tf_op jit(solution)/shard_map/ppermute | solution.py:324
  12.8 28.1 %collective-permute-start.5 = (bf16[1792,128]{1,0:T(8,128)(2,1)S(1)}, bf16[1792,128]{1,0:T(8,128)(2,1)}, u32[]{:S(2)}, u32[]{:S(2)}) collective-permute-start(bf16[1792,128]{1,0:T(8,128)(2,1)S(1)} %get-tuple-element.36), channel_id=1, source_target_pairs={{0,2},{2,4},{4,6},{6,0},{1,3},{3,5},{5,7},{7,1},{8,10},{10,12},{12... | collective-permute-start | bytes 1376264 | tf_op jit(solution)/shard_map/ppermute | solution.py:321
  15.0 28.1 %collective-permute-start.7 = (bf16[1792,128]{1,0:T(8,128)(2,1)S(1)}, bf16[1792,128]{1,0:T(8,128)(2,1)}, u32[]{:S(2)}, u32[]{:S(2)}) collective-permute-start(bf16[1792,128]{1,0:T(8,128)(2,1)S(1)} %get-tuple-element.37), channel_id=1, source_target_pairs={{0,6},{2,0},{4,2},{6,4},{1,7},{3,1},{5,3},{7,5},{8,14},{10,8},{12,... | collective-permute-start | bytes 1376264 | tf_op jit(solution)/shard_map/ppermute | solution.py:322
  40.9 28.7 %collective-permute-start.6 = (bf16[1792,128]{1,0:T(8,128)(2,1)}, bf16[1792,128]{1,0:T(8,128)(2,1)}, u32[]{:S(2)}, u32[]{:S(2)}) collective-permute-start(bf16[1792,128]{1,0:T(8,128)(2,1)} %collective-permute-done.5), channel_id=1, source_target_pairs={{0,2},{2,4},{4,6},{6,0},{1,3},{3,5},{5,7},{7,1},{8,10},{10,12},{12... | collective-permute-start | bytes 1376264 | tf_op jit(solution)/shard_map/ppermute | solution.py:329
  43.1 26.5 %collective-permute-start.8 = (bf16[1792,128]{1,0:T(8,128)(2,1)}, bf16[1792,128]{1,0:T(8,128)(2,1)}, u32[]{:S(2)}, u32[]{:S(2)}) collective-permute-start(bf16[1792,128]{1,0:T(8,128)(2,1)} %collective-permute-done.7), channel_id=1, source_target_pairs={{0,6},{2,0},{4,2},{6,4},{1,7},{3,1},{5,3},{7,5},{8,14},{10,8},{12,... | collective-permute-start | bytes 1376264 | tf_op jit(solution)/shard_map/ppermute | solution.py:330
  47.9 41.2 %all-to-all-start = ((bf16[16,120,128]{2,1,0:T(8,128)(2,1)}), bf16[16,120,128]{2,1,0:T(8,128)(2,1)S(1)}, u32[]{:S(2)}, u32[]{:S(2)}) async-start(bf16[16,120,128]{2,1,0:T(8,128)(2,1)} %shard_map.95), calls=%async_computation | async-start | bytes 983040 | tf_op jit(solution)/shard_map/all_to_all | solution.py:332
  62.7 8.1 %collective-permute-start = (bf16[3584,128]{1,0:T(8,128)(2,1)S(1)}, bf16[3584,128]{1,0:T(8,128)(2,1)}, u32[]{:S(2)}, u32[]{:S(2)}) collective-permute-start(bf16[3584,128]{1,0:T(8,128)(2,1)S(1)} %get-tuple-element.40.refs_0_), channel_id=1, source_target_pairs={{0,1},{1,0},{2,3},{3,2},{4,5},{5,4},{6,7},{7,6},{8,9},{9,8},{10,11... | collective-permute-start | bytes 2752520 | tf_op jit(solution)/shard_map/ppermute | solution.py:325
  65.3 5.6 %collective-permute-start.2 = (bf16[3584,128]{1,0:T(8,128)(2,1)}, bf16[3584,128]{1,0:T(8,128)(2,1)S(1)}, u32[]{:S(2)}, u32[]{:S(2)}) collective-permute-start(bf16[3584,128]{1,0:T(8,128)(2,1)} %collective-permute-done.1.refs_0_.refs_2_), channel_id=1, source_target_pairs={{0,1},{1,0},{2,3},{3,2},{4,5},{5,4},{6,7},{7,6},{8,9},{9,8},{10,11... | collective-permute-start | bytes 2752520 | tf_op jit(solution)/shard_map/ppermute | solution.py:335
  67.7 4.6 %collective-permute-start.4 = (bf16[3584,128]{1,0:T(8,128)(2,1)}, bf16[3584,128]{1,0:T(8,128)(2,1)S(1)}, u32[]{:S(2)}, u32[]{:S(2)}) collective-permute-start(bf16[3584,128]{1,0:T(8,128)(2,1)} %collective-permute-done.3.refs_1_.refs_4_), channel_id=1, source_target_pairs={{0,1},{1,0},{2,3},{3,2},{4,5},{5,4},{6,7},{7,6},{8,9},{9,8},{10,11... | collective-permute-start | bytes 2752520 | tf_op jit(solution)/shard_map/ppermute | solution.py:335
  70.8 20.3 %copy-start.3 = (bf16[3584,128]{1,0:T(8,128)(2,1)}, bf16[3584,128]{1,0:T(8,128)(2,1)S(1)}, u32[]{:S(2)}) copy-start(bf16[3584,128]{1,0:T(8,128)(2,1)S(1)} %collective-permute-done.2.refs_3_) | copy-start | bytes 2752516
  72.2 18.9 %copy-start.4 = (bf16[3584,128]{1,0:T(8,128)(2,1)}, bf16[3584,128]{1,0:T(8,128)(2,1)S(1)}, u32[]{:S(2)}) copy-start(bf16[3584,128]{1,0:T(8,128)(2,1)S(1)} %collective-permute-done.4.refs_5_) | copy-start | bytes 2752516
  90.1 18.4 %copy-start.1 = (s32[5]{0:T(128)S(1)}, s32[5]{0:T(128)}, u32[]{:S(2)}) copy-start(s32[5]{0:T(128)} %shard_map.96.scalars) | copy-start | bytes 64
  91.1 17.3 %all-to-all-start.1 = ((bf16[16,8,3712]{2,1,0:T(8,128)(2,1)}), bf16[16,8,3712]{2,1,0:T(8,128)(2,1)S(1)}, u32[]{:S(2)}, u32[]{:S(2)}) async-start(bf16[16,8,3712]{2,1,0:T(8,128)(2,1)} %bitcast.14), calls=%async_computation.1 | async-start | bytes 1900544 | tf_op jit(solution)/shard_map/all_to_all | solution.py:367
  95.8 4.3 %collective-permute-start.9 = (bf16[1792,128]{1,0:T(8,128)(2,1)}, bf16[1792,128]{1,0:T(8,128)(2,1)S(1)}, u32[]{:S(2)}, u32[]{:S(2)}) collective-permute-start(bf16[1792,128]{1,0:T(8,128)(2,1)} %collective-permute-done.6.refs_2_.refs_6_), channel_id=1, source_target_pairs={{0,1},{1,0},{2,3},{3,2},{4,5},{5,4},{6,7},{7,6},{8,9},{9,8},{10,11... | collective-permute-start | bytes 1376264 | tf_op jit(solution)/shard_map/ppermute | solution.py:341
  97.7 4.0 %collective-permute-start.10 = (bf16[1792,128]{1,0:T(8,128)(2,1)}, bf16[1792,128]{1,0:T(8,128)(2,1)S(1)}, u32[]{:S(2)}, u32[]{:S(2)}) collective-permute-start(bf16[1792,128]{1,0:T(8,128)(2,1)} %collective-permute-done.8.refs_3_.refs_7_), channel_id=1, source_target_pairs={{0,1},{1,0},{2,3},{3,2},{4,5},{5,4},{6,7},{7,6},{8,9},{9,8},{10,11... | collective-permute-start | bytes 1376264 | tf_op jit(solution)/shard_map/ppermute | solution.py:341
  115.0 12.3 %all-to-all-start.2 = ((bf16[4,128,512]{2,1,0:T(8,128)(2,1)}), bf16[4,128,512]{2,1,0:T(8,128)(2,1)S(1)}, u32[]{:S(2)}, u32[]{:S(2)}) async-start(bf16[4,128,512]{2,1,0:T(8,128)(2,1)} %shard_map.97), calls=%async_computation.2 | async-start | bytes 1048576 | tf_op jit(solution)/shard_map/all_to_all | solution.py:385

commit v13 on v12

--- a/solution.py
+++ b/solution.py
@@ -175,7 +175,7 @@
         out_shape=jax.ShapeDtypeStruct(scalars.shape, scalars.dtype),
         in_specs=[small] + [pl.BlockSpec(memory_space=pl.ANY)] * len(arrays),
         out_specs=small,
-        cost_estimate=pl.CostEstimate(flops=25 * 10**9, bytes_accessed=4096, transcendentals=0),
+        cost_estimate=pl.CostEstimate(flops=10**11, bytes_accessed=4096, transcendentals=0),
     )(scalars, *arrays)
 
 
@@ -326,9 +326,12 @@
     scalars = jnp.stack(
         [expert, chip, (chip + chips - 1) % chips, (chip + 1) % chips, (chip + 2) % chips]
     ).astype(jnp.int32)
+    scalars = mark(scalars, ahead, behind, far_up, far_down)
+    ahead, behind, far_up, far_down, scalars = lax.optimization_barrier(
+        (ahead, behind, far_up, far_down, scalars)
+    )
     far_up = lax.ppermute(far_up, "chip", ahead_of)
     far_down = lax.ppermute(far_down, "chip", behind_of)
-    scalars = mark(scalars, ahead, behind, far_up, far_down)
     recv = lax.all_to_all(sent, "node", split_axis=0, concat_axis=0, tiled=True)
     near = (here, here_too)
     for block in (ahead, behind):

time: 195 us -> 184 us (0.944)
  the two profiles are of different devices: /device:TPU:64 before, /device:TPU:32 now
where the time goes in v13:
time: 184 us; the launch traced here: 183 us
  blocking collectives  63.7 us (35%)
  starting transfers between devices  57.4 us (31%)
  waiting for transfers between devices  34.6 us (19%)
  Pallas kernels  20.5 us (11%)
  local copies, waits for them, and re-layouts  1.94 us (1%)
  other arithmetic  1.93 us (1%)
    all_to_all x1, blocking collectives, per_device(): lax.all_to_all(expanded, 'node', split_axis=0, concat_axis=0, tiled=True)  35.3 us
    pallas_call x5, Pallas kernels, call(): pl.pallas_call(kernel, out_shape=[jax.ShapeDtypeStruct(shape, jnp.bfloat1...  19.3 us
    all_to_all x1, starting transfers between devices, per_device(): recv = lax.all_to_all(sent, 'node', split_axis=0, concat_axis=0, tiled=True)  15.2 us
    all_to_all x1, blocking collectives, per_device(): lax.all_to_all(result.reshape(experts * chips, pairs, -1), ('expert', 'ch...  15.1 us
    all_gather x1, blocking collectives, per_device(): lax.all_gather(jnp.concatenate([active, grad_pre], 1), 'chip', axis=0)  13.3 us
    ppermute x2, waiting for transfers between devices, per_device(): far_up = lax.ppermute(far_up, 'chip', ahead_of)  11.9 us
    all_to_all x1, waiting for transfers between devices, per_device(): lax.all_to_all(spread, ('expert', 'chip'), split_axis=0, concat_axis=0, t...  9.55 us
    ppermute x2, starting transfers between devices, per_device(): far_down = lax.ppermute(far_down, 'chip', behind_of)  8.52 us
  transfers between devices with their start and end apart: 14, of which 7 were waited for; matrix products, arithmetic and copies ran while one was open for 0% of the time, Pallas kernels for 1%

profile of v13, /device:TPU:32, one launch (start us, length us, event | category | flops | bytes accessed | tf_op | source)
XLA Modules:
  0.0 182.8 jit_solution(10187002084966076630)
XLA Ops:
  0.7 0.1 pad_add_fusion.chips
  0.8 3.8 %shard_map.94 = (bf16[3584,128]{1,0:T(8,128)(2,1)S(1)}, bf16[3584,128]{1,0:T(8,128)(2,1)S(1)}, bf16[3584,128]{1,0:T(8,128)(2,1)S(1)}, bf16[1792,128]{1,0:T(8,128)(2,1)}, bf16[1792,128]{1,0:T(8,128)(2,1)S(1)}) custom-call(s32[4]{0:T(128)S(1)} %pad_add_fusion.chips, bf16[7168,128]{1,0:T(8,128)(2,1)} %up.1, bf16[128,7168]{1,0:T(8,128)(2,1)} %down.1), custom_call_target="tpu_custom_call" | custom-call | tf_op jit(solution)/shard_map/pallas_call | solution.py:260
  4.6 1.9 %shard_map.95 = bf16[16,120,128]{2,1,0:T(8,128)(2,1)} custom-call(bf16[2,2,4]{2,1,0:T(2,128)(2,1)S(1)} %bitcast.71, s32[2,4]{1,0:T(2,128)} %bitcast.76, s32[2,2,4]{2,1,0:T(2,128)} %bitcast.74, bf16[4,7168]{1,0:T(4,128)(2,1)} %tokens.1, bf16[4,7168]{1,0:T(4,128)(2,1)} %cotangent.1), custom_call_target="tpu_custom_call" | custom-call | tf_op jit(solution)/shard_map/pallas_call | solution.py:260
  6.5 3.4 %collective-permute-start.1 = (bf16[3584,128]{1,0:T(8,128)(2,1)S(1)}, bf16[3584,128]{1,0:T(8,128)(2,1)}, u32[]{:S(2)}, u32[]{:S(2)}) collective-permute-start(bf16[3584,128]{1,0:T(8,128)(2,1)S(1)} %get-tuple-element.39), channel_id=1, source_target_pairs={{0,2},{2,4},{4,6},{6,0},{1,3},{3,5},{5,7},{7,1},{8,10},{10,12},{12... | collective-permute-start | bytes 2752520 | tf_op jit(solution)/shard_map/ppermute | solution.py:323
  9.9 3.7 %collective-permute-start.2 = (bf16[3584,128]{1,0:T(8,128)(2,1)S(1)}, bf16[3584,128]{1,0:T(8,128)(2,1)}, u32[]{:S(2)}, u32[]{:S(2)}) collective-permute-start(bf16[3584,128]{1,0:T(8,128)(2,1)S(1)} %get-tuple-element.40), channel_id=1, source_target_pairs={{0,6},{2,0},{4,2},{6,4},{1,7},{3,1},{5,3},{7,5},{8,14},{10,8},{12,... | collective-permute-start | bytes 2752520 | tf_op jit(solution)/shard_map/ppermute | solution.py:324
  13.6 2.2 %collective-permute-start.3 = (bf16[1792,128]{1,0:T(8,128)(2,1)}, bf16[1792,128]{1,0:T(8,128)(2,1)}, u32[]{:S(2)}, u32[]{:S(2)}) collective-permute-start(bf16[1792,128]{1,0:T(8,128)(2,1)} %get-tuple-element.41), channel_id=1, source_target_pairs={{0,2},{2,4},{4,6},{6,0},{1,3},{3,5},{5,7},{7,1},{8,10},{10,12},{12... | collective-permute-start | bytes 1376264 | tf_op jit(solution)/shard_map/ppermute | solution.py:321
  15.8 4.9 %collective-permute-start.4 = (bf16[1792,128]{1,0:T(8,128)(2,1)S(1)}, bf16[1792,128]{1,0:T(8,128)(2,1)}, u32[]{:S(2)}, u32[]{:S(2)}) collective-permute-start(bf16[1792,128]{1,0:T(8,128)(2,1)S(1)} %get-tuple-element.42), channel_id=1, source_target_pairs={{0,6},{2,0},{4,2},{6,4},{1,7},{3,1},{5,3},{7,5},{8,14},{10,8},{12,... | collective-permute-start | bytes 1376264 | tf_op jit(solution)/shard_map/ppermute | solution.py:322
  20.6 15.2 %all-to-all-start = ((bf16[16,120,128]{2,1,0:T(8,128)(2,1)}), bf16[16,120,128]{2,1,0:T(8,128)(2,1)}, u32[]{:S(2)}, u32[]{:S(2)}) async-start(bf16[16,120,128]{2,1,0:T(8,128)(2,1)} %shard_map.95), calls=%async_computation | async-start | bytes 983040 | tf_op jit(solution)/shard_map/all_to_all | solution.py:335
  35.9 1.9 %collective-permute-start = (bf16[3584,128]{1,0:T(8,128)(2,1)S(1)}, bf16[3584,128]{1,0:T(8,128)(2,1)}, u32[]{:S(2)}, u32[]{:S(2)}) collective-permute-start(bf16[3584,128]{1,0:T(8,128)(2,1)S(1)} %get-tuple-element.50.refs_0_), channel_id=1, source_target_pairs={{0,1},{1,0},{2,3},{3,2},{4,5},{5,4},{6,7},{7,6},{8,9},{9,8},{10,11... | collective-permute-start | bytes 2752520 | tf_op jit(solution)/shard_map/ppermute | solution.py:325
  37.8 0.7 stack.49.scalars
  38.4 3.2 %collective-permute-done.3.refs_2_ = bf16[1792,128]{1,0:T(8,128)(2,1)} collective-permute-done((bf16[1792,128]{1,0:T(8,128)(2,1)}, bf16[1792,128]{1,0:T(8,128)(2,1)}, u32[]{:S(2)}, u32[]{:S(2)}) %collective-permute-start.3) | collective-permute-done | bytes 458784 | tf_op jit(solution)/shard_map/ppermute | solution.py:321
  41.6 1.9 %collective-permute-done.4.refs_3_ = bf16[1792,128]{1,0:T(8,128)(2,1)} collective-permute-done((bf16[1792,128]{1,0:T(8,128)(2,1)S(1)}, bf16[1792,128]{1,0:T(8,128)(2,1)}, u32[]{:S(2)}, u32[]{:S(2)}) %collective-permute-start.4) | collective-permute-done | bytes 458784 | tf_op jit(solution)/shard_map/ppermute | solution.py:322
  43.5 0.0 collective-permute-done.1.refs_0_.refs_2_
  43.5 0.0 collective-permute-done.2.refs_1_.refs_4_
  43.6 1.2 shard_map.96.scalars
  44.8 1.9 %collective-permute-start.5 = (bf16[3584,128]{1,0:T(8,128)(2,1)}, bf16[3584,128]{1,0:T(8,128)(2,1)S(1)}, u32[]{:S(2)}, u32[]{:S(2)}) collective-permute-start(bf16[3584,128]{1,0:T(8,128)(2,1)} %collective-permute-done.1.refs_0_.refs_2_), channel_id=1, source_target_pairs={{0,1},{1,0},{2,3},{3,2},{4,5},{5,4},{6,7},{7,6},{8,9},{9,8},{10,11... | collective-permute-start | bytes 2752520 | tf_op jit(solution)/shard_map/ppermute | solution.py:338
  46.7 2.4 %collective-permute-start.6 = (bf16[3584,128]{1,0:T(8,128)(2,1)}, bf16[3584,128]{1,0:T(8,128)(2,1)}, u32[]{:S(2)}, u32[]{:S(2)}) collective-permute-start(bf16[3584,128]{1,0:T(8,128)(2,1)} %collective-permute-done.2.refs_1_.refs_4_), channel_id=1, source_target_pairs={{0,1},{1,0},{2,3},{3,2},{4,5},{5,4},{6,7},{7,6},{8,9},{9,8},{10,11... | collective-permute-start | bytes 2752520 | tf_op jit(solution)/shard_map/ppermute | solution.py:338
  49.1 3.4 %collective-permute-start.7 = (bf16[1792,128]{1,0:T(8,128)(2,1)}, bf16[1792,128]{1,0:T(8,128)(2,1)S(1)}, u32[]{:S(2)}, u32[]{:S(2)}) collective-permute-start(bf16[1792,128]{1,0:T(8,128)(2,1)} %collective-permute-done.3.refs_2_), channel_id=1, source_target_pairs={{0,2},{2,4},{4,6},{6,0},{1,3},{3,5},{5,7},{7,1},{8,10},{10,12},{12... | collective-permute-start | bytes 1376264 | tf_op jit(solution)/shard_map/ppermute | solution.py:333
  52.5 3.7 %collective-permute-start.8 = (bf16[1792,128]{1,0:T(8,128)(2,1)}, bf16[1792,128]{1,0:T(8,128)(2,1)S(1)}, u32[]{:S(2)}, u32[]{:S(2)}) collective-permute-start(bf16[1792,128]{1,0:T(8,128)(2,1)} %collective-permute-done.4.refs_3_), channel_id=1, source_target_pairs={{0,6},{2,0},{4,2},{6,4},{1,7},{3,1},{5,3},{7,5},{8,14},{10,8},{12,... | collective-permute-start | bytes 1376264 | tf_op jit(solution)/shard_map/ppermute | solution.py:334
  56.2 0.0 collective-permute-done.refs_1_
  56.2 8.7 %collective-permute-done.7.refs_6_ = bf16[1792,128]{1,0:T(8,128)(2,1)S(1)} collective-permute-done((bf16[1792,128]{1,0:T(8,128)(2,1)}, bf16[1792,128]{1,0:T(8,128)(2,1)S(1)}, u32[]{:S(2)}, u32[]{:S(2)}) %collective-permute-start.7) | collective-permute-done | bytes 458784 | tf_op jit(solution)/shard_map/ppermute | solution.py:333
  64.9 1.9 %collective-permute-done.8.refs_7_ = bf16[1792,128]{1,0:T(8,128)(2,1)S(1)} collective-permute-done((bf16[1792,128]{1,0:T(8,128)(2,1)}, bf16[1792,128]{1,0:T(8,128)(2,1)S(1)}, u32[]{:S(2)}, u32[]{:S(2)}) %collective-permute-start.8) | collective-permute-done | bytes 458784 | tf_op jit(solution)/shard_map/ppermute | solution.py:334
  66.8 0.0 collective-permute-done.5.refs_3_
  66.8 1.2 compare_reduce_fusion
  68.0 0.1 copy.12
  68.1 0.1 add_reduce_fusion
  68.2 1.2 convolution_convert_fusion.1
  69.5 0.0 copy-start.1
  69.6 1.0 broadcast_in_dim.10
  70.6 7.0 %all-to-all-start.1 = ((bf16[16,8,3712]{2,1,0:T(8,128)(2,1)}), bf16[16,8,3712]{2,1,0:T(8,128)(2,1)S(1)}, u32[]{:S(2)}, u32[]{:S(2)}) async-start(bf16[16,8,3712]{2,1,0:T(8,128)(2,1)} %bitcast.14), calls=%async_computation.1 | async-start | bytes 1900544 | tf_op jit(solution)/shard_map/all_to_all | solution.py:370
  77.6 1.9 %collective-permute-start.9 = (bf16[1792,128]{1,0:T(8,128)(2,1)S(1)}, bf16[1792,128]{1,0:T(8,128)(2,1)S(1)}, u32[]{:S(2)}, u32[]{:S(2)}) collective-permute-start(bf16[1792,128]{1,0:T(8,128)(2,1)S(1)} %collective-permute-done.7.refs_6_), channel_id=1, source_target_pairs={{0,1},{1,0},{2,3},{3,2},{4,5},{5,4},{6,7},{7,6},{8,9},{9,8},{10,11... | collective-permute-start | bytes 1376264 | tf_op jit(solution)/shard_map/ppermute | solution.py:344
  79.5 2.4 %collective-permute-start.10 = (bf16[1792,128]{1,0:T(8,128)(2,1)S(1)}, bf16[1792,128]{1,0:T(8,128)(2,1)S(1)}, u32[]{:S(2)}, u32[]{:S(2)}) collective-permute-start(bf16[1792,128]{1,0:T(8,128)(2,1)S(1)} %collective-permute-done.8.refs_7_), channel_id=1, source_target_pairs={{0,1},{1,0},{2,3},{3,2},{4,5},{5,4},{6,7},{7,6},{8,9},{9,8},{10,11... | collective-permute-start | bytes 1376264 | tf_op jit(solution)/shard_map/ppermute | solution.py:344
  82.0 1.4 collective-permute-done.10.refs_9_
  83.4 9.6 %all-to-all-done.1 = bf16[16,8,3712]{2,1,0:T(8,128)(2,1)S(1)} async-done(((bf16[16,8,3712]{2,1,0:T(8,128)(2,1)}), bf16[16,8,3712]{2,1,0:T(8,128)(2,1)S(1)}, u32[]{:S(2)}, u32[]{:S(2)}) %all-to-all-start.1) | async-done | bytes 950304 | tf_op jit(solution)/shard_map/all_to_all | solution.py:370
  92.9 6.5 %shard_map.97 = bf16[4,128,512]{2,1,0:T(8,128)(2,1)} custom-call(s32[5]{0:T(128)S(1)} %copy-done.1, bf16[128,3712]{1,0:T(8,128)(2,1)S(1)} %bitcast.66, bf16[3584,128]{1,0:T(8,128)(2,1)} %copy-done, bf16[3584,128]{1,0:T(8,128)(2,1)} %collective-permute-done.refs_1_, bf16[3584,128]{1,0:T(8,128)(2,1)} %collective-permute-done.1.refs_0_.refs_2_, ...), custom_call_target="tpu_custom_call" | custom-call | tf_op jit(solution)/shard_map/pallas_call | solution.py:260
  99.4 3.5 %all-to-all-start.2 = ((bf16[4,128,512]{2,1,0:T(8,128)(2,1)}), bf16[4,128,512]{2,1,0:T(8,128)(2,1)S(1)}, u32[]{:S(2)}, u32[]{:S(2)}) async-start(bf16[4,128,512]{2,1,0:T(8,128)(2,1)} %shard_map.97), calls=%async_computation.2 | async-start | bytes 1048576 | tf_op jit(solution)/shard_map/all_to_all | solution.py:388
  102.9 0.1 select_reduce_fusion
  103.0 7.9 %all-to-all-done.2 = bf16[4,128,512]{2,1,0:T(8,128)(2,1)S(1)} async-done(((bf16[4,128,512]{2,1,0:T(8,128)(2,1)}), bf16[4,128,512]{2,1,0:T(8,128)(2,1)S(1)}, u32[]{:S(2)}, u32[]{:S(2)}) %all-to-all-start.2) | async-done | bytes 524320 | tf_op jit(solution)/shard_map/all_to_all | solution.py:388
  111.0 0.1 convert_reduce_fusion.1
  111.0 0.1 multiply_convert_fusion
  111.2 13.3 %all-gather = bf16[512,512]{1,0:T(8,128)(2,1)S(1)} all-gather(bf16[128,512]{1,0:T(8,128)(2,1)S(1)} %pad_maximum_fusion.1), channel_id=2, replica_groups=mesh['node'=16,'expert'=4,'chip'=4,'core'=2] {'chip'}, dimensions={0}, use_global_device_ids=true | all-gather | bytes 655360 | tf_op jit(solution)/shard_map/all_gather | solution.py:395
  124.5 5.4 %shard_map.98 = bf16[128,3712]{1,0:T(8,128)(2,1)S(1)} custom-call(s32[5]{0:T(128)S(1)} %copy-done.1, bf16[128,3712]{1,0:T(8,128)(2,1)S(1)} %bitcast.68, bf16[4,128,512]{2,1,0:T(8,128)(2,1)S(1)} %bitcast.70, bf16[3584,128]{1,0:T(8,128)(2,1)} %copy-done, bf16[3584,128]{1,0:T(8,128)(2,1)} %collective-permute-done.refs_1_, ...), custom_call_target="tpu_custom_call" | custom-call | tf_op jit(solution)/shard_map/pallas_call | solution.py:260
  129.9 15.1 %all_to_all.25 = bf16[16,8,3712]{2,1,0:T(8,128)(2,1)S(1)} all-to-all(bf16[16,8,3712]{2,1,0:T(8,128)(2,1)S(1)} %bitcast.69), channel_id=1, replica_groups=mesh['node'=16,'expert'=4,'chip'=4,'core'=2] {'expert','chip'}, dimensions={0} | all-to-all | bytes 1900544 | tf_op jit(solution)/shard_map/all_to_all | solution.py:409
  145.0 0.1 convert_reduce_fusion
  145.3 0.3 convolution_convert_fusion
  145.7 0.1 copy.14
  145.8 35.3 %all_to_all.26.home = bf16[16,120,128]{2,1,0:T(8,128)(2,1)S(1)} all-to-all(bf16[16,120,128]{2,1,0:T(8,128)(2,1)S(1)} %bitcast.73), channel_id=1, replica_groups=mesh['node'=16,'expert'=4,'chip'=4,'core'=2] {'node'}, dimensions={0} | all-to-all | bytes 983040 | tf_op jit(solution)/shard_map/all_to_all | solution.py:426
  181.0 1.7 shard_map.99
  (35 shorter events, 0.3 us)
Async XLA Ops:
  0.7 3.8 %copy-start.2 = (bf16[4,2,2]{0,2,1:T(2,128)(2,1)S(1)}, bf16[4,2,2]{0,2,1:T(2,128)(2,1)}, u32[]{:S(2)}) copy-start(bf16[4,2,2]{0,2,1:T(2,128)(2,1)} %param.11) | copy-start | bytes 100
  4.6 40.2 %copy-start = (bf16[3584,128]{1,0:T(8,128)(2,1)}, bf16[3584,128]{1,0:T(8,128)(2,1)S(1)}, u32[]{:S(2)}) copy-start(bf16[3584,128]{1,0:T(8,128)(2,1)S(1)} %get-tuple-element.50.refs_0_) | copy-start | bytes 2752516
  6.5 37.1 %collective-permute-start.1 = (bf16[3584,128]{1,0:T(8,128)(2,1)S(1)}, bf16[3584,128]{1,0:T(8,128)(2,1)}, u32[]{:S(2)}, u32[]{:S(2)}) collective-permute-start(bf16[3584,128]{1,0:T(8,128)(2,1)S(1)} %get-tuple-element.39), channel_id=1, source_target_pairs={{0,2},{2,4},{4,6},{6,0},{1,3},{3,5},{5,7},{7,1},{8,10},{10,12},{12... | collective-permute-start | bytes 2752520 | tf_op jit(solution)/shard_map/ppermute | solution.py:323
  9.9 33.6 %collective-permute-start.2 = (bf16[3584,128]{1,0:T(8,128)(2,1)S(1)}, bf16[3584,128]{1,0:T(8,128)(2,1)}, u32[]{:S(2)}, u32[]{:S(2)}) collective-permute-start(bf16[3584,128]{1,0:T(8,128)(2,1)S(1)} %get-tuple-element.40), channel_id=1, source_target_pairs={{0,6},{2,0},{4,2},{6,4},{1,7},{3,1},{5,3},{7,5},{8,14},{10,8},{12,... | collective-permute-start | bytes 2752520 | tf_op jit(solution)/shard_map/ppermute | solution.py:324
  13.6 28.1 %collective-permute-start.3 = (bf16[1792,128]{1,0:T(8,128)(2,1)}, bf16[1792,128]{1,0:T(8,128)(2,1)}, u32[]{:S(2)}, u32[]{:S(2)}) collective-permute-start(bf16[1792,128]{1,0:T(8,128)(2,1)} %get-tuple-element.41), channel_id=1, source_target_pairs={{0,2},{2,4},{4,6},{6,0},{1,3},{3,5},{5,7},{7,1},{8,10},{10,12},{12... | collective-permute-start | bytes 1376264 | tf_op jit(solution)/shard_map/ppermute | solution.py:321
  15.8 27.8 %collective-permute-start.4 = (bf16[1792,128]{1,0:T(8,128)(2,1)S(1)}, bf16[1792,128]{1,0:T(8,128)(2,1)}, u32[]{:S(2)}, u32[]{:S(2)}) collective-permute-start(bf16[1792,128]{1,0:T(8,128)(2,1)S(1)} %get-tuple-element.42), channel_id=1, source_target_pairs={{0,6},{2,0},{4,2},{6,4},{1,7},{3,1},{5,3},{7,5},{8,14},{10,8},{12,... | collective-permute-start | bytes 1376264 | tf_op jit(solution)/shard_map/ppermute | solution.py:322
  20.6 46.1 %all-to-all-start = ((bf16[16,120,128]{2,1,0:T(8,128)(2,1)}), bf16[16,120,128]{2,1,0:T(8,128)(2,1)}, u32[]{:S(2)}, u32[]{:S(2)}) async-start(bf16[16,120,128]{2,1,0:T(8,128)(2,1)} %shard_map.95), calls=%async_computation | async-start | bytes 983040 | tf_op jit(solution)/shard_map/all_to_all | solution.py:335
  35.9 20.3 %collective-permute-start = (bf16[3584,128]{1,0:T(8,128)(2,1)S(1)}, bf16[3584,128]{1,0:T(8,128)(2,1)}, u32[]{:S(2)}, u32[]{:S(2)}) collective-permute-start(bf16[3584,128]{1,0:T(8,128)(2,1)S(1)} %get-tuple-element.50.refs_0_), channel_id=1, source_target_pairs={{0,1},{1,0},{2,3},{3,2},{4,5},{5,4},{6,7},{7,6},{8,9},{9,8},{10,11... | collective-permute-start | bytes 2752520 | tf_op jit(solution)/shard_map/ppermute | solution.py:325
  44.8 22.0 %collective-permute-start.5 = (bf16[3584,128]{1,0:T(8,128)(2,1)}, bf16[3584,128]{1,0:T(8,128)(2,1)S(1)}, u32[]{:S(2)}, u32[]{:S(2)}) collective-permute-start(bf16[3584,128]{1,0:T(8,128)(2,1)} %collective-permute-done.1.refs_0_.refs_2_), channel_id=1, source_target_pairs={{0,1},{1,0},{2,3},{3,2},{4,5},{5,4},{6,7},{7,6},{8,9},{9,8},{10,11... | collective-permute-start | bytes 2752520 | tf_op jit(solution)/shard_map/ppermute | solution.py:338
  46.7 20.1 %collective-permute-start.6 = (bf16[3584,128]{1,0:T(8,128)(2,1)}, bf16[3584,128]{1,0:T(8,128)(2,1)}, u32[]{:S(2)}, u32[]{:S(2)}) collective-permute-start(bf16[3584,128]{1,0:T(8,128)(2,1)} %collective-permute-done.2.refs_1_.refs_4_), channel_id=1, source_target_pairs={{0,1},{1,0},{2,3},{3,2},{4,5},{5,4},{6,7},{7,6},{8,9},{9,8},{10,11... | collective-permute-start | bytes 2752520 | tf_op jit(solution)/shard_map/ppermute | solution.py:338
  49.1 15.8 %collective-permute-start.7 = (bf16[1792,128]{1,0:T(8,128)(2,1)}, bf16[1792,128]{1,0:T(8,128)(2,1)S(1)}, u32[]{:S(2)}, u32[]{:S(2)}) collective-permute-start(bf16[1792,128]{1,0:T(8,128)(2,1)} %collective-permute-done.3.refs_2_), channel_id=1, source_target_pairs={{0,2},{2,4},{4,6},{6,0},{1,3},{3,5},{5,7},{7,1},{8,10},{10,12},{12... | collective-permute-start | bytes 1376264 | tf_op jit(solution)/shard_map/ppermute | solution.py:333
  52.5 14.3 %collective-permute-start.8 = (bf16[1792,128]{1,0:T(8,128)(2,1)}, bf16[1792,128]{1,0:T(8,128)(2,1)S(1)}, u32[]{:S(2)}, u32[]{:S(2)}) collective-permute-start(bf16[1792,128]{1,0:T(8,128)(2,1)} %collective-permute-done.4.refs_3_), channel_id=1, source_target_pairs={{0,6},{2,0},{4,2},{6,4},{1,7},{3,1},{5,3},{7,5},{8,14},{10,8},{12,... | collective-permute-start | bytes 1376264 | tf_op jit(solution)/shard_map/ppermute | solution.py:334
  64.9 12.7 %copy-start.4 = (bf16[1792,128]{1,0:T(8,128)(2,1)}, bf16[1792,128]{1,0:T(8,128)(2,1)S(1)}, u32[]{:S(2)}) copy-start(bf16[1792,128]{1,0:T(8,128)(2,1)S(1)} %collective-permute-done.7.refs_6_) | copy-start | bytes 1376260
  66.8 26.2 %copy-start.5 = (bf16[1792,128]{1,0:T(8,128)(2,1)}, bf16[1792,128]{1,0:T(8,128)(2,1)S(1)}, u32[]{:S(2)}) copy-start(bf16[1792,128]{1,0:T(8,128)(2,1)S(1)} %collective-permute-done.8.refs_7_) | copy-start | bytes 1376260
  66.8 3.8 %copy-start.3 = (bf16[3584,128]{1,0:T(8,128)(2,1)}, bf16[3584,128]{1,0:T(8,128)(2,1)S(1)}, u32[]{:S(2)}) copy-start(bf16[3584,128]{1,0:T(8,128)(2,1)S(1)} %collective-permute-done.5.refs_3_) | copy-start | bytes 2752516
  69.5 23.4 %copy-start.1 = (s32[5]{0:T(128)S(1)}, s32[5]{0:T(128)}, u32[]{:S(2)}) copy-start(s32[5]{0:T(128)} %shard_map.96.scalars) | copy-start | bytes 64
  70.6 22.3 %all-to-all-start.1 = ((bf16[16,8,3712]{2,1,0:T(8,128)(2,1)}), bf16[16,8,3712]{2,1,0:T(8,128)(2,1)S(1)}, u32[]{:S(2)}, u32[]{:S(2)}) async-start(bf16[16,8,3712]{2,1,0:T(8,128)(2,1)} %bitcast.14), calls=%async_computation.1 | async-start | bytes 1900544 | tf_op jit(solution)/shard_map/all_to_all | solution.py:370
  77.6 4.3 %collective-permute-start.9 = (bf16[1792,128]{1,0:T(8,128)(2,1)S(1)}, bf16[1792,128]{1,0:T(8,128)(2,1)S(1)}, u32[]{:S(2)}, u32[]{:S(2)}) collective-permute-start(bf16[1792,128]{1,0:T(8,128)(2,1)S(1)} %collective-permute-done.7.refs_6_), channel_id=1, source_target_pairs={{0,1},{1,0},{2,3},{3,2},{4,5},{5,4},{6,7},{7,6},{8,9},{9,8},{10,11... | collective-permute-start | bytes 1376264 | tf_op jit(solution)/shard_map/ppermute | solution.py:344
  79.5 3.8 %collective-permute-start.10 = (bf16[1792,128]{1,0:T(8,128)(2,1)S(1)}, bf16[1792,128]{1,0:T(8,128)(2,1)S(1)}, u32[]{:S(2)}, u32[]{:S(2)}) collective-permute-start(bf16[1792,128]{1,0:T(8,128)(2,1)S(1)} %collective-permute-done.8.refs_7_), channel_id=1, source_target_pairs={{0,1},{1,0},{2,3},{3,2},{4,5},{5,4},{6,7},{7,6},{8,9},{9,8},{10,11... | collective-permute-start | bytes 1376264 | tf_op jit(solution)/shard_map/ppermute | solution.py:344
  99.4 11.5 %all-to-all-start.2 = ((bf16[4,128,512]{2,1,0:T(8,128)(2,1)}), bf16[4,128,512]{2,1,0:T(8,128)(2,1)S(1)}, u32[]{:S(2)}, u32[]{:S(2)}) async-start(bf16[4,128,512]{2,1,0:T(8,128)(2,1)} %shard_map.97), calls=%async_computation.2 | async-start | bytes 1048576 | tf_op jit(solution)/shard_map/all_to_all | solution.py:388

commit v14 on v13

--- a/solution.py
+++ b/solution.py
@@ -168,14 +168,14 @@
         refs[-1][i] = scalars[i]
 
 
-def mark(scalars, *arrays):
+def mark(scalars, flops, *arrays):
     small = pl.BlockSpec(memory_space=pltpu.SMEM)
     return pl.pallas_call(
         mark_kernel,
         out_shape=jax.ShapeDtypeStruct(scalars.shape, scalars.dtype),
         in_specs=[small] + [pl.BlockSpec(memory_space=pl.ANY)] * len(arrays),
         out_specs=small,
-        cost_estimate=pl.CostEstimate(flops=10**11, bytes_accessed=4096, transcendentals=0),
+        cost_estimate=pl.CostEstimate(flops=flops, bytes_accessed=4096, transcendentals=0),
     )(scalars, *arrays)
 
 
@@ -326,12 +326,13 @@
     scalars = jnp.stack(
         [expert, chip, (chip + chips - 1) % chips, (chip + 1) % chips, (chip + 2) % chips]
     ).astype(jnp.int32)
-    scalars = mark(scalars, ahead, behind, far_up, far_down)
+    scalars = mark(scalars, 10**11, ahead, behind, far_up, far_down)
     ahead, behind, far_up, far_down, scalars = lax.optimization_barrier(
         (ahead, behind, far_up, far_down, scalars)
     )
     far_up = lax.ppermute(far_up, "chip", ahead_of)
     far_down = lax.ppermute(far_down, "chip", behind_of)
+    scalars = mark(scalars, 7 * 10**9, far_up, far_down)
     recv = lax.all_to_all(sent, "node", split_axis=0, concat_axis=0, tiled=True)
     near = (here, here_too)
     for block in (ahead, behind):

time: 184 us -> 178 us (0.967)
  waiting for transfers between devices: 34.6 us -> 28.7 us
    ppermute x2, waiting for transfers between devices: 11.9 us -> 6.24 us  [per_device(): far_up = lax.ppermute(far_up, 'chip', ahead_of)]
  transfers between devices with their start and end apart: 14 -> 14, of which waited for: 7 -> 8; matrix products, arithmetic and copies ran while one was open for 0% -> 0% of each run, Pallas kernels for 1% -> 1%
where the time goes in v14:
time: 178 us; the launch traced here: 177 us
  blocking collectives  62.6 us (35%)
  starting transfers between devices  57.3 us (32%)
  waiting for transfers between devices  28.7 us (16%)
  Pallas kernels  21.7 us (12%)
  other arithmetic  1.93 us (1%)
  local copies, waits for them, and re-layouts  1.86 us (1%)
    all_to_all x1, blocking collectives, per_device(): lax.all_to_all(expanded, 'node', split_axis=0, concat_axis=0, tiled=True)  34.4 us
    pallas_call x5, Pallas kernels, call(): pl.pallas_call(kernel, out_shape=[jax.ShapeDtypeStruct(shape, jnp.bfloat1...  19.3 us
    all_to_all x1, blocking collectives, per_device(): lax.all_to_all(result.reshape(experts * chips, pairs, -1), ('expert', 'ch...  15.4 us
    all_to_all x1, starting transfers between devices, per_device(): recv = lax.all_to_all(sent, 'node', split_axis=0, concat_axis=0, tiled=True)  15.2 us
    all_gather x1, blocking collectives, per_device(): lax.all_gather(jnp.concatenate([active, grad_pre], 1), 'chip', axis=0)  12.8 us
    all_to_all x1, waiting for transfers between devices, per_device(): lax.all_to_all(outgoing, 'chip', split_axis=0, concat_axis=0, tiled=True)  8.73 us
    ppermute x2, starting transfers between devices, per_device(): far_down = lax.ppermute(far_down, 'chip', behind_of)  8.52 us
    all_to_all x1, waiting for transfers between devices, per_device(): lax.all_to_all(spread, ('expert', 'chip'), split_axis=0, concat_axis=0, t...  8.04 us
  transfers between devices with their start and end apart: 14, of which 8 were waited for; matrix products, arithmetic and copies ran while one was open for 0% of the time, Pallas kernels for 1%

profile of v14, /device:TPU:32, one launch (start us, length us, event | category | flops | bytes accessed | tf_op | source)
XLA Modules:
  0.0 176.8 jit_solution(1612006943159013978)
XLA Ops:
  0.7 0.1 pad_add_fusion.chips
  0.8 3.8 %shard_map.94 = (bf16[3584,128]{1,0:T(8,128)(2,1)S(1)}, bf16[3584,128]{1,0:T(8,128)(2,1)S(1)}, bf16[3584,128]{1,0:T(8,128)(2,1)S(1)}, bf16[1792,128]{1,0:T(8,128)(2,1)}, bf16[1792,128]{1,0:T(8,128)(2,1)S(1)}) custom-call(s32[4]{0:T(128)S(1)} %pad_add_fusion.chips, bf16[7168,128]{1,0:T(8,128)(2,1)} %up.1, bf16[128,7168]{1,0:T(8,128)(2,1)} %down.1), custom_call_target="tpu_custom_call" | custom-call | tf_op jit(solution)/shard_map/pallas_call | solution.py:260
  4.6 1.9 %shard_map.95 = bf16[16,120,128]{2,1,0:T(8,128)(2,1)} custom-call(bf16[2,2,4]{2,1,0:T(2,128)(2,1)S(1)} %bitcast.71, s32[2,4]{1,0:T(2,128)} %bitcast.76, s32[2,2,4]{2,1,0:T(2,128)} %bitcast.74, bf16[4,7168]{1,0:T(4,128)(2,1)} %tokens.1, bf16[4,7168]{1,0:T(4,128)(2,1)} %cotangent.1), custom_call_target="tpu_custom_call" | custom-call | tf_op jit(solution)/shard_map/pallas_call | solution.py:260
  6.5 3.4 %collective-permute-start.1 = (bf16[3584,128]{1,0:T(8,128)(2,1)S(1)}, bf16[3584,128]{1,0:T(8,128)(2,1)}, u32[]{:S(2)}, u32[]{:S(2)}) collective-permute-start(bf16[3584,128]{1,0:T(8,128)(2,1)S(1)} %get-tuple-element.39), channel_id=1, source_target_pairs={{0,2},{2,4},{4,6},{6,0},{1,3},{3,5},{5,7},{7,1},{8,10},{10,12},{12... | collective-permute-start | bytes 2752520 | tf_op jit(solution)/shard_map/ppermute | solution.py:323
  9.9 3.7 %collective-permute-start.2 = (bf16[3584,128]{1,0:T(8,128)(2,1)S(1)}, bf16[3584,128]{1,0:T(8,128)(2,1)}, u32[]{:S(2)}, u32[]{:S(2)}) collective-permute-start(bf16[3584,128]{1,0:T(8,128)(2,1)S(1)} %get-tuple-element.40), channel_id=1, source_target_pairs={{0,6},{2,0},{4,2},{6,4},{1,7},{3,1},{5,3},{7,5},{8,14},{10,8},{12,... | collective-permute-start | bytes 2752520 | tf_op jit(solution)/shard_map/ppermute | solution.py:324
  13.6 2.2 %collective-permute-start.3 = (bf16[1792,128]{1,0:T(8,128)(2,1)}, bf16[1792,128]{1,0:T(8,128)(2,1)}, u32[]{:S(2)}, u32[]{:S(2)}) collective-permute-start(bf16[1792,128]{1,0:T(8,128)(2,1)} %get-tuple-element.41), channel_id=1, source_target_pairs={{0,2},{2,4},{4,6},{6,0},{1,3},{3,5},{5,7},{7,1},{8,10},{10,12},{12... | collective-permute-start | bytes 1376264 | tf_op jit(solution)/shard_map/ppermute | solution.py:321
  15.8 4.9 %collective-permute-start.4 = (bf16[1792,128]{1,0:T(8,128)(2,1)S(1)}, bf16[1792,128]{1,0:T(8,128)(2,1)}, u32[]{:S(2)}, u32[]{:S(2)}) collective-permute-start(bf16[1792,128]{1,0:T(8,128)(2,1)S(1)} %get-tuple-element.42), channel_id=1, source_target_pairs={{0,6},{2,0},{4,2},{6,4},{1,7},{3,1},{5,3},{7,5},{8,14},{10,8},{12,... | collective-permute-start | bytes 1376264 | tf_op jit(solution)/shard_map/ppermute | solution.py:322
  20.6 15.2 %all-to-all-start = ((bf16[16,120,128]{2,1,0:T(8,128)(2,1)}), bf16[16,120,128]{2,1,0:T(8,128)(2,1)}, u32[]{:S(2)}, u32[]{:S(2)}) async-start(bf16[16,120,128]{2,1,0:T(8,128)(2,1)} %shard_map.95), calls=%async_computation | async-start | bytes 983040 | tf_op jit(solution)/shard_map/all_to_all | solution.py:336
  35.9 0.6 stack.49.scalars
  36.4 5.2 %collective-permute-done.3.refs_2_ = bf16[1792,128]{1,0:T(8,128)(2,1)} collective-permute-done((bf16[1792,128]{1,0:T(8,128)(2,1)}, bf16[1792,128]{1,0:T(8,128)(2,1)}, u32[]{:S(2)}, u32[]{:S(2)}) %collective-permute-start.3) | collective-permute-done | bytes 458784 | tf_op jit(solution)/shard_map/ppermute | solution.py:321
  41.6 1.9 %collective-permute-done.4.refs_3_ = bf16[1792,128]{1,0:T(8,128)(2,1)} collective-permute-done((bf16[1792,128]{1,0:T(8,128)(2,1)S(1)}, bf16[1792,128]{1,0:T(8,128)(2,1)}, u32[]{:S(2)}, u32[]{:S(2)}) %collective-permute-start.4) | collective-permute-done | bytes 458784 | tf_op jit(solution)/shard_map/ppermute | solution.py:322
  43.6 0.0 collective-permute-done.1.refs_0_.refs_2_
  43.6 0.0 collective-permute-done.2.refs_1_.refs_4_
  43.6 1.2 shard_map.96.scalars
  44.8 3.4 %collective-permute-start.7 = (bf16[1792,128]{1,0:T(8,128)(2,1)}, bf16[1792,128]{1,0:T(8,128)(2,1)S(1)}, u32[]{:S(2)}, u32[]{:S(2)}) collective-permute-start(bf16[1792,128]{1,0:T(8,128)(2,1)} %collective-permute-done.3.refs_2_), channel_id=1, source_target_pairs={{0,2},{2,4},{4,6},{6,0},{1,3},{3,5},{5,7},{7,1},{8,10},{10,12},{12... | collective-permute-start | bytes 1376264 | tf_op jit(solution)/shard_map/ppermute | solution.py:333
  48.2 3.7 %collective-permute-start.8 = (bf16[1792,128]{1,0:T(8,128)(2,1)}, bf16[1792,128]{1,0:T(8,128)(2,1)}, u32[]{:S(2)}, u32[]{:S(2)}) collective-permute-start(bf16[1792,128]{1,0:T(8,128)(2,1)} %collective-permute-done.4.refs_3_), channel_id=1, source_target_pairs={{0,6},{2,0},{4,2},{6,4},{1,7},{3,1},{5,3},{7,5},{8,14},{10,8},{12,... | collective-permute-start | bytes 1376264 | tf_op jit(solution)/shard_map/ppermute | solution.py:334
  51.8 1.9 %collective-permute-start = (bf16[3584,128]{1,0:T(8,128)(2,1)S(1)}, bf16[3584,128]{1,0:T(8,128)(2,1)S(1)}, u32[]{:S(2)}, u32[]{:S(2)}) collective-permute-start(bf16[3584,128]{1,0:T(8,128)(2,1)S(1)} %get-tuple-element.50.refs_0_), channel_id=1, source_target_pairs={{0,1},{1,0},{2,3},{3,2},{4,5},{5,4},{6,7},{7,6},{8,9},{9,8},{10,11... | collective-permute-start | bytes 2752520 | tf_op jit(solution)/shard_map/ppermute | solution.py:325
  53.8 2.4 %collective-permute-start.5 = (bf16[3584,128]{1,0:T(8,128)(2,1)}, bf16[3584,128]{1,0:T(8,128)(2,1)S(1)}, u32[]{:S(2)}, u32[]{:S(2)}) collective-permute-start(bf16[3584,128]{1,0:T(8,128)(2,1)} %collective-permute-done.1.refs_0_.refs_2_), channel_id=1, source_target_pairs={{0,1},{1,0},{2,3},{3,2},{4,5},{5,4},{6,7},{7,6},{8,9},{9,8},{10,11... | collective-permute-start | bytes 2752520 | tf_op jit(solution)/shard_map/ppermute | solution.py:339
  56.2 1.9 %collective-permute-start.6 = (bf16[3584,128]{1,0:T(8,128)(2,1)}, bf16[3584,128]{1,0:T(8,128)(2,1)}, u32[]{:S(2)}, u32[]{:S(2)}) collective-permute-start(bf16[3584,128]{1,0:T(8,128)(2,1)} %collective-permute-done.2.refs_1_.refs_4_), channel_id=1, source_target_pairs={{0,1},{1,0},{2,3},{3,2},{4,5},{5,4},{6,7},{7,6},{8,9},{9,8},{10,11... | collective-permute-start | bytes 2752520 | tf_op jit(solution)/shard_map/ppermute | solution.py:339
  58.1 1.0 collective-permute-done.7.refs_0_.refs_6_
  59.2 2.0 %collective-permute-done.8.refs_1_.refs_7_ = bf16[1792,128]{1,0:T(8,128)(2,1)} collective-permute-done((bf16[1792,128]{1,0:T(8,128)(2,1)}, bf16[1792,128]{1,0:T(8,128)(2,1)}, u32[]{:S(2)}, u32[]{:S(2)}) %collective-permute-start.8) | collective-permute-done | bytes 458784 | tf_op jit(solution)/shard_map/ppermute | solution.py:334
  61.2 1.2 shard_map.97.scalars
  62.4 0.2 all-to-all-done
  62.6 1.2 compare_reduce_fusion
  63.8 0.1 copy.12
  63.9 0.1 add_reduce_fusion
  64.0 1.2 convolution_convert_fusion.1
  65.3 0.0 copy-start.1
  65.4 1.0 broadcast_in_dim.10
  66.4 6.8 %all-to-all-start.1 = ((bf16[16,8,3712]{2,1,0:T(8,128)(2,1)}), bf16[16,8,3712]{2,1,0:T(8,128)(2,1)S(1)}, u32[]{:S(2)}, u32[]{:S(2)}) async-start(bf16[16,8,3712]{2,1,0:T(8,128)(2,1)} %bitcast.14), calls=%async_computation.1 | async-start | bytes 1900544 | tf_op jit(solution)/shard_map/all_to_all | solution.py:371
  73.2 1.9 %collective-permute-start.9 = (bf16[1792,128]{1,0:T(8,128)(2,1)S(1)}, bf16[1792,128]{1,0:T(8,128)(2,1)S(1)}, u32[]{:S(2)}, u32[]{:S(2)}) collective-permute-start(bf16[1792,128]{1,0:T(8,128)(2,1)S(1)} %copy-done.6), channel_id=1, source_target_pairs={{0,1},{1,0},{2,3},{3,2},{4,5},{5,4},{6,7},{7,6},{8,9},{9,8},{10,11... | collective-permute-start | bytes 1376264 | tf_op jit(solution)/shard_map/ppermute | solution.py:345
  75.2 2.4 %collective-permute-start.10 = (bf16[1792,128]{1,0:T(8,128)(2,1)}, bf16[1792,128]{1,0:T(8,128)(2,1)S(1)}, u32[]{:S(2)}, u32[]{:S(2)}) collective-permute-start(bf16[1792,128]{1,0:T(8,128)(2,1)} %collective-permute-done.8.refs_1_.refs_7_), channel_id=1, source_target_pairs={{0,1},{1,0},{2,3},{3,2},{4,5},{5,4},{6,7},{7,6},{8,9},{9,8},{10,11... | collective-permute-start | bytes 1376264 | tf_op jit(solution)/shard_map/ppermute | solution.py:345
  77.6 1.6 collective-permute-done.10.refs_9_
  79.2 8.0 %all-to-all-done.1 = bf16[16,8,3712]{2,1,0:T(8,128)(2,1)S(1)} async-done(((bf16[16,8,3712]{2,1,0:T(8,128)(2,1)}), bf16[16,8,3712]{2,1,0:T(8,128)(2,1)S(1)}, u32[]{:S(2)}, u32[]{:S(2)}) %all-to-all-start.1) | async-done | bytes 950304 | tf_op jit(solution)/shard_map/all_to_all | solution.py:371
  87.3 6.5 %shard_map.98 = bf16[4,128,512]{2,1,0:T(8,128)(2,1)} custom-call(s32[5]{0:T(128)S(1)} %copy-done.1, bf16[128,3712]{1,0:T(8,128)(2,1)S(1)} %bitcast.66, bf16[3584,128]{1,0:T(8,128)(2,1)} %copy-done, bf16[3584,128]{1,0:T(8,128)(2,1)} %copy-done.3, bf16[3584,128]{1,0:T(8,128)(2,1)} %collective-permute-done.1.refs_0_.refs_2_, bf16[3584,128]{1,0:T(8,128)(2,1)} %copy-done.4, ...), custom_call_target="tpu_custom_call" | custom-call | tf_op jit(solution)/shard_map/pallas_call | solution.py:260
  93.8 3.5 %all-to-all-start.2 = ((bf16[4,128,512]{2,1,0:T(8,128)(2,1)}), bf16[4,128,512]{2,1,0:T(8,128)(2,1)S(1)}, u32[]{:S(2)}, u32[]{:S(2)}) async-start(bf16[4,128,512]{2,1,0:T(8,128)(2,1)} %shard_map.98), calls=%async_computation.2 | async-start | bytes 1048576 | tf_op jit(solution)/shard_map/all_to_all | solution.py:389
  97.3 0.1 select_reduce_fusion
  97.4 8.7 %all-to-all-done.2 = bf16[4,128,512]{2,1,0:T(8,128)(2,1)S(1)} async-done(((bf16[4,128,512]{2,1,0:T(8,128)(2,1)}), bf16[4,128,512]{2,1,0:T(8,128)(2,1)S(1)}, u32[]{:S(2)}, u32[]{:S(2)}) %all-to-all-start.2) | async-done | bytes 524320 | tf_op jit(solution)/shard_map/all_to_all | solution.py:389
  106.1 0.1 convert_reduce_fusion.1
  106.2 0.1 multiply_convert_fusion
  106.3 12.8 %all-gather = bf16[512,512]{1,0:T(8,128)(2,1)S(1)} all-gather(bf16[128,512]{1,0:T(8,128)(2,1)S(1)} %pad_maximum_fusion.1), channel_id=2, replica_groups=mesh['node'=16,'expert'=4,'chip'=4,'core'=2] {'chip'}, dimensions={0}, use_global_device_ids=true | all-gather | bytes 655360 | tf_op jit(solution)/shard_map/all_gather | solution.py:396
  119.1 5.4 %shard_map.99 = bf16[128,3712]{1,0:T(8,128)(2,1)S(1)} custom-call(s32[5]{0:T(128)S(1)} %copy-done.1, bf16[128,3712]{1,0:T(8,128)(2,1)S(1)} %bitcast.68, bf16[4,128,512]{2,1,0:T(8,128)(2,1)S(1)} %bitcast.70, bf16[3584,128]{1,0:T(8,128)(2,1)} %copy-done, bf16[3584,128]{1,0:T(8,128)(2,1)} %copy-done.3, ...), custom_call_target="tpu_custom_call" | custom-call | tf_op jit(solution)/shard_map/pallas_call | solution.py:260
  124.5 15.4 %all_to_all.25 = bf16[16,8,3712]{2,1,0:T(8,128)(2,1)S(1)} all-to-all(bf16[16,8,3712]{2,1,0:T(8,128)(2,1)S(1)} %bitcast.69), channel_id=1, replica_groups=mesh['node'=16,'expert'=4,'chip'=4,'core'=2] {'expert','chip'}, dimensions={0} | all-to-all | bytes 1900544 | tf_op jit(solution)/shard_map/all_to_all | solution.py:410
  140.0 0.1 convert_reduce_fusion
  140.2 0.3 convolution_convert_fusion
  140.6 0.1 copy.14
  140.7 34.4 %all_to_all.26.home = bf16[16,120,128]{2,1,0:T(8,128)(2,1)S(1)} all-to-all(bf16[16,120,128]{2,1,0:T(8,128)(2,1)S(1)} %bitcast.73), channel_id=1, replica_groups=mesh['node'=16,'expert'=4,'chip'=4,'core'=2] {'node'}, dimensions={0} | all-to-all | bytes 983040 | tf_op jit(solution)/shard_map/all_to_all | solution.py:427
  175.1 1.7 shard_map.100
  (38 shorter events, 0.3 us)
Async XLA Ops:
  0.7 3.8 %copy-start.2 = (bf16[4,2,2]{0,2,1:T(2,128)(2,1)S(1)}, bf16[4,2,2]{0,2,1:T(2,128)(2,1)}, u32[]{:S(2)}) copy-start(bf16[4,2,2]{0,2,1:T(2,128)(2,1)} %param.11) | copy-start | bytes 100
  4.6 47.2 %copy-start = (bf16[3584,128]{1,0:T(8,128)(2,1)}, bf16[3584,128]{1,0:T(8,128)(2,1)S(1)}, u32[]{:S(2)}) copy-start(bf16[3584,128]{1,0:T(8,128)(2,1)S(1)} %get-tuple-element.50.refs_0_) | copy-start | bytes 2752516
  6.5 37.1 %collective-permute-start.1 = (bf16[3584,128]{1,0:T(8,128)(2,1)S(1)}, bf16[3584,128]{1,0:T(8,128)(2,1)}, u32[]{:S(2)}, u32[]{:S(2)}) collective-permute-start(bf16[3584,128]{1,0:T(8,128)(2,1)S(1)} %get-tuple-element.39), channel_id=1, source_target_pairs={{0,2},{2,4},{4,6},{6,0},{1,3},{3,5},{5,7},{7,1},{8,10},{10,12},{12... | collective-permute-start | bytes 2752520 | tf_op jit(solution)/shard_map/ppermute | solution.py:323
  9.9 33.6 %collective-permute-start.2 = (bf16[3584,128]{1,0:T(8,128)(2,1)S(1)}, bf16[3584,128]{1,0:T(8,128)(2,1)}, u32[]{:S(2)}, u32[]{:S(2)}) collective-permute-start(bf16[3584,128]{1,0:T(8,128)(2,1)S(1)} %get-tuple-element.40), channel_id=1, source_target_pairs={{0,6},{2,0},{4,2},{6,4},{1,7},{3,1},{5,3},{7,5},{8,14},{10,8},{12,... | collective-permute-start | bytes 2752520 | tf_op jit(solution)/shard_map/ppermute | solution.py:324
  13.6 28.1 %collective-permute-start.3 = (bf16[1792,128]{1,0:T(8,128)(2,1)}, bf16[1792,128]{1,0:T(8,128)(2,1)}, u32[]{:S(2)}, u32[]{:S(2)}) collective-permute-start(bf16[1792,128]{1,0:T(8,128)(2,1)} %get-tuple-element.41), channel_id=1, source_target_pairs={{0,2},{2,4},{4,6},{6,0},{1,3},{3,5},{5,7},{7,1},{8,10},{10,12},{12... | collective-permute-start | bytes 1376264 | tf_op jit(solution)/shard_map/ppermute | solution.py:321
  15.8 27.8 %collective-permute-start.4 = (bf16[1792,128]{1,0:T(8,128)(2,1)S(1)}, bf16[1792,128]{1,0:T(8,128)(2,1)}, u32[]{:S(2)}, u32[]{:S(2)}) collective-permute-start(bf16[1792,128]{1,0:T(8,128)(2,1)S(1)} %get-tuple-element.42), channel_id=1, source_target_pairs={{0,6},{2,0},{4,2},{6,4},{1,7},{3,1},{5,3},{7,5},{8,14},{10,8},{12,... | collective-permute-start | bytes 1376264 | tf_op jit(solution)/shard_map/ppermute | solution.py:322
  20.6 41.9 %all-to-all-start = ((bf16[16,120,128]{2,1,0:T(8,128)(2,1)}), bf16[16,120,128]{2,1,0:T(8,128)(2,1)}, u32[]{:S(2)}, u32[]{:S(2)}) async-start(bf16[16,120,128]{2,1,0:T(8,128)(2,1)} %shard_map.95), calls=%async_computation | async-start | bytes 983040 | tf_op jit(solution)/shard_map/all_to_all | solution.py:336
  44.8 14.4 %collective-permute-start.7 = (bf16[1792,128]{1,0:T(8,128)(2,1)}, bf16[1792,128]{1,0:T(8,128)(2,1)S(1)}, u32[]{:S(2)}, u32[]{:S(2)}) collective-permute-start(bf16[1792,128]{1,0:T(8,128)(2,1)} %collective-permute-done.3.refs_2_), channel_id=1, source_target_pairs={{0,2},{2,4},{4,6},{6,0},{1,3},{3,5},{5,7},{7,1},{8,10},{10,12},{12... | collective-permute-start | bytes 1376264 | tf_op jit(solution)/shard_map/ppermute | solution.py:333
  48.2 13.0 %collective-permute-start.8 = (bf16[1792,128]{1,0:T(8,128)(2,1)}, bf16[1792,128]{1,0:T(8,128)(2,1)}, u32[]{:S(2)}, u32[]{:S(2)}) collective-permute-start(bf16[1792,128]{1,0:T(8,128)(2,1)} %collective-permute-done.4.refs_3_), channel_id=1, source_target_pairs={{0,6},{2,0},{4,2},{6,4},{1,7},{3,1},{5,3},{7,5},{8,14},{10,8},{12,... | collective-permute-start | bytes 1376264 | tf_op jit(solution)/shard_map/ppermute | solution.py:334
  51.8 10.5 %collective-permute-start = (bf16[3584,128]{1,0:T(8,128)(2,1)S(1)}, bf16[3584,128]{1,0:T(8,128)(2,1)S(1)}, u32[]{:S(2)}, u32[]{:S(2)}) collective-permute-start(bf16[3584,128]{1,0:T(8,128)(2,1)S(1)} %get-tuple-element.50.refs_0_), channel_id=1, source_target_pairs={{0,1},{1,0},{2,3},{3,2},{4,5},{5,4},{6,7},{7,6},{8,9},{9,8},{10,11... | collective-permute-start | bytes 2752520 | tf_op jit(solution)/shard_map/ppermute | solution.py:325
  53.8 8.6 %collective-permute-start.5 = (bf16[3584,128]{1,0:T(8,128)(2,1)}, bf16[3584,128]{1,0:T(8,128)(2,1)S(1)}, u32[]{:S(2)}, u32[]{:S(2)}) collective-permute-start(bf16[3584,128]{1,0:T(8,128)(2,1)} %collective-permute-done.1.refs_0_.refs_2_), channel_id=1, source_target_pairs={{0,1},{1,0},{2,3},{3,2},{4,5},{5,4},{6,7},{7,6},{8,9},{9,8},{10,11... | collective-permute-start | bytes 2752520 | tf_op jit(solution)/shard_map/ppermute | solution.py:339
  56.2 6.2 %collective-permute-start.6 = (bf16[3584,128]{1,0:T(8,128)(2,1)}, bf16[3584,128]{1,0:T(8,128)(2,1)}, u32[]{:S(2)}, u32[]{:S(2)}) collective-permute-start(bf16[3584,128]{1,0:T(8,128)(2,1)} %collective-permute-done.2.refs_1_.refs_4_), channel_id=1, source_target_pairs={{0,1},{1,0},{2,3},{3,2},{4,5},{5,4},{6,7},{7,6},{8,9},{9,8},{10,11... | collective-permute-start | bytes 2752520 | tf_op jit(solution)/shard_map/ppermute | solution.py:339
  59.1 2.0 %copy-start.5 = (bf16[1792,128]{1,0:T(8,128)(2,1)}, bf16[1792,128]{1,0:T(8,128)(2,1)S(1)}, u32[]{:S(2)}) copy-start(bf16[1792,128]{1,0:T(8,128)(2,1)S(1)} %collective-permute-done.7.refs_0_.refs_6_) | copy-start | bytes 1376260
  62.4 4.0 %copy-start.3 = (bf16[3584,128]{1,0:T(8,128)(2,1)}, bf16[3584,128]{1,0:T(8,128)(2,1)S(1)}, u32[]{:S(2)}) copy-start(bf16[3584,128]{1,0:T(8,128)(2,1)S(1)} %collective-permute-done.refs_1_) | copy-start | bytes 2752516
  62.4 4.0 %copy-start.4 = (bf16[3584,128]{1,0:T(8,128)(2,1)}, bf16[3584,128]{1,0:T(8,128)(2,1)S(1)}, u32[]{:S(2)}) copy-start(bf16[3584,128]{1,0:T(8,128)(2,1)S(1)} %collective-permute-done.5.refs_3_) | copy-start | bytes 2752516
  65.3 7.9 %copy-start.6 = (bf16[1792,128]{1,0:T(8,128)(2,1)S(1)}, bf16[1792,128]{1,0:T(8,128)(2,1)}, u32[]{:S(2)}) copy-start(bf16[1792,128]{1,0:T(8,128)(2,1)} %copy-done.5) | copy-start | bytes 1376260
  65.3 21.9 %copy-start.1 = (s32[5]{0:T(128)S(1)}, s32[5]{0:T(128)}, u32[]{:S(2)}) copy-start(s32[5]{0:T(128)} %shard_map.97.scalars) | copy-start | bytes 64
  66.4 20.9 %all-to-all-start.1 = ((bf16[16,8,3712]{2,1,0:T(8,128)(2,1)}), bf16[16,8,3712]{2,1,0:T(8,128)(2,1)S(1)}, u32[]{:S(2)}, u32[]{:S(2)}) async-start(bf16[16,8,3712]{2,1,0:T(8,128)(2,1)} %bitcast.14), calls=%async_computation.1 | async-start | bytes 1900544 | tf_op jit(solution)/shard_map/all_to_all | solution.py:371
  73.2 4.3 %collective-permute-start.9 = (bf16[1792,128]{1,0:T(8,128)(2,1)S(1)}, bf16[1792,128]{1,0:T(8,128)(2,1)S(1)}, u32[]{:S(2)}, u32[]{:S(2)}) collective-permute-start(bf16[1792,128]{1,0:T(8,128)(2,1)S(1)} %copy-done.6), channel_id=1, source_target_pairs={{0,1},{1,0},{2,3},{3,2},{4,5},{5,4},{6,7},{7,6},{8,9},{9,8},{10,11... | collective-permute-start | bytes 1376264 | tf_op jit(solution)/shard_map/ppermute | solution.py:345
  75.2 4.0 %collective-permute-start.10 = (bf16[1792,128]{1,0:T(8,128)(2,1)}, bf16[1792,128]{1,0:T(8,128)(2,1)S(1)}, u32[]{:S(2)}, u32[]{:S(2)}) collective-permute-start(bf16[1792,128]{1,0:T(8,128)(2,1)} %collective-permute-done.8.refs_1_.refs_7_), channel_id=1, source_target_pairs={{0,1},{1,0},{2,3},{3,2},{4,5},{5,4},{6,7},{7,6},{8,9},{9,8},{10,11... | collective-permute-start | bytes 1376264 | tf_op jit(solution)/shard_map/ppermute | solution.py:345
  93.8 12.3 %all-to-all-start.2 = ((bf16[4,128,512]{2,1,0:T(8,128)(2,1)}), bf16[4,128,512]{2,1,0:T(8,128)(2,1)S(1)}, u32[]{:S(2)}, u32[]{:S(2)}) async-start(bf16[4,128,512]{2,1,0:T(8,128)(2,1)} %shard_map.98), calls=%async_computation.2 | async-start | bytes 1048576 | tf_op jit(solution)/shard_map/all_to_all | solution.py:389

commit v15 on v14

--- a/solution.py
+++ b/solution.py
@@ -334,15 +334,6 @@
     far_down = lax.ppermute(far_down, "chip", behind_of)
     scalars = mark(scalars, 7 * 10**9, far_up, far_down)
     recv = lax.all_to_all(sent, "node", split_axis=0, concat_axis=0, tiled=True)
-    near = (here, here_too)
-    for block in (ahead, behind):
-        near += (block, lax.ppermute(block, "core", swap))
-    recv, near, far_up, far_down, scalars = lax.optimization_barrier(
-        (recv, near, far_up, far_down, scalars)
-    )
-    blocks = near + (far_up, far_down)
-    for block in (far_up, far_down):
-        blocks += (lax.ppermute(block, "core", swap),)
     held = [
         pltpu.VMEM((chips * CORES, 2 * wide, hidden), bf16),
         pltpu.SemaphoreType.DMA((4, chips * CORES, 2)),
@@ -368,6 +359,15 @@
     spread = jnp.broadcast_to(parts[None], (experts,) + parts.shape).reshape(
         experts * chips, pairs, -1
     )
+    near = (here, here_too)
+    for block in (ahead, behind):
+        near += (block, lax.ppermute(block, "core", swap))
+    spread, near, far_up, far_down, scalars = lax.optimization_barrier(
+        (spread, near, far_up, far_down, scalars)
+    )
+    blocks = near + (far_up, far_down)
+    for block in (far_up, far_down):
+        blocks += (lax.ppermute(block, "core", swap),)
     rows = lax.all_to_all(
         spread, ("expert", "chip"), split_axis=0, concat_axis=0, tiled=True
     ).reshape(experts * chips * pairs, -1)

time: 178 us -> 178 us (level)
  transfers between devices with their start and end apart: 14 -> 14, of which waited for: 8 -> 8; matrix products, arithmetic and copies ran while one was open for 0% -> 2% of each run, Pallas kernels for 1% -> 1%
where the time goes in v15:
time: 178 us; the launch traced here: 177 us
  blocking collectives  62.6 us (35%)
  starting transfers between devices  57.2 us (32%)
  waiting for transfers between devices  28.8 us (16%)
  Pallas kernels  21.7 us (12%)
  local copies, waits for them, and re-layouts  2.09 us (1%)
  other arithmetic  1.89 us (1%)
    all_to_all x1, blocking collectives, per_device(): lax.all_to_all(expanded, 'node', split_axis=0, concat_axis=0, tiled=True)  34.3 us
    pallas_call x5, Pallas kernels, call(): pl.pallas_call(kernel, out_shape=[jax.ShapeDtypeStruct(shape, jnp.bfloat1...  19.3 us
    all_to_all x1, blocking collectives, per_device(): lax.all_to_all(result.reshape(experts * chips, pairs, -1), ('expert', 'ch...  15.5 us
    all_to_all x1, starting transfers between devices, per_device(): recv = lax.all_to_all(sent, 'node', split_axis=0, concat_axis=0, tiled=True)  15.2 us
    all_gather x1, blocking collectives, per_device(): lax.all_gather(jnp.concatenate([active, grad_pre], 1), 'chip', axis=0)  12.8 us
    all_to_all x1, waiting for transfers between devices, per_device(): lax.all_to_all(outgoing, 'chip', split_axis=0, concat_axis=0, tiled=True)  8.73 us
    ppermute x2, starting transfers between devices, per_device(): far_down = lax.ppermute(far_down, 'chip', behind_of)  8.52 us
    all_to_all x1, waiting for transfers between devices, per_device(): lax.all_to_all(spread, ('expert', 'chip'), split_axis=0, concat_axis=0, t...  8.04 us
  transfers between devices with their start and end apart: 14, of which 8 were waited for; matrix products, arithmetic and copies ran while one was open for 2% of the time, Pallas kernels for 1%

profile of v15, /device:TPU:32, one launch (start us, length us, event | category | flops | bytes accessed | tf_op | source)
XLA Modules:
  0.0 176.9 jit_solution(14871745353264501235)
XLA Ops:
  0.7 0.1 pad_add_fusion.chips
  0.8 3.8 %shard_map.94 = (bf16[3584,128]{1,0:T(8,128)(2,1)S(1)}, bf16[3584,128]{1,0:T(8,128)(2,1)S(1)}, bf16[3584,128]{1,0:T(8,128)(2,1)S(1)}, bf16[1792,128]{1,0:T(8,128)(2,1)}, bf16[1792,128]{1,0:T(8,128)(2,1)S(1)}) custom-call(s32[4]{0:T(128)S(1)} %pad_add_fusion.chips, bf16[7168,128]{1,0:T(8,128)(2,1)} %up.1, bf16[128,7168]{1,0:T(8,128)(2,1)} %down.1), custom_call_target="tpu_custom_call" | custom-call | tf_op jit(solution)/shard_map/pallas_call | solution.py:260
  4.6 1.9 %shard_map.95 = bf16[16,120,128]{2,1,0:T(8,128)(2,1)} custom-call(bf16[2,2,4]{2,1,0:T(2,128)(2,1)S(1)} %bitcast.71, s32[2,4]{1,0:T(2,128)} %bitcast.76, s32[2,2,4]{2,1,0:T(2,128)} %bitcast.74, bf16[4,7168]{1,0:T(4,128)(2,1)} %tokens.1, bf16[4,7168]{1,0:T(4,128)(2,1)} %cotangent.1), custom_call_target="tpu_custom_call" | custom-call | tf_op jit(solution)/shard_map/pallas_call | solution.py:260
  6.5 3.4 %collective-permute-start.1 = (bf16[3584,128]{1,0:T(8,128)(2,1)S(1)}, bf16[3584,128]{1,0:T(8,128)(2,1)}, u32[]{:S(2)}, u32[]{:S(2)}) collective-permute-start(bf16[3584,128]{1,0:T(8,128)(2,1)S(1)} %get-tuple-element.39), channel_id=1, source_target_pairs={{0,2},{2,4},{4,6},{6,0},{1,3},{3,5},{5,7},{7,1},{8,10},{10,12},{12... | collective-permute-start | bytes 2752520 | tf_op jit(solution)/shard_map/ppermute | solution.py:323
  9.9 3.7 %collective-permute-start.2 = (bf16[3584,128]{1,0:T(8,128)(2,1)S(1)}, bf16[3584,128]{1,0:T(8,128)(2,1)}, u32[]{:S(2)}, u32[]{:S(2)}) collective-permute-start(bf16[3584,128]{1,0:T(8,128)(2,1)S(1)} %get-tuple-element.40), channel_id=1, source_target_pairs={{0,6},{2,0},{4,2},{6,4},{1,7},{3,1},{5,3},{7,5},{8,14},{10,8},{12,... | collective-permute-start | bytes 2752520 | tf_op jit(solution)/shard_map/ppermute | solution.py:324
  13.6 2.2 %collective-permute-start.3 = (bf16[1792,128]{1,0:T(8,128)(2,1)}, bf16[1792,128]{1,0:T(8,128)(2,1)}, u32[]{:S(2)}, u32[]{:S(2)}) collective-permute-start(bf16[1792,128]{1,0:T(8,128)(2,1)} %get-tuple-element.41), channel_id=1, source_target_pairs={{0,2},{2,4},{4,6},{6,0},{1,3},{3,5},{5,7},{7,1},{8,10},{10,12},{12... | collective-permute-start | bytes 1376264 | tf_op jit(solution)/shard_map/ppermute | solution.py:321
  15.8 4.9 %collective-permute-start.4 = (bf16[1792,128]{1,0:T(8,128)(2,1)S(1)}, bf16[1792,128]{1,0:T(8,128)(2,1)}, u32[]{:S(2)}, u32[]{:S(2)}) collective-permute-start(bf16[1792,128]{1,0:T(8,128)(2,1)S(1)} %get-tuple-element.42), channel_id=1, source_target_pairs={{0,6},{2,0},{4,2},{6,4},{1,7},{3,1},{5,3},{7,5},{8,14},{10,8},{12,... | collective-permute-start | bytes 1376264 | tf_op jit(solution)/shard_map/ppermute | solution.py:322
  20.6 15.2 %all-to-all-start = ((bf16[16,120,128]{2,1,0:T(8,128)(2,1)}), bf16[16,120,128]{2,1,0:T(8,128)(2,1)}, u32[]{:S(2)}, u32[]{:S(2)}) async-start(bf16[16,120,128]{2,1,0:T(8,128)(2,1)} %shard_map.95), calls=%async_computation | async-start | bytes 983040 | tf_op jit(solution)/shard_map/all_to_all | solution.py:336
  35.9 0.6 stack.54.scalars
  36.4 5.2 %collective-permute-done.3.refs_2_ = bf16[1792,128]{1,0:T(8,128)(2,1)} collective-permute-done((bf16[1792,128]{1,0:T(8,128)(2,1)}, bf16[1792,128]{1,0:T(8,128)(2,1)}, u32[]{:S(2)}, u32[]{:S(2)}) %collective-permute-start.3) | collective-permute-done | bytes 458784 | tf_op jit(solution)/shard_map/ppermute | solution.py:321
  41.6 1.9 %collective-permute-done.4.refs_3_ = bf16[1792,128]{1,0:T(8,128)(2,1)} collective-permute-done((bf16[1792,128]{1,0:T(8,128)(2,1)S(1)}, bf16[1792,128]{1,0:T(8,128)(2,1)}, u32[]{:S(2)}, u32[]{:S(2)}) %collective-permute-start.4) | collective-permute-done | bytes 458784 | tf_op jit(solution)/shard_map/ppermute | solution.py:322
  43.6 1.2 shard_map.96.scalars
  44.8 3.4 %collective-permute-start.7 = (bf16[1792,128]{1,0:T(8,128)(2,1)}, bf16[1792,128]{1,0:T(8,128)(2,1)S(1)}, u32[]{:S(2)}, u32[]{:S(2)}) collective-permute-start(bf16[1792,128]{1,0:T(8,128)(2,1)} %collective-permute-done.3.refs_2_), channel_id=1, source_target_pairs={{0,2},{2,4},{4,6},{6,0},{1,3},{3,5},{5,7},{7,1},{8,10},{10,12},{12... | collective-permute-start | bytes 1376264 | tf_op jit(solution)/shard_map/ppermute | solution.py:333
  48.2 3.7 %collective-permute-start.8 = (bf16[1792,128]{1,0:T(8,128)(2,1)}, bf16[1792,128]{1,0:T(8,128)(2,1)}, u32[]{:S(2)}, u32[]{:S(2)}) collective-permute-start(bf16[1792,128]{1,0:T(8,128)(2,1)} %collective-permute-done.4.refs_3_), channel_id=1, source_target_pairs={{0,6},{2,0},{4,2},{6,4},{1,7},{3,1},{5,3},{7,5},{8,14},{10,8},{12,... | collective-permute-start | bytes 1376264 | tf_op jit(solution)/shard_map/ppermute | solution.py:334
  51.8 1.9 %collective-permute-start = (bf16[3584,128]{1,0:T(8,128)(2,1)S(1)}, bf16[3584,128]{1,0:T(8,128)(2,1)S(1)}, u32[]{:S(2)}, u32[]{:S(2)}) collective-permute-start(bf16[3584,128]{1,0:T(8,128)(2,1)S(1)} %get-tuple-element.50.refs_0_), channel_id=1, source_target_pairs={{0,1},{1,0},{2,3},{3,2},{4,5},{5,4},{6,7},{7,6},{8,9},{9,8},{10,11... | collective-permute-start | bytes 2752520 | tf_op jit(solution)/shard_map/ppermute | solution.py:325
  53.8 2.4 %collective-permute-start.5 = (bf16[3584,128]{1,0:T(8,128)(2,1)}, bf16[3584,128]{1,0:T(8,128)(2,1)S(1)}, u32[]{:S(2)}, u32[]{:S(2)}) collective-permute-start(bf16[3584,128]{1,0:T(8,128)(2,1)} %collective-permute-done.1.refs_0_.refs_2_), channel_id=1, source_target_pairs={{0,1},{1,0},{2,3},{3,2},{4,5},{5,4},{6,7},{7,6},{8,9},{9,8},{10,11... | collective-permute-start | bytes 2752520 | tf_op jit(solution)/shard_map/ppermute | solution.py:364
  56.2 1.9 %collective-permute-start.6 = (bf16[3584,128]{1,0:T(8,128)(2,1)}, bf16[3584,128]{1,0:T(8,128)(2,1)}, u32[]{:S(2)}, u32[]{:S(2)}) collective-permute-start(bf16[3584,128]{1,0:T(8,128)(2,1)} %collective-permute-done.2.refs_1_.refs_4_), channel_id=1, source_target_pairs={{0,1},{1,0},{2,3},{3,2},{4,5},{5,4},{6,7},{7,6},{8,9},{9,8},{10,11... | collective-permute-start | bytes 2752520 | tf_op jit(solution)/shard_map/ppermute | solution.py:364
  58.1 1.0 collective-permute-done.7.refs_0_.refs_6_
  59.1 2.0 %collective-permute-done.8.refs_1_.refs_7_ = bf16[1792,128]{1,0:T(8,128)(2,1)} collective-permute-done((bf16[1792,128]{1,0:T(8,128)(2,1)}, bf16[1792,128]{1,0:T(8,128)(2,1)}, u32[]{:S(2)}, u32[]{:S(2)}) %collective-permute-start.8) | collective-permute-done | bytes 458784 | tf_op jit(solution)/shard_map/ppermute | solution.py:334
  61.2 1.2 shard_map.97.scalars
  62.4 0.2 all-to-all-done
  62.5 1.1 compare_reduce_fusion
  63.7 0.1 copy.12
  63.8 0.1 add_reduce_fusion
  63.9 1.2 convolution_convert_fusion.1
  65.3 0.0 copy-start.1
  65.4 0.0 collective-permute-done.6.refs_5_
  65.4 1.0 broadcast_in_dim.10
  66.4 0.2 copy-done.4
  66.6 6.8 %all-to-all-start.1 = ((bf16[16,8,3712]{2,1,0:T(8,128)(2,1)}), bf16[16,8,3712]{2,1,0:T(8,128)(2,1)S(1)}, u32[]{:S(2)}, u32[]{:S(2)}) async-start(bf16[16,8,3712]{2,1,0:T(8,128)(2,1)} %bitcast.12), calls=%async_computation.1 | async-start | bytes 1900544 | tf_op jit(solution)/shard_map/all_to_all | solution.py:371
  73.4 1.9 %collective-permute-start.9 = (bf16[1792,128]{1,0:T(8,128)(2,1)S(1)}, bf16[1792,128]{1,0:T(8,128)(2,1)S(1)}, u32[]{:S(2)}, u32[]{:S(2)}) collective-permute-start(bf16[1792,128]{1,0:T(8,128)(2,1)S(1)} %copy-done.6), channel_id=1, source_target_pairs={{0,1},{1,0},{2,3},{3,2},{4,5},{5,4},{6,7},{7,6},{8,9},{9,8},{10,11... | collective-permute-start | bytes 1376264 | tf_op jit(solution)/shard_map/ppermute | solution.py:370
  75.4 2.4 %collective-permute-start.10 = (bf16[1792,128]{1,0:T(8,128)(2,1)}, bf16[1792,128]{1,0:T(8,128)(2,1)S(1)}, u32[]{:S(2)}, u32[]{:S(2)}) collective-permute-start(bf16[1792,128]{1,0:T(8,128)(2,1)} %collective-permute-done.8.refs_1_.refs_7_), channel_id=1, source_target_pairs={{0,1},{1,0},{2,3},{3,2},{4,5},{5,4},{6,7},{7,6},{8,9},{9,8},{10,11... | collective-permute-start | bytes 1376264 | tf_op jit(solution)/shard_map/ppermute | solution.py:370
  77.8 1.6 collective-permute-done.10.refs_9_
  79.4 8.0 %all-to-all-done.1 = bf16[16,8,3712]{2,1,0:T(8,128)(2,1)S(1)} async-done(((bf16[16,8,3712]{2,1,0:T(8,128)(2,1)}), bf16[16,8,3712]{2,1,0:T(8,128)(2,1)S(1)}, u32[]{:S(2)}, u32[]{:S(2)}) %all-to-all-start.1) | async-done | bytes 950304 | tf_op jit(solution)/shard_map/all_to_all | solution.py:371
  87.5 6.5 %shard_map.98 = bf16[4,128,512]{2,1,0:T(8,128)(2,1)} custom-call(s32[5]{0:T(128)S(1)} %copy-done.1, bf16[128,3712]{1,0:T(8,128)(2,1)S(1)} %bitcast.66, bf16[3584,128]{1,0:T(8,128)(2,1)} %copy-done, bf16[3584,128]{1,0:T(8,128)(2,1)} %copy-done.3, bf16[3584,128]{1,0:T(8,128)(2,1)} %collective-permute-done.1.refs_0_.refs_2_, bf16[3584,128]{1,0:T(8,128)(2,1)} %copy-done.4, ...), custom_call_target="tpu_custom_call" | custom-call | tf_op jit(solution)/shard_map/pallas_call | solution.py:260
  94.0 3.5 %all-to-all-start.2 = ((bf16[4,128,512]{2,1,0:T(8,128)(2,1)}), bf16[4,128,512]{2,1,0:T(8,128)(2,1)S(1)}, u32[]{:S(2)}, u32[]{:S(2)}) async-start(bf16[4,128,512]{2,1,0:T(8,128)(2,1)} %shard_map.98), calls=%async_computation.2 | async-start | bytes 1048576 | tf_op jit(solution)/shard_map/all_to_all | solution.py:389
  97.5 0.1 select_reduce_fusion
  97.6 8.7 %all-to-all-done.2 = bf16[4,128,512]{2,1,0:T(8,128)(2,1)S(1)} async-done(((bf16[4,128,512]{2,1,0:T(8,128)(2,1)}), bf16[4,128,512]{2,1,0:T(8,128)(2,1)S(1)}, u32[]{:S(2)}, u32[]{:S(2)}) %all-to-all-start.2) | async-done | bytes 524320 | tf_op jit(solution)/shard_map/all_to_all | solution.py:389
  106.3 0.1 convert_reduce_fusion.1
  106.4 0.1 multiply_convert_fusion
  106.5 12.8 %all-gather = bf16[512,512]{1,0:T(8,128)(2,1)S(1)} all-gather(bf16[128,512]{1,0:T(8,128)(2,1)S(1)} %pad_maximum_fusion.1), channel_id=2, replica_groups=mesh['node'=16,'expert'=4,'chip'=4,'core'=2] {'chip'}, dimensions={0}, use_global_device_ids=true | all-gather | bytes 655360 | tf_op jit(solution)/shard_map/all_gather | solution.py:396
  119.3 5.4 %shard_map.99 = bf16[128,3712]{1,0:T(8,128)(2,1)S(1)} custom-call(s32[5]{0:T(128)S(1)} %copy-done.1, bf16[128,3712]{1,0:T(8,128)(2,1)S(1)} %bitcast.68, bf16[4,128,512]{2,1,0:T(8,128)(2,1)S(1)} %bitcast.70, bf16[3584,128]{1,0:T(8,128)(2,1)} %copy-done, bf16[3584,128]{1,0:T(8,128)(2,1)} %copy-done.3, ...), custom_call_target="tpu_custom_call" | custom-call | tf_op jit(solution)/shard_map/pallas_call | solution.py:260
  124.7 15.5 %all_to_all.25 = bf16[16,8,3712]{2,1,0:T(8,128)(2,1)S(1)} all-to-all(bf16[16,8,3712]{2,1,0:T(8,128)(2,1)S(1)} %bitcast.69), channel_id=1, replica_groups=mesh['node'=16,'expert'=4,'chip'=4,'core'=2] {'expert','chip'}, dimensions={0} | all-to-all | bytes 1900544 | tf_op jit(solution)/shard_map/all_to_all | solution.py:410
  140.2 0.1 convert_reduce_fusion
  140.4 0.3 convolution_convert_fusion
  140.8 0.1 copy.14
  140.9 34.3 %all_to_all.26.home = bf16[16,120,128]{2,1,0:T(8,128)(2,1)S(1)} all-to-all(bf16[16,120,128]{2,1,0:T(8,128)(2,1)S(1)} %bitcast.73), channel_id=1, replica_groups=mesh['node'=16,'expert'=4,'chip'=4,'core'=2] {'node'}, dimensions={0} | all-to-all | bytes 983040 | tf_op jit(solution)/shard_map/all_to_all | solution.py:427
  175.2 1.7 shard_map.100
  (38 shorter events, 0.3 us)
Async XLA Ops:
  0.7 3.8 %copy-start.2 = (bf16[4,2,2]{0,2,1:T(2,128)(2,1)S(1)}, bf16[4,2,2]{0,2,1:T(2,128)(2,1)}, u32[]{:S(2)}) copy-start(bf16[4,2,2]{0,2,1:T(2,128)(2,1)} %param.11) | copy-start | bytes 100
  4.6 47.2 %copy-start = (bf16[3584,128]{1,0:T(8,128)(2,1)}, bf16[3584,128]{1,0:T(8,128)(2,1)S(1)}, u32[]{:S(2)}) copy-start(bf16[3584,128]{1,0:T(8,128)(2,1)S(1)} %get-tuple-element.50.refs_0_) | copy-start | bytes 2752516
  6.5 37.1 %collective-permute-start.1 = (bf16[3584,128]{1,0:T(8,128)(2,1)S(1)}, bf16[3584,128]{1,0:T(8,128)(2,1)}, u32[]{:S(2)}, u32[]{:S(2)}) collective-permute-start(bf16[3584,128]{1,0:T(8,128)(2,1)S(1)} %get-tuple-element.39), channel_id=1, source_target_pairs={{0,2},{2,4},{4,6},{6,0},{1,3},{3,5},{5,7},{7,1},{8,10},{10,12},{12... | collective-permute-start | bytes 2752520 | tf_op jit(solution)/shard_map/ppermute | solution.py:323
  9.9 33.6 %collective-permute-start.2 = (bf16[3584,128]{1,0:T(8,128)(2,1)S(1)}, bf16[3584,128]{1,0:T(8,128)(2,1)}, u32[]{:S(2)}, u32[]{:S(2)}) collective-permute-start(bf16[3584,128]{1,0:T(8,128)(2,1)S(1)} %get-tuple-element.40), channel_id=1, source_target_pairs={{0,6},{2,0},{4,2},{6,4},{1,7},{3,1},{5,3},{7,5},{8,14},{10,8},{12,... | collective-permute-start | bytes 2752520 | tf_op jit(solution)/shard_map/ppermute | solution.py:324
  13.6 28.1 %collective-permute-start.3 = (bf16[1792,128]{1,0:T(8,128)(2,1)}, bf16[1792,128]{1,0:T(8,128)(2,1)}, u32[]{:S(2)}, u32[]{:S(2)}) collective-permute-start(bf16[1792,128]{1,0:T(8,128)(2,1)} %get-tuple-element.41), channel_id=1, source_target_pairs={{0,2},{2,4},{4,6},{6,0},{1,3},{3,5},{5,7},{7,1},{8,10},{10,12},{12... | collective-permute-start | bytes 1376264 | tf_op jit(solution)/shard_map/ppermute | solution.py:321
  15.8 27.8 %collective-permute-start.4 = (bf16[1792,128]{1,0:T(8,128)(2,1)S(1)}, bf16[1792,128]{1,0:T(8,128)(2,1)}, u32[]{:S(2)}, u32[]{:S(2)}) collective-permute-start(bf16[1792,128]{1,0:T(8,128)(2,1)S(1)} %get-tuple-element.42), channel_id=1, source_target_pairs={{0,6},{2,0},{4,2},{6,4},{1,7},{3,1},{5,3},{7,5},{8,14},{10,8},{12,... | collective-permute-start | bytes 1376264 | tf_op jit(solution)/shard_map/ppermute | solution.py:322
  20.6 41.9 %all-to-all-start = ((bf16[16,120,128]{2,1,0:T(8,128)(2,1)}), bf16[16,120,128]{2,1,0:T(8,128)(2,1)}, u32[]{:S(2)}, u32[]{:S(2)}) async-start(bf16[16,120,128]{2,1,0:T(8,128)(2,1)} %shard_map.95), calls=%async_computation | async-start | bytes 983040 | tf_op jit(solution)/shard_map/all_to_all | solution.py:336
  44.8 14.4 %collective-permute-start.7 = (bf16[1792,128]{1,0:T(8,128)(2,1)}, bf16[1792,128]{1,0:T(8,128)(2,1)S(1)}, u32[]{:S(2)}, u32[]{:S(2)}) collective-permute-start(bf16[1792,128]{1,0:T(8,128)(2,1)} %collective-permute-done.3.refs_2_), channel_id=1, source_target_pairs={{0,2},{2,4},{4,6},{6,0},{1,3},{3,5},{5,7},{7,1},{8,10},{10,12},{12... | collective-permute-start | bytes 1376264 | tf_op jit(solution)/shard_map/ppermute | solution.py:333
  48.2 13.0 %collective-permute-start.8 = (bf16[1792,128]{1,0:T(8,128)(2,1)}, bf16[1792,128]{1,0:T(8,128)(2,1)}, u32[]{:S(2)}, u32[]{:S(2)}) collective-permute-start(bf16[1792,128]{1,0:T(8,128)(2,1)} %collective-permute-done.4.refs_3_), channel_id=1, source_target_pairs={{0,6},{2,0},{4,2},{6,4},{1,7},{3,1},{5,3},{7,5},{8,14},{10,8},{12,... | collective-permute-start | bytes 1376264 | tf_op jit(solution)/shard_map/ppermute | solution.py:334
  51.8 13.5 %collective-permute-start = (bf16[3584,128]{1,0:T(8,128)(2,1)S(1)}, bf16[3584,128]{1,0:T(8,128)(2,1)S(1)}, u32[]{:S(2)}, u32[]{:S(2)}) collective-permute-start(bf16[3584,128]{1,0:T(8,128)(2,1)S(1)} %get-tuple-element.50.refs_0_), channel_id=1, source_target_pairs={{0,1},{1,0},{2,3},{3,2},{4,5},{5,4},{6,7},{7,6},{8,9},{9,8},{10,11... | collective-permute-start | bytes 2752520 | tf_op jit(solution)/shard_map/ppermute | solution.py:325
  53.8 11.6 %collective-permute-start.5 = (bf16[3584,128]{1,0:T(8,128)(2,1)}, bf16[3584,128]{1,0:T(8,128)(2,1)S(1)}, u32[]{:S(2)}, u32[]{:S(2)}) collective-permute-start(bf16[3584,128]{1,0:T(8,128)(2,1)} %collective-permute-done.1.refs_0_.refs_2_), channel_id=1, source_target_pairs={{0,1},{1,0},{2,3},{3,2},{4,5},{5,4},{6,7},{7,6},{8,9},{9,8},{10,11... | collective-permute-start | bytes 2752520 | tf_op jit(solution)/shard_map/ppermute | solution.py:364
  56.2 9.2 %collective-permute-start.6 = (bf16[3584,128]{1,0:T(8,128)(2,1)}, bf16[3584,128]{1,0:T(8,128)(2,1)}, u32[]{:S(2)}, u32[]{:S(2)}) collective-permute-start(bf16[3584,128]{1,0:T(8,128)(2,1)} %collective-permute-done.2.refs_1_.refs_4_), channel_id=1, source_target_pairs={{0,1},{1,0},{2,3},{3,2},{4,5},{5,4},{6,7},{7,6},{8,9},{9,8},{10,11... | collective-permute-start | bytes 2752520 | tf_op jit(solution)/shard_map/ppermute | solution.py:364
  59.1 2.0 %copy-start.5 = (bf16[1792,128]{1,0:T(8,128)(2,1)}, bf16[1792,128]{1,0:T(8,128)(2,1)S(1)}, u32[]{:S(2)}) copy-start(bf16[1792,128]{1,0:T(8,128)(2,1)S(1)} %collective-permute-done.7.refs_0_.refs_6_) | copy-start | bytes 1376260
  65.3 8.2 %copy-start.6 = (bf16[1792,128]{1,0:T(8,128)(2,1)S(1)}, bf16[1792,128]{1,0:T(8,128)(2,1)}, u32[]{:S(2)}) copy-start(bf16[1792,128]{1,0:T(8,128)(2,1)} %copy-done.5) | copy-start | bytes 1376260
  65.3 22.2 %copy-start.1 = (s32[5]{0:T(128)S(1)}, s32[5]{0:T(128)}, u32[]{:S(2)}) copy-start(s32[5]{0:T(128)} %shard_map.97.scalars) | copy-start | bytes 64
  65.3 22.1 %copy-start.3 = (bf16[3584,128]{1,0:T(8,128)(2,1)}, bf16[3584,128]{1,0:T(8,128)(2,1)S(1)}, u32[]{:S(2)}) copy-start(bf16[3584,128]{1,0:T(8,128)(2,1)S(1)} %collective-permute-done.refs_1_) | copy-start | bytes 2752516
  65.4 1.3 copy-start.4
  66.6 20.8 %all-to-all-start.1 = ((bf16[16,8,3712]{2,1,0:T(8,128)(2,1)}), bf16[16,8,3712]{2,1,0:T(8,128)(2,1)S(1)}, u32[]{:S(2)}, u32[]{:S(2)}) async-start(bf16[16,8,3712]{2,1,0:T(8,128)(2,1)} %bitcast.12), calls=%async_computation.1 | async-start | bytes 1900544 | tf_op jit(solution)/shard_map/all_to_all | solution.py:371
  73.4 4.3 %collective-permute-start.9 = (bf16[1792,128]{1,0:T(8,128)(2,1)S(1)}, bf16[1792,128]{1,0:T(8,128)(2,1)S(1)}, u32[]{:S(2)}, u32[]{:S(2)}) collective-permute-start(bf16[1792,128]{1,0:T(8,128)(2,1)S(1)} %copy-done.6), channel_id=1, source_target_pairs={{0,1},{1,0},{2,3},{3,2},{4,5},{5,4},{6,7},{7,6},{8,9},{9,8},{10,11... | collective-permute-start | bytes 1376264 | tf_op jit(solution)/shard_map/ppermute | solution.py:370
  75.4 4.0 %collective-permute-start.10 = (bf16[1792,128]{1,0:T(8,128)(2,1)}, bf16[1792,128]{1,0:T(8,128)(2,1)S(1)}, u32[]{:S(2)}, u32[]{:S(2)}) collective-permute-start(bf16[1792,128]{1,0:T(8,128)(2,1)} %collective-permute-done.8.refs_1_.refs_7_), channel_id=1, source_target_pairs={{0,1},{1,0},{2,3},{3,2},{4,5},{5,4},{6,7},{7,6},{8,9},{9,8},{10,11... | collective-permute-start | bytes 1376264 | tf_op jit(solution)/shard_map/ppermute | solution.py:370
  94.0 12.3 %all-to-all-start.2 = ((bf16[4,128,512]{2,1,0:T(8,128)(2,1)}), bf16[4,128,512]{2,1,0:T(8,128)(2,1)S(1)}, u32[]{:S(2)}, u32[]{:S(2)}) async-start(bf16[4,128,512]{2,1,0:T(8,128)(2,1)} %shard_map.98), calls=%async_computation.2 | async-start | bytes 1048576 | tf_op jit(solution)/shard_map/all_to_all | solution.py:389

commit v16 on v14

--- a/solution.py
+++ b/solution.py
@@ -163,18 +163,18 @@
     return [item for items in lists for item in items]
 
 
-def mark_kernel(scalars, *refs):
-    for i in range(scalars.shape[0]):
-        refs[-1][i] = scalars[i]
+def mark_kernel(*refs):
+    pass
 
 
 def mark(scalars, flops, *arrays):
-    small = pl.BlockSpec(memory_space=pltpu.SMEM)
+    spec = pl.BlockSpec(memory_space=pl.ANY)
     return pl.pallas_call(
         mark_kernel,
         out_shape=jax.ShapeDtypeStruct(scalars.shape, scalars.dtype),
-        in_specs=[small] + [pl.BlockSpec(memory_space=pl.ANY)] * len(arrays),
-        out_specs=small,
+        in_specs=[spec] * (1 + len(arrays)),
+        out_specs=spec,
+        input_output_aliases={0: 0},
         cost_estimate=pl.CostEstimate(flops=flops, bytes_accessed=4096, transcendentals=0),
     )(scalars, *arrays)
 

time: 178 us -> 176 us (0.989)
  waiting for transfers between devices: 28.7 us -> 31.1 us
  Pallas kernels: 21.7 us -> 19.3 us
  starting transfers between devices: 57.3 us -> 55.1 us
    all_to_all x1, waiting for transfers between devices: 0.16 us -> 2.56 us  [per_device(): recv = lax.all_to_all(sent, 'node', split_axis=0, concat_axis=0, tiled=True)]
    pallas_call x2, Pallas kernels: 2.37 us -> 0.01 us  [mark(): pl.pallas_call(mark_kernel, out_shape=jax.ShapeDtypeStruct(scalars.shape,...]
    all_to_all x1, starting transfers between devices: 6.83 us -> 4.65 us  [per_device(): lax.all_to_all(spread, ('expert', 'chip'), split_axis=0, concat_axis=0, t...]
  transfers between devices with their start and end apart: 14 -> 14, of which waited for: 8 -> 8; matrix products, arithmetic and copies ran while one was open for 0% -> 0% of each run, Pallas kernels for 1% -> 0%
where the time goes in v16:
time: 176 us; the launch traced here: 175 us
  blocking collectives  63.1 us (36%)
  starting transfers between devices  55.1 us (31%)
  waiting for transfers between devices  31.1 us (18%)
  Pallas kernels  19.3 us (11%)
  local copies, waits for them, and re-layouts  1.97 us (1%)
  other arithmetic  1.89 us (1%)
    all_to_all x1, blocking collectives, per_device(): lax.all_to_all(expanded, 'node', split_axis=0, concat_axis=0, tiled=True)  34.6 us
    pallas_call x5, Pallas kernels, call(): pl.pallas_call(kernel, out_shape=[jax.ShapeDtypeStruct(shape, jnp.bfloat1...  19.3 us
    all_to_all x1, starting transfers between devices, per_device(): recv = lax.all_to_all(sent, 'node', split_axis=0, concat_axis=0, tiled=True)  15.2 us
    all_to_all x1, blocking collectives, per_device(): lax.all_to_all(result.reshape(experts * chips, pairs, -1), ('expert', 'ch...  15.1 us
    all_gather x1, blocking collectives, per_device(): lax.all_gather(jnp.concatenate([active, grad_pre], 1), 'chip', axis=0)  13.4 us
    all_to_all x1, waiting for transfers between devices, per_device(): lax.all_to_all(spread, ('expert', 'chip'), split_axis=0, concat_axis=0, t...  8.91 us
    ppermute x2, starting transfers between devices, per_device(): far_down = lax.ppermute(far_down, 'chip', behind_of)  8.52 us
    all_to_all x1, waiting for transfers between devices, per_device(): lax.all_to_all(outgoing, 'chip', split_axis=0, concat_axis=0, tiled=True)  7.93 us
  transfers between devices with their start and end apart: 14, of which 8 were waited for; matrix products, arithmetic and copies ran while one was open for 0% of the time, Pallas kernels for 0%

profile of v16, /device:TPU:32, one launch (start us, length us, event | category | flops | bytes accessed | tf_op | source)
XLA Modules:
  0.0 175.1 jit_solution(5863406666456491759)
XLA Ops:
  0.7 0.1 pad_add_fusion.chips
  0.8 3.8 %shard_map.94 = (bf16[3584,128]{1,0:T(8,128)(2,1)S(1)}, bf16[3584,128]{1,0:T(8,128)(2,1)S(1)}, bf16[3584,128]{1,0:T(8,128)(2,1)S(1)}, bf16[1792,128]{1,0:T(8,128)(2,1)}, bf16[1792,128]{1,0:T(8,128)(2,1)S(1)}) custom-call(s32[4]{0:T(128)S(1)} %pad_add_fusion.chips, bf16[7168,128]{1,0:T(8,128)(2,1)} %up.1, bf16[128,7168]{1,0:T(8,128)(2,1)} %down.1), custom_call_target="tpu_custom_call" | custom-call | tf_op jit(solution)/shard_map/pallas_call | solution.py:260
  4.6 1.9 %shard_map.95 = bf16[16,120,128]{2,1,0:T(8,128)(2,1)} custom-call(bf16[2,2,4]{2,1,0:T(2,128)(2,1)S(1)} %bitcast.71, s32[2,4]{1,0:T(2,128)} %bitcast.76, s32[2,2,4]{2,1,0:T(2,128)} %bitcast.74, bf16[4,7168]{1,0:T(4,128)(2,1)} %tokens.1, bf16[4,7168]{1,0:T(4,128)(2,1)} %cotangent.1), custom_call_target="tpu_custom_call" | custom-call | tf_op jit(solution)/shard_map/pallas_call | solution.py:260
  6.5 3.4 %collective-permute-start.1 = (bf16[3584,128]{1,0:T(8,128)(2,1)S(1)}, bf16[3584,128]{1,0:T(8,128)(2,1)}, u32[]{:S(2)}, u32[]{:S(2)}) collective-permute-start(bf16[3584,128]{1,0:T(8,128)(2,1)S(1)} %get-tuple-element.39), channel_id=1, source_target_pairs={{0,2},{2,4},{4,6},{6,0},{1,3},{3,5},{5,7},{7,1},{8,10},{10,12},{12... | collective-permute-start | bytes 2752520 | tf_op jit(solution)/shard_map/ppermute | solution.py:323
  9.9 3.7 %collective-permute-start.2 = (bf16[3584,128]{1,0:T(8,128)(2,1)S(1)}, bf16[3584,128]{1,0:T(8,128)(2,1)}, u32[]{:S(2)}, u32[]{:S(2)}) collective-permute-start(bf16[3584,128]{1,0:T(8,128)(2,1)S(1)} %get-tuple-element.40), channel_id=1, source_target_pairs={{0,6},{2,0},{4,2},{6,4},{1,7},{3,1},{5,3},{7,5},{8,14},{10,8},{12,... | collective-permute-start | bytes 2752520 | tf_op jit(solution)/shard_map/ppermute | solution.py:324
  13.6 2.2 %collective-permute-start.3 = (bf16[1792,128]{1,0:T(8,128)(2,1)}, bf16[1792,128]{1,0:T(8,128)(2,1)}, u32[]{:S(2)}, u32[]{:S(2)}) collective-permute-start(bf16[1792,128]{1,0:T(8,128)(2,1)} %get-tuple-element.41), channel_id=1, source_target_pairs={{0,2},{2,4},{4,6},{6,0},{1,3},{3,5},{5,7},{7,1},{8,10},{10,12},{12... | collective-permute-start | bytes 1376264 | tf_op jit(solution)/shard_map/ppermute | solution.py:321
  15.8 4.9 %collective-permute-start.4 = (bf16[1792,128]{1,0:T(8,128)(2,1)S(1)}, bf16[1792,128]{1,0:T(8,128)(2,1)}, u32[]{:S(2)}, u32[]{:S(2)}) collective-permute-start(bf16[1792,128]{1,0:T(8,128)(2,1)S(1)} %get-tuple-element.42), channel_id=1, source_target_pairs={{0,6},{2,0},{4,2},{6,4},{1,7},{3,1},{5,3},{7,5},{8,14},{10,8},{12,... | collective-permute-start | bytes 1376264 | tf_op jit(solution)/shard_map/ppermute | solution.py:322
  20.6 15.2 %all-to-all-start = ((bf16[16,120,128]{2,1,0:T(8,128)(2,1)}), bf16[16,120,128]{2,1,0:T(8,128)(2,1)}, u32[]{:S(2)}, u32[]{:S(2)}) async-start(bf16[16,120,128]{2,1,0:T(8,128)(2,1)} %shard_map.95), calls=%async_computation | async-start | bytes 983040 | tf_op jit(solution)/shard_map/all_to_all | solution.py:336
  35.9 0.7 stack.49.refs_0_
  36.5 5.1 %collective-permute-done.3.refs_3_ = bf16[1792,128]{1,0:T(8,128)(2,1)} collective-permute-done((bf16[1792,128]{1,0:T(8,128)(2,1)}, bf16[1792,128]{1,0:T(8,128)(2,1)}, u32[]{:S(2)}, u32[]{:S(2)}) %collective-permute-start.3) | collective-permute-done | bytes 458784 | tf_op jit(solution)/shard_map/ppermute | solution.py:321
  41.6 1.9 %collective-permute-done.4.refs_4_ = bf16[1792,128]{1,0:T(8,128)(2,1)} collective-permute-done((bf16[1792,128]{1,0:T(8,128)(2,1)S(1)}, bf16[1792,128]{1,0:T(8,128)(2,1)}, u32[]{:S(2)}, u32[]{:S(2)}) %collective-permute-start.4) | collective-permute-done | bytes 458784 | tf_op jit(solution)/shard_map/ppermute | solution.py:322
  43.6 0.0 collective-permute-done.1.refs_1_.refs_2_
  43.6 0.0 collective-permute-done.2.refs_2_.refs_4_
  43.6 3.4 %collective-permute-start.7 = (bf16[1792,128]{1,0:T(8,128)(2,1)}, bf16[1792,128]{1,0:T(8,128)(2,1)S(1)}, u32[]{:S(2)}, u32[]{:S(2)}) collective-permute-start(bf16[1792,128]{1,0:T(8,128)(2,1)} %collective-permute-done.3.refs_3_), channel_id=1, source_target_pairs={{0,2},{2,4},{4,6},{6,0},{1,3},{3,5},{5,7},{7,1},{8,10},{10,12},{12... | collective-permute-start | bytes 1376264 | tf_op jit(solution)/shard_map/ppermute | solution.py:333
  47.0 3.7 %collective-permute-start.8 = (bf16[1792,128]{1,0:T(8,128)(2,1)}, bf16[1792,128]{1,0:T(8,128)(2,1)}, u32[]{:S(2)}, u32[]{:S(2)}) collective-permute-start(bf16[1792,128]{1,0:T(8,128)(2,1)} %collective-permute-done.4.refs_4_), channel_id=1, source_target_pairs={{0,6},{2,0},{4,2},{6,4},{1,7},{3,1},{5,3},{7,5},{8,14},{10,8},{12,... | collective-permute-start | bytes 1376264 | tf_op jit(solution)/shard_map/ppermute | solution.py:334
  50.6 1.9 %collective-permute-start = (bf16[3584,128]{1,0:T(8,128)(2,1)S(1)}, bf16[3584,128]{1,0:T(8,128)(2,1)S(1)}, u32[]{:S(2)}, u32[]{:S(2)}) collective-permute-start(bf16[3584,128]{1,0:T(8,128)(2,1)S(1)} %get-tuple-element.50.refs_0_), channel_id=1, source_target_pairs={{0,1},{1,0},{2,3},{3,2},{4,5},{5,4},{6,7},{7,6},{8,9},{9,8},{10,11... | collective-permute-start | bytes 2752520 | tf_op jit(solution)/shard_map/ppermute | solution.py:325
  52.6 2.4 %collective-permute-start.5 = (bf16[3584,128]{1,0:T(8,128)(2,1)}, bf16[3584,128]{1,0:T(8,128)(2,1)S(1)}, u32[]{:S(2)}, u32[]{:S(2)}) collective-permute-start(bf16[3584,128]{1,0:T(8,128)(2,1)} %collective-permute-done.1.refs_1_.refs_2_), channel_id=1, source_target_pairs={{0,1},{1,0},{2,3},{3,2},{4,5},{5,4},{6,7},{7,6},{8,9},{9,8},{10,11... | collective-permute-start | bytes 2752520 | tf_op jit(solution)/shard_map/ppermute | solution.py:339
  55.0 1.9 %collective-permute-start.6 = (bf16[3584,128]{1,0:T(8,128)(2,1)}, bf16[3584,128]{1,0:T(8,128)(2,1)}, u32[]{:S(2)}, u32[]{:S(2)}) collective-permute-start(bf16[3584,128]{1,0:T(8,128)(2,1)} %collective-permute-done.2.refs_2_.refs_4_), channel_id=1, source_target_pairs={{0,1},{1,0},{2,3},{3,2},{4,5},{5,4},{6,7},{7,6},{8,9},{9,8},{10,11... | collective-permute-start | bytes 2752520 | tf_op jit(solution)/shard_map/ppermute | solution.py:339
  56.9 1.0 collective-permute-done.7.refs_1_.refs_6_
  58.0 2.0 %collective-permute-done.8.refs_2_.refs_7_ = bf16[1792,128]{1,0:T(8,128)(2,1)} collective-permute-done((bf16[1792,128]{1,0:T(8,128)(2,1)}, bf16[1792,128]{1,0:T(8,128)(2,1)}, u32[]{:S(2)}, u32[]{:S(2)}) %collective-permute-start.8) | collective-permute-done | bytes 458784 | tf_op jit(solution)/shard_map/ppermute | solution.py:334
  60.0 0.0 collective-permute-done.refs_1_
  60.0 0.0 collective-permute-done.5.refs_3_
  60.0 0.0 collective-permute-done.6.refs_5_
  60.0 2.6 %all-to-all-done = bf16[16,120,128]{2,1,0:T(8,128)(2,1)} async-done(((bf16[16,120,128]{2,1,0:T(8,128)(2,1)}), bf16[16,120,128]{2,1,0:T(8,128)(2,1)}, u32[]{:S(2)}, u32[]{:S(2)}) %all-to-all-start) | async-done | bytes 491552 | tf_op jit(solution)/shard_map/all_to_all | solution.py:336
  62.6 1.1 compare_reduce_fusion
  63.7 0.1 copy.14
  63.8 0.1 add_reduce_fusion
  64.0 1.2 convolution_convert_fusion.1
  65.3 1.0 broadcast_in_dim.10
  66.4 4.6 %all-to-all-start.1 = ((bf16[16,8,3712]{2,1,0:T(8,128)(2,1)}), bf16[16,8,3712]{2,1,0:T(8,128)(2,1)S(1)}, u32[]{:S(2)}, u32[]{:S(2)}) async-start(bf16[16,8,3712]{2,1,0:T(8,128)(2,1)} %bitcast.14), calls=%async_computation.1 | async-start | bytes 1900544 | tf_op jit(solution)/shard_map/all_to_all | solution.py:371
  71.0 1.9 %collective-permute-start.9 = (bf16[1792,128]{1,0:T(8,128)(2,1)S(1)}, bf16[1792,128]{1,0:T(8,128)(2,1)S(1)}, u32[]{:S(2)}, u32[]{:S(2)}) collective-permute-start(bf16[1792,128]{1,0:T(8,128)(2,1)S(1)} %copy-done.6), channel_id=1, source_target_pairs={{0,1},{1,0},{2,3},{3,2},{4,5},{5,4},{6,7},{7,6},{8,9},{9,8},{10,11... | collective-permute-start | bytes 1376264 | tf_op jit(solution)/shard_map/ppermute | solution.py:345
  72.9 2.4 %collective-permute-start.10 = (bf16[1792,128]{1,0:T(8,128)(2,1)}, bf16[1792,128]{1,0:T(8,128)(2,1)S(1)}, u32[]{:S(2)}, u32[]{:S(2)}) collective-permute-start(bf16[1792,128]{1,0:T(8,128)(2,1)} %collective-permute-done.8.refs_2_.refs_7_), channel_id=1, source_target_pairs={{0,1},{1,0},{2,3},{3,2},{4,5},{5,4},{6,7},{7,6},{8,9},{9,8},{10,11... | collective-permute-start | bytes 1376264 | tf_op jit(solution)/shard_map/ppermute | solution.py:345
  75.4 1.6 collective-permute-done.10.refs_9_
  77.0 8.9 %all-to-all-done.1 = bf16[16,8,3712]{2,1,0:T(8,128)(2,1)S(1)} async-done(((bf16[16,8,3712]{2,1,0:T(8,128)(2,1)}), bf16[16,8,3712]{2,1,0:T(8,128)(2,1)S(1)}, u32[]{:S(2)}, u32[]{:S(2)}) %all-to-all-start.1) | async-done | bytes 950304 | tf_op jit(solution)/shard_map/all_to_all | solution.py:371
  85.9 6.5 %shard_map.98 = bf16[4,128,512]{2,1,0:T(8,128)(2,1)} custom-call(s32[5]{0:T(128)S(1)} %copy-done.1, bf16[128,3712]{1,0:T(8,128)(2,1)S(1)} %bitcast.66, bf16[3584,128]{1,0:T(8,128)(2,1)} %copy-done, bf16[3584,128]{1,0:T(8,128)(2,1)} %copy-done.3, bf16[3584,128]{1,0:T(8,128)(2,1)} %collective-permute-done.1.refs_1_.refs_2_, bf16[3584,128]{1,0:T(8,128)(2,1)} %copy-done.4, ...), custom_call_target="tpu_custom_call" | custom-call | tf_op jit(solution)/shard_map/pallas_call | solution.py:260
  92.4 3.5 %all-to-all-start.2 = ((bf16[4,128,512]{2,1,0:T(8,128)(2,1)}), bf16[4,128,512]{2,1,0:T(8,128)(2,1)S(1)}, u32[]{:S(2)}, u32[]{:S(2)}) async-start(bf16[4,128,512]{2,1,0:T(8,128)(2,1)} %shard_map.98), calls=%async_computation.2 | async-start | bytes 1048576 | tf_op jit(solution)/shard_map/all_to_all | solution.py:389
  95.9 0.1 select_reduce_fusion
  96.0 7.9 %all-to-all-done.2 = bf16[4,128,512]{2,1,0:T(8,128)(2,1)S(1)} async-done(((bf16[4,128,512]{2,1,0:T(8,128)(2,1)}), bf16[4,128,512]{2,1,0:T(8,128)(2,1)S(1)}, u32[]{:S(2)}, u32[]{:S(2)}) %all-to-all-start.2) | async-done | bytes 524320 | tf_op jit(solution)/shard_map/all_to_all | solution.py:389
  104.0 0.1 convert_reduce_fusion.1
  104.0 0.1 multiply_convert_fusion
  104.1 13.4 %all-gather = bf16[512,512]{1,0:T(8,128)(2,1)S(1)} all-gather(bf16[128,512]{1,0:T(8,128)(2,1)S(1)} %pad_maximum_fusion.1), channel_id=2, replica_groups=mesh['node'=16,'expert'=4,'chip'=4,'core'=2] {'chip'}, dimensions={0}, use_global_device_ids=true | all-gather | bytes 655360 | tf_op jit(solution)/shard_map/all_gather | solution.py:396
  117.6 5.4 %shard_map.99 = bf16[128,3712]{1,0:T(8,128)(2,1)S(1)} custom-call(s32[5]{0:T(128)S(1)} %copy-done.1, bf16[128,3712]{1,0:T(8,128)(2,1)S(1)} %bitcast.68, bf16[4,128,512]{2,1,0:T(8,128)(2,1)S(1)} %bitcast.70, bf16[3584,128]{1,0:T(8,128)(2,1)} %copy-done, bf16[3584,128]{1,0:T(8,128)(2,1)} %copy-done.3, ...), custom_call_target="tpu_custom_call" | custom-call | tf_op jit(solution)/shard_map/pallas_call | solution.py:260
  123.0 15.1 %all_to_all.25 = bf16[16,8,3712]{2,1,0:T(8,128)(2,1)S(1)} all-to-all(bf16[16,8,3712]{2,1,0:T(8,128)(2,1)S(1)} %bitcast.69), channel_id=1, replica_groups=mesh['node'=16,'expert'=4,'chip'=4,'core'=2] {'expert','chip'}, dimensions={0} | all-to-all | bytes 1900544 | tf_op jit(solution)/shard_map/all_to_all | solution.py:410
  138.1 0.1 convert_reduce_fusion
  138.4 0.3 convolution_convert_fusion
  138.8 0.1 copy.16
  138.9 34.6 %all_to_all.26.home = bf16[16,120,128]{2,1,0:T(8,128)(2,1)S(1)} all-to-all(bf16[16,120,128]{2,1,0:T(8,128)(2,1)S(1)} %bitcast.73), channel_id=1, replica_groups=mesh['node'=16,'expert'=4,'chip'=4,'core'=2] {'node'}, dimensions={0} | all-to-all | bytes 983040 | tf_op jit(solution)/shard_map/all_to_all | solution.py:427
  173.4 1.7 shard_map.100
  (38 shorter events, 0.3 us)
Async XLA Ops:
  0.7 3.8 %copy-start.2 = (bf16[4,2,2]{0,2,1:T(2,128)(2,1)S(1)}, bf16[4,2,2]{0,2,1:T(2,128)(2,1)}, u32[]{:S(2)}) copy-start(bf16[4,2,2]{0,2,1:T(2,128)(2,1)} %param.11) | copy-start | bytes 100
  4.6 46.0 %copy-start = (bf16[3584,128]{1,0:T(8,128)(2,1)}, bf16[3584,128]{1,0:T(8,128)(2,1)S(1)}, u32[]{:S(2)}) copy-start(bf16[3584,128]{1,0:T(8,128)(2,1)S(1)} %get-tuple-element.50.refs_0_) | copy-start | bytes 2752516
  6.5 37.1 %collective-permute-start.1 = (bf16[3584,128]{1,0:T(8,128)(2,1)S(1)}, bf16[3584,128]{1,0:T(8,128)(2,1)}, u32[]{:S(2)}, u32[]{:S(2)}) collective-permute-start(bf16[3584,128]{1,0:T(8,128)(2,1)S(1)} %get-tuple-element.39), channel_id=1, source_target_pairs={{0,2},{2,4},{4,6},{6,0},{1,3},{3,5},{5,7},{7,1},{8,10},{10,12},{12... | collective-permute-start | bytes 2752520 | tf_op jit(solution)/shard_map/ppermute | solution.py:323
  9.9 33.6 %collective-permute-start.2 = (bf16[3584,128]{1,0:T(8,128)(2,1)S(1)}, bf16[3584,128]{1,0:T(8,128)(2,1)}, u32[]{:S(2)}, u32[]{:S(2)}) collective-permute-start(bf16[3584,128]{1,0:T(8,128)(2,1)S(1)} %get-tuple-element.40), channel_id=1, source_target_pairs={{0,6},{2,0},{4,2},{6,4},{1,7},{3,1},{5,3},{7,5},{8,14},{10,8},{12,... | collective-permute-start | bytes 2752520 | tf_op jit(solution)/shard_map/ppermute | solution.py:324
  13.6 28.1 %collective-permute-start.3 = (bf16[1792,128]{1,0:T(8,128)(2,1)}, bf16[1792,128]{1,0:T(8,128)(2,1)}, u32[]{:S(2)}, u32[]{:S(2)}) collective-permute-start(bf16[1792,128]{1,0:T(8,128)(2,1)} %get-tuple-element.41), channel_id=1, source_target_pairs={{0,2},{2,4},{4,6},{6,0},{1,3},{3,5},{5,7},{7,1},{8,10},{10,12},{12... | collective-permute-start | bytes 1376264 | tf_op jit(solution)/shard_map/ppermute | solution.py:321
  15.8 27.8 %collective-permute-start.4 = (bf16[1792,128]{1,0:T(8,128)(2,1)S(1)}, bf16[1792,128]{1,0:T(8,128)(2,1)}, u32[]{:S(2)}, u32[]{:S(2)}) collective-permute-start(bf16[1792,128]{1,0:T(8,128)(2,1)S(1)} %get-tuple-element.42), channel_id=1, source_target_pairs={{0,6},{2,0},{4,2},{6,4},{1,7},{3,1},{5,3},{7,5},{8,14},{10,8},{12,... | collective-permute-start | bytes 1376264 | tf_op jit(solution)/shard_map/ppermute | solution.py:322
  20.6 41.9 %all-to-all-start = ((bf16[16,120,128]{2,1,0:T(8,128)(2,1)}), bf16[16,120,128]{2,1,0:T(8,128)(2,1)}, u32[]{:S(2)}, u32[]{:S(2)}) async-start(bf16[16,120,128]{2,1,0:T(8,128)(2,1)} %shard_map.95), calls=%async_computation | async-start | bytes 983040 | tf_op jit(solution)/shard_map/all_to_all | solution.py:336
  43.6 14.4 %collective-permute-start.7 = (bf16[1792,128]{1,0:T(8,128)(2,1)}, bf16[1792,128]{1,0:T(8,128)(2,1)S(1)}, u32[]{:S(2)}, u32[]{:S(2)}) collective-permute-start(bf16[1792,128]{1,0:T(8,128)(2,1)} %collective-permute-done.3.refs_3_), channel_id=1, source_target_pairs={{0,2},{2,4},{4,6},{6,0},{1,3},{3,5},{5,7},{7,1},{8,10},{10,12},{12... | collective-permute-start | bytes 1376264 | tf_op jit(solution)/shard_map/ppermute | solution.py:333
  47.0 13.0 %collective-permute-start.8 = (bf16[1792,128]{1,0:T(8,128)(2,1)}, bf16[1792,128]{1,0:T(8,128)(2,1)}, u32[]{:S(2)}, u32[]{:S(2)}) collective-permute-start(bf16[1792,128]{1,0:T(8,128)(2,1)} %collective-permute-done.4.refs_4_), channel_id=1, source_target_pairs={{0,6},{2,0},{4,2},{6,4},{1,7},{3,1},{5,3},{7,5},{8,14},{10,8},{12,... | collective-permute-start | bytes 1376264 | tf_op jit(solution)/shard_map/ppermute | solution.py:334
  50.6 9.3 %collective-permute-start = (bf16[3584,128]{1,0:T(8,128)(2,1)S(1)}, bf16[3584,128]{1,0:T(8,128)(2,1)S(1)}, u32[]{:S(2)}, u32[]{:S(2)}) collective-permute-start(bf16[3584,128]{1,0:T(8,128)(2,1)S(1)} %get-tuple-element.50.refs_0_), channel_id=1, source_target_pairs={{0,1},{1,0},{2,3},{3,2},{4,5},{5,4},{6,7},{7,6},{8,9},{9,8},{10,11... | collective-permute-start | bytes 2752520 | tf_op jit(solution)/shard_map/ppermute | solution.py:325
  52.6 7.4 %collective-permute-start.5 = (bf16[3584,128]{1,0:T(8,128)(2,1)}, bf16[3584,128]{1,0:T(8,128)(2,1)S(1)}, u32[]{:S(2)}, u32[]{:S(2)}) collective-permute-start(bf16[3584,128]{1,0:T(8,128)(2,1)} %collective-permute-done.1.refs_1_.refs_2_), channel_id=1, source_target_pairs={{0,1},{1,0},{2,3},{3,2},{4,5},{5,4},{6,7},{7,6},{8,9},{9,8},{10,11... | collective-permute-start | bytes 2752520 | tf_op jit(solution)/shard_map/ppermute | solution.py:339
  55.0 5.0 %collective-permute-start.6 = (bf16[3584,128]{1,0:T(8,128)(2,1)}, bf16[3584,128]{1,0:T(8,128)(2,1)}, u32[]{:S(2)}, u32[]{:S(2)}) collective-permute-start(bf16[3584,128]{1,0:T(8,128)(2,1)} %collective-permute-done.2.refs_2_.refs_4_), channel_id=1, source_target_pairs={{0,1},{1,0},{2,3},{3,2},{4,5},{5,4},{6,7},{7,6},{8,9},{9,8},{10,11... | collective-permute-start | bytes 2752520 | tf_op jit(solution)/shard_map/ppermute | solution.py:339
  58.0 2.0 %copy-start.5 = (bf16[1792,128]{1,0:T(8,128)(2,1)}, bf16[1792,128]{1,0:T(8,128)(2,1)S(1)}, u32[]{:S(2)}) copy-start(bf16[1792,128]{1,0:T(8,128)(2,1)S(1)} %collective-permute-done.7.refs_1_.refs_6_) | copy-start | bytes 1376260
  60.0 6.4 %copy-start.3 = (bf16[3584,128]{1,0:T(8,128)(2,1)}, bf16[3584,128]{1,0:T(8,128)(2,1)S(1)}, u32[]{:S(2)}) copy-start(bf16[3584,128]{1,0:T(8,128)(2,1)S(1)} %collective-permute-done.refs_1_) | copy-start | bytes 2752516
  60.0 6.4 %copy-start.4 = (bf16[3584,128]{1,0:T(8,128)(2,1)}, bf16[3584,128]{1,0:T(8,128)(2,1)S(1)}, u32[]{:S(2)}) copy-start(bf16[3584,128]{1,0:T(8,128)(2,1)S(1)} %collective-permute-done.5.refs_3_) | copy-start | bytes 2752516
  65.3 5.7 %copy-start.6 = (bf16[1792,128]{1,0:T(8,128)(2,1)S(1)}, bf16[1792,128]{1,0:T(8,128)(2,1)}, u32[]{:S(2)}) copy-start(bf16[1792,128]{1,0:T(8,128)(2,1)} %copy-done.5) | copy-start | bytes 1376260
  65.3 20.6 %copy-start.1 = (s32[5]{0:T(128)S(1)}, s32[5]{0:T(128)}, u32[]{:S(2)}) copy-start(s32[5]{0:T(128)} %shard_map.97.scalars) | copy-start | bytes 64
  66.4 19.6 %all-to-all-start.1 = ((bf16[16,8,3712]{2,1,0:T(8,128)(2,1)}), bf16[16,8,3712]{2,1,0:T(8,128)(2,1)S(1)}, u32[]{:S(2)}, u32[]{:S(2)}) async-start(bf16[16,8,3712]{2,1,0:T(8,128)(2,1)} %bitcast.14), calls=%async_computation.1 | async-start | bytes 1900544 | tf_op jit(solution)/shard_map/all_to_all | solution.py:371
  71.0 4.3 %collective-permute-start.9 = (bf16[1792,128]{1,0:T(8,128)(2,1)S(1)}, bf16[1792,128]{1,0:T(8,128)(2,1)S(1)}, u32[]{:S(2)}, u32[]{:S(2)}) collective-permute-start(bf16[1792,128]{1,0:T(8,128)(2,1)S(1)} %copy-done.6), channel_id=1, source_target_pairs={{0,1},{1,0},{2,3},{3,2},{4,5},{5,4},{6,7},{7,6},{8,9},{9,8},{10,11... | collective-permute-start | bytes 1376264 | tf_op jit(solution)/shard_map/ppermute | solution.py:345
  72.9 4.0 %collective-permute-start.10 = (bf16[1792,128]{1,0:T(8,128)(2,1)}, bf16[1792,128]{1,0:T(8,128)(2,1)S(1)}, u32[]{:S(2)}, u32[]{:S(2)}) collective-permute-start(bf16[1792,128]{1,0:T(8,128)(2,1)} %collective-permute-done.8.refs_2_.refs_7_), channel_id=1, source_target_pairs={{0,1},{1,0},{2,3},{3,2},{4,5},{5,4},{6,7},{7,6},{8,9},{9,8},{10,11... | collective-permute-start | bytes 1376264 | tf_op jit(solution)/shard_map/ppermute | solution.py:345
  92.4 11.5 %all-to-all-start.2 = ((bf16[4,128,512]{2,1,0:T(8,128)(2,1)}), bf16[4,128,512]{2,1,0:T(8,128)(2,1)S(1)}, u32[]{:S(2)}, u32[]{:S(2)}) async-start(bf16[4,128,512]{2,1,0:T(8,128)(2,1)} %shard_map.98), calls=%async_computation.2 | async-start | bytes 1048576 | tf_op jit(solution)/shard_map/all_to_all | solution.py:389
